TPU v7x, 32 devices: a whole 2x2x4 slice. The times are simulated.
32 devices in a mesh: leaf: 2 (over x), row: 4 (over y, core), col: 4 (over z).
Axes of the slice: x: 2, y: 2, z: 4, core: 2. Of those that a mesh axis runs over, the one named last changes fastest.
Arguments:
- tokens: bfloat16 [20480, 1152], P(('leaf', 'col'), 'row'), parts along dimension 0, may hold values from -6 to 6
- attention_gain: bfloat16 [1152], P('row'), may hold values from 0.5 to 1.5
- joint_weight: bfloat16 [1152, 1920], P('row', 'col'), may hold values from -0.1875 to 0.1875
- output_weight: bfloat16 [1152, 1152], P('col', 'row'), may hold values from -4 to 4
- feed_gain: bfloat16 [1152], P('row'), may hold values from 0.5 to 1.5
- gate_weight: bfloat16 [1152, 3072], P('row', 'col'), may hold values from -0.1875 to 0.1875
- up_weight: bfloat16 [1152, 3072], P('row', 'col'), may hold values from -0.1875 to 0.1875
- down_weight: bfloat16 [3072, 1152], P('col', 'row'), may hold values from -0.109375 to 0.109375
- cotangent: bfloat16 [20480, 1152], P(('leaf', 'col'), 'row'), parts along dimension 0, may hold values from -6 to 6
- segment_lengths: int32 [26], P('leaf'), parts along dimension 0, may hold values from 256 to 4096, as said below
- parents: int32 [26], P('leaf'), parts along dimension 0, may hold values from 0 to 4, as said below
Outputs:
- layer_output: bfloat16 [20480, 1152], P(('leaf', 'col'), 'row'), parts along dimension 0
- input_gradient: float32 [20480, 1152], P(('leaf', 'col'), 'row'), parts along dimension 0
- attention_gain_gradient: float32 [2304], P(('leaf', 'row')), parts along dimension 0
- joint_gradient: float32 [2304, 1920], P(('leaf', 'row'), 'col'), parts along dimension 0
- output_gradient: float32 [2304, 1152], P(('leaf', 'col'), 'row'), parts along dimension 0
- feed_gain_gradient: float32 [2304], P(('leaf', 'row')), parts along dimension 0
- gate_gradient: float32 [2304, 3072], P(('leaf', 'row'), 'col'), parts along dimension 0
- up_gradient: float32 [2304, 3072], P(('leaf', 'row'), 'col'), parts along dimension 0
- down_gradient: float32 [6144, 1152], P(('leaf', 'col'), 'row'), parts along dimension 0
There are 2 independent parts, one for each index of `leaf`. A program takes and returns all parts, laid end to end along the dimension named above; an argument that names none is the same for every part. Nothing has to cross between parts.
Inputs may be any that keep to these rules, and one draw needn't show every extreme that they name: `segment_lengths`: each tree has 13 segments laid out in this order: a trunk of 4096 tokens, four branches, eight leaves; each tree holds 10240 tokens. `parents`: segment numbers count from 0 within each part. A trunk is its own parent, every branch's parent is its tree's trunk, and each branch is the parent of two leaves of its tree.
All inputs are finite; a program needn't handle non-finite values.
Results may differ from a plain program's by a relative error of at most 0.035.
Values may be sent and summed in bfloat16 or wider, within the bound.
No kernel may reach another device: no remote copies, remote signals or barrier semaphores. Data moves between devices by JAX's collectives and lax.ppermute only.
A program may use at most 384 MiB of HBM per device.

v0:
```python
from functools import partial

import jax
import jax.numpy as jnp
from jax import lax
from jax.sharding import PartitionSpec as P

D = 1152
HEADS = 18
KV_HEADS = 6
HEAD_DIM = 64


EPSILON = 1e-05
THETA = 10000.0
KEY_SPAN = 1024


def tree_tables(segment_lengths, parents):
    count = segment_lengths.shape[0]
    ends = jnp.cumsum(segment_lengths)
    starts = ends - segment_lengths
    labels = jnp.arange(count, dtype=jnp.int32)
    grand = parents[parents]
    self_mark = labels[:, None] == labels[None, :]
    parent_mark = parents[:, None] == labels[None, :]
    grand_mark = grand[:, None] == labels[None, :]
    ancestry = (self_mark | parent_mark | grand_mark).astype(jnp.float32)
    strict = (parent_mark | grand_mark) & jnp.logical_not(self_mark)
    offsets = jnp.sum(jnp.where(strict, segment_lengths[None, :], 0), axis=1)
    return (ends, starts, ancestry, offsets)


def token_info(index, tables):
    ends, starts, ancestry, offsets = tables
    count = ends.shape[0]
    segment = jnp.sum((index[:, None] >= ends[None, :]).astype(jnp.int32), axis=1)
    segment_hot = segment[:, None] == jnp.arange(count, dtype=jnp.int32)[None, :]
    shift = jnp.sum(jnp.where(segment_hot, (offsets - starts)[None, :], 0), axis=1)
    depth = index + shift
    return (segment_hot.astype(jnp.float32), depth)


def rotary_tables(depth):
    half = HEAD_DIM // 2
    rates = THETA ** (-jnp.arange(half, dtype=jnp.float32) / half)
    angles = depth.astype(jnp.float32)[:, None] * rates[None, :]
    return (jnp.cos(angles), jnp.sin(angles))


def turn(value, cosines, sines):
    half = value.shape[-1] // 2
    former, latter = (value[..., :half], value[..., half:])
    cos_part = cosines[:, None, :]
    sin_part = sines[:, None, :]
    return jnp.concatenate(
        [former * cos_part - latter * sin_part, latter * cos_part + former * sin_part], axis=-1
    )


def turn_back(value, cosines, sines):
    half = value.shape[-1] // 2
    former, latter = (value[..., :half], value[..., half:])
    cos_part = cosines[:, None, :]
    sin_part = sines[:, None, :]
    return jnp.concatenate(
        [former * cos_part + latter * sin_part, latter * cos_part - former * sin_part], axis=-1
    )


def scan_blocks(carry, pieces, start, block_fn):
    key_piece, value_piece = pieces
    total_rows = key_piece.shape[0]
    count = -(-total_rows // KEY_SPAN)
    while total_rows % count:
        count += 1
    span = total_rows // count
    stacked_keys = key_piece.reshape(count, span, key_piece.shape[1])
    stacked_values = value_piece.reshape(count, span, value_piece.shape[1])
    firsts = jnp.arange(count, dtype=jnp.int32) * span

    def inner(state, item):
        return (block_fn(state, item[0], item[1], item[2]), None)

    carry, _ = lax.scan(inner, carry, (stacked_keys, stacked_values, firsts))
    return carry


def attend(joint_heads, index, tables, row_count, column_count):
    shard_rows = joint_heads.shape[0]
    groups = KV_HEADS
    repeat = HEADS // KV_HEADS
    attend_width = HEADS * HEAD_DIM
    key_width = KV_HEADS * HEAD_DIM
    scale = HEAD_DIM ** (-0.5)
    segment_hot, depth = token_info(index, tables)
    reach = jnp.dot(segment_hot, tables[2], preferred_element_type=jnp.float32)
    cosines, sines = rotary_tables(depth)
    raw = joint_heads.astype(jnp.float32)
    queries = turn(raw[:, :attend_width].reshape(shard_rows, HEADS, HEAD_DIM), cosines, sines)
    queries = queries.astype(jnp.bfloat16).reshape(shard_rows, groups, repeat, HEAD_DIM)
    keys = turn(
        raw[:, attend_width : attend_width + key_width].reshape(shard_rows, groups, HEAD_DIM),
        cosines,
        sines,
    )
    keys = keys.astype(jnp.bfloat16).reshape(shard_rows, key_width)
    values = joint_heads[:, attend_width + key_width :]

    def over_keys(step_fn, start_state):
        return step_fn(
            start_state,
            (
                lax.all_gather(keys, ("row", "col"), axis=0, tiled=True),
                lax.all_gather(values, ("row", "col"), axis=0, tiled=True),
            ),
            jnp.int32(0),
        )

    def scores_at(key_block, first):
        span = key_block.shape[0]
        position = first + jnp.arange(span, dtype=jnp.int32)
        key_hot, _ = token_info(position, tables)
        allowed = (jnp.dot(reach, key_hot.T, preferred_element_type=jnp.float32) > 0.5) & (
            position[None, :] <= index[:, None]
        )
        scores = (
            jnp.einsum(
                "qgrd,kgd->grqk",
                queries,
                key_block.reshape(span, groups, HEAD_DIM),
                preferred_element_type=jnp.float32,
            )
            * scale
        )
        return (scores, allowed[None, None])

    def top_block(state, key_block, value_block, first):
        top, total = state
        scores, allowed = scores_at(key_block, first)
        new_top = jnp.maximum(top, jnp.max(jnp.where(allowed, scores, -1e30), axis=-1))
        weights = jnp.where(allowed, jnp.exp(scores - new_top[..., None]), 0.0)
        return (new_top, total * jnp.exp(top - new_top) + jnp.sum(weights, axis=-1))

    start_state = (
        jnp.full((groups, repeat, shard_rows), -1e30, jnp.float32),
        jnp.zeros((groups, repeat, shard_rows), jnp.float32),
    )
    top, total = over_keys(partial(scan_blocks, block_fn=top_block), start_state)
    log_total = top + jnp.log(total)

    def out_block(summed, key_block, value_block, first):
        span = key_block.shape[0]
        scores, allowed = scores_at(key_block, first)
        weights = jnp.where(allowed, jnp.exp(scores - log_total[..., None]), 0.0).astype(
            jnp.bfloat16
        )
        return summed + jnp.einsum(
            "grqk,kgd->qgrd",
            weights,
            value_block.reshape(span, groups, HEAD_DIM),
            preferred_element_type=jnp.float32,
        )

    summed = over_keys(
        partial(scan_blocks, block_fn=out_block),
        jnp.zeros((shard_rows, groups, repeat, HEAD_DIM), jnp.float32),
    )
    attended = summed.reshape(shard_rows, attend_width)

    def backward(heads_back):
        heads_grouped = heads_back.reshape(shard_rows, groups, repeat, HEAD_DIM)
        delta = jnp.sum(
            (heads_back.astype(jnp.float32) * attended).reshape(
                shard_rows, groups, repeat, HEAD_DIM
            ),
            axis=-1,
        ).transpose(1, 2, 0)

        def grad_block(state, key_block, value_block, first):
            query_back, key_back = state
            span = key_block.shape[0]
            scores, allowed = scores_at(key_block, first)
            chances = jnp.where(allowed, jnp.exp(scores - log_total[..., None]), 0.0)
            key_heads = key_block.reshape(span, groups, HEAD_DIM)
            value_heads = value_block.reshape(span, groups, HEAD_DIM)
            chance_back = jnp.einsum(
                "qgrd,kgd->grqk", heads_grouped, value_heads, preferred_element_type=jnp.float32
            )
            score_back = (chances * (chance_back - delta[..., None])).astype(jnp.bfloat16)
            query_back = (
                query_back
                + jnp.einsum(
                    "grqk,kgd->qgrd", score_back, key_heads, preferred_element_type=jnp.float32
                )
                * scale
            )
            key_part = (
                jnp.einsum(
                    "grqk,qgrd->kgd", score_back, queries, preferred_element_type=jnp.float32
                )
                * scale
            )
            value_part = jnp.einsum(
                "grqk,qgrd->kgd",
                chances.astype(jnp.bfloat16),
                heads_grouped,
                preferred_element_type=jnp.float32,
            )
            update = jnp.concatenate(
                [key_part.reshape(span, key_width), value_part.reshape(span, key_width)], axis=1
            )
            previous = lax.dynamic_slice_in_dim(key_back, first, span, 0)
            return (
                query_back,
                lax.dynamic_update_slice_in_dim(key_back, previous + update, first, 0),
            )

        zero_state = (
            jnp.zeros((shard_rows, groups, repeat, HEAD_DIM), jnp.float32),
            jnp.zeros((shard_rows * row_count * column_count, 2 * key_width), jnp.float32),
        )
        query_back, key_back = over_keys(partial(scan_blocks, block_fn=grad_block), zero_state)
        own_back = lax.psum_scatter(
            key_back.astype(jnp.bfloat16), ("row", "col"), scatter_dimension=0, tiled=True
        ).astype(jnp.float32)
        query_plain = turn_back(
            query_back.reshape(shard_rows, HEADS, HEAD_DIM), cosines, sines
        ).reshape(shard_rows, attend_width)
        key_plain = turn_back(
            own_back[:, :key_width].reshape(shard_rows, groups, HEAD_DIM), cosines, sines
        ).reshape(shard_rows, key_width)
        return jnp.concatenate([query_plain, key_plain, own_back[:, key_width:]], axis=1).astype(
            jnp.bfloat16
        )

    return (attended.astype(jnp.bfloat16), backward)


def norm_apply(value, gain, total_fn):
    square_sum = total_fn(jnp.sum(value * value, axis=1))
    scale_rows = lax.rsqrt(square_sum / D + EPSILON)
    normed = (value * scale_rows[:, None] * gain[None, :]).astype(jnp.bfloat16)
    return (normed, scale_rows)


def norm_back(upstream, value, scale_rows, gain, total_fn):
    weighted = upstream * gain[None, :]
    inner = total_fn(jnp.sum(weighted * value, axis=1))
    value_back = (
        scale_rows[:, None] * weighted
        - value * (scale_rows * scale_rows * scale_rows * inner / D)[:, None]
    )
    gain_back = jnp.sum(upstream * value * scale_rows[:, None], axis=0)
    return (value_back, gain_back)


def swiglu(gate, up_value):
    return gate * jax.nn.sigmoid(gate) * up_value


def swiglu_back(mixed_back, gate, up_value):
    sigmoid_gate = jax.nn.sigmoid(gate)
    gate_back = mixed_back * up_value * (sigmoid_gate * (1.0 + gate * (1.0 - sigmoid_gate)))
    up_back = mixed_back * gate * sigmoid_gate
    return (gate_back, up_back)


def contract(left, right):
    return lax.dot_general(
        left, right, (((0,), (0,)), ((), ())), preferred_element_type=jnp.float32
    )


def per_device(
    tokens,
    attention_gain,
    joint_weight,
    output_weight,
    feed_gain,
    gate_weight,
    up_weight,
    down_weight,
    cotangent,
    segment_lengths,
    parents,
):
    row_count = lax.axis_size("row")
    column_count = lax.axis_size("col")
    tables = tree_tables(segment_lengths, parents)
    gain_one = attention_gain.astype(jnp.float32)
    gain_two = feed_gain.astype(jnp.float32)

    def row_total(value):
        return lax.psum(value, "row")

    def through_rows(part, weight):
        whole = lax.all_gather(part, "col", axis=0, tiled=True)

        def term(begin, count):
            return jnp.dot(whole, weight, preferred_element_type=jnp.float32)

        return (
            whole,
            lax.psum_scatter(
                term(jnp.int32(0), whole.shape[0] // row_count * lax.axis_size("row")).astype(
                    jnp.bfloat16
                ),
                "row",
                scatter_dimension=0,
                tiled=True,
            ).astype(jnp.float32),
        )

    def through_columns(part, weight):
        whole = lax.all_gather(part, "row", axis=0, tiled=True)

        def term(begin, count):
            return jnp.dot(whole, weight, preferred_element_type=jnp.float32)

        return (
            whole,
            lax.psum_scatter(
                term(jnp.int32(0), whole.shape[0] // column_count * lax.axis_size("col")).astype(
                    jnp.bfloat16
                ),
                "col",
                scatter_dimension=0,
                tiled=True,
            ).astype(jnp.float32),
        )

    def to_heads(value):
        return lax.all_to_all(value, "col", split_axis=0, concat_axis=1, tiled=True)

    def to_tokens(value):
        return lax.all_to_all(value, "col", split_axis=1, concat_axis=0, tiled=True)

    stream = tokens.astype(jnp.float32)
    normed_one, scale_one = norm_apply(stream, gain_one, row_total)
    normed_one_all, joint_part = through_rows(normed_one, joint_weight)
    joint_heads = to_heads(joint_part.astype(jnp.bfloat16))
    shard_rows = joint_heads.shape[0]
    place = lax.axis_index("row") * column_count + lax.axis_index("col")
    index = place * shard_rows + jnp.arange(shard_rows, dtype=jnp.int32)
    attended, attention_back = attend(joint_heads, index, tables, row_count, column_count)
    attended_all, attention_out = through_columns(to_tokens(attended), output_weight)
    hidden = stream + attention_out
    normed_two, scale_two = norm_apply(hidden, gain_two, row_total)
    pair_weight = jnp.concatenate([gate_weight, up_weight], axis=1)
    normed_two_all, pair_part = through_rows(normed_two, pair_weight)
    width = gate_weight.shape[1]
    gate_part, up_part = (pair_part[:, :width], pair_part[:, width:])
    mixed = swiglu(gate_part, up_part).astype(jnp.bfloat16)
    mixed_all, feed_out = through_columns(mixed, down_weight)
    layer_output = (hidden + feed_out).astype(jnp.bfloat16)
    cotangent_all, mixed_back = through_rows(cotangent, down_weight.T)
    down_gradient = contract(mixed_all, cotangent_all)
    gate_back, up_back = swiglu_back(mixed_back, gate_part, up_part)
    pair_back = jnp.concatenate([gate_back, up_back], axis=1).astype(jnp.bfloat16)
    pair_back_all, normed_two_back = through_columns(pair_back, pair_weight.T)
    pair_gradient = contract(normed_two_all, pair_back_all)
    hidden_part, gain_two_part = norm_back(normed_two_back, hidden, scale_two, gain_two, row_total)
    hidden_back = cotangent.astype(jnp.float32) + hidden_part
    hidden_low_all, attended_back = through_rows(hidden_back.astype(jnp.bfloat16), output_weight.T)
    output_gradient = contract(attended_all, hidden_low_all)
    joint_back = attention_back(to_heads(attended_back.astype(jnp.bfloat16)))
    joint_back_all, normed_one_back = through_columns(to_tokens(joint_back), joint_weight.T)
    joint_gradient = contract(normed_one_all, joint_back_all)
    stream_part, gain_one_part = norm_back(normed_one_back, stream, scale_one, gain_one, row_total)
    input_gradient = hidden_back + stream_part
    gain_one_gradient, gain_two_gradient = lax.psum((gain_one_part, gain_two_part), "col")
    return (
        layer_output,
        input_gradient,
        gain_one_gradient,
        joint_gradient,
        output_gradient,
        gain_two_gradient,
        pair_gradient[:, :width],
        pair_gradient[:, width:],
        down_gradient,
    )


def solution(mesh):
    return jax.shard_map(
        per_device,
        mesh=mesh,
        in_specs=(
            P(("leaf", "col"), "row"),
            P("row"),
            P("row", "col"),
            P("col", "row"),
            P("row"),
            P("row", "col"),
            P("row", "col"),
            P("col", "row"),
            P(("leaf", "col"), "row"),
            P("leaf"),
            P("leaf"),
        ),
        out_specs=(
            P(("leaf", "col"), "row"),
            P(("leaf", "col"), "row"),
            P(("leaf", "row")),
            P(("leaf", "row"), "col"),
            P(("leaf", "col"), "row"),
            P(("leaf", "row")),
            P(("leaf", "row"), "col"),
            P(("leaf", "row"), "col"),
            P(("leaf", "col"), "row"),
        ),
        check_vma=False,
    )
```

profile of v0, /device:TPU:0, one launch (start us, length us, event | category | flops | bytes accessed | tf_op | source)
XLA Modules:
  0.0 4297.5 jit_solution(18237324206554225666)
XLA Ops:
  25.3 109.3 %all-gather.11.cloned.1.call-done = bf16[10240,288]{0,1:T(8,128)(2,1)} async-done(((bf16[2560,288]{0,1:T(8,128)(2,1)}), bf16[10240,288]{0,1:T(8,128)(2,1)}) %all-gather.11.cloned.1.call-update) | async-done | bytes 5898256 | tf_op jit(solution)/shard_map/all_gather | solution.py:298
  145.3 79.4 %reduce-scatter.14.cloned.1.call-done = bf16[2560,480]{0,1:T(8,128)(2,1)} async-done(((bf16[10240,480]{0,1:T(8,128)(2,1)}), bf16[2560,480]{0,1:T(8,128)(2,1)}) %reduce-scatter.14.cloned.1.call-update) | async-done | bytes 2457616 | tf_op jit(solution)/shard_map/reduce_scatter | solution.py:305
  226.6 60.3 %all_to_all.67 = bf16[4,640,480]{1,2,0:T(8,128)(2,1)S(1)} all-to-all(bf16[4,640,480]{1,2,0:T(8,128)(2,1)S(1)} %bitcast.264), channel_id=1, replica_groups=mesh['leaf'=2,'row'=4,'col'=4] {'col'}, dimensions={0} | all-to-all | bytes 4915200 | tf_op jit(solution)/shard_map/all_to_all | solution.py:334
  300.0 58.9 %all-gather.13.cloned.1.call-done = bf16[10240,384]{0,1:T(8,128)(2,1)} async-done(((bf16[640,384]{0,1:T(8,128)(2,1)}), bf16[10240,384]{0,1:T(8,128)(2,1)}) %all-gather.13.cloned.1.call-update) | async-done | bytes 7864336 | tf_op jit(solution)/shard_map/all_gather | solution.py:115
  380.2 51.3 %all-gather.15.cloned.1.call-done = bf16[10240,384]{0,1:T(8,128)(2,1)} async-done(((bf16[640,384]{0,1:T(8,128)(2,1)}), bf16[10240,384]{0,1:T(8,128)(2,1)}) %all-gather.15.cloned.1.call-update) | async-done | bytes 7864336 | tf_op jit(solution)/shard_map/all_gather | solution.py:114
  452.8 434.5 %while.37 = (s32[]{:T(128)}, f32[6,3,640]{2,1,0:T(4,128)S(1)}, f32[6,3,640]{2,1,0:T(4,128)S(1)}, s32[10]{0:T(128)S(1)}, s32[13]{0:T(128)S(1)}, /*index=5*/bf16[6...) while((s32[]{:T(128)}, f32[6,3,640]{2,1,0:T(4,128)S(1)}, ...), condition=%wide.region_11.12_spmd.clone, body=%wide.region_7.11_spmd.clone.sunk | while | flops 1611641728 | bytes 100813256 | solution.py:85
  457.4 18.6 fusion.147
  476.1 20.0 fusion.148
  500.9 18.6 fusion.147
  519.5 20.0 fusion.148
  544.3 18.6 fusion.147
  563.0 20.0 fusion.148
  606.4 20.0 fusion.148
  631.2 18.6 fusion.147
  649.9 20.0 fusion.148
  693.3 20.0 fusion.148
  718.1 18.6 fusion.147
  736.8 20.0 fusion.148
  780.2 20.0 fusion.148
  805.1 18.6 fusion.147
  823.7 20.0 fusion.148
  867.2 20.0 fusion.148
  888.0 214.3 %while.38 = (s32[]{:T(128)}, f32[640,6,3,64]{0,3,2,1:T(8,128)}, bf16[10,1024,384]{1,2,0:T(8,128)(2,1)}, s32[10]{0:T(128)S(1)}, s32[13]{0:T(128)S(1)}, /*index=5*...) while((s32[]{:T(128)}, f32[640,6,3,64]{0,3,2,1:T(8,128)}, ...), condition=%wide.region_14.15_spmd.clone, body=%wide.region_12.14_spmd.clone.sunk | while | flops 3087618560 | bytes 13490643 | solution.py:85
  1104.3 38.4 all_to_all.68
  1144.0 42.4 all-gather.17.cloned.1.call-done
  1195.6 103.9 %reduce-scatter.16.cloned.1.call-done = bf16[2560,288]{0,1:T(8,128)(2,1)} async-done(((bf16[10240,288]{0,1:T(8,128)(2,1)}), bf16[2560,288]{0,1:T(8,128)(2,1)}) %reduce-scatter.16.cloned.1.call-update) | async-done | bytes 1474576 | tf_op jit(solution)/shard_map/reduce_scatter | solution.py:323
  1319.9 104.2 %all-gather.19.cloned.1.call-done = bf16[10240,288]{0,1:T(8,128)(2,1)} async-done(((bf16[2560,288]{0,1:T(8,128)(2,1)}), bf16[10240,288]{0,1:T(8,128)(2,1)}) %all-gather.19.cloned.1.call-update) | async-done | bytes 5898256 | tf_op jit(solution)/shard_map/all_gather | solution.py:298
  1424.1 23.8 convolution_convert_fusion
  1448.0 84.8 %all-gather.23.cloned.1.call-done = bf16[10240,288]{0,1:T(8,128)(2,1)} async-done(((bf16[2560,288]{0,1:T(8,128)(2,1)}), bf16[10240,288]{0,1:T(8,128)(2,1)}) %all-gather.23.cloned.1.call-update) | async-done | bytes 5898256 | tf_op jit(solution)/shard_map/all_gather | solution.py:298
  1548.3 207.0 %reduce-scatter.30.cloned.1.call-done = bf16[2560,1536]{1,0:T(8,128)(2,1)} async-done(((bf16[10240,1536]{1,0:T(8,128)(2,1)}), bf16[2560,1536]{1,0:T(8,128)(2,1)}) %reduce-scatter.30.cloned.1.call-update) | async-done | bytes 7864336
  1768.8 109.0 %reduce-scatter.20.cloned.1.call-done = bf16[2560,768]{1,0:T(8,128)(2,1)} async-done(((bf16[10240,768]{1,0:T(8,128)(2,1)}), bf16[2560,768]{1,0:T(8,128)(2,1)}) %reduce-scatter.20.cloned.1.call-update) | async-done | bytes 3932176 | tf_op jit(solution)/shard_map/reduce_scatter | solution.py:305
  1898.6 189.7 %all-gather.25.cloned.1.call-done = bf16[10240,1536]{1,0:T(8,128)(2,1)} async-done(((bf16[2560,1536]{1,0:T(8,128)(2,1)}), bf16[10240,1536]{1,0:T(8,128)(2,1)}) %all-gather.25.cloned.1.call-update) | async-done | bytes 31457296 | tf_op jit(solution)/shard_map/all_gather | solution.py:316
  2105.1 104.5 %reduce-scatter.22.cloned.1.call-done = bf16[2560,288]{0,1:T(8,128)(2,1)} async-done(((bf16[10240,288]{0,1:T(8,128)(2,1)}), bf16[2560,288]{0,1:T(8,128)(2,1)}) %reduce-scatter.22.cloned.1.call-update) | async-done | bytes 1474576 | tf_op jit(solution)/shard_map/reduce_scatter | solution.py:323
  2229.0 108.6 %all-gather.27.cloned.1.call-done = bf16[10240,288]{0,1:T(8,128)(2,1)} async-done(((bf16[2560,288]{0,1:T(8,128)(2,1)}), bf16[10240,288]{0,1:T(8,128)(2,1)}) %all-gather.27.cloned.1.call-update) | async-done | bytes 5898256 | tf_op jit(solution)/shard_map/all_gather | solution.py:298
  2346.2 54.1 %reduce-scatter.24.cloned.1.call-done = bf16[2560,288]{0,1:T(8,128)(2,1)} async-done(((bf16[10240,288]{0,1:T(8,128)(2,1)}), bf16[2560,288]{0,1:T(8,128)(2,1)}) %reduce-scatter.24.cloned.1.call-update) | async-done | bytes 1474576 | tf_op jit(solution)/shard_map/reduce_scatter | solution.py:305
  2407.5 34.8 all-to-all-done.2
  2459.6 1188.1 %while.39 = (s32[]{:T(128)}, f32[640,6,3,64]{0,3,2,1:T(8,128)}, f32[10240,768]{0,1:T(8,128)}, bf16[10,1024,384]{1,2,0:T(8,128)(2,1)}, s32[10]{0:T(128)S(1)}, /*i...) while((s32[]{:T(128)}, f32[640,6,3,64]{0,3,2,1:T(8,128)}, ...), condition=%wide.region_28.29_spmd.clone, body=%wide.region_26.28_spmd.clone.sunk | while | flops 7690949120 | bytes 268747360 | solution.py:85
  2485.6 19.6 fusion.168
  2505.2 27.1 fusion.167
  2603.7 19.6 fusion.168
  2623.3 27.1 fusion.167
  2722.6 19.6 fusion.168
  2742.3 27.1 fusion.167
  2841.6 19.6 fusion.168
  2861.2 27.1 fusion.167
  2960.5 19.6 fusion.168
  2980.1 27.1 fusion.167
  3079.4 19.6 fusion.168
  3099.1 27.1 fusion.167
  3198.4 19.6 fusion.168
  3218.0 27.1 fusion.167
  3317.4 19.6 fusion.168
  3337.0 27.1 fusion.167
  3436.3 19.6 fusion.168
  3455.9 27.1 fusion.167
  3555.2 19.6 fusion.168
  3574.8 27.1 fusion.167
  3664.1 20.5 copy.96
  3688.0 151.9 %reduce-scatter.28.cloned.1.call-done = bf16[640,768]{1,0:T(8,128)(2,1)} async-done(((bf16[10240,768]{1,0:T(8,128)(2,1)}), bf16[640,768]{1,0:T(8,128)(2,1)}) %reduce-scatter.28.cloned.1.call-update) | async-done | bytes 983056
  3842.2 58.9 %all_to_all.69 = bf16[640,4,480]{0,2,1:T(8,128)(2,1)S(1)} all-to-all(bf16[640,4,480]{0,2,1:T(8,128)(2,1)S(1)} %bitcast.263), channel_id=1, replica_groups=mesh['leaf'=2,'row'=4,'col'=4] {'col'}, dimensions={1} | all-to-all | bytes 4915200 | tf_op jit(solution)/shard_map/all_to_all | solution.py:337
  3903.4 64.9 %all-gather.29.cloned.1.call-done = bf16[10240,480]{0,1:T(8,128)(2,1)} async-done(((bf16[2560,480]{0,1:T(8,128)(2,1)}), bf16[10240,480]{0,1:T(8,128)(2,1)}) %all-gather.29.cloned.1.call-update) | async-done | bytes 9830416 | tf_op jit(solution)/shard_map/all_gather | solution.py:316
  3977.2 92.6 %all-gather.21.cloned.1.call-done = bf16[10240,768]{1,0:T(8,128)(2,1)} async-done(((bf16[2560,768]{1,0:T(8,128)(2,1)}), bf16[10240,768]{1,0:T(8,128)(2,1)}) %all-gather.21.cloned.1.call-update) | async-done | bytes 15728656 | tf_op jit(solution)/shard_map/all_gather | solution.py:316
  4132.1 44.4 %reduce-scatter.26.cloned.1.call-done = bf16[2560,288]{0,1:T(8,128)(2,1)} async-done(((bf16[10240,288]{0,1:T(8,128)(2,1)}), bf16[2560,288]{0,1:T(8,128)(2,1)}) %reduce-scatter.26.cloned.1.call-update) | async-done | bytes 1474576 | tf_op jit(solution)/shard_map/reduce_scatter | solution.py:323
  4201.8 82.1 %reduce-scatter.18.cloned.1.call-done = bf16[2560,288]{0,1:T(8,128)(2,1)} async-done(((bf16[10240,288]{0,1:T(8,128)(2,1)}), bf16[2560,288]{0,1:T(8,128)(2,1)}) %reduce-scatter.18.cloned.1.call-update) | async-done | bytes 1474576 | tf_op jit(solution)/shard_map/reduce_scatter | solution.py:323
  (526 shorter events, 1402.3 us)
Async XLA Ops:
  7.2 1525.7 %copy-start = (bf16[768,288]{0,1:T(8,128)(2,1)S(1)}, bf16[768,288]{0,1:T(8,128)(2,1)}, u32[]{:S(2)}) copy-start(bf16[768,288]{0,1:T(8,128)(2,1)} %param.24) | copy-start | bytes 1327108
  7.2 127.4 %all-gather.11.cloned.1.call-start = ((), (), s32[]{:S(2)}) async-start(), calls=%async_computation.13 | async-start | bytes 7372800 | tf_op jit(solution)/shard_map/all_gather | solution.py:298
  8.0 17.3 copy-start.25
  8.0 126.6 %copy-start.30 = (bf16[288,480]{1,0:T(8,128)(2,1)S(1)}, bf16[288,480]{1,0:T(8,128)(2,1)}, u32[]{:S(2)}) copy-start(bf16[288,480]{1,0:T(8,128)(2,1)} %param.19) | copy-start | bytes 829444
  22.3 122.9 %copy-start.21 = (f32[2560]{0:T(1024)}, f32[2560]{0:T(1024)S(1)}, u32[]{:S(2)}) copy-start(f32[2560]{0:T(1024)S(1)} %psum.42) | copy-start | bytes 30724
  22.4 122.9 %copy-start.17 = (f32[2560]{0:T(1024)}, f32[2560]{0:T(1024)S(1)}, u32[]{:S(2)}) copy-start(f32[2560]{0:T(1024)S(1)} %add_rsqrt_fusion.1) | copy-start | bytes 30724
  25.3 199.4 %reduce-scatter.14.cloned.1.call-start = ((), (), s32[]{:S(2)}) async-start(), calls=%async_computation.14 | async-start | bytes 12288000 | tf_op jit(solution)/shard_map/reduce_scatter | solution.py:305
  145.3 213.6 %all-gather.13.cloned.1.call-start = ((), (), s32[]{:S(2)}) async-start(), calls=%async_computation.15 | async-start | bytes 8355840 | tf_op jit(solution)/shard_map/all_gather | solution.py:115
  226.6 62.7 %copy-start.1 = (s32[13]{0:T(128)S(1)}, s32[13]{0:T(128)}, u32[]{:S(2)}) copy-start(s32[13]{0:T(128)} %param.27) | copy-start | bytes 160
  226.6 63.4 %copy-start.28 = (s32[13]{0:T(128)S(1)}, s32[13]{0:T(128)}, u32[]{:S(2)}) copy-start(s32[13]{0:T(128)} %param.26) | copy-start | bytes 160
  289.2 142.2 %all-gather.15.cloned.1.call-start = ((), (), s32[]{:S(2)}) async-start(), calls=%async_computation.16 | async-start | bytes 8355840 | tf_op jit(solution)/shard_map/all_gather | solution.py:114
  296.2 890.1 %all-gather.17.cloned.1.call-start = ((), (), s32[]{:S(2)}) async-start(), calls=%async_computation.17 | async-start | bytes 7372800 | tf_op jit(solution)/shard_map/all_gather | solution.py:316
  1142.7 43.7 %copy-start.16 = (bf16[288,288]{1,0:T(8,128)(2,1)S(1)}, bf16[288,288]{1,0:T(8,128)(2,1)}, u32[]{:S(2)}) copy-start(bf16[288,288]{1,0:T(8,128)(2,1)} %param.20) | copy-start | bytes 497668
  1143.9 155.5 %reduce-scatter.16.cloned.1.call-start = ((), (), s32[]{:S(2)}) async-start(), calls=%async_computation.18 | async-start | bytes 7372800 | tf_op jit(solution)/shard_map/reduce_scatter | solution.py:323
  1194.9 104.6 %copy-start.2 = (bf16[2560,288]{0,1:T(8,128)(2,1)S(1)}, bf16[2560,288]{0,1:T(8,128)(2,1)}, u32[]{:S(2)}) copy-start(bf16[2560,288]{0,1:T(8,128)(2,1)} %param.17) | copy-start | bytes 4423684
  1194.9 229.2 %all-gather.19.cloned.1.call-start = ((), (), s32[]{:S(2)}) async-start(), calls=%async_computation.19 | async-start | bytes 7372800 | tf_op jit(solution)/shard_map/all_gather | solution.py:298
  1195.5 1028.9 %copy-start.23 = (f32[288]{0:T(512)}, f32[288]{0:T(512)S(1)}, u32[]{:S(2)}) copy-start(f32[288]{0:T(512)S(1)} %convert_element_type.149) | copy-start | bytes 3460
  1312.4 912.1 %copy-start.14 = (f32[2560]{0:T(1024)}, f32[2560]{0:T(1024)S(1)}, u32[]{:S(2)}) copy-start(f32[2560]{0:T(1024)S(1)} %add_rsqrt_fusion) | copy-start | bytes 30724
  1315.5 217.3 %all-gather.23.cloned.1.call-start = ((), (), s32[]{:S(2)}) async-start(), calls=%async_computation.22 | async-start | bytes 7372800 | tf_op jit(solution)/shard_map/all_gather | solution.py:298
  1316.3 439.0 %reduce-scatter.30.cloned.1.call-start = ((), (), s32[]{:S(2)}) async-start(), calls=%async_computation.31 | async-start | bytes 39321600
  1448.0 429.8 %reduce-scatter.20.cloned.1.call-start = ((), (), s32[]{:S(2)}) async-start(), calls=%async_computation.23 | async-start | bytes 19660800 | tf_op jit(solution)/shard_map/reduce_scatter | solution.py:305
  1547.9 540.5 %all-gather.25.cloned.1.call-start = ((), (), s32[]{:S(2)}) async-start(), calls=%async_computation.24 | async-start | bytes 39321600 | tf_op jit(solution)/shard_map/all_gather | solution.py:316
  1898.6 311.1 %reduce-scatter.22.cloned.1.call-start = ((), (), s32[]{:S(2)}) async-start(), calls=%async_computation.25 | async-start | bytes 7372800 | tf_op jit(solution)/shard_map/reduce_scatter | solution.py:323
  2105.1 232.5 %all-gather.27.cloned.1.call-start = ((), (), s32[]{:S(2)}) async-start(), calls=%async_computation.26 | async-start | bytes 7372800 | tf_op jit(solution)/shard_map/all_gather | solution.py:298
  2229.0 171.4 %reduce-scatter.24.cloned.1.call-start = ((), (), s32[]{:S(2)}) async-start(), calls=%async_computation.27 | async-start | bytes 7372800 | tf_op jit(solution)/shard_map/reduce_scatter | solution.py:305
  2402.9 39.4 all-to-all-start.2
  2407.5 1432.4 %reduce-scatter.28.cloned.1.call-start = ((), (), s32[]{:S(2)}) async-start(), calls=%async_computation.30 | async-start | bytes 16711680
  2544.0 13.5 copy-start.4
  2562.1 15.7 copy-start.9
  2662.1 14.3 copy-start.4
  2681.0 15.7 copy-start.9
  2781.0 14.3 copy-start.4
  2800.0 15.7 copy-start.9
  2900.0 14.3 copy-start.4
  2918.9 15.7 copy-start.9
  3018.9 14.3 copy-start.4
  3037.9 15.7 copy-start.9
  3137.8 14.3 copy-start.4
  3156.8 15.7 copy-start.9
  3256.8 14.3 copy-start.4
  3275.7 15.8 copy-start.9
  3375.8 14.3 copy-start.4
  3394.7 15.7 copy-start.9
  3494.7 14.3 copy-start.4
  3513.6 15.7 copy-start.9
  3613.6 14.3 copy-start.4
  3632.4 14.9 copy-start.9
  3684.7 283.6 %all-gather.29.cloned.1.call-start = ((), (), s32[]{:S(2)}) async-start(), calls=%async_computation.28 | async-start | bytes 12288000 | tf_op jit(solution)/shard_map/all_gather | solution.py:316
  3902.7 65.6 %copy-start.31 = (bf16[288,480]{1,0:T(8,128)(2,1)S(1)}, bf16[288,480]{1,0:T(8,128)(2,1)}, u32[]{:S(2)}) copy-start(bf16[288,480]{1,0:T(8,128)(2,1)} %param.19) | copy-start | bytes 829444
  3902.8 167.1 %all-gather.21.cloned.1.call-start = ((), (), s32[]{:S(2)}) async-start(), calls=%async_computation.20 | async-start | bytes 19660800 | tf_op jit(solution)/shard_map/all_gather | solution.py:316
  3903.4 273.2 %reduce-scatter.26.cloned.1.call-start = ((), (), s32[]{:S(2)}) async-start(), calls=%async_computation.29 | async-start | bytes 7372800 | tf_op jit(solution)/shard_map/reduce_scatter | solution.py:323
  3977.2 306.8 %reduce-scatter.18.cloned.1.call-start = ((), (), s32[]{:S(2)}) async-start(), calls=%async_computation.21 | async-start | bytes 7372800 | tf_op jit(solution)/shard_map/reduce_scatter | solution.py:323
  4087.5 30.8 slice-start.1
  4100.6 17.7 slice-start.2
  4116.9 8.0 slice-start.3
  4124.9 51.6 %copy-start.3 = (bf16[2560,288]{0,1:T(8,128)(2,1)S(1)}, bf16[2560,288]{0,1:T(8,128)(2,1)}, u32[]{:S(2)}) copy-start(bf16[2560,288]{0,1:T(8,128)(2,1)} %param.17) | copy-start | bytes 4423684
  4125.0 51.6 %copy-start.18 = (f32[2560]{0:T(1024)S(1)}, f32[2560]{0:T(1024)}, u32[]{:S(2)}) copy-start(f32[2560]{0:T(1024)} %copy-done.17) | copy-start | bytes 30724
  4125.0 51.6 %copy-start.26 = (f32[288]{0:T(512)S(1)}, f32[288]{0:T(512)}, u32[]{:S(2)}) copy-start(f32[288]{0:T(512)} %copy-done.25) | copy-start | bytes 3460
  4132.1 47.2 %copy-start.27 = (f32[288]{0:T(512)S(1)}, f32[288]{0:T(512)}, u32[]{:S(2)}) copy-start(f32[288]{0:T(512)} %get-tuple-element.434) | copy-start | bytes 3460
  4132.1 69.8 %copy-start.22 = (f32[2560]{0:T(1024)S(1)}, f32[2560]{0:T(1024)}, u32[]{:S(2)}) copy-start(f32[2560]{0:T(1024)} %copy-done.21) | copy-start | bytes 30724
  4132.1 151.9 %copy-start.5 = (bf16[2560,288]{0,1:T(8,128)(2,1)S(1)}, bf16[2560,288]{0,1:T(8,128)(2,1)}, u32[]{:S(2)}) copy-start(bf16[2560,288]{0,1:T(8,128)(2,1)} %reduce-scatter.16.cloned.1.call-done) | copy-start | bytes 4423684
  4132.1 151.9 %copy-start.15 = (f32[2560]{0:T(1024)S(1)}, f32[2560]{0:T(1024)}, u32[]{:S(2)}) copy-start(f32[2560]{0:T(1024)} %copy-done.14) | copy-start | bytes 30724
  4132.1 151.9 %copy-start.20 = (f32[2560]{0:T(1024)S(1)}, f32[2560]{0:T(1024)}, u32[]{:S(2)}) copy-start(f32[2560]{0:T(1024)} %copy-done.19) | copy-start | bytes 30724
  4132.1 151.9 %copy-start.24 = (f32[288]{0:T(512)S(1)}, f32[288]{0:T(512)}, u32[]{:S(2)}) copy-start(f32[288]{0:T(512)} %copy-done.23) | copy-start | bytes 3460
  (20 other events, 65.9 us)
Sparse Core Ops, SparseCore 0:
  25.4 109.1 all-gather.10
  145.4 79.2 reduce-scatter.13
  289.3 69.5 all-gather.12
  361.5 69.8 all-gather.14
  1144.1 42.2 all-gather.16
  1195.0 104.3 reduce-scatter.15
  1315.6 108.4 all-gather.18
  1425.7 107.0 all-gather.22
  1535.4 219.7 reduce-scatter.29
  1757.9 119.8 reduce-scatter.19
  1898.7 189.6 all-gather.24
  2105.2 104.3 reduce-scatter.21
  2229.1 108.4 all-gather.26
  2346.3 53.9 reduce-scatter.23
  3684.8 155.0 reduce-scatter.27
  3902.9 65.4 all-gather.28
  3969.8 99.9 all-gather.20
  4072.1 104.3 reduce-scatter.25
  4178.9 104.9 reduce-scatter.17
where the time goes:
time: 4310 us; the launch traced here: 4300 us
  waiting for transfers between devices  1880 us (44%)
  matrix products  1480 us (34%)
  other arithmetic  361 us (8%)
  local copies, waits for them, and re-layouts  317 us (7%)
  blocking collectives  215 us (5%)
    all_gather x4, waiting for transfers between devices, through_rows(): whole = lax.all_gather(part, 'col', axis=0, tiled=True)  407 us
    all_gather x4, waiting for transfers between devices, through_columns(): whole = lax.all_gather(part, 'row', axis=0, tiled=True)  390 us
    dot_general x20, matrix products, scores_at(): jnp.einsum('qgrd,kgd->grqk', queries, key_block.reshape(span, groups, HEA...  368 us
    unnamed x21, waiting for transfers between devices  360 us
    reduce_scatter x4, waiting for transfers between devices, through_columns(): lax.psum_scatter(term(jnp.int32(0), whole.shape[0] // column_count * lax....  335 us
    dot_general x10, matrix products, grad_block(): jnp.einsum('qgrd,kgd->grqk', heads_grouped, value_heads, preferred_elemen...  271 us
    reduce_scatter x3, waiting for transfers between devices, through_rows(): lax.psum_scatter(term(jnp.int32(0), whole.shape[0] // row_count * lax.axi...  242 us
    reduce_sum x10, other arithmetic, top_block(): return (new_top, total * jnp.exp(top - new_top) + jnp.sum(weights, axis=-1))  200 us
  transfers between devices with their start and end apart: 20, of which 20 were waited for; matrix products, arithmetic and copies ran while one was open for 4% of the time, Pallas kernels for 0%

commit v1 on v0

v1 whole, which is shorter than its diff:
```python
import functools

import jax
import jax.numpy as jnp
from jax import lax
from jax.experimental import pallas as pl
from jax.experimental.pallas import tpu as pltpu
from jax.sharding import Mesh
from jax.sharding import PartitionSpec as P

D = 1152
HEADS = 18
KV_HEADS = 6
HEAD_DIM = 64
REPEAT = HEADS // KV_HEADS
ATT = HEADS * HEAD_DIM
KEYS = KV_HEADS * HEAD_DIM

EPSILON = 1e-05
THETA = 10000.0
BIG = 2.0**30
LOG2E = 1.4426950408889634
KEY_BLOCK = 256
UNROLL = 8
BF16 = jnp.bfloat16
F32 = jnp.float32
NT = (((1,), (1,)), ((), ()))
NN = (((1,), (0,)), ((), ()))


def dg(a, b, dims):
    return lax.dot_general(a, b, dims, preferred_element_type=F32)


def tree_tables(segment_lengths, parents):
    count = segment_lengths.shape[0]
    labels = jnp.arange(count, dtype=jnp.int32)
    ends = jnp.sum(jnp.where(labels[None, :] <= labels[:, None], segment_lengths[None, :], 0), axis=1)
    starts = ends - segment_lengths
    parent_hot = parents[:, None] == labels[None, :]
    grand = jnp.sum(jnp.where(parent_hot, parents[None, :], 0), axis=1)
    self_mark = labels[:, None] == labels[None, :]
    grand_mark = grand[:, None] == labels[None, :]
    ancestry = (self_mark | parent_hot | grand_mark).astype(F32)
    strict = (parent_hot | grand_mark) & jnp.logical_not(self_mark)
    offsets = jnp.sum(jnp.where(strict, segment_lengths[None, :], 0), axis=1)
    return (ends, starts, ancestry, offsets)


def segment_hot(index, tables):
    ends, starts, _, _ = tables
    return (index[:, None] >= starts[None, :]) & (index[:, None] < ends[None, :])


def rotary_tables(index, tables):
    hot = segment_hot(index, tables)
    depth = index + jnp.sum(jnp.where(hot, (tables[3] - tables[1])[None, :], 0), axis=1)
    half = HEAD_DIM // 2
    rates = THETA ** (-jnp.arange(half, dtype=F32) / half)
    angles = depth.astype(F32)[:, None] * rates[None, :]
    return (jnp.cos(angles), jnp.sin(angles))


def turn(value, cosines, sines):
    half = value.shape[-1] // 2
    former, latter = (value[..., :half], value[..., half:])
    cos_part = cosines[:, None, :]
    sin_part = sines[:, None, :]
    return jnp.concatenate(
        [former * cos_part - latter * sin_part, latter * cos_part + former * sin_part], axis=-1
    )


def block_lists(first, blocks, block, total, tables):
    ends, starts, ancestry, _ = tables
    key_count = total // KEY_BLOCK
    low = first + jnp.arange(blocks, dtype=jnp.int32) * block
    high = low + block
    query_has = ((starts[None, :] < high[:, None]) & (ends[None, :] > low[:, None])).astype(F32)
    key_low = jnp.arange(key_count, dtype=jnp.int32) * KEY_BLOCK
    key_has = ((starts[None, :] < key_low[:, None] + KEY_BLOCK) & (ends[None, :] > key_low[:, None])).astype(F32)
    reach = jnp.sum(query_has[:, :, None] * ancestry[None], axis=1)
    seen = jnp.sum(reach[:, None, :] * key_has[None], axis=2) > 0.5
    seen = seen & (key_low[None, :] < high[:, None])
    labels = jnp.arange(key_count, dtype=jnp.int32)
    before = labels[None, :] < labels[:, None]
    rank = jnp.sum((seen[:, None, :] & before[None]).astype(jnp.int32), axis=2)
    place = seen[:, None, :] & (rank[:, None, :] == labels[None, :, None])
    lists = jnp.sum(jnp.where(place, labels[None, None, :], 0), axis=2)
    counts = jnp.sum(seen.astype(jnp.int32), axis=1) - 1
    return (lists.reshape(-1).astype(jnp.int32), counts.astype(jnp.int32))


def cascade(count, unroll, steps):
    def body(i, c):
        steps(i * unroll, unroll)
        return c

    whole = count // unroll
    lax.fori_loop(0, whole, body, 0)
    start = whole * unroll
    size = unroll // 2
    while size:
        some = ((count - start) // size) > 0
        pl.when(some)(functools.partial(steps, start, size))
        start = start + jnp.where(some, size, 0)
        size //= 2


def causal(scores, gap, heads):
    rows = gap + lax.broadcasted_iota(jnp.int32, scores.shape, 0)
    columns = lax.rem(lax.broadcasted_iota(jnp.int32, scores.shape, 1), scores.shape[1] // heads)
    return jnp.where(rows <= columns, scores, -BIG)


def left_half(shape):
    return lax.broadcasted_iota(jnp.int32, shape, 1) < HEAD_DIM


def forward_kernel(lists, counts, first, q_ref, kv_ref, mark_ref, o_ref, lse_ref, top_ref, sum_ref, vt_ref):
    block = pl.program_id(1)
    heads, rows = q_ref.shape[1], q_ref.shape[2]
    total = kv_ref.shape[1]
    stride = total // KEY_BLOCK
    place = first[0] + block * rows
    count = counts[block]

    @pl.when(block == 0)
    def _():
        def flip(i, c):
            k0 = pl.multiple_of(i * KEY_BLOCK, KEY_BLOCK)
            turned = kv_ref[0, pl.ds(k0, KEY_BLOCK), :].T
            vt_ref[:HEAD_DIM, pl.ds(k0, KEY_BLOCK)] = turned[HEAD_DIM:]
            return c

        lax.fori_loop(0, stride, flip, 0)
        tail = (vt_ref.shape[0] - HEAD_DIM, total)
        vt_ref[HEAD_DIM:] = jnp.where(lax.broadcasted_iota(jnp.int32, tail, 0) == 0, 1.0, 0.0).astype(BF16)

    def queries():
        return q_ref[0].reshape(heads * rows, 2 * HEAD_DIM)

    def blocks(start, n):
        offs = [pl.multiple_of(lists[block * stride + start + u] * KEY_BLOCK, KEY_BLOCK) for u in range(n)]
        kv = jnp.concatenate([kv_ref[0, pl.ds(k0, KEY_BLOCK), :] for k0 in offs], axis=0)
        mark = jnp.concatenate([mark_ref[pl.ds(k0, KEY_BLOCK), :] for k0 in offs], axis=0)
        vt = jnp.concatenate([vt_ref[:, pl.ds(k0, KEY_BLOCK)] for k0 in offs], axis=1)
        return offs, jnp.where(left_half(kv.shape), kv, mark), vt

    offs, k, vt = blocks(count, 1)
    scores = causal(dg(k, queries(), NT), offs[0] - place, heads)
    top = jnp.max(scores, axis=0, keepdims=True)
    top_ref[...] = top
    sum_ref[...] = dg(vt, jnp.exp2(scores - top).astype(BF16), NN)

    def steps(start, n):
        _, k, vt = blocks(start, n)
        weights = jnp.exp2(dg(k, queries(), NT) - top_ref[...]).astype(BF16)
        sum_ref[...] += dg(vt, weights, NN)

    cascade(count, UNROLL, steps)

    @pl.when(jnp.logical_not(jnp.max(sum_ref[HEAD_DIM : HEAD_DIM + 1, :]) < 2.0**100))
    def _():
        top_ref[...] = jnp.full(top_ref.shape, -4.0 * BIG, F32)
        sum_ref[...] = jnp.zeros(sum_ref.shape, F32)

        def online(n, c):
            offs, k, vt = blocks(n, 1)
            scores = causal(dg(k, queries(), NT), offs[0] - place, heads)
            old = top_ref[...]
            new = jnp.maximum(old, jnp.max(scores, axis=0, keepdims=True))
            top_ref[...] = new
            sum_ref[...] = sum_ref[...] * jnp.exp2(old - new) + dg(vt, jnp.exp2(scores - new).astype(BF16), NN)
            return c

        lax.fori_loop(0, count + 1, online, 0)

    total_row = sum_ref[HEAD_DIM : HEAD_DIM + 1, :]
    o_ref[0] = (sum_ref[:HEAD_DIM, :] / total_row).T.astype(BF16).reshape(heads, rows, HEAD_DIM)
    lse_ref[0, 0] = top_ref[...] + jnp.log2(total_row)


def attention_forward(lists, counts, first, q, kv, marks):
    groups, heads, tokens, wide = q.shape
    total = kv.shape[1]
    blocks = counts.shape[0]
    rows = tokens // blocks
    tall = HEAD_DIM + 16
    return pl.pallas_call(
        forward_kernel,
        grid_spec=pltpu.PrefetchScalarGridSpec(
            num_scalar_prefetch=3,
            grid=(groups, blocks),
            in_specs=[
                pl.BlockSpec((1, heads, rows, wide), lambda g, b, *_: (g, 0, b, 0)),
                pl.BlockSpec((1, total, wide), lambda g, b, *_: (g, 0, 0)),
                pl.BlockSpec((total, wide), lambda g, b, *_: (0, 0)),
            ],
            out_specs=[
                pl.BlockSpec((1, heads, rows, HEAD_DIM), lambda g, b, *_: (g, 0, b, 0)),
                pl.BlockSpec((1, 1, 1, heads * rows), lambda g, b, *_: (g, b, 0, 0)),
            ],
            scratch_shapes=[
                pltpu.VMEM((1, heads * rows), F32),
                pltpu.VMEM((tall, heads * rows), F32),
                pltpu.VMEM((tall, total), BF16),
            ],
        ),
        out_shape=[
            jax.ShapeDtypeStruct((groups, heads, tokens, HEAD_DIM), BF16),
            jax.ShapeDtypeStruct((groups, blocks, 1, heads * rows), F32),
        ],
        compiler_params=pltpu.CompilerParams(vmem_limit_bytes=48 * 2**20),
        cost_estimate=pl.CostEstimate(
            flops=groups * heads * tokens * total * 256, bytes_accessed=groups * total * 512, transcendentals=0
        ),
        name="attention_forward",
    )(lists, counts, first, q, kv, marks)


def backward_kernel(
    lists, counts, first, q_ref, do_ref, kv_ref, mark_ref, lse_ref, delta_ref, dq_ref, dkv_ref, dq_sum, dkv_sum, kt_ref
):
    block = pl.program_id(1)
    heads, rows = q_ref.shape[1], q_ref.shape[2]
    total = kv_ref.shape[1]
    stride = total // KEY_BLOCK
    place = first[0] + block * rows
    count = counts[block]

    @pl.when(block == 0)
    def _():
        dkv_sum[...] = jnp.zeros(dkv_sum.shape, F32)

        def flip(i, c):
            k0 = pl.multiple_of(i * KEY_BLOCK, KEY_BLOCK)
            turned = kv_ref[0, pl.ds(k0, KEY_BLOCK), :].T
            kt_ref[:, pl.ds(k0, KEY_BLOCK)] = turned[:HEAD_DIM]
            return c

        lax.fori_loop(0, stride, flip, 0)

    dq_sum[...] = jnp.zeros(dq_sum.shape, F32)

    def steps(start, n, masked):
        q = q_ref[0].reshape(heads * rows, 2 * HEAD_DIM)
        do = do_ref[0].reshape(heads * rows, 2 * HEAD_DIM)
        offs = [pl.multiple_of(lists[block * stride + start + u] * KEY_BLOCK, KEY_BLOCK) for u in range(n)]
        kv = jnp.concatenate([kv_ref[0, pl.ds(k0, KEY_BLOCK), :] for k0 in offs], axis=0)
        mark = jnp.concatenate([mark_ref[pl.ds(k0, KEY_BLOCK), :] for k0 in offs], axis=0)
        kt = jnp.concatenate([kt_ref[:, pl.ds(k0, KEY_BLOCK)] for k0 in offs], axis=1)
        scores = dg(jnp.where(left_half(kv.shape), kv, mark), q, NT) - lse_ref[0, 0]
        if masked:
            scores = causal(scores, offs[0] - place, heads)
        chances = jnp.exp2(scores)
        back = dg(kv, do, NT) - delta_ref[0, 0]
        score_back = (chances * back).astype(BF16)
        only_q = jnp.where(left_half(q.shape), q, jnp.zeros_like(q))
        update = dg(score_back, only_q, NN) + dg(chances.astype(BF16), do, NN)
        dq_sum[...] += dg(kt, score_back, NN)
        for u in range(n):
            dkv_sum[pl.ds(offs[u], KEY_BLOCK), :] += update[u * KEY_BLOCK : (u + 1) * KEY_BLOCK]

    steps(count, 1, True)
    cascade(count, UNROLL, lambda start, n: steps(start, n, False))
    dq_ref[0] = (dq_sum[...] * HEAD_DIM**-0.5).T.astype(BF16).reshape(heads, rows, HEAD_DIM)

    @pl.when(block == pl.num_programs(1) - 1)
    def _():
        summed = dkv_sum[...]
        dkv_ref[0] = jnp.where(left_half(summed.shape), summed * (1.0 / LOG2E), summed).astype(BF16)


def attention_backward(lists, counts, first, q, do, kv, marks, lse, delta):
    groups, heads, tokens, wide = q.shape
    total = kv.shape[1]
    blocks = counts.shape[0]
    rows = tokens // blocks
    return pl.pallas_call(
        backward_kernel,
        grid_spec=pltpu.PrefetchScalarGridSpec(
            num_scalar_prefetch=3,
            grid=(groups, blocks),
            in_specs=[
                pl.BlockSpec((1, heads, rows, wide), lambda g, b, *_: (g, 0, b, 0)),
                pl.BlockSpec((1, heads, rows, wide), lambda g, b, *_: (g, 0, b, 0)),
                pl.BlockSpec((1, total, wide), lambda g, b, *_: (g, 0, 0)),
                pl.BlockSpec((total, wide), lambda g, b, *_: (0, 0)),
                pl.BlockSpec((1, 1, 1, heads * rows), lambda g, b, *_: (g, b, 0, 0)),
                pl.BlockSpec((1, 1, 1, heads * rows), lambda g, b, *_: (g, b, 0, 0)),
            ],
            out_specs=[
                pl.BlockSpec((1, heads, rows, HEAD_DIM), lambda g, b, *_: (g, 0, b, 0)),
                pl.BlockSpec((1, total, wide), lambda g, b, *_: (g, 0, 0)),
            ],
            scratch_shapes=[
                pltpu.VMEM((HEAD_DIM, heads * rows), F32),
                pltpu.VMEM((total, wide), F32),
                pltpu.VMEM((HEAD_DIM, total), BF16),
            ],
        ),
        out_shape=[
            jax.ShapeDtypeStruct((groups, heads, tokens, HEAD_DIM), BF16),
            jax.ShapeDtypeStruct((groups, total, wide), BF16),
        ],
        compiler_params=pltpu.CompilerParams(vmem_limit_bytes=60 * 2**20),
        cost_estimate=pl.CostEstimate(
            flops=groups * heads * tokens * total * 640, bytes_accessed=groups * total * 1024, transcendentals=0
        ),
        name="attention_backward",
    )(lists, counts, first, q, do, kv, marks, lse, delta)


def norm_apply(value, gain):
    scale_rows = lax.rsqrt(jnp.sum(value * value, axis=1) / D + EPSILON)
    normed = (value * scale_rows[:, None] * gain[None, :]).astype(BF16)
    return (normed, scale_rows)


def norm_back(upstream, value, scale_rows, gain):
    weighted = upstream * gain[None, :]
    inner = jnp.sum(weighted * value, axis=1)
    value_back = (
        scale_rows[:, None] * weighted
        - value * (scale_rows * scale_rows * scale_rows * inner / D)[:, None]
    )
    gain_back = jnp.sum(upstream * value * scale_rows[:, None], axis=0)
    return (value_back, gain_back)


ROW = ("high", "core")
ALL_ROW = ("high", "core", "col")
ALL_COL = ("col", "high", "core")


def gather(value, axes):
    return lax.all_gather(value, axes, axis=0, tiled=True)


def scatter(value, axes):
    return lax.psum_scatter(value, axes, scatter_dimension=0, tiled=True)


def per_device(
    tokens,
    attention_gain,
    joint_weight,
    output_weight,
    feed_gain,
    gate_weight,
    up_weight,
    down_weight,
    cotangent,
    segment_lengths,
    parents,
):
    rows = lax.axis_size(ROW)
    columns = lax.axis_size("col")
    cores = lax.axis_size("core")
    total = tokens.shape[0] * columns
    own = tokens.shape[0] // rows
    held = own * cores
    groups = KV_HEADS // cores
    tables = tree_tables(segment_lengths, parents)
    row = lax.axis_index(ROW)
    column = lax.axis_index("col")
    index = column * tokens.shape[0] + row * own + jnp.arange(own, dtype=jnp.int32)
    cosines, sines = rotary_tables(index, tables)
    first = column * tokens.shape[0] + lax.axis_index("high") * held
    query_block = 256 if held % 256 == 0 else 128
    lists, counts = block_lists(first, held // query_block, query_block, total, tables)
    first = jnp.reshape(first, (1,)).astype(jnp.int32)
    key_hot = segment_hot(jnp.arange(total, dtype=jnp.int32), tables).astype(F32)
    marks = jnp.pad(key_hot, ((0, 0), (HEAD_DIM, HEAD_DIM - key_hot.shape[1]))).astype(BF16)
    held_hot = segment_hot(first[0] + jnp.arange(held, dtype=jnp.int32), tables).astype(F32)
    reach = jnp.sum(held_hot[:, :, None] * tables[2][None], axis=1)
    bars = jnp.pad((reach - 1.0) * BIG, ((0, 0), (0, HEAD_DIM - reach.shape[1]))).astype(BF16)

    def to_tokens(value):
        return lax.all_to_all(value, ROW, split_axis=0, concat_axis=1, tiled=True)

    def to_features(value):
        return lax.all_to_all(value, ROW, split_axis=1, concat_axis=0, tiled=True)

    def swap_cores(value):
        return lax.all_to_all(value, "core", split_axis=0, concat_axis=0, tiled=True)

    stream = to_tokens(tokens).astype(F32)
    gain_one = gather(attention_gain, ROW).astype(F32)
    gain_two = gather(feed_gain, ROW).astype(F32)
    joint_full = gather(joint_weight, ALL_COL).reshape(columns, D, -1)
    joint_full = joint_full.transpose(1, 0, 2).reshape(D, -1)

    normed_one, scale_one = norm_apply(stream, gain_one)
    joint = jnp.dot(normed_one, joint_full, preferred_element_type=F32).astype(BF16)
    raw = joint.astype(F32)
    queries = turn(raw[:, :ATT].reshape(own, HEADS, HEAD_DIM), cosines, sines)
    queries = (queries * (LOG2E * HEAD_DIM**-0.5)).astype(BF16).reshape(own, cores, -1)
    keys = turn(raw[:, ATT : ATT + KEYS].reshape(own, KV_HEADS, HEAD_DIM), cosines, sines).astype(BF16)
    values = joint[:, ATT + KEYS :].reshape(own, KV_HEADS, HEAD_DIM)
    pairs = jnp.concatenate([keys, values], axis=2).reshape(own, cores, -1)
    packed = jnp.concatenate([queries, pairs], axis=2).transpose(1, 0, 2)
    packed = swap_cores(packed).reshape(held, -1)
    wide = groups * REPEAT * HEAD_DIM
    queries = packed[:, :wide].reshape(held, groups, REPEAT, HEAD_DIM).transpose(1, 2, 0, 3)
    queries = jnp.concatenate([queries, jnp.broadcast_to(bars, queries.shape)], axis=3)
    pairs = packed[:, wide:].reshape(held, groups, 2 * HEAD_DIM)
    all_pairs = [gather(pairs[:, g], ("col", "high")) for g in range(groups)]
    results = [
        attention_forward(lists, counts, first, queries[g : g + 1], all_pairs[g][None], marks) for g in range(groups)
    ]
    attended = jnp.concatenate([r[0] for r in results], axis=0)
    lse = [r[1] for r in results]
    by_core = attended.reshape(groups * REPEAT, cores, own, HEAD_DIM).transpose(1, 2, 0, 3)
    attended_rows = swap_cores(by_core.reshape(cores, own, -1)).transpose(1, 0, 2).reshape(own, ATT)

    output_full = gather(output_weight, ALL_ROW).reshape(rows, ATT, -1)
    output_full = output_full.transpose(1, 0, 2).reshape(ATT, D)
    gate_full = gather(gate_weight, ALL_COL).reshape(columns, D, -1)
    up_full = gather(up_weight, ALL_COL).reshape(columns, D, -1)
    down_full = gather(down_weight, ALL_ROW).reshape(rows, -1, D // rows)
    down_full = down_full.transpose(1, 0, 2).reshape(-1, D)
    gate_full = gate_full.transpose(1, 0, 2).reshape(D, -1)
    up_full = up_full.transpose(1, 0, 2).reshape(D, -1)
    hidden = stream + jnp.dot(attended_rows, output_full, preferred_element_type=F32)
    normed_two, scale_two = norm_apply(hidden, gain_two)
    gate = jnp.dot(normed_two, gate_full, preferred_element_type=F32)
    up_value = jnp.dot(normed_two, up_full, preferred_element_type=F32)
    sigmoid = jax.nn.sigmoid(gate)
    mixed = (gate * sigmoid * up_value).astype(BF16)
    output = hidden + jnp.dot(mixed, down_full, preferred_element_type=F32)
    layer_output = to_features(output.astype(BF16))

    upstream = to_tokens(cotangent)
    mixed_back = dg(upstream, down_full, NT)
    gate_back = (mixed_back * up_value * (sigmoid * (1.0 + gate * (1.0 - sigmoid)))).astype(BF16)
    up_back = (mixed_back * gate * sigmoid).astype(BF16)

    def by_columns(left, right):
        part = lax.dot_general(left, right, (((0,), (0,)), ((), ())), preferred_element_type=F32).astype(BF16)
        part = part.reshape(part.shape[0], columns, -1).transpose(1, 0, 2)
        return scatter(part.reshape(-1, part.shape[2]), ALL_COL).astype(F32)

    def by_rows(left, right):
        part = lax.dot_general(left, right, (((0,), (0,)), ((), ())), preferred_element_type=F32).astype(BF16)
        part = part.reshape(part.shape[0], rows, -1).transpose(1, 0, 2)
        return scatter(part.reshape(-1, part.shape[2]), ALL_ROW).astype(F32)

    down_gradient = by_rows(mixed, upstream)
    gate_gradient = by_columns(normed_two, gate_back)
    up_gradient = by_columns(normed_two, up_back)
    normed_two_back = dg(gate_back, gate_full, NT) + dg(up_back, up_full, NT)
    hidden_part, gain_two_part = norm_back(normed_two_back, hidden, scale_two, gain_two)
    hidden_back = upstream.astype(F32) + hidden_part
    hidden_low = hidden_back.astype(BF16)
    attended_back = dg(hidden_low, output_full, NT).astype(BF16)
    output_gradient = by_rows(attended_rows, hidden_low)

    heads_back = swap_cores(attended_back.reshape(own, cores, -1).transpose(1, 0, 2)).reshape(held, -1)
    heads_back = heads_back.reshape(held, groups, REPEAT, HEAD_DIM).transpose(1, 2, 0, 3)
    delta = jnp.sum(heads_back.astype(F32) * attended.astype(F32), axis=3)
    delta = delta.reshape(groups, REPEAT, -1, query_block).transpose(0, 2, 1, 3)
    delta = delta.reshape(groups, -1, 1, REPEAT * query_block)
    heads_back = jnp.pad(heads_back, ((0, 0), (0, 0), (0, 0), (HEAD_DIM, 0)))
    backs = [
        attention_backward(
            lists,
            counts,
            first,
            queries[g : g + 1],
            heads_back[g : g + 1],
            all_pairs[g][None],
            marks,
            lse[g],
            delta[g : g + 1],
        )
        for g in range(groups)
    ]
    query_back = jnp.concatenate([b[0] for b in backs], axis=0)
    query_back = query_back.reshape(groups * REPEAT, held, HEAD_DIM).transpose(1, 0, 2).reshape(held, -1)
    pair_back = [scatter(b[1][0], ("col", "high")) for b in backs]
    packed = jnp.concatenate([query_back, *pair_back], axis=1).reshape(cores, own, -1)
    packed = swap_cores(packed)
    query_back = packed[:, :, :wide].transpose(1, 0, 2).reshape(own, HEADS, HEAD_DIM)
    pair_back = packed[:, :, wide:].transpose(1, 0, 2).reshape(own, KV_HEADS, 2 * HEAD_DIM)
    query_back = turn(query_back.astype(F32), cosines, -sines).astype(BF16).reshape(own, ATT)
    key_back = turn(pair_back[:, :, :HEAD_DIM].astype(F32), cosines, -sines).astype(BF16).reshape(own, KEYS)
    value_back = pair_back[:, :, HEAD_DIM:].reshape(own, KEYS)
    joint_back = jnp.concatenate([query_back, key_back, value_back], axis=1)
    normed_one_back = dg(joint_back, joint_full, NT)
    joint_gradient = by_columns(normed_one, joint_back)
    stream_part, gain_one_part = norm_back(normed_one_back, stream, scale_one, gain_one)
    input_gradient = to_features((hidden_back + stream_part).astype(BF16)).astype(F32)
    gains = lax.psum(jnp.stack([gain_one_part, gain_two_part]), ALL_COL)
    gains = lax.dynamic_slice_in_dim(gains, row * (D // rows), D // rows, 1)
    return (
        layer_output,
        input_gradient,
        gains[0],
        joint_gradient,
        output_gradient,
        gains[1],
        gate_gradient,
        up_gradient,
        down_gradient,
    )


def solution(mesh):
    leaves, rows, columns = (mesh.shape[name] for name in ("leaf", "row", "col"))
    split = Mesh(mesh.devices.reshape(leaves, rows // 2, 2, columns), ("leaf", "high", "core", "col"))
    return jax.shard_map(
        per_device,
        mesh=split,
        in_specs=(
            P(("leaf", "col"), ROW),
            P(ROW),
            P(ROW, "col"),
            P("col", ROW),
            P(ROW),
            P(ROW, "col"),
            P(ROW, "col"),
            P("col", ROW),
            P(("leaf", "col"), ROW),
            P("leaf"),
            P("leaf"),
        ),
        out_specs=(
            P(("leaf", "col"), ROW),
            P(("leaf", "col"), ROW),
            P(("leaf", *ROW)),
            P(("leaf", *ROW), "col"),
            P(("leaf", "col"), ROW),
            P(("leaf", *ROW)),
            P(("leaf", *ROW), "col"),
            P(("leaf", *ROW), "col"),
            P(("leaf", "col"), ROW),
        ),
        check_vma=False,
    )
```

time: 4310 us -> 1290 us (0.30)
  matrix products: 1480 us -> 123 us
  waiting for transfers between devices: 1880 us -> 700 us
  other arithmetic: 361 us -> 35.9 us
  blocking collectives: 215 us -> 96.4 us
  local copies, waits for them, and re-layouts: 317 us -> 202 us
  Pallas kernels: 0 us -> 92.1 us
    dot_general x113 -> x15, matrix products: 1480 us -> 123 us  [the longest x5 39.9 us: dg(): return lax.dot_general(a, b, dims, preferred_element_type=F32)]
    all_gather x10 -> x8, waiting for transfers between devices: 907 us -> 268 us  [gather(): return lax.all_gather(value, axes, axis=0, tiled=True)]
    unnamed x21 -> x17, waiting for transfers between devices: 360 us -> 80.8 us
    reduce_scatter x7, waiting for transfers between devices: 577 us -> 334 us  [scatter(): return lax.psum_scatter(value, axes, scatter_dimension=0, tiled=True)]
    reduce_sum x47 -> x10, other arithmetic: 216 us -> 4.95 us  [the longest x1 3.44 us: per_device(): delta = jnp.sum(heads_back.astype(F32) * attended.astype(F32), axis=3)]
    dynamic_update_slice x10 -> x0, local copies, waits for them, and re-layouts: 156 us -> none  [grad_block(): lax.dynamic_update_slice_in_dim(key_back, previous + update, first, 0)]
    all_to_all x3 -> x4, blocking collectives: 158 us -> 22.4 us  [swap_cores(): lax.all_to_all(value, 'core', split_axis=0, concat_axis=0, tiled=True)]
    pallas_call x0 -> x6, Pallas kernels: none -> 92.1 us  [the longest x3 54.6 us: attention_backward(): pl.pallas_call(backward_kernel, grid_spec=pltpu.PrefetchScalarGridSpec(nu...]
  transfers between devices with their start and end apart: 20 -> 20, of which waited for: 20 -> 15; matrix products, arithmetic and copies ran while one was open for 4% -> 22% of each run, Pallas kernels for 0% -> 6%
where the time goes in v1:
time: 1290 us; the launch traced here: 1280 us
  waiting for transfers between devices  700 us (54%)
  local copies, waits for them, and re-layouts  202 us (16%)
  matrix products  123 us (10%)
  blocking collectives  96.4 us (7%)
  Pallas kernels  92.1 us (7%)
  other arithmetic  35.9 us (3%)
  starting transfers between devices  16.8 us (1%)
  between operations  15.8 us (1%)
    reduce_scatter x7, waiting for transfers between devices, scatter(): return lax.psum_scatter(value, axes, scatter_dimension=0, tiled=True)  334 us
    all_gather x8, waiting for transfers between devices, gather(): return lax.all_gather(value, axes, axis=0, tiled=True)  268 us
    unnamed x17, waiting for transfers between devices  80.8 us
    pallas_call x3, Pallas kernels, attention_backward(): pl.pallas_call(backward_kernel, grid_spec=pltpu.PrefetchScalarGridSpec(nu...  54.6 us
    psum x1, blocking collectives, per_device(): gains = lax.psum(jnp.stack([gain_one_part, gain_two_part]), ALL_COL)  52 us
    dot_general x5, matrix products, dg(): return lax.dot_general(a, b, dims, preferred_element_type=F32)  39.9 us
    pallas_call x3, Pallas kernels, attention_forward(): pl.pallas_call(forward_kernel, grid_spec=pltpu.PrefetchScalarGridSpec(num...  37.4 us
    unnamed x116, local copies, waits for them, and re-layouts  33.5 us
  transfers between devices with their start and end apart: 20, of which 15 were waited for; matrix products, arithmetic and copies ran while one was open for 22% of the time, Pallas kernels for 6%

profile of v1, /device:TPU:0, one launch (start us, length us, event | category | flops | bytes accessed | tf_op | source)
XLA Modules:
  0.0 1281.7 jit_solution(9614467585979270402)
XLA Ops:
  11.4 4.2 all-to-all-start
  17.4 22.0 %all-reduce.5 = (bf16[1152]{0:T(1024)(128)(2,1)S(1)}, bf16[1152]{0:T(1024)(128)(2,1)S(1)}) all-reduce(bf16[1152]{0:T(1024)(128)(2,1)S(1)} %dynamic-update-slice, bf16[1152]{0:T(1024)(128)(2,1)S(1)} %dynamic-update-slice.1), channel_id=1, replica_groups=mesh['leaf'=2,'high'=2,'core'=2,'col'=4] {'high','core'}, use_global_device_ids=true, to_apply=%add.3 | all-reduce | flops 2304 | bytes 9216
  41.8 27.3 %all-gather.12.cloned.1.call-done = bf16[4608,480]{1,0:T(8,128)(2,1)} async-done(((bf16[288,480]{1,0:T(8,128)(2,1)}), bf16[4608,480]{1,0:T(8,128)(2,1)}) %all-gather.12.cloned.1.call-update) | async-done | bytes 4423696 | tf_op jit(solution)/shard_map/all_gather | solution.py:338
  69.0 8.4 copy.270
  80.3 3.9 convolution_convert_fusion.6
  88.6 4.8 copy.223
  96.2 5.8 all_to_all.84
  112.7 3.6 all-to-all-start.4
  124.7 4.8 copy.235
  129.4 9.4 all-to-all-done.4
  141.1 7.3 copy.271
  148.4 3.8 copy.234
  158.4 18.3 %all-gather.22.cloned.1.call-done = bf16[10240,1,128]{2,0,1:T(8,128)(2,1)} async-done(((bf16[1280,1,128]{2,0,1:T(8,128)(2,1)}), bf16[10240,1,128]{2,0,1:T(8,128)(2,1)}) %all-gather.22.cloned.1.call-update) | async-done | bytes 2621456 | tf_op jit(solution)/shard_map/all_gather | solution.py:338
  178.5 12.3 attention_forward.3
  192.5 40.2 %all-gather.24.cloned.1.call-done = bf16[10240,1,128]{2,0,1:T(8,128)(2,1)} async-done(((bf16[1280,1,128]{2,0,1:T(8,128)(2,1)}), bf16[10240,1,128]{2,0,1:T(8,128)(2,1)}) %all-gather.24.cloned.1.call-update) | async-done | bytes 2621456 | tf_op jit(solution)/shard_map/all_gather | solution.py:338
  234.4 12.8 %attention_forward.4 = (bf16[1,3,1280,64]{3,2,1,0:T(8,128)(2,1)S(1)}, f32[1,5,1,768]{3,2,1,0:T(1,128)S(1)}) custom-call(s32[200]{0:T(256)S(1)} %reshape.572.lists, s32[5]{0:T(128)S(1)} %broadcast_add_fusion.counts, s32[1]{0:T(128)} %bitcast.2.first, bf16[1,3,1280,128]{3,2,1,0:T(8,128)(2,1)S(1)} %get-tuple-element.88.q_ref, ...), custom_call_target="tpu_custom_call" | custom-call | flops 10066329600 | bytes 5242880 | tf_op jit(solution)/shard_map/attention_forward/pallas_call | solution.py:190
  248.3 40.3 %all-gather.26.cloned.1.call-done = bf16[10240,1,128]{2,0,1:T(8,128)(2,1)} async-done(((bf16[1280,1,128]{2,0,1:T(8,128)(2,1)}), bf16[10240,1,128]{2,0,1:T(8,128)(2,1)}) %all-gather.26.cloned.1.call-update) | async-done | bytes 2621456 | tf_op jit(solution)/shard_map/all_gather | solution.py:338
  290.4 12.3 attention_forward.5
  306.9 5.3 all_to_all.85
  312.2 4.7 multiply_reduce_fusion.5
  318.6 37.5 %all-gather.18.cloned.1.call-done = bf16[4608,768]{1,0:T(8,128)(2,1)} async-done(((bf16[288,768]{1,0:T(8,128)(2,1)}), bf16[4608,768]{1,0:T(8,128)(2,1)}) %all-gather.18.cloned.1.call-update) | async-done | bytes 7077904 | tf_op jit(solution)/shard_map/all_gather | solution.py:338
  356.1 10.5 copy.237
  366.7 56.9 %all-gather.16.cloned.1.call-done = bf16[4608,768]{1,0:T(8,128)(2,1)} async-done(((bf16[288,768]{1,0:T(8,128)(2,1)}), bf16[4608,768]{1,0:T(8,128)(2,1)}) %all-gather.16.cloned.1.call-update) | async-done | bytes 7077904 | tf_op jit(solution)/shard_map/all_gather | solution.py:338
  423.5 10.3 copy.236
  433.9 9.9 fusion.34
  443.7 47.0 %all-gather.20.cloned.1.call-done = bf16[12288,288]{0,1:T(8,128)(2,1)} async-done(((bf16[768,288]{0,1:T(8,128)(2,1)}), bf16[12288,288]{0,1:T(8,128)(2,1)}) %all-gather.20.cloned.1.call-update) | async-done | bytes 7077904 | tf_op jit(solution)/shard_map/all_gather | solution.py:338
  490.7 10.1 fusion.4
  500.8 16.1 %fusion.3 = (bf16[640,3072]{1,0:T(8,128)(2,1)S(1)}, bf16[640,3072]{1,0:T(8,128)(2,1)}, bf16[640,3072]{1,0:T(8,128)(2,1)}) fusion(f32[640,3072,1]{1,0,2:T(8,128)} %fusion.4, f32[640,3072]{1,0:T(8,128)} %fusion.34, bf16[640,1152]{1,0:T(8,128)(2,1)S(1)} %copy-done.29, bf16[1152,3072]{0,1:T(8,128)(2,1)} %bitcast.197), kind=kOutput, calls=%fused_computation.8 | convolution fusion | flops 4561305600 | bytes 36077568 | tf_op jit(solution)/shard_map/dot_general | solution.py:428
  516.9 10.8 fusion.35
  527.7 9.4 multiply_reduce_fusion.1
  542.7 5.3 all_to_all.86
  561.1 18.0 %attention_backward.3 = (bf16[1,3,1280,64]{3,2,1,0:T(8,128)(2,1)}, bf16[1,10240,128]{2,1,0:T(8,128)(2,1)}) custom-call(s32[200]{0:T(256)} %copy-done.3, s32[5]{0:T(128)} %copy-done.7, s32[1]{0:T(128)} %bitcast.2.first, bf16[1,3,1280,128]{3,2,1,0:T(8,128)(2,1)} %copy-done.2, bf16[1,3,1280,128]{3,2,1,0:T(8,128)(2,1)} %get-tuple-element.93.do_ref, ...), custom_call_target="tpu_custom_call" | custom-call | flops 25165824000 | bytes 10485760 | tf_op jit(solution)/shard_map/attention_backward/pallas_call | solution.py:280
  579.9 18.2 %attention_backward.4 = (bf16[1,3,1280,64]{3,2,1,0:T(8,128)(2,1)}, bf16[1,10240,128]{2,1,0:T(8,128)(2,1)}) custom-call(s32[200]{0:T(256)} %copy-done.3, s32[5]{0:T(128)} %copy-done.7, s32[1]{0:T(128)} %bitcast.2.first, bf16[1,3,1280,128]{3,2,1,0:T(8,128)(2,1)} %copy-done.1, bf16[1,3,1280,128]{3,2,1,0:T(8,128)(2,1)} %get-tuple-element.95.do_ref, ...), custom_call_target="tpu_custom_call" | custom-call | flops 25165824000 | bytes 10485760 | tf_op jit(solution)/shard_map/attention_backward/pallas_call | solution.py:280
  598.8 18.4 %attention_backward.5 = (bf16[1,3,1280,64]{3,2,1,0:T(8,128)(2,1)}, bf16[1,10240,128]{2,1,0:T(8,128)(2,1)}) custom-call(s32[200]{0:T(256)} %copy-done.3, s32[5]{0:T(128)} %copy-done.7, s32[1]{0:T(128)} %bitcast.2.first, bf16[1,3,1280,128]{3,2,1,0:T(8,128)(2,1)} %copy-done, bf16[1,3,1280,128]{3,2,1,0:T(8,128)(2,1)} %get-tuple-element.94.do_ref, ...), custom_call_target="tpu_custom_call" | custom-call | flops 25165824000 | bytes 10485760 | tf_op jit(solution)/shard_map/attention_backward/pallas_call | solution.py:280
  617.3 5.3 convolution_convert_fusion.3
  622.6 4.7 copy.265
  628.6 10.3 convolution_convert_fusion.2
  638.9 13.9 %reshape.603 = bf16[1152,4,768]{2,1,0:T(4,128)(2,1)} reshape(bf16[1152,3072]{1,0:T(8,128)(2,1)} %convolution_convert_fusion.2) | data formatting | bytes 14155776 | tf_op jit(solution)/shard_map/reshape | solution.py:442
  652.8 6.8 copy.266
  659.7 9.7 convolution_convert_fusion.1
  669.5 13.9 %reshape.605 = bf16[1152,4,768]{2,1,0:T(4,128)(2,1)} reshape(bf16[1152,3072]{1,0:T(8,128)(2,1)} %convolution_convert_fusion.1) | data formatting | bytes 14155776 | tf_op jit(solution)/shard_map/reshape | solution.py:442
  683.4 6.9 copy.267
  691.6 8.0 convolution_convert_fusion
  699.6 3.7 copy.286
  713.8 51.8 %reduce-scatter.13.cloned.1.call-done = bf16[1280,128]{1,0:T(8,128)(2,1)} async-done(((bf16[10240,128]{1,0:T(8,128)(2,1)}), bf16[1280,128]{1,0:T(8,128)(2,1)}) %reduce-scatter.13.cloned.1.call-update) | async-done | bytes 327696 | tf_op jit(solution)/shard_map/reduce_scatter | solution.py:342
  767.1 71.3 %reduce-scatter.15.cloned.1.call-done = bf16[1280,128]{1,0:T(8,128)(2,1)} async-done(((bf16[10240,128]{1,0:T(8,128)(2,1)}), bf16[1280,128]{1,0:T(8,128)(2,1)}) %reduce-scatter.15.cloned.1.call-update) | async-done | bytes 327696 | tf_op jit(solution)/shard_map/reduce_scatter | solution.py:342
  839.8 3.8 pad_maximum_fusion.1
  843.9 6.0 all_to_all.87
  853.8 7.1 convolution_convert_fusion.4
  860.9 6.7 copy.263
  867.6 6.6 copy.274
  874.3 3.9 copy.293
  878.2 7.9 fusion.7
  886.1 3.6 copy.239
  889.7 4.5 all-to-all-start.3
  894.3 7.4 multiply_reduce_fusion.2
  903.5 3.6 copy.259
  907.2 8.4 all-to-all-done.3
  915.5 3.6 all-to-all-start.7
  923.7 52.0 %psum.7 = f32[2,1152]{1,0:T(2,128)S(1)} all-reduce(f32[2,1152]{1,0:T(2,128)S(1)} %pad_maximum_fusion.9), channel_id=1, replica_groups=mesh['leaf'=2,'high'=2,'core'=2,'col'=4] {'col','high','core'}, use_global_device_ids=true, to_apply=%region_20.21 | all-reduce | flops 2304 | bytes 18432 | tf_op jit(solution)/shard_map/psum | solution.py:495
  978.6 27.4 %reduce-scatter.19.cloned.1.call-done = bf16[288,768]{1,0:T(8,128)(2,1)} async-done(((bf16[4608,768]{1,0:T(8,128)(2,1)}), bf16[288,768]{1,0:T(8,128)(2,1)}) %reduce-scatter.19.cloned.1.call-update) | async-done | bytes 442384 | tf_op jit(solution)/shard_map/reduce_scatter | solution.py:342
  1007.9 92.0 %reduce-scatter.21.cloned.1.call-done = bf16[288,768]{1,0:T(8,128)(2,1)} async-done(((bf16[4608,768]{1,0:T(8,128)(2,1)}), bf16[288,768]{1,0:T(8,128)(2,1)}) %reduce-scatter.21.cloned.1.call-update) | async-done | bytes 442384 | tf_op jit(solution)/shard_map/reduce_scatter | solution.py:342
  1102.0 91.5 %reduce-scatter.23.cloned.1.call-done = bf16[768,288]{0,1:T(8,128)(2,1)} async-done(((bf16[12288,288]{0,1:T(8,128)(2,1)}), bf16[768,288]{0,1:T(8,128)(2,1)}) %reduce-scatter.23.cloned.1.call-update) | async-done | bytes 442384 | tf_op jit(solution)/shard_map/reduce_scatter | solution.py:342
  1195.4 77.3 %reduce-scatter.25.cloned.1.call-done = bf16[288,480]{1,0:T(8,128)(2,1)} async-done(((bf16[4608,480]{1,0:T(8,128)(2,1)}), bf16[288,480]{1,0:T(8,128)(2,1)}) %reduce-scatter.25.cloned.1.call-update) | async-done | bytes 276496
  (256 shorter events, 116.3 us)
Async XLA Ops:
  7.2 61.9 %all-gather.12.cloned.1.call-start = ((), (), s32[]{:S(2)}) async-start(), calls=%async_computation.16 | async-start | bytes 5013504 | tf_op jit(solution)/shard_map/all_gather | solution.py:338
  7.9 133.2 %all-gather.14.cloned.1.call-start = ((), (), s32[]{:S(2)}) async-start(), calls=%async_computation.17 | async-start | bytes 3760128 | tf_op jit(solution)/shard_map/all_gather | solution.py:338
  8.7 6.9 copy-start.49
  8.7 8.2 copy-start.47
  8.7 8.4 copy-start.48
  8.7 30.8 %copy-start.46 = (s32[13]{0:T(128)S(1)}, s32[13]{0:T(128)}, u32[]{:S(2)}) copy-start(s32[13]{0:T(128)} %param.21) | copy-start | bytes 160
  8.7 30.9 %copy-start.45 = (s32[13]{0:T(128)S(1)}, s32[13]{0:T(128)}, u32[]{:S(2)}) copy-start(s32[13]{0:T(128)} %param.20) | copy-start | bytes 160
  11.4 29.6 %all-to-all-start = ((bf16[4,640,288]{1,2,0:T(8,128)(2,1)}), bf16[4,640,288]{1,2,0:T(8,128)(2,1)S(1)}, u32[]{:S(2)}, u32[]{:S(2)}) async-start(bf16[4,640,288]{1,2,0:T(8,128)(2,1)} %bitcast.165), calls=%async_computation | async-start | bytes 2949120 | tf_op jit(solution)/shard_map/all_to_all | solution.py:381
  15.6 161.2 %all-gather.22.cloned.1.call-start = ((), (), s32[]{:S(2)}) async-start(), calls=%async_computation.28 | async-start | bytes 2949120 | tf_op jit(solution)/shard_map/all_gather | solution.py:338
  39.3 2.0 copy-start.42
  41.0 53.6 %copy-start.27 = (f32[640,32]{0,1:T(8,128)}, f32[640,32]{0,1:T(8,128)S(1)}, u32[]{:S(2)}) copy-start(f32[640,32]{0,1:T(8,128)S(1)} %get-tuple-element.110) | copy-start | bytes 245764
  41.4 36.1 %copy-start.40 = (f32[640]{0:T(1024)}, f32[640]{0:T(1024)S(1)}, u32[]{:S(2)}) copy-start(f32[640]{0:T(1024)S(1)} %multiply_reduce_fusion.6) | copy-start | bytes 7684
  41.4 36.0 %copy-start.38 = (f32[640]{0:T(1024)}, f32[640]{0:T(1024)S(1)}, u32[]{:S(2)}) copy-start(f32[640]{0:T(1024)S(1)} %add_rsqrt_fusion.1) | copy-start | bytes 7684
  80.3 3.9 copy-start.25
  93.3 1.9 copy-start.18
  93.3 1.9 copy-start.36
  102.2 1.4 copy-start.20
  103.7 7.8 copy-start.31
  106.5 126.2 %all-gather.24.cloned.1.call-start = ((), (), s32[]{:S(2)}) async-start(), calls=%async_computation.29 | async-start | bytes 2949120 | tf_op jit(solution)/shard_map/all_gather | solution.py:338
  108.4 180.2 %all-gather.26.cloned.1.call-start = ((), (), s32[]{:S(2)}) async-start(), calls=%async_computation.30 | async-start | bytes 2949120 | tf_op jit(solution)/shard_map/all_gather | solution.py:338
  109.4 246.7 %all-gather.18.cloned.1.call-start = ((), (), s32[]{:S(2)}) async-start(), calls=%async_computation.19 | async-start | bytes 7520256 | tf_op jit(solution)/shard_map/all_gather | solution.py:338
  110.0 313.6 %all-gather.16.cloned.1.call-start = ((), (), s32[]{:S(2)}) async-start(), calls=%async_computation.18 | async-start | bytes 7520256 | tf_op jit(solution)/shard_map/all_gather | solution.py:338
  110.7 380.0 %all-gather.20.cloned.1.call-start = ((), (), s32[]{:S(2)}) async-start(), calls=%async_computation.20 | async-start | bytes 7520256 | tf_op jit(solution)/shard_map/all_gather | solution.py:338
  112.7 26.1 %all-to-all-start.4 = ((bf16[4,640,288]{1,2,0:T(8,128)(2,1)}), bf16[4,640,288]{1,2,0:T(8,128)(2,1)S(1)}, u32[]{:S(2)}, u32[]{:S(2)}) async-start(bf16[4,640,288]{1,2,0:T(8,128)(2,1)} %bitcast.204), calls=%async_computation.4 | async-start | bytes 2949120 | tf_op jit(solution)/shard_map/all_to_all | solution.py:381
  116.3 596.1 %reduce-scatter.11.cloned.1.call-start = ((), (), s32[]{:S(2)}) async-start(), calls=%async_computation.21 | async-start | bytes 2949120 | tf_op jit(solution)/shard_map/reduce_scatter | solution.py:342
  118.2 170.4 %copy-start.3 = (s32[200]{0:T(256)}, s32[200]{0:T(256)S(1)}, u32[]{:S(2)}) copy-start(s32[200]{0:T(256)S(1)} %reshape.572.lists) | copy-start | bytes 2404
  119.0 169.6 %copy-start.7 = (s32[5]{0:T(128)}, s32[5]{0:T(128)S(1)}, u32[]{:S(2)}) copy-start(s32[5]{0:T(128)S(1)} %broadcast_add_fusion.counts) | copy-start | bytes 64
  138.8 9.6 copy-start.23
  148.4 3.8 copy-start.21
  152.3 2.7 copy-start.34
  154.9 1.9 copy-start.19
  158.4 32.4 %copy-start.2 = (bf16[1,3,1280,128]{3,2,1,0:T(8,128)(2,1)}, bf16[1,3,1280,128]{3,2,1,0:T(8,128)(2,1)S(1)}, u32[]{:S(2)}) copy-start(bf16[1,3,1280,128]{3,2,1,0:T(8,128)(2,1)S(1)} %get-tuple-element.87.q_ref) | copy-start | bytes 2949124
  158.4 74.3 %copy-start.1 = (bf16[1,3,1280,128]{3,2,1,0:T(8,128)(2,1)}, bf16[1,3,1280,128]{3,2,1,0:T(8,128)(2,1)S(1)}, u32[]{:S(2)}) copy-start(bf16[1,3,1280,128]{3,2,1,0:T(8,128)(2,1)S(1)} %get-tuple-element.88.q_ref) | copy-start | bytes 2949124
  158.4 130.2 %copy-start = (bf16[1,3,1280,128]{3,2,1,0:T(8,128)(2,1)}, bf16[1,3,1280,128]{3,2,1,0:T(8,128)(2,1)S(1)}, u32[]{:S(2)}) copy-start(bf16[1,3,1280,128]{3,2,1,0:T(8,128)(2,1)S(1)} %get-tuple-element.86.q_ref) | copy-start | bytes 2949124
  176.8 1.7 copy-start.6
  232.7 1.7 copy-start.5
  247.3 55.4 %copy-start.9 = (f32[1,5,1,768]{3,2,1,0:T(1,128)}, f32[1,5,1,768]{3,2,1,0:T(1,128)S(1)}, u32[]{:S(2)}) copy-start(f32[1,5,1,768]{3,2,1,0:T(1,128)S(1)} %get-tuple-element.26.lse_ref) | copy-start | bytes 46084
  288.6 1.7 copy-start.4
  302.7 4.2 copy-start.8
  306.9 5.3 copy-start.13
  312.2 4.7 copy-start.32
  316.9 220.2 %copy-start.11 = (f32[640,1152]{1,0:T(8,128)}, f32[640,1152]{1,0:T(8,128)S(1)}, u32[]{:S(2)}) copy-start(f32[640,1152]{1,0:T(8,128)S(1)} %get-tuple-element.112) | copy-start | bytes 8847364
  490.7 10.1 copy-start.29
  516.9 10.9 copy-start.50
  527.7 9.4 copy-start.22
  537.1 2.3 copy-start.26
  537.9 1.6 copy-start.15
  579.2 186.5 %reduce-scatter.13.cloned.1.call-start = ((), (), s32[]{:S(2)}) async-start(), calls=%async_computation.22 | async-start | bytes 2949120 | tf_op jit(solution)/shard_map/reduce_scatter | solution.py:342
  598.1 240.3 %reduce-scatter.15.cloned.1.call-start = ((), (), s32[]{:S(2)}) async-start(), calls=%async_computation.23 | async-start | bytes 2949120 | tf_op jit(solution)/shard_map/reduce_scatter | solution.py:342
  598.8 18.5 %copy-start.16 = (f32[640,1152]{1,0:T(8,128)S(1)}, f32[640,1152]{1,0:T(8,128)}, u32[]{:S(2)}) copy-start(f32[640,1152]{1,0:T(8,128)} %copy-done.15) | copy-start | bytes 8847364
  617.2 304.7 %reduce-scatter.17.cloned.1.call-start = ((), (), s32[]{:S(2)}) async-start(), calls=%async_computation.24 | async-start | bytes 3760128 | tf_op jit(solution)/shard_map/reduce_scatter | solution.py:342
  627.3 378.7 %reduce-scatter.19.cloned.1.call-start = ((), (), s32[]{:S(2)}) async-start(), calls=%async_computation.25 | async-start | bytes 7520256 | tf_op jit(solution)/shard_map/reduce_scatter | solution.py:342
  659.7 440.3 %reduce-scatter.21.cloned.1.call-start = ((), (), s32[]{:S(2)}) async-start(), calls=%async_computation.26 | async-start | bytes 7520256 | tf_op jit(solution)/shard_map/reduce_scatter | solution.py:342
  690.2 1.4 copy-start.24
  690.3 503.2 %reduce-scatter.23.cloned.1.call-start = ((), (), s32[]{:S(2)}) async-start(), calls=%async_computation.27 | async-start | bytes 7520256 | tf_op jit(solution)/shard_map/reduce_scatter | solution.py:342
  703.4 569.4 %reduce-scatter.25.cloned.1.call-start = ((), (), s32[]{:S(2)}) async-start(), calls=%async_computation.31 | async-start | bytes 5013504
  851.3 2.5 copy-start.14
  851.3 2.5 copy-start.39
  874.3 3.9 copy-start.12
  889.7 25.8 %all-to-all-start.3 = ((bf16[640,4,288]{0,2,1:T(8,128)(2,1)}), bf16[640,4,288]{0,2,1:T(8,128)(2,1)}, u32[]{:S(2)}, u32[]{:S(2)}) async-start(bf16[640,4,288]{0,2,1:T(8,128)(2,1)} %bitcast.205), calls=%async_computation.3 | async-start | bytes 2949120 | tf_op jit(solution)/shard_map/all_to_all | solution.py:384
  894.3 7.4 copy-start.41
  894.3 7.4 copy-start.17
  903.5 15.6 %copy-start.44 = (f32[1152]{0:T(1024)S(1)}, f32[1152]{0:T(1024)}, u32[]{:S(2)}) copy-start(f32[1152]{0:T(1024)} %get-tuple-element.71) | copy-start | bytes 13828
  915.5 60.9 %all-to-all-start.7 = ((bf16[640,4,288]{0,2,1:T(8,128)(2,1)}), bf16[640,4,288]{0,2,1:T(8,128)(2,1)S(1)}, u32[]{:S(2)}, u32[]{:S(2)}) async-start(bf16[640,4,288]{0,2,1:T(8,128)(2,1)} %bitcast.67), calls=%async_computation.10 | async-start | bytes 2949120 | tf_op jit(solution)/shard_map/all_to_all | solution.py:384
  (7 other events, 6.6 us)
Sparse Core Ops, SparseCore 0:
  10.3 58.7 all-gather.11
  71.3 45.7 all-gather.13
  119.9 56.7 all-gather.21
  179.4 53.2 all-gather.23
  235.3 53.3 all-gather.25
  290.8 65.3 all-gather.17
  358.4 65.0 all-gather.15
  425.8 64.9 all-gather.19
  579.3 113.8 reduce-scatter.10
  696.5 69.0 reduce-scatter.12
  769.2 69.1 reduce-scatter.14
  842.1 67.6 reduce-scatter.16
  913.8 92.1 reduce-scatter.18
  1010.3 89.5 reduce-scatter.20
  1103.8 89.5 reduce-scatter.22
  1197.6 75.0 reduce-scatter.24

commit v2 on v1

v2 whole, which is shorter than its diff:
```python
import functools

import jax
import jax.numpy as jnp
from jax import lax
from jax.experimental import pallas as pl
from jax.experimental.pallas import tpu as pltpu
from jax.sharding import Mesh
from jax.sharding import PartitionSpec as P

D = 1152
HEADS = 18
KV_HEADS = 6
HEAD_DIM = 64
REPEAT = HEADS // KV_HEADS
ATT = HEADS * HEAD_DIM
KEYS = KV_HEADS * HEAD_DIM

EPSILON = 1e-05
THETA = 10000.0
BIG = 2.0**30
LOG2E = 1.4426950408889634
UNROLL = 8
BF16 = jnp.bfloat16
F32 = jnp.float32
NT = (((1,), (1,)), ((), ()))
NN = (((1,), (0,)), ((), ()))


def dg(a, b, dims):
    return lax.dot_general(a, b, dims, preferred_element_type=F32)


def tree_tables(segment_lengths, parents):
    count = segment_lengths.shape[0]
    labels = jnp.arange(count, dtype=jnp.int32)
    ends = jnp.sum(jnp.where(labels[None, :] <= labels[:, None], segment_lengths[None, :], 0), axis=1)
    starts = ends - segment_lengths
    parent_hot = parents[:, None] == labels[None, :]
    grand = jnp.sum(jnp.where(parent_hot, parents[None, :], 0), axis=1)
    self_mark = labels[:, None] == labels[None, :]
    grand_mark = grand[:, None] == labels[None, :]
    ancestry = (self_mark | parent_hot | grand_mark).astype(F32)
    strict = (parent_hot | grand_mark) & jnp.logical_not(self_mark)
    offsets = jnp.sum(jnp.where(strict, segment_lengths[None, :], 0), axis=1)
    return (ends, starts, ancestry, offsets)


def segment_hot(index, tables):
    ends, starts, _, _ = tables
    return (index[:, None] >= starts[None, :]) & (index[:, None] < ends[None, :])


def rotary_tables(index, tables):
    hot = segment_hot(index, tables)
    depth = index + jnp.sum(jnp.where(hot, (tables[3] - tables[1])[None, :], 0), axis=1)
    half = HEAD_DIM // 2
    rates = THETA ** (-jnp.arange(half, dtype=F32) / half)
    angles = depth.astype(F32)[:, None] * rates[None, :]
    return (jnp.cos(angles), jnp.sin(angles))


def turn(value, cosines, sines):
    half = value.shape[-1] // 2
    former, latter = (value[..., :half], value[..., half:])
    cos_part = cosines[:, None, :]
    sin_part = sines[:, None, :]
    return jnp.concatenate(
        [former * cos_part - latter * sin_part, latter * cos_part + former * sin_part], axis=-1
    )


def block_lists(first, key_index, block, held, tables):
    ends, starts, ancestry, _ = tables
    blocks = held // block
    key_low = key_index[::block]
    labels = jnp.arange(key_low.shape[0], dtype=jnp.int32)
    low = first + jnp.arange(blocks, dtype=jnp.int32) * block
    high = low + block
    query_has = ((starts[None, :] < high[:, None]) & (ends[None, :] > low[:, None])).astype(F32)
    key_has = ((starts[None, :] < key_low[:, None] + block) & (ends[None, :] > key_low[:, None])).astype(F32)
    reach = jnp.sum(query_has[:, :, None] * ancestry[None], axis=1)
    seen = jnp.sum(reach[:, None, :] * key_has[None], axis=2) > 0.5
    seen = seen & (key_low[None, :] < low[:, None])
    before = labels[None, :] < labels[:, None]
    rank = jnp.sum((seen[:, None, :] & before[None]).astype(jnp.int32), axis=2)
    place = seen[:, None, :] & (rank[:, None, :] == labels[None, :, None])
    lists = jnp.sum(jnp.where(place, labels[None, None, :], 0), axis=2)
    counts = jnp.sum(seen.astype(jnp.int32), axis=1)
    own = jnp.sum(jnp.where(key_low[None, :] == low[:, None], labels[None, :], 0), axis=1)
    lists = jnp.where(labels[None, :] == counts[:, None], own[:, None], lists)
    return (lists.reshape(-1).astype(jnp.int32), counts.astype(jnp.int32))


def cascade(count, unroll, steps):
    def body(i, c):
        steps(i * unroll, unroll)
        return c

    whole = count // unroll
    lax.fori_loop(0, whole, body, 0)
    start = whole * unroll
    size = unroll // 2
    while size:
        some = ((count - start) // size) > 0
        pl.when(some)(functools.partial(steps, start, size))
        start = start + jnp.where(some, size, 0)
        size //= 2


def causal(scores, heads):
    rows = lax.broadcasted_iota(jnp.int32, scores.shape, 0)
    columns = lax.rem(lax.broadcasted_iota(jnp.int32, scores.shape, 1), scores.shape[1] // heads)
    return jnp.where(rows <= columns, scores, -BIG)


def left_half(shape):
    return lax.broadcasted_iota(jnp.int32, shape, 1) < HEAD_DIM


def fetch(pieces, group, kv_ref, sems):
    copies, start = [], 0
    for i, piece in enumerate(pieces):
        lanes = pl.ds(pl.multiple_of(group * 2 * HEAD_DIM, 2 * HEAD_DIM), 2 * HEAD_DIM)
        target = kv_ref.at[pl.ds(start, piece.shape[0])]
        copies.append(pltpu.make_async_copy(piece.at[:, lanes], target, sems.at[i]))
        start += piece.shape[0]
    for copy in copies:
        copy.start()
    for copy in copies:
        copy.wait()


def forward_kernel(lists, counts, q_ref, mark_ref, *refs):
    *pieces, o_ref, lse_ref, top_ref, sum_ref, kv_ref, vt_ref, sems = refs
    block = pl.program_id(1)
    heads, rows = q_ref.shape[1], q_ref.shape[2]
    total = kv_ref.shape[0]
    stride = total // rows
    count = counts[block]

    @pl.when(block == 0)
    def _():
        fetch(pieces, pl.program_id(0), kv_ref, sems)

        def flip(i, c):
            k0 = pl.multiple_of(i * rows, rows)
            turned = kv_ref[pl.ds(k0, rows), :].T
            vt_ref[:HEAD_DIM, pl.ds(k0, rows)] = turned[HEAD_DIM:]
            return c

        lax.fori_loop(0, stride, flip, 0)
        tail = (vt_ref.shape[0] - HEAD_DIM, total)
        vt_ref[HEAD_DIM:] = jnp.where(lax.broadcasted_iota(jnp.int32, tail, 0) == 0, 1.0, 0.0).astype(BF16)

    def queries():
        return q_ref[0].reshape(heads * rows, 2 * HEAD_DIM)

    def blocks(start, n):
        offs = [pl.multiple_of(lists[block * stride + start + u] * rows, rows) for u in range(n)]
        kv = jnp.concatenate([kv_ref[pl.ds(k0, rows), :] for k0 in offs], axis=0)
        mark = jnp.concatenate([mark_ref[pl.ds(k0, rows), :] for k0 in offs], axis=0)
        vt = jnp.concatenate([vt_ref[:, pl.ds(k0, rows)] for k0 in offs], axis=1)
        return jnp.where(left_half(kv.shape), kv, mark), vt

    def begin():
        k, vt = blocks(count, 1)
        scores = causal(dg(k, queries(), NT), heads)
        top = jnp.max(scores, axis=0, keepdims=True)
        top_ref[...] = top
        sum_ref[...] = dg(vt, jnp.exp2(scores - top).astype(BF16), NN)

    def steps(start, n):
        k, vt = blocks(start, n)
        weights = jnp.exp2(dg(k, queries(), NT) - top_ref[...]).astype(BF16)
        sum_ref[...] += dg(vt, weights, NN)

    begin()
    cascade(count, UNROLL, steps)

    @pl.when(jnp.logical_not(jnp.max(sum_ref[HEAD_DIM : HEAD_DIM + 1, :]) < 2.0**100))
    def _():
        begin()

        def online(n, c):
            k, vt = blocks(n, 1)
            scores = dg(k, queries(), NT)
            old = top_ref[...]
            new = jnp.maximum(old, jnp.max(scores, axis=0, keepdims=True))
            top_ref[...] = new
            sum_ref[...] = sum_ref[...] * jnp.exp2(old - new) + dg(vt, jnp.exp2(scores - new).astype(BF16), NN)
            return c

        lax.fori_loop(0, count, online, 0)

    total_row = sum_ref[HEAD_DIM : HEAD_DIM + 1, :]
    o_ref[0] = (sum_ref[:HEAD_DIM, :] / total_row).T.astype(BF16).reshape(heads, rows, HEAD_DIM)
    lse_ref[0, 0] = top_ref[...] + jnp.log2(total_row)


def attention_forward(lists, counts, q, pieces, marks):
    groups, heads, tokens, wide = q.shape
    total = marks.shape[0]
    blocks = counts.shape[0]
    rows = tokens // blocks
    tall = HEAD_DIM + 16
    return pl.pallas_call(
        forward_kernel,
        grid_spec=pltpu.PrefetchScalarGridSpec(
            num_scalar_prefetch=2,
            grid=(groups, blocks),
            in_specs=[
                pl.BlockSpec((1, heads, rows, wide), lambda g, b, *_: (g, 0, b, 0)),
                pl.BlockSpec((total, wide), lambda g, b, *_: (0, 0)),
                *(pl.BlockSpec(memory_space=pl.ANY) for _ in pieces),
            ],
            out_specs=[
                pl.BlockSpec((1, heads, rows, HEAD_DIM), lambda g, b, *_: (g, 0, b, 0)),
                pl.BlockSpec((1, 1, 1, heads * rows), lambda g, b, *_: (g, b, 0, 0)),
            ],
            scratch_shapes=[
                pltpu.VMEM((1, heads * rows), F32),
                pltpu.VMEM((tall, heads * rows), F32),
                pltpu.VMEM((total, wide), BF16),
                pltpu.VMEM((tall, total), BF16),
                pltpu.SemaphoreType.DMA((len(pieces),)),
            ],
        ),
        out_shape=[
            jax.ShapeDtypeStruct((groups, heads, tokens, HEAD_DIM), BF16),
            jax.ShapeDtypeStruct((groups, blocks, 1, heads * rows), F32),
        ],
        compiler_params=pltpu.CompilerParams(vmem_limit_bytes=48 * 2**20),
        cost_estimate=pl.CostEstimate(
            flops=groups * heads * tokens * total * 256, bytes_accessed=groups * total * 512, transcendentals=0
        ),
        name="attention_forward",
    )(lists, counts, q, marks, *pieces)


def backward_kernel(group, lists, counts, q_ref, do_ref, mark_ref, lse_ref, delta_ref, *refs):
    *pieces, dq_ref, dkv_ref, dq_sum, dkv_sum, kv_ref, kt_ref, sems = refs
    block = pl.program_id(0)
    heads, rows = q_ref.shape[1], q_ref.shape[2]
    total = kv_ref.shape[0]
    stride = total // rows
    count = counts[block]

    @pl.when(block == 0)
    def _():
        dkv_sum[...] = jnp.zeros(dkv_sum.shape, F32)
        fetch(pieces, group, kv_ref, sems)

        def flip(i, c):
            k0 = pl.multiple_of(i * rows, rows)
            turned = kv_ref[pl.ds(k0, rows), :].T
            kt_ref[:, pl.ds(k0, rows)] = turned[:HEAD_DIM]
            return c

        lax.fori_loop(0, stride, flip, 0)

    dq_sum[...] = jnp.zeros(dq_sum.shape, F32)

    def steps(start, n, masked):
        q = q_ref[0].reshape(heads * rows, 2 * HEAD_DIM)
        do = do_ref[0].reshape(heads * rows, 2 * HEAD_DIM)
        offs = [pl.multiple_of(lists[block * stride + start + u] * rows, rows) for u in range(n)]
        kv = jnp.concatenate([kv_ref[pl.ds(k0, rows), :] for k0 in offs], axis=0)
        mark = jnp.concatenate([mark_ref[pl.ds(k0, rows), :] for k0 in offs], axis=0)
        kt = jnp.concatenate([kt_ref[:, pl.ds(k0, rows)] for k0 in offs], axis=1)
        scores = dg(jnp.where(left_half(kv.shape), kv, mark), q, NT) - lse_ref[0, 0]
        if masked:
            scores = causal(scores, heads)
        chances = jnp.exp2(scores)
        back = dg(kv, do, NT) - delta_ref[0, 0]
        score_back = (chances * back).astype(BF16)
        only_q = jnp.where(left_half(q.shape), q, jnp.zeros_like(q))
        update = dg(score_back, only_q, NN) + dg(chances.astype(BF16), do, NN)
        dq_sum[...] += dg(kt, score_back, NN)
        for u in range(n):
            dkv_sum[pl.ds(offs[u], rows), :] += update[u * rows : (u + 1) * rows]

    steps(count, 1, True)
    cascade(count, UNROLL, lambda start, n: steps(start, n, False))
    dq_ref[0] = (dq_sum[...] * HEAD_DIM**-0.5).T.astype(BF16).reshape(heads, rows, HEAD_DIM)

    @pl.when(block == pl.num_programs(0) - 1)
    def _():
        summed = dkv_sum[...]
        dkv_ref[...] = jnp.where(left_half(summed.shape), summed * (1.0 / LOG2E), summed).astype(BF16)


def attention_backward(group, lists, counts, q, do, pieces, marks, lse, delta):
    _, heads, tokens, wide = q.shape
    total = marks.shape[0]
    blocks = counts.shape[0]
    rows = tokens // blocks
    return pl.pallas_call(
        functools.partial(backward_kernel, group),
        grid_spec=pltpu.PrefetchScalarGridSpec(
            num_scalar_prefetch=2,
            grid=(blocks,),
            in_specs=[
                pl.BlockSpec((1, heads, rows, wide), lambda b, *_: (group, 0, b, 0)),
                pl.BlockSpec((1, heads, rows, wide), lambda b, *_: (group, 0, b, 0)),
                pl.BlockSpec((total, wide), lambda b, *_: (0, 0)),
                pl.BlockSpec((1, 1, 1, heads * rows), lambda b, *_: (group, b, 0, 0)),
                pl.BlockSpec((1, 1, 1, heads * rows), lambda b, *_: (group, b, 0, 0)),
                *(pl.BlockSpec(memory_space=pl.ANY) for _ in pieces),
            ],
            out_specs=[
                pl.BlockSpec((1, heads, rows, HEAD_DIM), lambda b, *_: (0, 0, b, 0)),
                pl.BlockSpec((total, wide), lambda b, *_: (0, 0)),
            ],
            scratch_shapes=[
                pltpu.VMEM((HEAD_DIM, heads * rows), F32),
                pltpu.VMEM((total, wide), F32),
                pltpu.VMEM((total, wide), BF16),
                pltpu.VMEM((HEAD_DIM, total), BF16),
                pltpu.SemaphoreType.DMA((len(pieces),)),
            ],
        ),
        out_shape=[
            jax.ShapeDtypeStruct((1, heads, tokens, HEAD_DIM), BF16),
            jax.ShapeDtypeStruct((total, wide), BF16),
        ],
        compiler_params=pltpu.CompilerParams(vmem_limit_bytes=60 * 2**20),
        cost_estimate=pl.CostEstimate(flops=heads * tokens * total * 640, bytes_accessed=total * 1024, transcendentals=0),
        name="attention_backward",
    )(lists, counts, q, do, marks, lse, delta, *pieces)


def feed_kernel(normed_ref, back_ref, gate_ref, up_ref, down_ref, mixed_ref, gate_back_ref, up_back_ref, out_ref, normed_back_ref):
    @pl.when((pl.program_id(0) == 0) & (pl.program_id(1) == 0))
    def _():
        out_ref[...] = jnp.zeros(out_ref.shape, F32)
        normed_back_ref[...] = jnp.zeros(normed_back_ref.shape, F32)

    gate = dg(normed_ref[...], gate_ref[0], NN)
    up_value = dg(normed_ref[...], up_ref[0], NN)
    mixed_back = dg(back_ref[...], down_ref[0], NN)
    sigmoid = jax.nn.sigmoid(gate)
    silu = gate * sigmoid
    mixed = (silu * up_value).astype(BF16)
    gate_back = (mixed_back * up_value * (sigmoid * (1.0 + gate * (1.0 - sigmoid)))).astype(BF16)
    up_back = (mixed_back * silu).astype(BF16)
    mixed_ref[...] = mixed
    gate_back_ref[...] = gate_back
    up_back_ref[...] = up_back
    out_ref[...] += dg(mixed, down_ref[0], NT)
    normed_back_ref[...] += dg(gate_back, gate_ref[0], NT) + dg(up_back, up_ref[0], NT)


def feed_forward(normed, back, pair, down):
    tokens = normed.shape[0]
    columns, _, width = down.shape
    parts = 2 if width % 256 == 0 else 1
    part = width // parts
    whole = pl.BlockSpec((tokens, D), lambda c, j: (0, 0))
    block = pl.BlockSpec((1, D, part), lambda c, j: (c, 0, j))
    out = pl.BlockSpec((tokens, part), lambda c, j: (0, c * parts + j))
    return pl.pallas_call(
        feed_kernel,
        grid=(columns, parts),
        in_specs=[whole, whole, block, pl.BlockSpec((1, D, part), lambda c, j: (c, 0, j + parts)), block],
        out_specs=[out, out, out, whole, whole],
        out_shape=[jax.ShapeDtypeStruct((tokens, columns * width), BF16)] * 3 + [jax.ShapeDtypeStruct((tokens, D), F32)] * 2,
        compiler_params=pltpu.CompilerParams(vmem_limit_bytes=56 * 2**20),
        cost_estimate=pl.CostEstimate(
            flops=12 * tokens * D * columns * width, bytes_accessed=6 * D * columns * width, transcendentals=0
        ),
        name="feed_forward",
    )(normed, back, pair, pair, down)


def gradient_kernel(rights, summed, order, left_ref, *refs):
    right_refs, refs = refs[:rights], refs[rights:]
    sums_ref = refs[0] if summed else None
    refs = refs[1:] if summed else refs
    (mine_ref, other_ref), (lefts, *held) = refs[:2], refs[2:]
    step = pl.program_id(0)
    features = lefts.shape[2]

    @pl.when(step == 0)
    def _():
        for r in range(lefts.shape[0]):
            lefts[r] = left_ref[:, r * features : (r + 1) * features]
        if held:
            width = held[0].shape[2]
            for c in range(held[0].shape[0]):
                held[0][c] = right_refs[0][:, c * width : (c + 1) * width]

    steps = pl.num_programs(0)
    column, row, core = order[step], order[steps + step] * 2, order[2 * steps]
    start = 0
    for right in right_refs:
        value = held[0][column] if held else right[...]
        width = value.shape[1]
        for target, r in ((mine_ref, row + core), (other_ref, row + 1 - core)):
            part = lax.dot_general(lefts[r], value, (((0,), (0,)), ((), ())), preferred_element_type=F32)
            target[0, :features, start : start + width] = part.astype(BF16)
        start += width
    if sums_ref is not None:
        for target, r in ((mine_ref, row + core), (other_ref, row + 1 - core)):
            target[0, features:, :] = sums_ref[r].astype(BF16)


def gradient_parts(order, left, *rights, sums=None):
    tokens = left.shape[0]
    steps = (order.shape[0] - 1) // 2
    columns = steps // 2
    width = rights[0].shape[1] // columns
    features = left.shape[1] // 4
    aligned = width % 128 == 0
    if aligned:
        right_spec = pl.BlockSpec((tokens, width), lambda s, order: (0, order[s]))
    else:
        right_spec = pl.BlockSpec(rights[0].shape, lambda s, order: (0, 0))
    wide = width * len(rights)
    tall = features if sums is None else features + 16
    out = pl.BlockSpec((1, tall, wide), lambda s, order: (s, 0, 0))
    shape = jax.ShapeDtypeStruct((steps, tall, wide), BF16)
    held = [] if aligned else [pltpu.VMEM((columns, tokens, width), BF16)]
    more, more_specs = [], []
    if sums is not None:
        lines = -(-features // wide)
        more = [jnp.pad(sums.reshape(4, lines, -1), ((0, 0), (0, 16 - lines), (0, wide - features // lines)))]
        more_specs = [pl.BlockSpec((4, 16, wide), lambda s, order: (0, 0, 0))]
    return pl.pallas_call(
        functools.partial(gradient_kernel, len(rights), sums is not None),
        grid_spec=pltpu.PrefetchScalarGridSpec(
            num_scalar_prefetch=1,
            grid=(steps,),
            in_specs=[
                pl.BlockSpec(left.shape, lambda s, order: (0, 0)),
                *(right_spec for _ in rights),
                *more_specs,
            ],
            out_specs=[out, out],
            scratch_shapes=[pltpu.VMEM((4, tokens, features), BF16), *held],
        ),
        out_shape=[shape, shape],
        compiler_params=pltpu.CompilerParams(vmem_limit_bytes=56 * 2**20),
        cost_estimate=pl.CostEstimate(
            flops=2 * tokens * left.shape[1] * wide * columns, bytes_accessed=2 * left.shape[1] * wide * columns, transcendentals=0
        ),
        name="gradient_parts",
    )(order, left, *rights, *more)


def norm_apply(value, gain):
    scale_rows = lax.rsqrt(jnp.sum(value * value, axis=1) / D + EPSILON)
    normed = (value * scale_rows[:, None] * gain[None, :]).astype(BF16)
    return (normed, scale_rows)


def norm_back(upstream, value, scale_rows, gain):
    weighted = upstream * gain[None, :]
    inner = jnp.sum(weighted * value, axis=1)
    value_back = (
        scale_rows[:, None] * weighted
        - value * (scale_rows * scale_rows * scale_rows * inner / D)[:, None]
    )
    gain_back = jnp.sum(upstream * value * scale_rows[:, None], axis=0)
    return (value_back, gain_back)


ROW = ("high", "core")
ALL_ROW = ("high", "core", "col")
ALL_COL = ("col", "high", "core")
RING = ("high", "col")


def ring_steps(columns):
    path = [*range(columns), *reversed(range(columns, 2 * columns))]
    ahead = [(path[i], path[(i + 1) % len(path)]) for i in range(len(path))]
    return ahead, [(b, a) for a, b in ahead]


def ring_gather(value, columns):
    ahead, behind = ring_steps(columns)
    count = 2 * columns
    to_next, to_last = value, value
    fronts, backs = [], []
    for _ in range(count // 2 - 1):
        to_next = lax.ppermute(to_next, RING, ahead)
        to_last = lax.ppermute(to_last, RING, behind)
        fronts.append(to_next)
        backs.append(to_last)
    half = value.shape[0] // 2
    upper = lax.ppermute(to_next[:half], RING, ahead)
    lower = lax.ppermute(to_last[half:], RING, behind)
    return [value, *backs, upper, lower, *reversed(fronts)]


class RingScatter:
    def __init__(self, part, columns):
        self.part, (self.ahead, self.behind), self.count = part, ring_steps(columns), 2 * columns
        self.left = self.count // 2
        self.send(part(self.left, 0), part(self.left, 1))

    def send(self, out, back):
        out, back = lax.optimization_barrier((out.astype(BF16), back.astype(BF16)))
        self.arrived = (lax.ppermute(out, RING, self.ahead), lax.ppermute(back, RING, self.behind))
        self.left -= 1

    def step(self):
        out, back = self.part(self.left, None), self.part(self.count - self.left, None)
        front, rear = (v.astype(F32) for v in self.arrived)
        if front.shape[0] == out.shape[0]:
            self.send(out + front, back + rear)
        else:
            half = front.shape[0]
            out = jnp.concatenate([out[:half] + front, out[half:]], axis=0)
            self.send(out, jnp.concatenate([back[:half], back[half:] + rear], axis=0))

    def finish(self):
        while self.left:
            self.step()
        return self.part(0, None) + self.arrived[0].astype(F32) + self.arrived[1].astype(F32)


def after(value, rings):
    value, arrived = lax.optimization_barrier((value, [r.arrived for r in rings]))
    for ring, a in zip(rings, arrived, strict=True):
        ring.arrived = a
    return value


def halves(value, half):
    if half is None:
        return value
    middle = value.shape[0] // 2
    return value[middle:] if half else value[:middle]


def gather(value, axes):
    return lax.all_gather(value, axes, axis=0, tiled=True)


def per_device(
    tokens,
    attention_gain,
    joint_weight,
    output_weight,
    feed_gain,
    gate_weight,
    up_weight,
    down_weight,
    cotangent,
    segment_lengths,
    parents,
):
    rows = lax.axis_size(ROW)
    columns = lax.axis_size("col")
    cores = lax.axis_size("core")
    own = tokens.shape[0] // rows
    held = own * cores
    groups = KV_HEADS // cores
    tables = tree_tables(segment_lengths, parents)
    row = lax.axis_index(ROW)
    column = lax.axis_index("col")
    high = lax.axis_index("high")
    core = lax.axis_index("core")
    index = column * tokens.shape[0] + row * own + jnp.arange(own, dtype=jnp.int32)
    cosines, sines = rotary_tables(index, tables)
    first = column * tokens.shape[0] + high * held

    spot = jnp.where(high == 0, column, 2 * columns - 1 - column)
    spots = lax.rem(spot + jnp.arange(2 * columns, dtype=jnp.int32), 2 * columns)
    far = spots >= columns
    ring_column = jnp.where(far, 2 * columns - 1 - spots, spots)
    ring_high = far.astype(jnp.int32)
    order = jnp.concatenate([ring_column, ring_high, jnp.reshape(core, (1,))]).astype(jnp.int32)
    key_first = ring_column * tokens.shape[0] + ring_high * held
    key_index = (key_first[:, None] + jnp.arange(held, dtype=jnp.int32)[None, :]).reshape(-1)

    block = 256 if held % 256 == 0 else 128
    lists, counts = block_lists(first, key_index, block, held, tables)
    key_hot = segment_hot(key_index, tables).astype(F32)
    marks = jnp.pad(key_hot, ((0, 0), (HEAD_DIM, HEAD_DIM - key_hot.shape[1]))).astype(BF16)
    held_hot = segment_hot(first + jnp.arange(held, dtype=jnp.int32), tables).astype(F32)
    reach = jnp.sum(held_hot[:, :, None] * tables[2][None], axis=1)
    bars = jnp.pad((reach - 1.0) * BIG, ((0, 0), (0, HEAD_DIM - reach.shape[1]))).astype(BF16)

    def to_tokens(value):
        return lax.all_to_all(value, ROW, split_axis=0, concat_axis=1, tiled=True)

    def to_features(value):
        return lax.all_to_all(value, ROW, split_axis=1, concat_axis=0, tiled=True)

    def swap_cores(value):
        return lax.all_to_all(value, "core", split_axis=0, concat_axis=0, tiled=True)

    joint_full = gather(joint_weight, ALL_COL).reshape(columns, D, -1)
    joint_full = joint_full.transpose(1, 0, 2).reshape(D, -1)
    gains = jnp.broadcast_to(jnp.stack([attention_gain, feed_gain])[None], (rows, 2, attention_gain.shape[0]))
    extended = jnp.concatenate([tokens.reshape(rows, own, -1), jnp.pad(gains, ((0, 0), (0, 14), (0, 0)))], axis=1)
    extended = to_tokens(extended.reshape(rows * (own + 16), -1))
    stream = extended[:own].astype(F32)
    gain_one = extended[own].astype(F32)
    gain_two = extended[own + 1].astype(F32)

    normed_one, scale_one = norm_apply(stream, gain_one)
    joint = jnp.dot(normed_one, joint_full, preferred_element_type=F32).astype(BF16)
    raw = joint.astype(F32)
    queries = turn(raw[:, :ATT].reshape(own, HEADS, HEAD_DIM), cosines, sines)
    queries = (queries * (LOG2E * HEAD_DIM**-0.5)).astype(BF16).reshape(own, cores, -1)
    keys = turn(raw[:, ATT : ATT + KEYS].reshape(own, KV_HEADS, HEAD_DIM), cosines, sines).astype(BF16)
    values = joint[:, ATT + KEYS :].reshape(own, KV_HEADS, HEAD_DIM)
    pairs = jnp.concatenate([keys, values], axis=2).reshape(own, cores, -1)
    packed = jnp.concatenate([queries, pairs], axis=2).transpose(1, 0, 2)
    packed = swap_cores(packed).reshape(held, -1)
    wide = groups * REPEAT * HEAD_DIM
    pieces = ring_gather(packed[:, wide:], columns)
    queries = packed[:, :wide].reshape(held, groups, REPEAT, HEAD_DIM).transpose(1, 2, 0, 3)
    queries = jnp.concatenate([queries, jnp.broadcast_to(bars, queries.shape)], axis=3)
    attended, lse = attention_forward(lists, counts, queries, pieces, marks)
    by_core = attended.reshape(groups * REPEAT, cores, own, HEAD_DIM).transpose(1, 2, 0, 3)
    attended_rows = swap_cores(by_core.reshape(cores, own, -1)).transpose(1, 0, 2).reshape(own, ATT)

    output_full = gather(output_weight, ALL_ROW).reshape(rows, ATT, -1)
    output_full = output_full.transpose(1, 0, 2).reshape(ATT, D)
    pair_full = gather(jnp.concatenate([gate_weight, up_weight], axis=1), ALL_COL).reshape(columns, D, -1)
    down_full = gather(down_weight.T, ALL_COL).reshape(columns, D, -1)
    upstream = to_tokens(cotangent)
    hidden = stream + jnp.dot(attended_rows, output_full, preferred_element_type=F32)
    normed_two, scale_two = norm_apply(hidden, gain_two)
    mixed, gate_back, up_back, feed_out, normed_two_back = feed_forward(normed_two, upstream, pair_full, down_full)
    layer_output = to_features((hidden + feed_out).astype(BF16))

    def scatter_gradient(left, *rights, sums=None):
        mine, other = gradient_parts(order, left, *rights, sums=sums)
        other = lax.ppermute(other, "core", [(0, 1), (1, 0)])

        def part(s, half):
            return halves(mine[s], half).astype(F32) + halves(other[s], half).astype(F32)

        return RingScatter(part, columns)

    down_ring = scatter_gradient(upstream, mixed)
    pair_ring = scatter_gradient(normed_two, gate_back, up_back)
    hidden_part, gain_two_part = norm_back(normed_two_back, hidden, scale_two, gain_two)
    hidden_back = upstream.astype(F32) + hidden_part
    hidden_low = hidden_back.astype(BF16)
    attended_back = dg(hidden_low, output_full, NT).astype(BF16)
    output_ring = scatter_gradient(hidden_low, attended_rows, sums=gain_two_part)

    heads_back = swap_cores(attended_back.reshape(own, cores, -1).transpose(1, 0, 2)).reshape(held, -1)
    heads_back = heads_back.reshape(held, groups, REPEAT, HEAD_DIM).transpose(1, 2, 0, 3)
    delta = jnp.sum(heads_back.astype(F32) * attended.astype(F32), axis=3)
    delta = delta.reshape(groups, REPEAT, -1, block).transpose(0, 2, 1, 3)
    delta = delta.reshape(groups, -1, 1, REPEAT * block)
    heads_back = jnp.pad(heads_back, ((0, 0), (0, 0), (0, 0), (HEAD_DIM, 0)))
    query_backs, pair_rings = [], []
    down_ring.step()
    down_ring.step()
    for g in range(groups):
        if g == 0:
            heads_back = after(heads_back, [down_ring, pair_ring])
            down_ring.step()
            pair_ring.step()
        else:
            rings = [pair_ring, output_ring, *pair_rings] + ([down_ring] if g == 1 else [])
            heads_back = after(heads_back, rings)
            for ring in (pair_ring, output_ring, *pair_rings):
                if ring.left and (ring is not pair_ring or g < 2):
                    ring.step()
        query_back, pair_back = attention_backward(g, lists, counts, queries, heads_back, pieces, marks, lse, delta)
        pair_back = pair_back.reshape(2 * columns, held, -1)
        query_backs.append(query_back)
        pair_rings.append(RingScatter(lambda s, half, v=pair_back: halves(v[s], half).astype(F32), columns))
    pair_backs = [ring.finish() for ring in pair_rings]
    pair_backs[0] = after(pair_backs[0], [pair_ring, output_ring])
    held_pairs = jnp.concatenate([p.astype(BF16) for p in pair_backs], axis=1)
    held_pairs = after(held_pairs, [pair_ring, output_ring])
    query_back = jnp.concatenate(query_backs, axis=0)
    query_back = query_back.reshape(groups * REPEAT, held, HEAD_DIM).transpose(1, 0, 2).reshape(held, -1)
    packed = jnp.concatenate([query_back, held_pairs], axis=1).reshape(cores, own, -1)
    packed = swap_cores(packed)
    query_back = packed[:, :, :wide].transpose(1, 0, 2).reshape(own, HEADS, HEAD_DIM)
    pair_back = packed[:, :, wide:].transpose(1, 0, 2).reshape(own, KV_HEADS, 2 * HEAD_DIM)
    query_back = turn(query_back.astype(F32), cosines, -sines).astype(BF16).reshape(own, ATT)
    key_back = turn(pair_back[:, :, :HEAD_DIM].astype(F32), cosines, -sines).astype(BF16).reshape(own, KEYS)
    value_back = pair_back[:, :, HEAD_DIM:].reshape(own, KEYS)
    joint_back = jnp.concatenate([query_back, key_back, value_back], axis=1)
    normed_one_back = dg(joint_back, joint_full, NT)
    stream_part, gain_one_part = norm_back(normed_one_back, stream, scale_one, gain_one)
    joint_ring = scatter_gradient(normed_one, joint_back, sums=gain_one_part)
    input_gradient = to_features((hidden_back + stream_part).astype(BF16)).astype(F32)
    down_gradient = down_ring.finish().T
    pair_gradient = pair_ring.finish()
    output_summed = output_ring.finish()
    joint_summed = joint_ring.finish()
    features = D // rows

    def carried(summed):
        lines = -(-features // summed.shape[1])
        return summed[features : features + lines, : features // lines].reshape(-1)

    width = gate_weight.shape[1]
    return (
        layer_output,
        input_gradient,
        carried(joint_summed),
        joint_summed[:features],
        output_summed[:features].T,
        carried(output_summed),
        pair_gradient[:, :width],
        pair_gradient[:, width:],
        down_gradient,
    )


def solution(mesh):
    leaves, rows, columns = (mesh.shape[name] for name in ("leaf", "row", "col"))
    split = Mesh(mesh.devices.reshape(leaves, rows // 2, 2, columns), ("leaf", "high", "core", "col"))
    return jax.shard_map(
        per_device,
        mesh=split,
        in_specs=(
            P(("leaf", "col"), ROW),
            P(ROW),
            P(ROW, "col"),
            P("col", ROW),
            P(ROW),
            P(ROW, "col"),
            P(ROW, "col"),
            P("col", ROW),
            P(("leaf", "col"), ROW),
            P("leaf"),
            P("leaf"),
        ),
        out_specs=(
            P(("leaf", "col"), ROW),
            P(("leaf", "col"), ROW),
            P(("leaf", *ROW)),
            P(("leaf", *ROW), "col"),
            P(("leaf", "col"), ROW),
            P(("leaf", *ROW)),
            P(("leaf", *ROW), "col"),
            P(("leaf", *ROW), "col"),
            P(("leaf", "col"), ROW),
        ),
        check_vma=False,
    )
```

time: 1290 us -> 1050 us (0.81)
  waiting for transfers between devices: 700 us -> 264 us
  starting transfers between devices: 16.8 us -> 253 us
  matrix products: 123 us -> 22.5 us
  Pallas kernels: 92.1 us -> 190 us
  other arithmetic: 35.9 us -> 117 us
  blocking collectives: 96.4 us -> 23.7 us
  local copies, waits for them, and re-layouts: 202 us -> 151 us
    reduce_scatter x7 -> x0, waiting for transfers between devices: 334 us -> none  [scatter(): return lax.psum_scatter(value, axes, scatter_dimension=0, tiled=True)]
    ppermute x0 -> x68, starting transfers between devices: none -> 237 us  [the longest x28 163 us: send(): lax.ppermute(out, RING, self.ahead)]
    all_gather x8 -> x4, waiting for transfers between devices: 268 us -> 51.2 us  [gather(): return lax.all_gather(value, axes, axis=0, tiled=True)]
    ppermute x0 -> x68, waiting for transfers between devices: none -> 187 us  [the longest x3 86.5 us: ring_gather(): to_next = lax.ppermute(to_next, RING, ahead)]
    pallas_call x3 -> x8, Pallas kernels: 54.6 us -> 154 us  [the longest x3 55.8 us: attention_backward(): pl.pallas_call(functools.partial(backward_kernel, group), grid_spec=pltpu...]
    unnamed x17 -> x4, waiting for transfers between devices: 80.8 us -> 2.07 us
    dot_general x8 -> x0, matrix products: 74.3 us -> none  [the longest x3 27.1 us: by_columns(): lax.dot_general(left, right, (((0,), (0,)), ((), ())), preferred_element_...]
    psum x1 -> x0, blocking collectives: 52 us -> none  [per_device(): gains = lax.psum(jnp.stack([gain_one_part, gain_two_part]), ALL_COL)]
  transfers between devices with their start and end apart: 20 -> 76, of which waited for: 15 -> 33; matrix products, arithmetic and copies ran while one was open for 22% -> 24% of each run, Pallas kernels for 6% -> 9%
where the time goes in v2:
time: 1050 us; the launch traced here: 1040 us
  waiting for transfers between devices  264 us (25%)
  starting transfers between devices  253 us (24%)
  Pallas kernels  190 us (18%)
  local copies, waits for them, and re-layouts  151 us (14%)
  other arithmetic  117 us (11%)
  blocking collectives  23.7 us (2%)
  matrix products  22.5 us (2%)
  between operations  15.5 us (1%)
    ppermute x28, starting transfers between devices, send(): lax.ppermute(out, RING, self.ahead)  163 us
    ppermute x3, waiting for transfers between devices, ring_gather(): to_next = lax.ppermute(to_next, RING, ahead)  86.5 us
    ppermute x28, starting transfers between devices, send(): lax.ppermute(back, RING, self.behind)  60.4 us
    pallas_call x3, Pallas kernels, attention_backward(): pl.pallas_call(functools.partial(backward_kernel, group), grid_spec=pltpu...  55.8 us
    all_gather x4, waiting for transfers between devices, gather(): return lax.all_gather(value, axes, axis=0, tiled=True)  51.2 us
    pallas_call x4, Pallas kernels, gradient_parts(): pl.pallas_call(functools.partial(gradient_kernel, len(rights), sums is no...  50.7 us
    ppermute x28, waiting for transfers between devices, send(): lax.ppermute(out, RING, self.ahead)  50.5 us
    pallas_call x1, Pallas kernels, feed_forward(): pl.pallas_call(feed_kernel, grid=(columns, parts), in_specs=[whole, whole...  47.2 us
  transfers between devices with their start and end apart: 76, of which 33 were waited for; matrix products, arithmetic and copies ran while one was open for 24% of the time, Pallas kernels for 9%

profile of v2, /device:TPU:0, one launch (start us, length us, event | category | flops | bytes accessed | tf_op | source)
XLA Modules:
  0.0 1036.3 jit_solution(3853388455220478567)
XLA Ops:
  14.6 4.4 all-to-all-start
  19.8 5.6 compare_and_fusion
  29.4 14.9 %all-to-all-done = bf16[4,656,288]{1,2,0:T(8,128)(2,1)S(1)} async-done(((bf16[4,656,288]{1,2,0:T(8,128)(2,1)}), bf16[4,656,288]{1,2,0:T(8,128)(2,1)S(1)}, u32[]{:S(2)}, u32[]{:S(2)}) %all-to-all-start) | async-done | bytes 1511456 | tf_op jit(solution)/shard_map/all_to_all | solution.py:587
  46.7 22.6 %all-gather.5.cloned.1.call-done = bf16[4608,480]{1,0:T(8,128)(2,1)} async-done(((bf16[288,480]{1,0:T(8,128)(2,1)}), bf16[4608,480]{1,0:T(8,128)(2,1)}) %all-gather.5.cloned.1.call-update) | async-done | bytes 4423696 | tf_op jit(solution)/shard_map/all_gather | solution.py:538
  69.2 8.4 copy.246
  93.6 6.1 all_to_all.84
  99.7 4.3 all-to-all-start.3
  111.8 38.2 %collective-permute-done.3.refs_8_ = bf16[1280,384]{1,0:T(8,128)(2,1)S(1)} collective-permute-done((bf16[1280,384]{1,0:T(8,128)(2,1)S(1)}, bf16[1280,384]{1,0:T(8,128)(2,1)S(1)}, u32[]{:S(2)}, u32[]{:S(2)}) %collective-permute-start.3) | collective-permute-done | bytes 983072 | tf_op jit(solution)/shard_map/ppermute | solution.py:486
  155.1 30.7 %collective-permute-done.4.refs_7_ = bf16[1280,384]{1,0:T(8,128)(2,1)} collective-permute-done((bf16[1280,384]{1,0:T(8,128)(2,1)S(1)}, bf16[1280,384]{1,0:T(8,128)(2,1)}, u32[]{:S(2)}, u32[]{:S(2)}) %collective-permute-start.4) | collective-permute-done | bytes 983072 | tf_op jit(solution)/shard_map/ppermute | solution.py:486
  188.6 7.5 collective-permute-done.1.refs_2_
  206.3 17.6 %collective-permute-done.5.refs_6_ = bf16[1280,384]{1,0:T(8,128)(2,1)S(1)} collective-permute-done((bf16[1280,384]{1,0:T(8,128)(2,1)}, bf16[1280,384]{1,0:T(8,128)(2,1)S(1)}, u32[]{:S(2)}, u32[]{:S(2)}) %collective-permute-start.5) | collective-permute-done | bytes 983072 | tf_op jit(solution)/shard_map/ppermute | solution.py:486
  229.8 4.9 copy.212
  234.8 7.3 copy.247
  259.0 36.7 %attention_forward.1 = (bf16[3,3,1280,64]{3,2,1,0:T(8,128)(2,1)}, f32[3,5,1,768]{3,2,1,0:T(1,128)S(1)}) custom-call(s32[200]{0:T(256)S(1)} %select_n.49.lists, s32[5]{0:T(128)S(1)} %get-tuple-element.293.counts, bf16[3,3,1280,128]{3,2,1,0:T(8,128)(2,1)} %pad_maximum_fusion.q_ref, bf16[10240,128]{1,0:T(8,128)(2,1)} %convert_convert_fusion.mark_ref, ...), custom_call_target="tpu_custom_call" | custom-call | flops 30198988800 | bytes 15728640 | tf_op jit(solution)/shard_map/attention_forward/pallas_call | solution.py:207
  299.5 5.6 all_to_all.85
  305.0 4.8 multiply_reduce_fusion.5
  311.3 28.7 %all-gather.9.cloned.1.call-done = bf16[4608,1536]{1,0:T(8,128)(2,1)} async-done(((bf16[288,1536]{1,0:T(8,128)(2,1)}), bf16[4608,1536]{1,0:T(8,128)(2,1)}) %all-gather.9.cloned.1.call-update) | async-done | bytes 14155792 | tf_op jit(solution)/shard_map/all_gather | solution.py:538
  339.9 47.2 %feed_forward.1 = (bf16[640,3072]{1,0:T(8,128)(2,1)}, bf16[640,3072]{1,0:T(8,128)(2,1)}, bf16[640,3072]{1,0:T(8,128)(2,1)}, f32[640,1152]{1,0:T(8,128)}, f32[640,1152]{1,0:T(8,128)}) custom-call(bf16[640,1152]{1,0:T(8,128)(2,1)} %multiply_convert_fusion.1.normed_ref.left_ref, bf16[640,1152]{1,0:T(8,128)(2,1)} %copy.214.back_ref.left_ref, ...), custom_call_target="tpu_custom_call" | custom-call | flops 27179089920 | bytes 21233664 | tf_op jit(solution)/shard_map/feed_forward/pallas_call | solution.py:362
  387.1 18.0 %gradient_parts.5 = (bf16[8,288,1536]{2,1,0:T(8,128)(2,1)}, bf16[8,288,1536]{2,1,0:T(8,128)(2,1)}) custom-call(s32[17]{0:T(128)} %pad_add_fusion.order, bf16[640,1152]{1,0:T(8,128)(2,1)} %multiply_convert_fusion.1.normed_ref.left_ref, bf16[640,3072]{1,0:T(8,128)(2,1)} %get-tuple-element.131.refs_0_, bf16[640,3072]{1,0:T(8,128)(2,1)} %get-tuple-element.132.refs_1_), custom_call_target="tpu_custom_call" | custom-call | flops 9059696640 | bytes 14155776 | tf_op jit(solution)/shard_map/gradient_parts/pallas_call | solution.py:429
  405.4 12.5 %gradient_parts.4 = (bf16[8,288,768]{2,1,0:T(8,128)(2,1)}, bf16[8,288,768]{2,1,0:T(8,128)(2,1)}) custom-call(s32[17]{0:T(128)} %pad_add_fusion.order, bf16[640,1152]{1,0:T(8,128)(2,1)} %copy.214.back_ref.left_ref, bf16[640,3072]{1,0:T(8,128)(2,1)} %get-tuple-element.122.refs_0_), custom_call_target="tpu_custom_call" | custom-call | flops 4529848320 | bytes 7077888 | tf_op jit(solution)/shard_map/gradient_parts/pallas_call | solution.py:429
  425.0 4.1 fusion.72.left_ref
  429.1 9.7 gradient_parts.6
  442.8 5.6 convolution_convert_fusion
  452.0 6.1 all_to_all.86
  460.7 4.6 reshape_reshape.3
  465.3 4.1 copy.220
  469.4 4.6 pad.32.do_ref
  483.2 15.7 %collective-permute-start.9 = (bf16[144,768]{1,0:T(8,128)(2,1)S(1)}, bf16[144,768]{1,0:T(8,128)(2,1)S(1)}, u32[]{:S(2)}, u32[]{:S(2)}) collective-permute-start(bf16[144,768]{1,0:T(8,128)(2,1)S(1)} %get-tuple-element.125), channel_id=1, source_target_pairs={{0,1},{1,2},{2,3},{3,11},{11,10},{10,9},{9,8},{8,0},{4,5},{5,6},{6... | collective-permute-start | bytes 663560 | tf_op jit(solution)/shard_map/ppermute | solution.py:504
  506.0 8.2 collective-permute-start.11
  522.1 4.2 collective-permute-done.11
  537.4 4.3 collective-permute-done.13
  544.2 4.4 collective-permute-done.16
  560.2 18.6 %attention_backward.3 = (bf16[1,3,1280,64]{3,2,1,0:T(8,128)(2,1)}, bf16[10240,128]{1,0:T(8,128)(2,1)}) custom-call(s32[200]{0:T(256)} %copy-done.4, s32[5]{0:T(128)} %copy-done.3, bf16[3,3,1280,128]{3,2,1,0:T(8,128)(2,1)} %pad_maximum_fusion.q_ref, bf16[3,3,1280,128]{3,2,1,0:T(8,128)(2,1)} %pad.32.do_ref, bf16[10240,128]{1,0:T(8,128)(2,1)} %convert_convert_fusion.mark_ref, ...), custom_call_target="tpu_custom_call" | custom-call | flops 25165824000 | bytes 10485760 | tf_op jit(solution)/shard_map/attention_backward/pallas_call | solution.py:298
  580.8 13.3 %collective-permute-start.26 = (bf16[288,768]{1,0:T(8,128)(2,1)}, bf16[288,768]{1,0:T(8,128)(2,1)}, u32[]{:S(2)}, u32[]{:S(2)}) collective-permute-start(bf16[288,768]{1,0:T(8,128)(2,1)} %get-tuple-element.154), channel_id=1, source_target_pairs={{1,0},{2,1},{3,2},{11,3},{10,11},{9,10},{8,9},{0,8},{5,4},{6,5},{7... | collective-permute-start | bytes 1327112 | tf_op jit(solution)/shard_map/ppermute | solution.py:504
  594.1 13.0 %collective-permute-start.23 = (bf16[640,128]{1,0:T(8,128)(2,1)S(1)}, bf16[640,128]{1,0:T(8,128)(2,1)S(1)}, u32[]{:S(2)}, u32[]{:S(2)}) collective-permute-start(bf16[640,128]{1,0:T(8,128)(2,1)S(1)} %get-tuple-element.149), channel_id=1, source_target_pairs={{0,1},{1,2},{2,3},{3,11},{11,10},{10,9},{9,8},{8,0},{4,5},{5,6},{6... | collective-permute-start | bytes 491528 | tf_op jit(solution)/shard_map/ppermute | solution.py:504
  607.1 14.3 %collective-permute-done.23 = bf16[640,128]{1,0:T(8,128)(2,1)S(1)} collective-permute-done((bf16[640,128]{1,0:T(8,128)(2,1)S(1)}, bf16[640,128]{1,0:T(8,128)(2,1)S(1)}, u32[]{:S(2)}, u32[]{:S(2)}) %collective-permute-start.23) | collective-permute-done | bytes 163872 | tf_op jit(solution)/shard_map/ppermute | solution.py:504
  621.4 10.5 %collective-permute-start.24 = (bf16[640,128]{1,0:T(8,128)(2,1)S(1)}, bf16[640,128]{1,0:T(8,128)(2,1)S(1)}, u32[]{:S(2)}, u32[]{:S(2)}) collective-permute-start(bf16[640,128]{1,0:T(8,128)(2,1)S(1)} %get-tuple-element.150), channel_id=1, source_target_pairs={{1,0},{2,1},{3,2},{11,3},{10,11},{9,10},{8,9},{0,8},{5,4},{6,5},{7... | collective-permute-start | bytes 491528 | tf_op jit(solution)/shard_map/ppermute | solution.py:504
  635.4 18.6 %attention_backward.4 = (bf16[1,3,1280,64]{3,2,1,0:T(8,128)(2,1)}, bf16[10240,128]{1,0:T(8,128)(2,1)}) custom-call(s32[200]{0:T(256)} %copy-done.4, s32[5]{0:T(128)} %copy-done.3, bf16[3,3,1280,128]{3,2,1,0:T(8,128)(2,1)} %pad_maximum_fusion.q_ref, bf16[3,3,1280,128]{3,2,1,0:T(8,128)(2,1)} %pad.32.do_ref, bf16[10240,128]{1,0:T(8,128)(2,1)} %convert_convert_fusion.mark_ref, ...), custom_call_target="tpu_custom_call" | custom-call | flops 25165824000 | bytes 10485760 | tf_op jit(solution)/shard_map/attention_backward/pallas_call | solution.py:298
  656.0 23.6 %collective-permute-start.33 = (bf16[640,128]{1,0:T(8,128)(2,1)S(1)}, bf16[640,128]{1,0:T(8,128)(2,1)S(1)}, u32[]{:S(2)}, u32[]{:S(2)}) collective-permute-start(bf16[640,128]{1,0:T(8,128)(2,1)S(1)} %get-tuple-element.170), channel_id=1, source_target_pairs={{0,1},{1,2},{2,3},{3,11},{11,10},{10,9},{9,8},{8,0},{4,5},{5,6},{6... | collective-permute-start | bytes 491528 | tf_op jit(solution)/shard_map/ppermute | solution.py:504
  683.0 15.8 %collective-permute-start.29 = (bf16[304,288]{1,0:T(8,128)(2,1)}, bf16[304,288]{1,0:T(8,128)(2,1)}, u32[]{:S(2)}, u32[]{:S(2)}) collective-permute-start(bf16[304,288]{1,0:T(8,128)(2,1)} %pad_maximum_fusion.21), channel_id=1, source_target_pairs={{0,1},{1,2},{2,3},{3,11},{11,10},{10,9},{9,8},{8,0},{4,5},{5,6},{6... | collective-permute-start | bytes 525320 | tf_op jit(solution)/shard_map/ppermute | solution.py:504
  698.8 4.4 fusion.6
  703.2 7.5 collective-permute-start.27
  730.3 9.6 collective-permute-done.30
  749.6 18.6 %attention_backward.5 = (bf16[1,3,1280,64]{3,2,1,0:T(8,128)(2,1)}, bf16[10240,128]{1,0:T(8,128)(2,1)}) custom-call(s32[200]{0:T(256)} %copy-done.4, s32[5]{0:T(128)} %copy-done.3, bf16[3,3,1280,128]{3,2,1,0:T(8,128)(2,1)} %pad_maximum_fusion.q_ref, bf16[3,3,1280,128]{3,2,1,0:T(8,128)(2,1)} %pad.32.do_ref, bf16[10240,128]{1,0:T(8,128)(2,1)} %convert_convert_fusion.mark_ref, ...), custom_call_target="tpu_custom_call" | custom-call | flops 25165824000 | bytes 10485760 | tf_op jit(solution)/shard_map/attention_backward/pallas_call | solution.py:298
  770.3 27.2 %collective-permute-start.47 = (bf16[640,128]{1,0:T(8,128)(2,1)}, bf16[640,128]{1,0:T(8,128)(2,1)}, u32[]{:S(2)}, u32[]{:S(2)}) collective-permute-start(bf16[640,128]{1,0:T(8,128)(2,1)} %get-tuple-element.196), channel_id=1, source_target_pairs={{0,1},{1,2},{2,3},{3,11},{11,10},{10,9},{9,8},{8,0},{4,5},{5,6},{6... | collective-permute-start | bytes 491528 | tf_op jit(solution)/shard_map/ppermute | solution.py:504
  802.8 4.2 copy.228
  806.9 4.2 concatenate.121
  811.1 10.4 %collective-permute-start.36 = (bf16[1280,128]{1,0:T(8,128)(2,1)}, bf16[1280,128]{1,0:T(8,128)(2,1)S(1)}, u32[]{:S(2)}, u32[]{:S(2)}) collective-permute-start(bf16[1280,128]{1,0:T(8,128)(2,1)} %get-tuple-element.177), channel_id=1, source_target_pairs={{1,0},{2,1},{3,2},{11,3},{10,11},{9,10},{8,9},{0,8},{5,4},{6,5},{7... | collective-permute-start | bytes 983048 | tf_op jit(solution)/shard_map/ppermute | solution.py:504
  821.6 4.9 collective-permute-start.41
  827.8 6.2 collective-permute-start.42
  834.0 6.8 collective-permute-start.49
  843.5 4.4 collective-permute-start.37
  881.9 4.2 copy.231
  886.1 4.8 pad_maximum_fusion.2
  891.3 5.9 all_to_all.87
  912.6 8.3 multiply_reduce_fusion.1
  921.6 10.5 %gradient_parts.7 = (bf16[8,304,480]{2,1,0:T(8,128)(2,1)}, bf16[8,304,480]{2,1,0:T(8,128)(2,1)}) custom-call(s32[17]{0:T(128)} %pad_add_fusion.order, bf16[640,1152]{1,0:T(8,128)(2,1)} %get-tuple-element.323.left_ref, bf16[640,1920]{1,0:T(8,128)(2,1)} %pad_maximum_fusion.3.refs_0_, f32[4,16,480]{2,1,0:T(8,128)} %pad.34.refs_1_), custom_call_target="tpu_custom_call" | custom-call | flops 2831155200 | bytes 4423680 | tf_op jit(solution)/shard_map/gradient_parts/pallas_call | solution.py:429
  932.4 4.6 fusion.3
  943.1 4.2 add_convert_fusion
  956.8 7.9 collective-permute-done.64
  971.7 10.8 %collective-permute-done.57 = bf16[152,480]{1,0:T(8,128)(2,1)S(1)} collective-permute-done((bf16[152,480]{1,0:T(8,128)(2,1)S(1)}, bf16[152,480]{1,0:T(8,128)(2,1)S(1)}, u32[]{:S(2)}, u32[]{:S(2)}) %collective-permute-start.57) | collective-permute-done | bytes 145952 | tf_op jit(solution)/shard_map/ppermute | solution.py:504
  987.0 5.2 collective-permute-done.58
  1011.3 9.0 all-to-all-done.4
  1021.6 4.9 collective-permute-done.62
  (463 shorter events, 303.2 us)
Async XLA Ops:
  7.2 62.1 %all-gather.5.cloned.1.call-start = ((), (), s32[]{:S(2)}) async-start(), calls=%async_computation.8 | async-start | bytes 5013504 | tf_op jit(solution)/shard_map/all_gather | solution.py:538
  7.9 226.9 %all-gather.7.cloned.1.call-start = ((), (), s32[]{:S(2)}) async-start(), calls=%async_computation.9 | async-start | bytes 3760128 | tf_op jit(solution)/shard_map/all_gather | solution.py:538
  8.7 302.6 %all-gather.11.cloned.1.call-start = ((), (), s32[]{:S(2)}) async-start(), calls=%async_computation.11 | async-start | bytes 7520256 | tf_op jit(solution)/shard_map/all_gather | solution.py:538
  9.4 330.5 %all-gather.9.cloned.1.call-start = ((), (), s32[]{:S(2)}) async-start(), calls=%async_computation.10 | async-start | bytes 15040512 | tf_op jit(solution)/shard_map/all_gather | solution.py:538
  14.6 29.7 %all-to-all-start = ((bf16[4,656,288]{1,2,0:T(8,128)(2,1)}), bf16[4,656,288]{1,2,0:T(8,128)(2,1)S(1)}, u32[]{:S(2)}, u32[]{:S(2)}) async-start(bf16[4,656,288]{1,2,0:T(8,128)(2,1)} %copy.197), calls=%async_computation | async-start | bytes 3538944 | tf_op jit(solution)/shard_map/all_to_all | solution.py:587
  99.7 102.9 %all-to-all-start.3 = ((bf16[4,640,288]{1,2,0:T(8,128)(2,1)}), bf16[4,640,288]{1,2,0:T(8,128)(2,1)}, u32[]{:S(2)}, u32[]{:S(2)}) async-start(bf16[4,640,288]{1,2,0:T(8,128)(2,1)} %bitcast.262), calls=%async_computation.3 | async-start | bytes 2949120 | tf_op jit(solution)/shard_map/all_to_all | solution.py:587
  109.4 40.7 %collective-permute-start.3 = (bf16[1280,384]{1,0:T(8,128)(2,1)S(1)}, bf16[1280,384]{1,0:T(8,128)(2,1)S(1)}, u32[]{:S(2)}, u32[]{:S(2)}) collective-permute-start(bf16[1280,384]{1,0:T(8,128)(2,1)S(1)} %slice.820.refs_0_), channel_id=1, source_target_pairs={{0,1},{1,2},{2,3},{3,11},{11,10},{10,9},{9,8},{8,0},{4,5},{5,6},{6... | collective-permute-start | bytes 2949128 | tf_op jit(solution)/shard_map/ppermute | solution.py:486
  111.1 38.9 %collective-permute-start = (bf16[1280,384]{1,0:T(8,128)(2,1)S(1)}, bf16[1280,384]{1,0:T(8,128)(2,1)S(1)}, u32[]{:S(2)}, u32[]{:S(2)}) collective-permute-start(bf16[1280,384]{1,0:T(8,128)(2,1)S(1)} %slice.820.refs_0_), channel_id=1, source_target_pairs={{1,0},{2,1},{3,2},{11,3},{10,11},{9,10},{8,9},{0,8},{5,4},{6,5},{7... | collective-permute-start | bytes 2949128 | tf_op jit(solution)/shard_map/ppermute | solution.py:487
  150.0 35.8 %collective-permute-start.4 = (bf16[1280,384]{1,0:T(8,128)(2,1)S(1)}, bf16[1280,384]{1,0:T(8,128)(2,1)}, u32[]{:S(2)}, u32[]{:S(2)}) collective-permute-start(bf16[1280,384]{1,0:T(8,128)(2,1)S(1)} %collective-permute-done.3.refs_8_), channel_id=1, source_target_pairs={{0,1},{1,2},{2,3},{3,11},{11,10},{10,9},{9,8},{8,0},{4,5},{5,6},{6... | collective-permute-start | bytes 2949128 | tf_op jit(solution)/shard_map/ppermute | solution.py:486
  150.0 46.1 %collective-permute-start.1 = (bf16[1280,384]{1,0:T(8,128)(2,1)S(1)}, bf16[1280,384]{1,0:T(8,128)(2,1)}, u32[]{:S(2)}, u32[]{:S(2)}) collective-permute-start(bf16[1280,384]{1,0:T(8,128)(2,1)S(1)} %collective-permute-done.refs_1_), channel_id=1, source_target_pairs={{1,0},{2,1},{3,2},{11,3},{10,11},{9,10},{8,9},{0,8},{5,4},{6,5},{7... | collective-permute-start | bytes 2949128 | tf_op jit(solution)/shard_map/ppermute | solution.py:487
  185.8 38.0 %collective-permute-start.5 = (bf16[1280,384]{1,0:T(8,128)(2,1)}, bf16[1280,384]{1,0:T(8,128)(2,1)S(1)}, u32[]{:S(2)}, u32[]{:S(2)}) collective-permute-start(bf16[1280,384]{1,0:T(8,128)(2,1)} %collective-permute-done.4.refs_7_), channel_id=1, source_target_pairs={{0,1},{1,2},{2,3},{3,11},{11,10},{10,9},{9,8},{8,0},{4,5},{5,6},{6... | collective-permute-start | bytes 2949128 | tf_op jit(solution)/shard_map/ppermute | solution.py:486
  196.1 31.0 %collective-permute-start.2 = (bf16[1280,384]{1,0:T(8,128)(2,1)}, bf16[1280,384]{1,0:T(8,128)(2,1)S(1)}, u32[]{:S(2)}, u32[]{:S(2)}) collective-permute-start(bf16[1280,384]{1,0:T(8,128)(2,1)} %collective-permute-done.1.refs_2_), channel_id=1, source_target_pairs={{1,0},{2,1},{3,2},{11,3},{10,11},{9,10},{8,9},{0,8},{5,4},{6,5},{7... | collective-permute-start | bytes 2949128 | tf_op jit(solution)/shard_map/ppermute | solution.py:487
  224.7 34.2 %collective-permute-start.6 = (bf16[640,384]{1,0:T(8,128)(2,1)}, bf16[640,384]{1,0:T(8,128)(2,1)S(1)}, u32[]{:S(2)}, u32[]{:S(2)}) collective-permute-start(bf16[640,384]{1,0:T(8,128)(2,1)} %slice.821), channel_id=1, source_target_pairs={{0,1},{1,2},{2,3},{3,11},{11,10},{10,9},{9,8},{8,0},{4,5},{5,6},{6... | collective-permute-start | bytes 1474568 | tf_op jit(solution)/shard_map/ppermute | solution.py:491
  228.0 30.9 %collective-permute-start.7 = (bf16[640,384]{1,0:T(8,128)(2,1)}, bf16[640,384]{1,0:T(8,128)(2,1)}, u32[]{:S(2)}, u32[]{:S(2)}) collective-permute-start(bf16[640,384]{1,0:T(8,128)(2,1)} %slice.822), channel_id=1, source_target_pairs={{1,0},{2,1},{3,2},{11,3},{10,11},{9,10},{8,9},{0,8},{5,4},{6,5},{7... | collective-permute-start | bytes 1474568 | tf_op jit(solution)/shard_map/ppermute | solution.py:492
  405.1 125.9 %collective-permute-start.15 = (bf16[8,288,1536]{2,1,0:T(8,128)(2,1)}, bf16[8,288,1536]{2,1,0:T(8,128)(2,1)}, u32[]{:S(2)}, u32[]{:S(2)}) collective-permute-start(bf16[8,288,1536]{2,1,0:T(8,128)(2,1)} %get-tuple-element.134), channel_id=1, source_target_pairs={{0,4},{4,0},{1,5},{5,1},{2,6},{6,2},{3,7},{7,3},{8,12},{12,8},{9,1... | collective-permute-start | bytes 21233672 | tf_op jit(solution)/shard_map/ppermute | solution.py:634
  417.9 63.9 %collective-permute-start.8 = (bf16[8,288,768]{2,1,0:T(8,128)(2,1)}, bf16[8,288,768]{2,1,0:T(8,128)(2,1)}, u32[]{:S(2)}, u32[]{:S(2)}) collective-permute-start(bf16[8,288,768]{2,1,0:T(8,128)(2,1)} %get-tuple-element.124), channel_id=1, source_target_pairs={{0,4},{4,0},{1,5},{5,1},{2,6},{6,2},{3,7},{7,3},{8,12},{12,8},{9,1... | collective-permute-start | bytes 10616840 | tf_op jit(solution)/shard_map/ppermute | solution.py:634
  442.6 33.7 %collective-permute-start.20 = (bf16[8,304,288]{1,2,0:T(8,128)(2,1)}, bf16[8,304,288]{1,2,0:T(8,128)(2,1)}, u32[]{:S(2)}, u32[]{:S(2)}) collective-permute-start(bf16[8,304,288]{1,2,0:T(8,128)(2,1)} %copy.223), channel_id=1, source_target_pairs={{0,4},{4,0},{1,5},{5,1},{2,6},{6,2},{3,7},{7,3},{8,12},{12,8},{9,1... | collective-permute-start | bytes 4202504 | tf_op jit(solution)/shard_map/ppermute | solution.py:634
  479.3 101.5 %collective-permute-start.21 = (bf16[152,288]{1,0:T(8,128)(2,1)}, bf16[152,288]{1,0:T(8,128)(2,1)S(1)}, u32[]{:S(2)}, u32[]{:S(2)}) collective-permute-start(bf16[152,288]{1,0:T(8,128)(2,1)} %get-tuple-element.146), channel_id=1, source_target_pairs={{0,1},{1,2},{2,3},{3,11},{11,10},{10,9},{9,8},{8,0},{4,5},{5,6},{6... | collective-permute-start | bytes 262664 | tf_op jit(solution)/shard_map/ppermute | solution.py:504
  483.1 21.2 %collective-permute-start.10 = (bf16[144,768]{1,0:T(8,128)(2,1)S(1)}, bf16[144,768]{1,0:T(8,128)(2,1)S(1)}, u32[]{:S(2)}, u32[]{:S(2)}) collective-permute-start(bf16[144,768]{1,0:T(8,128)(2,1)S(1)} %get-tuple-element.126), channel_id=1, source_target_pairs={{1,0},{2,1},{3,2},{11,3},{10,11},{9,10},{8,9},{0,8},{5,4},{6,5},{7... | collective-permute-start | bytes 663560 | tf_op jit(solution)/shard_map/ppermute | solution.py:504
  483.2 22.0 %collective-permute-start.9 = (bf16[144,768]{1,0:T(8,128)(2,1)S(1)}, bf16[144,768]{1,0:T(8,128)(2,1)S(1)}, u32[]{:S(2)}, u32[]{:S(2)}) collective-permute-start(bf16[144,768]{1,0:T(8,128)(2,1)S(1)} %get-tuple-element.125), channel_id=1, source_target_pairs={{0,1},{1,2},{2,3},{3,11},{11,10},{10,9},{9,8},{8,0},{4,5},{5,6},{6... | collective-permute-start | bytes 663560 | tf_op jit(solution)/shard_map/ppermute | solution.py:504
  506.0 20.2 %collective-permute-start.11 = (bf16[288,768]{1,0:T(8,128)(2,1)}, bf16[288,768]{1,0:T(8,128)(2,1)}, u32[]{:S(2)}, u32[]{:S(2)}) collective-permute-start(bf16[288,768]{1,0:T(8,128)(2,1)} %pad_maximum_fusion.11), channel_id=1, source_target_pairs={{0,1},{1,2},{2,3},{3,11},{11,10},{10,9},{9,8},{8,0},{4,5},{5,6},{6... | collective-permute-start | bytes 1327112 | tf_op jit(solution)/shard_map/ppermute | solution.py:504
  514.2 12.0 %collective-permute-start.12 = (bf16[288,768]{1,0:T(8,128)(2,1)}, bf16[288,768]{1,0:T(8,128)(2,1)}, u32[]{:S(2)}, u32[]{:S(2)}) collective-permute-start(bf16[288,768]{1,0:T(8,128)(2,1)} %pad_maximum_fusion.12), channel_id=1, source_target_pairs={{1,0},{2,1},{3,2},{11,3},{10,11},{9,10},{8,9},{0,8},{5,4},{6,5},{7... | collective-permute-start | bytes 1327112 | tf_op jit(solution)/shard_map/ppermute | solution.py:504
  528.2 13.5 %collective-permute-start.13 = (bf16[288,768]{1,0:T(8,128)(2,1)S(1)}, bf16[288,768]{1,0:T(8,128)(2,1)S(1)}, u32[]{:S(2)}, u32[]{:S(2)}) collective-permute-start(bf16[288,768]{1,0:T(8,128)(2,1)S(1)} %get-tuple-element.129), channel_id=1, source_target_pairs={{0,1},{1,2},{2,3},{3,11},{11,10},{10,9},{9,8},{8,0},{4,5},{5,6},{6... | collective-permute-start | bytes 1327112 | tf_op jit(solution)/shard_map/ppermute | solution.py:504
  531.1 13.1 %collective-permute-start.14 = (bf16[288,768]{1,0:T(8,128)(2,1)S(1)}, bf16[288,768]{1,0:T(8,128)(2,1)S(1)}, u32[]{:S(2)}, u32[]{:S(2)}) collective-permute-start(bf16[288,768]{1,0:T(8,128)(2,1)S(1)} %get-tuple-element.130), channel_id=1, source_target_pairs={{1,0},{2,1},{3,2},{11,3},{10,11},{9,10},{8,9},{0,8},{5,4},{6,5},{7... | collective-permute-start | bytes 1327112 | tf_op jit(solution)/shard_map/ppermute | solution.py:504
  532.7 15.8 %collective-permute-start.16 = (bf16[144,1536]{1,0:T(8,128)(2,1)S(1)}, bf16[144,1536]{1,0:T(8,128)(2,1)S(1)}, u32[]{:S(2)}, u32[]{:S(2)}) collective-permute-start(bf16[144,1536]{1,0:T(8,128)(2,1)S(1)} %get-tuple-element.135), channel_id=1, source_target_pairs={{0,1},{1,2},{2,3},{3,11},{11,10},{10,9},{9,8},{8,0},{4,5},{5,6},{6... | collective-permute-start | bytes 1327112 | tf_op jit(solution)/shard_map/ppermute | solution.py:504
  534.8 17.2 %collective-permute-start.17 = (bf16[144,1536]{1,0:T(8,128)(2,1)S(1)}, bf16[144,1536]{1,0:T(8,128)(2,1)S(1)}, u32[]{:S(2)}, u32[]{:S(2)}) collective-permute-start(bf16[144,1536]{1,0:T(8,128)(2,1)S(1)} %get-tuple-element.136), channel_id=1, source_target_pairs={{1,0},{2,1},{3,2},{11,3},{10,11},{9,10},{8,9},{0,8},{5,4},{6,5},{7... | collective-permute-start | bytes 1327112 | tf_op jit(solution)/shard_map/ppermute | solution.py:504
  541.7 52.4 %collective-permute-start.22 = (bf16[152,288]{1,0:T(8,128)(2,1)}, bf16[152,288]{1,0:T(8,128)(2,1)}, u32[]{:S(2)}, u32[]{:S(2)}) collective-permute-start(bf16[152,288]{1,0:T(8,128)(2,1)} %get-tuple-element.147), channel_id=1, source_target_pairs={{1,0},{2,1},{3,2},{11,3},{10,11},{9,10},{8,9},{0,8},{5,4},{6,5},{7... | collective-permute-start | bytes 262664 | tf_op jit(solution)/shard_map/ppermute | solution.py:504
  554.6 80.1 %collective-permute-start.25 = (bf16[288,768]{1,0:T(8,128)(2,1)}, bf16[288,768]{1,0:T(8,128)(2,1)}, u32[]{:S(2)}, u32[]{:S(2)}) collective-permute-start(bf16[288,768]{1,0:T(8,128)(2,1)} %get-tuple-element.153), channel_id=1, source_target_pairs={{0,1},{1,2},{2,3},{3,11},{11,10},{10,9},{9,8},{8,0},{4,5},{5,6},{6... | collective-permute-start | bytes 1327112 | tf_op jit(solution)/shard_map/ppermute | solution.py:504
  558.2 77.2 %collective-permute-start.18 = (bf16[288,1536]{1,0:T(8,128)(2,1)}, bf16[288,1536]{1,0:T(8,128)(2,1)}, u32[]{:S(2)}, u32[]{:S(2)}) collective-permute-start(bf16[288,1536]{1,0:T(8,128)(2,1)} %pad_maximum_fusion.8), channel_id=1, source_target_pairs={{0,1},{1,2},{2,3},{3,11},{11,10},{10,9},{9,8},{8,0},{4,5},{5,6},{6... | collective-permute-start | bytes 2654216 | tf_op jit(solution)/shard_map/ppermute | solution.py:504
  559.3 76.1 %collective-permute-start.19 = (bf16[288,1536]{1,0:T(8,128)(2,1)}, bf16[288,1536]{1,0:T(8,128)(2,1)}, u32[]{:S(2)}, u32[]{:S(2)}) collective-permute-start(bf16[288,1536]{1,0:T(8,128)(2,1)} %pad_maximum_fusion.9), channel_id=1, source_target_pairs={{1,0},{2,1},{3,2},{11,3},{10,11},{9,10},{8,9},{0,8},{5,4},{6,5},{7... | collective-permute-start | bytes 2654216 | tf_op jit(solution)/shard_map/ppermute | solution.py:504
  580.8 54.6 %collective-permute-start.26 = (bf16[288,768]{1,0:T(8,128)(2,1)}, bf16[288,768]{1,0:T(8,128)(2,1)}, u32[]{:S(2)}, u32[]{:S(2)}) collective-permute-start(bf16[288,768]{1,0:T(8,128)(2,1)} %get-tuple-element.154), channel_id=1, source_target_pairs={{1,0},{2,1},{3,2},{11,3},{10,11},{9,10},{8,9},{0,8},{5,4},{6,5},{7... | collective-permute-start | bytes 1327112 | tf_op jit(solution)/shard_map/ppermute | solution.py:504
  594.1 27.3 %collective-permute-start.23 = (bf16[640,128]{1,0:T(8,128)(2,1)S(1)}, bf16[640,128]{1,0:T(8,128)(2,1)S(1)}, u32[]{:S(2)}, u32[]{:S(2)}) collective-permute-start(bf16[640,128]{1,0:T(8,128)(2,1)S(1)} %get-tuple-element.149), channel_id=1, source_target_pairs={{0,1},{1,2},{2,3},{3,11},{11,10},{10,9},{9,8},{8,0},{4,5},{5,6},{6... | collective-permute-start | bytes 491528 | tf_op jit(solution)/shard_map/ppermute | solution.py:504
  621.4 13.3 %collective-permute-start.24 = (bf16[640,128]{1,0:T(8,128)(2,1)S(1)}, bf16[640,128]{1,0:T(8,128)(2,1)S(1)}, u32[]{:S(2)}, u32[]{:S(2)}) collective-permute-start(bf16[640,128]{1,0:T(8,128)(2,1)S(1)} %get-tuple-element.150), channel_id=1, source_target_pairs={{1,0},{2,1},{3,2},{11,3},{10,11},{9,10},{8,9},{0,8},{5,4},{6,5},{7... | collective-permute-start | bytes 491528 | tf_op jit(solution)/shard_map/ppermute | solution.py:504
  656.0 57.3 %collective-permute-start.33 = (bf16[640,128]{1,0:T(8,128)(2,1)S(1)}, bf16[640,128]{1,0:T(8,128)(2,1)S(1)}, u32[]{:S(2)}, u32[]{:S(2)}) collective-permute-start(bf16[640,128]{1,0:T(8,128)(2,1)S(1)} %get-tuple-element.170), channel_id=1, source_target_pairs={{0,1},{1,2},{2,3},{3,11},{11,10},{10,9},{9,8},{8,0},{4,5},{5,6},{6... | collective-permute-start | bytes 491528 | tf_op jit(solution)/shard_map/ppermute | solution.py:504
  679.6 37.2 %collective-permute-start.34 = (bf16[640,128]{1,0:T(8,128)(2,1)S(1)}, bf16[640,128]{1,0:T(8,128)(2,1)S(1)}, u32[]{:S(2)}, u32[]{:S(2)}) collective-permute-start(bf16[640,128]{1,0:T(8,128)(2,1)S(1)} %get-tuple-element.171), channel_id=1, source_target_pairs={{1,0},{2,1},{3,2},{11,3},{10,11},{9,10},{8,9},{0,8},{5,4},{6,5},{7... | collective-permute-start | bytes 491528 | tf_op jit(solution)/shard_map/ppermute | solution.py:504
  683.0 42.6 %collective-permute-start.29 = (bf16[304,288]{1,0:T(8,128)(2,1)}, bf16[304,288]{1,0:T(8,128)(2,1)}, u32[]{:S(2)}, u32[]{:S(2)}) collective-permute-start(bf16[304,288]{1,0:T(8,128)(2,1)} %pad_maximum_fusion.21), channel_id=1, source_target_pairs={{0,1},{1,2},{2,3},{3,11},{11,10},{10,9},{9,8},{8,0},{4,5},{5,6},{6... | collective-permute-start | bytes 525320 | tf_op jit(solution)/shard_map/ppermute | solution.py:504
  703.2 36.7 %collective-permute-start.27 = (bf16[288,1536]{1,0:T(8,128)(2,1)}, bf16[288,1536]{1,0:T(8,128)(2,1)}, u32[]{:S(2)}, u32[]{:S(2)}) collective-permute-start(bf16[288,1536]{1,0:T(8,128)(2,1)} %get-tuple-element.159), channel_id=1, source_target_pairs={{0,1},{1,2},{2,3},{3,11},{11,10},{10,9},{9,8},{8,0},{4,5},{5,6},{6... | collective-permute-start | bytes 2654216 | tf_op jit(solution)/shard_map/ppermute | solution.py:504
  710.7 29.2 %collective-permute-start.28 = (bf16[288,1536]{1,0:T(8,128)(2,1)}, bf16[288,1536]{1,0:T(8,128)(2,1)}, u32[]{:S(2)}, u32[]{:S(2)}) collective-permute-start(bf16[288,1536]{1,0:T(8,128)(2,1)} %get-tuple-element.160), channel_id=1, source_target_pairs={{1,0},{2,1},{3,2},{11,3},{10,11},{9,10},{8,9},{0,8},{5,4},{6,5},{7... | collective-permute-start | bytes 2654216 | tf_op jit(solution)/shard_map/ppermute | solution.py:504
  713.3 26.5 %collective-permute-start.31 = (bf16[1280,128]{1,0:T(8,128)(2,1)}, bf16[1280,128]{1,0:T(8,128)(2,1)}, u32[]{:S(2)}, u32[]{:S(2)}) collective-permute-start(bf16[1280,128]{1,0:T(8,128)(2,1)} %pad_maximum_fusion.13), channel_id=1, source_target_pairs={{0,1},{1,2},{2,3},{3,11},{11,10},{10,9},{9,8},{8,0},{4,5},{5,6},{6... | collective-permute-start | bytes 983048 | tf_op jit(solution)/shard_map/ppermute | solution.py:504
  717.5 22.4 %collective-permute-start.32 = (bf16[1280,128]{1,0:T(8,128)(2,1)}, bf16[1280,128]{1,0:T(8,128)(2,1)}, u32[]{:S(2)}, u32[]{:S(2)}) collective-permute-start(bf16[1280,128]{1,0:T(8,128)(2,1)} %pad_maximum_fusion.14), channel_id=1, source_target_pairs={{1,0},{2,1},{3,2},{11,3},{10,11},{9,10},{8,9},{0,8},{5,4},{6,5},{7... | collective-permute-start | bytes 983048 | tf_op jit(solution)/shard_map/ppermute | solution.py:504
  725.6 14.3 %collective-permute-start.30 = (bf16[304,288]{1,0:T(8,128)(2,1)}, bf16[304,288]{1,0:T(8,128)(2,1)S(1)}, u32[]{:S(2)}, u32[]{:S(2)}) collective-permute-start(bf16[304,288]{1,0:T(8,128)(2,1)} %pad_maximum_fusion.22), channel_id=1, source_target_pairs={{1,0},{2,1},{3,2},{11,3},{10,11},{9,10},{8,9},{0,8},{5,4},{6,5},{7... | collective-permute-start | bytes 525320 | tf_op jit(solution)/shard_map/ppermute | solution.py:504
  742.0 121.4 %collective-permute-start.39 = (bf16[304,288]{1,0:T(8,128)(2,1)}, bf16[304,288]{1,0:T(8,128)(2,1)S(1)}, u32[]{:S(2)}, u32[]{:S(2)}) collective-permute-start(bf16[304,288]{1,0:T(8,128)(2,1)} %get-tuple-element.184), channel_id=1, source_target_pairs={{0,1},{1,2},{2,3},{3,11},{11,10},{10,9},{9,8},{8,0},{4,5},{5,6},{6... | collective-permute-start | bytes 525320 | tf_op jit(solution)/shard_map/ppermute | solution.py:504
  745.3 118.3 %collective-permute-start.40 = (bf16[304,288]{1,0:T(8,128)(2,1)}, bf16[304,288]{1,0:T(8,128)(2,1)}, u32[]{:S(2)}, u32[]{:S(2)}) collective-permute-start(bf16[304,288]{1,0:T(8,128)(2,1)} %get-tuple-element.185), channel_id=1, source_target_pairs={{1,0},{2,1},{3,2},{11,3},{10,11},{9,10},{8,9},{0,8},{5,4},{6,5},{7... | collective-permute-start | bytes 525320 | tf_op jit(solution)/shard_map/ppermute | solution.py:504
  747.6 80.2 %collective-permute-start.35 = (bf16[1280,128]{1,0:T(8,128)(2,1)}, bf16[1280,128]{1,0:T(8,128)(2,1)}, u32[]{:S(2)}, u32[]{:S(2)}) collective-permute-start(bf16[1280,128]{1,0:T(8,128)(2,1)} %get-tuple-element.176), channel_id=1, source_target_pairs={{0,1},{1,2},{2,3},{3,11},{11,10},{10,9},{9,8},{8,0},{4,5},{5,6},{6... | collective-permute-start | bytes 983048 | tf_op jit(solution)/shard_map/ppermute | solution.py:504
  770.3 40.8 %collective-permute-start.47 = (bf16[640,128]{1,0:T(8,128)(2,1)}, bf16[640,128]{1,0:T(8,128)(2,1)}, u32[]{:S(2)}, u32[]{:S(2)}) collective-permute-start(bf16[640,128]{1,0:T(8,128)(2,1)} %get-tuple-element.196), channel_id=1, source_target_pairs={{0,1},{1,2},{2,3},{3,11},{11,10},{10,9},{9,8},{8,0},{4,5},{5,6},{6... | collective-permute-start | bytes 491528 | tf_op jit(solution)/shard_map/ppermute | solution.py:504
  797.5 24.1 %collective-permute-start.48 = (bf16[640,128]{1,0:T(8,128)(2,1)}, bf16[640,128]{1,0:T(8,128)(2,1)}, u32[]{:S(2)}, u32[]{:S(2)}) collective-permute-start(bf16[640,128]{1,0:T(8,128)(2,1)} %get-tuple-element.197), channel_id=1, source_target_pairs={{1,0},{2,1},{3,2},{11,3},{10,11},{9,10},{8,9},{0,8},{5,4},{6,5},{7... | collective-permute-start | bytes 491528 | tf_op jit(solution)/shard_map/ppermute | solution.py:504
  811.1 22.9 %collective-permute-start.36 = (bf16[1280,128]{1,0:T(8,128)(2,1)}, bf16[1280,128]{1,0:T(8,128)(2,1)S(1)}, u32[]{:S(2)}, u32[]{:S(2)}) collective-permute-start(bf16[1280,128]{1,0:T(8,128)(2,1)} %get-tuple-element.177), channel_id=1, source_target_pairs={{1,0},{2,1},{3,2},{11,3},{10,11},{9,10},{8,9},{0,8},{5,4},{6,5},{7... | collective-permute-start | bytes 983048 | tf_op jit(solution)/shard_map/ppermute | solution.py:504
  821.6 20.7 %collective-permute-start.41 = (bf16[1280,128]{1,0:T(8,128)(2,1)}, bf16[1280,128]{1,0:T(8,128)(2,1)S(1)}, u32[]{:S(2)}, u32[]{:S(2)}) collective-permute-start(bf16[1280,128]{1,0:T(8,128)(2,1)} %pad_maximum_fusion.15), channel_id=1, source_target_pairs={{0,1},{1,2},{2,3},{3,11},{11,10},{10,9},{9,8},{8,0},{4,5},{5,6},{6... | collective-permute-start | bytes 983048 | tf_op jit(solution)/shard_map/ppermute | solution.py:504
  827.8 15.7 %collective-permute-start.42 = (bf16[1280,128]{1,0:T(8,128)(2,1)}, bf16[1280,128]{1,0:T(8,128)(2,1)S(1)}, u32[]{:S(2)}, u32[]{:S(2)}) collective-permute-start(bf16[1280,128]{1,0:T(8,128)(2,1)} %pad_maximum_fusion.16), channel_id=1, source_target_pairs={{1,0},{2,1},{3,2},{11,3},{10,11},{9,10},{8,9},{0,8},{5,4},{6,5},{7... | collective-permute-start | bytes 983048 | tf_op jit(solution)/shard_map/ppermute | solution.py:504
  834.0 15.2 %collective-permute-start.49 = (bf16[1280,128]{1,0:T(8,128)(2,1)S(1)}, bf16[1280,128]{1,0:T(8,128)(2,1)S(1)}, u32[]{:S(2)}, u32[]{:S(2)}) collective-permute-start(bf16[1280,128]{1,0:T(8,128)(2,1)S(1)} %pad_maximum_fusion.17), channel_id=1, source_target_pairs={{0,1},{1,2},{2,3},{3,11},{11,10},{10,9},{9,8},{8,0},{4,5},{5,6},{6... | collective-permute-start | bytes 983048 | tf_op jit(solution)/shard_map/ppermute | solution.py:504
  843.5 12.9 %collective-permute-start.37 = (bf16[1280,128]{1,0:T(8,128)(2,1)S(1)}, bf16[1280,128]{1,0:T(8,128)(2,1)S(1)}, u32[]{:S(2)}, u32[]{:S(2)}) collective-permute-start(bf16[1280,128]{1,0:T(8,128)(2,1)S(1)} %get-tuple-element.178), channel_id=1, source_target_pairs={{0,1},{1,2},{2,3},{3,11},{11,10},{10,9},{9,8},{8,0},{4,5},{5,6},{6... | collective-permute-start | bytes 983048 | tf_op jit(solution)/shard_map/ppermute | solution.py:504
  849.3 10.7 %collective-permute-start.38 = (bf16[1280,128]{1,0:T(8,128)(2,1)S(1)}, bf16[1280,128]{1,0:T(8,128)(2,1)S(1)}, u32[]{:S(2)}, u32[]{:S(2)}) collective-permute-start(bf16[1280,128]{1,0:T(8,128)(2,1)S(1)} %get-tuple-element.179), channel_id=1, source_target_pairs={{1,0},{2,1},{3,2},{11,3},{10,11},{9,10},{8,9},{0,8},{5,4},{6,5},{7... | collective-permute-start | bytes 983048 | tf_op jit(solution)/shard_map/ppermute | solution.py:504
  852.7 11.0 %collective-permute-start.43 = (bf16[1280,128]{1,0:T(8,128)(2,1)S(1)}, bf16[1280,128]{1,0:T(8,128)(2,1)S(1)}, u32[]{:S(2)}, u32[]{:S(2)}) collective-permute-start(bf16[1280,128]{1,0:T(8,128)(2,1)S(1)} %get-tuple-element.191), channel_id=1, source_target_pairs={{0,1},{1,2},{2,3},{3,11},{11,10},{10,9},{9,8},{8,0},{4,5},{5,6},{6... | collective-permute-start | bytes 983048 | tf_op jit(solution)/shard_map/ppermute | solution.py:504
  932.2 34.6 %collective-permute-start.55 = (bf16[8,304,480]{2,1,0:T(8,128)(2,1)}, bf16[8,304,480]{2,1,0:T(8,128)(2,1)}, u32[]{:S(2)}, u32[]{:S(2)}) collective-permute-start(bf16[8,304,480]{2,1,0:T(8,128)(2,1)} %get-tuple-element.210), channel_id=1, source_target_pairs={{0,4},{4,0},{1,5},{5,1},{2,6},{6,2},{3,7},{7,3},{8,12},{12,8},{9,1... | collective-permute-start | bytes 7004168 | tf_op jit(solution)/shard_map/ppermute | solution.py:634
  937.0 63.9 %collective-permute-start.66 = (bf16[288,1536]{1,0:T(8,128)(2,1)}, bf16[288,1536]{1,0:T(8,128)(2,1)}, u32[]{:S(2)}, u32[]{:S(2)}) collective-permute-start(bf16[288,1536]{1,0:T(8,128)(2,1)} %get-tuple-element.225), channel_id=1, source_target_pairs={{0,1},{1,2},{2,3},{3,11},{11,10},{10,9},{9,8},{8,0},{4,5},{5,6},{6... | collective-permute-start | bytes 2654216 | tf_op jit(solution)/shard_map/ppermute | solution.py:504
  938.6 62.3 %collective-permute-start.67 = (bf16[288,1536]{1,0:T(8,128)(2,1)}, bf16[288,1536]{1,0:T(8,128)(2,1)}, u32[]{:S(2)}, u32[]{:S(2)}) collective-permute-start(bf16[288,1536]{1,0:T(8,128)(2,1)} %get-tuple-element.226), channel_id=1, source_target_pairs={{1,0},{2,1},{3,2},{11,3},{10,11},{9,10},{8,9},{0,8},{5,4},{6,5},{7... | collective-permute-start | bytes 2654216 | tf_op jit(solution)/shard_map/ppermute | solution.py:504
  941.0 23.7 %collective-permute-start.64 = (bf16[304,288]{1,0:T(8,128)(2,1)}, bf16[304,288]{1,0:T(8,128)(2,1)}, u32[]{:S(2)}, u32[]{:S(2)}) collective-permute-start(bf16[304,288]{1,0:T(8,128)(2,1)} %get-tuple-element.221), channel_id=1, source_target_pairs={{0,1},{1,2},{2,3},{3,11},{11,10},{10,9},{9,8},{8,0},{4,5},{5,6},{6... | collective-permute-start | bytes 525320 | tf_op jit(solution)/shard_map/ppermute | solution.py:504
  942.7 22.9 %collective-permute-start.65 = (bf16[304,288]{1,0:T(8,128)(2,1)S(1)}, bf16[304,288]{1,0:T(8,128)(2,1)}, u32[]{:S(2)}, u32[]{:S(2)}) collective-permute-start(bf16[304,288]{1,0:T(8,128)(2,1)S(1)} %get-tuple-element.222), channel_id=1, source_target_pairs={{1,0},{2,1},{3,2},{11,3},{10,11},{9,10},{8,9},{0,8},{5,4},{6,5},{7... | collective-permute-start | bytes 525320 | tf_op jit(solution)/shard_map/ppermute | solution.py:504
  951.1 46.3 %all-to-all-start.7 = ((bf16[640,4,288]{0,2,1:T(8,128)(2,1)}), bf16[640,4,288]{0,2,1:T(8,128)(2,1)S(1)}, u32[]{:S(2)}, u32[]{:S(2)}) async-start(bf16[640,4,288]{0,2,1:T(8,128)(2,1)} %bitcast.76), calls=%async_computation.7 | async-start | bytes 2949120 | tf_op jit(solution)/shard_map/all_to_all | solution.py:590
  968.1 14.4 %collective-permute-start.57 = (bf16[152,480]{1,0:T(8,128)(2,1)S(1)}, bf16[152,480]{1,0:T(8,128)(2,1)S(1)}, u32[]{:S(2)}, u32[]{:S(2)}) collective-permute-start(bf16[152,480]{1,0:T(8,128)(2,1)S(1)} %get-tuple-element.212), channel_id=1, source_target_pairs={{1,0},{2,1},{3,2},{11,3},{10,11},{9,10},{8,9},{0,8},{5,4},{6,5},{7... | collective-permute-start | bytes 437768 | tf_op jit(solution)/shard_map/ppermute | solution.py:504
  970.9 12.3 %collective-permute-start.56 = (bf16[152,480]{1,0:T(8,128)(2,1)S(1)}, bf16[152,480]{1,0:T(8,128)(2,1)S(1)}, u32[]{:S(2)}, u32[]{:S(2)}) collective-permute-start(bf16[152,480]{1,0:T(8,128)(2,1)S(1)} %get-tuple-element.211), channel_id=1, source_target_pairs={{0,1},{1,2},{2,3},{3,11},{11,10},{10,9},{9,8},{8,0},{4,5},{5,6},{6... | collective-permute-start | bytes 437768 | tf_op jit(solution)/shard_map/ppermute | solution.py:504
  997.3 23.0 %all-to-all-start.4 = ((bf16[640,4,288]{0,2,1:T(8,128)(2,1)}), bf16[640,4,288]{0,2,1:T(8,128)(2,1)S(1)}, u32[]{:S(2)}, u32[]{:S(2)}) async-start(bf16[640,4,288]{0,2,1:T(8,128)(2,1)} %bitcast.28), calls=%async_computation.4 | async-start | bytes 2949120 | tf_op jit(solution)/shard_map/all_to_all | solution.py:590
  1007.1 19.4 %collective-permute-start.62 = (bf16[304,480]{1,0:T(8,128)(2,1)}, bf16[304,480]{1,0:T(8,128)(2,1)S(1)}, u32[]{:S(2)}, u32[]{:S(2)}) collective-permute-start(bf16[304,480]{1,0:T(8,128)(2,1)} %get-tuple-element.217), channel_id=1, source_target_pairs={{0,1},{1,2},{2,3},{3,11},{11,10},{10,9},{9,8},{8,0},{4,5},{5,6},{6... | collective-permute-start | bytes 875528 | tf_op jit(solution)/shard_map/ppermute | solution.py:504
  1008.9 17.7 %collective-permute-start.63 = (bf16[304,480]{1,0:T(8,128)(2,1)}, bf16[304,480]{1,0:T(8,128)(2,1)}, u32[]{:S(2)}, u32[]{:S(2)}) collective-permute-start(bf16[304,480]{1,0:T(8,128)(2,1)} %get-tuple-element.218), channel_id=1, source_target_pairs={{1,0},{2,1},{3,2},{11,3},{10,11},{9,10},{8,9},{0,8},{5,4},{6,5},{7... | collective-permute-start | bytes 875528 | tf_op jit(solution)/shard_map/ppermute | solution.py:504
  (87 other events, 1698.9 us)
Sparse Core Ops, SparseCore 0:
  10.3 58.8 all-gather.4
  71.6 48.8 all-gather.6
  122.8 93.7 all-gather.10
  219.3 120.5 all-gather.8

commit v3 on v2

--- a/solution.py
+++ b/solution.py
@@ -57,17 +57,8 @@
     half = HEAD_DIM // 2
     rates = THETA ** (-jnp.arange(half, dtype=F32) / half)
     angles = depth.astype(F32)[:, None] * rates[None, :]
-    return (jnp.cos(angles), jnp.sin(angles))
-
-
-def turn(value, cosines, sines):
-    half = value.shape[-1] // 2
-    former, latter = (value[..., :half], value[..., half:])
-    cos_part = cosines[:, None, :]
-    sin_part = sines[:, None, :]
-    return jnp.concatenate(
-        [former * cos_part - latter * sin_part, latter * cos_part + former * sin_part], axis=-1
-    )
+    cosines, sines = jnp.cos(angles), jnp.sin(angles)
+    return (jnp.concatenate([cosines] * 4, axis=1), jnp.concatenate([-sines, sines] * 2, axis=1))
 
 
 def block_lists(first, key_index, block, held, tables):
@@ -114,6 +105,16 @@
     return jnp.where(rows <= columns, scores, -BIG)
 
 
+def stacked(ref):
+    value, wide = ref[...], 2 * HEAD_DIM
+    return jnp.concatenate([value[:, h * wide : (h + 1) * wide] for h in range(value.shape[1] // wide)], axis=0)
+
+
+def beside(value, heads):
+    rows = value.shape[0] // heads
+    return jnp.concatenate([value[h * rows : (h + 1) * rows] for h in range(heads)], axis=1)
+
+
 def left_half(shape):
     return lax.broadcasted_iota(jnp.int32, shape, 1) < HEAD_DIM
 
@@ -134,7 +135,7 @@
 def forward_kernel(lists, counts, q_ref, mark_ref, *refs):
     *pieces, o_ref, lse_ref, top_ref, sum_ref, kv_ref, vt_ref, sems = refs
     block = pl.program_id(1)
-    heads, rows = q_ref.shape[1], q_ref.shape[2]
+    heads, rows = q_ref.shape[1] // (2 * HEAD_DIM), q_ref.shape[0]
     total = kv_ref.shape[0]
     stride = total // rows
     count = counts[block]
@@ -154,7 +155,7 @@
         vt_ref[HEAD_DIM:] = jnp.where(lax.broadcasted_iota(jnp.int32, tail, 0) == 0, 1.0, 0.0).astype(BF16)
 
     def queries():
-        return q_ref[0].reshape(heads * rows, 2 * HEAD_DIM)
+        return stacked(q_ref)
 
     def blocks(start, n):
         offs = [pl.multiple_of(lists[block * stride + start + u] * rows, rows) for u in range(n)]
@@ -194,12 +195,14 @@
         lax.fori_loop(0, count, online, 0)
 
     total_row = sum_ref[HEAD_DIM : HEAD_DIM + 1, :]
-    o_ref[0] = (sum_ref[:HEAD_DIM, :] / total_row).T.astype(BF16).reshape(heads, rows, HEAD_DIM)
+    spread = jnp.concatenate([jnp.zeros((HEAD_DIM, heads * rows), F32), sum_ref[:HEAD_DIM, :] / total_row], axis=0)
+    o_ref[...] = beside(spread.T.astype(BF16), heads)
     lse_ref[0, 0] = top_ref[...] + jnp.log2(total_row)
 
 
 def attention_forward(lists, counts, q, pieces, marks):
-    groups, heads, tokens, wide = q.shape
+    tokens, wide, heads = q.shape[0], 2 * HEAD_DIM, REPEAT
+    groups = q.shape[1] // (wide * (heads + 1))
     total = marks.shape[0]
     blocks = counts.shape[0]
     rows = tokens // blocks
@@ -210,12 +213,12 @@
             num_scalar_prefetch=2,
             grid=(groups, blocks),
             in_specs=[
-                pl.BlockSpec((1, heads, rows, wide), lambda g, b, *_: (g, 0, b, 0)),
+                pl.BlockSpec((rows, heads * wide), lambda g, b, *_: (b, g)),
                 pl.BlockSpec((total, wide), lambda g, b, *_: (0, 0)),
                 *(pl.BlockSpec(memory_space=pl.ANY) for _ in pieces),
             ],
             out_specs=[
-                pl.BlockSpec((1, heads, rows, HEAD_DIM), lambda g, b, *_: (g, 0, b, 0)),
+                pl.BlockSpec((rows, heads * wide), lambda g, b, *_: (b, g)),
                 pl.BlockSpec((1, 1, 1, heads * rows), lambda g, b, *_: (g, b, 0, 0)),
             ],
             scratch_shapes=[
@@ -227,7 +230,7 @@
             ],
         ),
         out_shape=[
-            jax.ShapeDtypeStruct((groups, heads, tokens, HEAD_DIM), BF16),
+            jax.ShapeDtypeStruct((tokens, groups * heads * wide), BF16),
             jax.ShapeDtypeStruct((groups, blocks, 1, heads * rows), F32),
         ],
         compiler_params=pltpu.CompilerParams(vmem_limit_bytes=48 * 2**20),
@@ -238,10 +241,118 @@
     )(lists, counts, q, marks, *pieces)
 
 
-def backward_kernel(group, lists, counts, q_ref, do_ref, mark_ref, lse_ref, delta_ref, *refs):
-    *pieces, dq_ref, dkv_ref, dq_sum, dkv_sum, kv_ref, kt_ref, sems = refs
+def stage_kernel(begins, ends, lists, counts, q_ref, mark_ref, *refs):
+    refs = list(refs)
+    sums_in, tops_in = ([refs.pop(0), refs.pop(0)] if not begins else (None, None))
+    *pieces, first_ref, second_ref, top_ref, sum_ref, kv_ref, vt_ref, sems = refs
+    block = pl.program_id(1)
+    heads, rows = q_ref.shape[1] // (2 * HEAD_DIM), q_ref.shape[0]
+    total = kv_ref.shape[0]
+    stride = total // rows
+    count = counts[block]
+
+    @pl.when(block == 0)
+    def _():
+        fetch(pieces, pl.program_id(0), kv_ref, sems)
+
+        def flip(i, c):
+            k0 = pl.multiple_of(i * rows, rows)
+            turned = kv_ref[pl.ds(k0, rows), :].T
+            vt_ref[:HEAD_DIM, pl.ds(k0, rows)] = turned[HEAD_DIM:]
+            return c
+
+        lax.fori_loop(0, stride, flip, 0)
+        tail = (vt_ref.shape[0] - HEAD_DIM, total)
+        vt_ref[HEAD_DIM:] = jnp.where(lax.broadcasted_iota(jnp.int32, tail, 0) == 0, 1.0, 0.0).astype(BF16)
+
+    def queries():
+        return stacked(q_ref)
+
+    def blocks(start, n):
+        offs = [pl.multiple_of(lists[block * stride + start + u] * rows, rows) for u in range(n)]
+        kv = jnp.concatenate([kv_ref[pl.ds(k0, rows), :] for k0 in offs], axis=0)
+        mark = jnp.concatenate([mark_ref[pl.ds(k0, rows), :] for k0 in offs], axis=0)
+        vt = jnp.concatenate([vt_ref[:, pl.ds(k0, rows)] for k0 in offs], axis=1)
+        return jnp.where(left_half(kv.shape), kv, mark), vt
+
+    if begins:
+        k, vt = blocks(count, 1)
+        scores = causal(dg(k, queries(), NT), heads)
+        top = jnp.max(scores, axis=0, keepdims=True)
+        top_ref[...] = top
+        sum_ref[...] = dg(vt, jnp.exp2(scores - top).astype(BF16), NN)
+    else:
+        top_ref[...] = tops_in[0, 0]
+        sum_ref[...] = sums_in[0, 0]
+
+    def steps(start, n):
+        k, vt = blocks(start, n)
+        weights = jnp.exp2(dg(k, queries(), NT) - top_ref[...]).astype(BF16)
+        sum_ref[...] += dg(vt, weights, NN)
+
+    cascade(count, UNROLL, steps)
+    if ends:
+        total_row = sum_ref[HEAD_DIM : HEAD_DIM + 1, :]
+        spread = jnp.concatenate([jnp.zeros((HEAD_DIM, heads * rows), F32), sum_ref[:HEAD_DIM, :] / total_row], axis=0)
+        first_ref[...] = beside(spread.T.astype(BF16), heads)
+        second_ref[0, 0] = jnp.where(total_row < 2.0**100, top_ref[...] + jnp.log2(total_row), jnp.nan)
+    else:
+        first_ref[0, 0] = sum_ref[...]
+        second_ref[0, 0] = top_ref[...]
+
+
+def attention_stage(lists, counts, q, pieces, marks, state, ends):
+    tokens, wide, heads = q.shape[0], 2 * HEAD_DIM, REPEAT
+    groups = q.shape[1] // (wide * (heads + 1))
+    total = marks.shape[0]
+    blocks = counts.shape[0]
+    rows = tokens // blocks
+    tall = HEAD_DIM + 16
+    lanes = heads * rows
+    held_specs = [
+        pl.BlockSpec((1, 1, tall, lanes), lambda g, b, *_: (g, b, 0, 0)),
+        pl.BlockSpec((1, 1, 1, lanes), lambda g, b, *_: (g, b, 0, 0)),
+    ]
+    tops = jax.ShapeDtypeStruct((groups, blocks, 1, lanes), F32)
+    if ends:
+        out_specs = [pl.BlockSpec((rows, heads * wide), lambda g, b, *_: (b, g)), held_specs[1]]
+        out_shape = [jax.ShapeDtypeStruct((tokens, groups * heads * wide), BF16), tops]
+    else:
+        out_specs = held_specs
+        out_shape = [jax.ShapeDtypeStruct((groups, blocks, tall, lanes), F32), tops]
+    return pl.pallas_call(
+        functools.partial(stage_kernel, state is None, ends),
+        grid_spec=pltpu.PrefetchScalarGridSpec(
+            num_scalar_prefetch=2,
+            grid=(groups, blocks),
+            in_specs=[
+                pl.BlockSpec((rows, heads * wide), lambda g, b, *_: (b, g)),
+                pl.BlockSpec((total, wide), lambda g, b, *_: (0, 0)),
+                *([] if state is None else held_specs),
+                *(pl.BlockSpec(memory_space=pl.ANY) for _ in pieces),
+            ],
+            out_specs=out_specs,
+            scratch_shapes=[
+                pltpu.VMEM((1, lanes), F32),
+                pltpu.VMEM((tall, lanes), F32),
+                pltpu.VMEM((total, wide), BF16),
+                pltpu.VMEM((tall, total), BF16),
+                pltpu.SemaphoreType.DMA((len(pieces),)),
+            ],
+        ),
+        out_shape=out_shape,
+        compiler_params=pltpu.CompilerParams(vmem_limit_bytes=40 * 2**20),
+        cost_estimate=pl.CostEstimate(
+            flops=groups * heads * tokens * total * 256, bytes_accessed=groups * total * 512, transcendentals=0
+        ),
+        name="attention_stage",
+    )(lists, counts, q, marks, *(() if state is None else state), *pieces)
+
+
+def backward_kernel(group, lists, counts, q_ref, do_ref, o_ref, mark_ref, lse_ref, *refs):
+    *pieces, dq_ref, dkv_ref, dq_sum, dkv_sum, kv_ref, kt_ref, delta_ref, sems = refs
     block = pl.program_id(0)
-    heads, rows = q_ref.shape[1], q_ref.shape[2]
+    heads, rows = q_ref.shape[1] // (2 * HEAD_DIM), q_ref.shape[0]
     total = kv_ref.shape[0]
     stride = total // rows
     count = counts[block]
@@ -260,10 +371,11 @@
         lax.fori_loop(0, stride, flip, 0)
 
     dq_sum[...] = jnp.zeros(dq_sum.shape, F32)
+    products = stacked(do_ref).astype(F32) * stacked(o_ref).astype(F32)
+    delta_ref[...] = jnp.sum(products.T, axis=0, keepdims=True)
 
     def steps(start, n, masked):
-        q = q_ref[0].reshape(heads * rows, 2 * HEAD_DIM)
-        do = do_ref[0].reshape(heads * rows, 2 * HEAD_DIM)
+        q, do = stacked(q_ref), stacked(do_ref)
         offs = [pl.multiple_of(lists[block * stride + start + u] * rows, rows) for u in range(n)]
         kv = jnp.concatenate([kv_ref[pl.ds(k0, rows), :] for k0 in offs], axis=0)
         mark = jnp.concatenate([mark_ref[pl.ds(k0, rows), :] for k0 in offs], axis=0)
@@ -272,7 +384,7 @@
         if masked:
             scores = causal(scores, heads)
         chances = jnp.exp2(scores)
-        back = dg(kv, do, NT) - delta_ref[0, 0]
+        back = dg(kv, do, NT) - delta_ref[...]
         score_back = (chances * back).astype(BF16)
         only_q = jnp.where(left_half(q.shape), q, jnp.zeros_like(q))
         update = dg(score_back, only_q, NN) + dg(chances.astype(BF16), do, NN)
@@ -282,7 +394,8 @@
 
     steps(count, 1, True)
     cascade(count, UNROLL, lambda start, n: steps(start, n, False))
-    dq_ref[0] = (dq_sum[...] * HEAD_DIM**-0.5).T.astype(BF16).reshape(heads, rows, HEAD_DIM)
+    spread = jnp.concatenate([dq_sum[...] * HEAD_DIM**-0.5, jnp.zeros(dq_sum.shape, F32)], axis=0)
+    dq_ref[...] = beside(spread.T.astype(BF16), heads)
 
     @pl.when(block == pl.num_programs(0) - 1)
     def _():
@@ -290,26 +403,27 @@
         dkv_ref[...] = jnp.where(left_half(summed.shape), summed * (1.0 / LOG2E), summed).astype(BF16)
 
 
-def attention_backward(group, lists, counts, q, do, pieces, marks, lse, delta):
-    _, heads, tokens, wide = q.shape
+def attention_backward(group, lists, counts, q, do, o, pieces, marks, lse):
+    tokens, wide, heads = q.shape[0], 2 * HEAD_DIM, REPEAT
     total = marks.shape[0]
     blocks = counts.shape[0]
     rows = tokens // blocks
+    block = pl.BlockSpec((rows, heads * wide), lambda b, *_: (b, group))
     return pl.pallas_call(
         functools.partial(backward_kernel, group),
         grid_spec=pltpu.PrefetchScalarGridSpec(
             num_scalar_prefetch=2,
             grid=(blocks,),
             in_specs=[
-                pl.BlockSpec((1, heads, rows, wide), lambda b, *_: (group, 0, b, 0)),
-                pl.BlockSpec((1, heads, rows, wide), lambda b, *_: (group, 0, b, 0)),
+                block,
+                block,
+                block,
                 pl.BlockSpec((total, wide), lambda b, *_: (0, 0)),
-                pl.BlockSpec((1, 1, 1, heads * rows), lambda b, *_: (group, b, 0, 0)),
                 pl.BlockSpec((1, 1, 1, heads * rows), lambda b, *_: (group, b, 0, 0)),
                 *(pl.BlockSpec(memory_space=pl.ANY) for _ in pieces),
             ],
             out_specs=[
-                pl.BlockSpec((1, heads, rows, HEAD_DIM), lambda b, *_: (0, 0, b, 0)),
+                pl.BlockSpec((rows, heads * wide), lambda b, *_: (b, 0)),
                 pl.BlockSpec((total, wide), lambda b, *_: (0, 0)),
             ],
             scratch_shapes=[
@@ -317,17 +431,224 @@
                 pltpu.VMEM((total, wide), F32),
                 pltpu.VMEM((total, wide), BF16),
                 pltpu.VMEM((HEAD_DIM, total), BF16),
+                pltpu.VMEM((1, heads * rows), F32),
                 pltpu.SemaphoreType.DMA((len(pieces),)),
             ],
         ),
         out_shape=[
-            jax.ShapeDtypeStruct((1, heads, tokens, HEAD_DIM), BF16),
+            jax.ShapeDtypeStruct((tokens, heads * wide), BF16),
             jax.ShapeDtypeStruct((total, wide), BF16),
         ],
         compiler_params=pltpu.CompilerParams(vmem_limit_bytes=60 * 2**20),
         cost_estimate=pl.CostEstimate(flops=heads * tokens * total * 640, bytes_accessed=total * 1024, transcendentals=0),
         name="attention_backward",
-    )(lists, counts, q, do, marks, lse, delta, *pieces)
+    )(lists, counts, q, do, o, marks, lse, *pieces)
+
+
+def roll_half(value):
+    return pltpu.roll(value, HEAD_DIM, 1)
+
+
+def swap_quarters(value):
+    quarter = HEAD_DIM // 2
+    lane = lax.broadcasted_iota(jnp.int32, value.shape, 1)
+    first = lax.rem(lane, HEAD_DIM) < quarter
+    return jnp.where(first, pltpu.roll(value, value.shape[1] - quarter, 1), pltpu.roll(value, quarter, 1))
+
+
+def root_mean(value):
+    return lax.rsqrt(jnp.sum(value * value, axis=1, keepdims=True) / D + EPSILON)
+
+
+def project_kernel(x4_ref, w_ref, cos_ref, sin_ref, bars_ref, x_ref, xa_ref, full_ref, packed_ref, gains_ref, joint_ref):
+    own = x_ref.shape[0]
+    wide = 2 * HEAD_DIM
+    x = jnp.concatenate([x4_ref[r, :own, :] for r in range(x4_ref.shape[0])], axis=1)
+    gains = jnp.concatenate([x4_ref[r, own : own + 16, :] for r in range(x4_ref.shape[0])], axis=1).astype(F32)
+    x_ref[...] = x
+    gains_ref[...] = gains[:8]
+    value = x.astype(F32)
+    xa_ref[...] = (value * root_mean(value) * gains[0:1]).astype(BF16)
+    full_ref[...] = jnp.concatenate([w_ref[c] for c in range(w_ref.shape[0])], axis=1)
+    joint_ref[...] = dg(xa_ref[...], full_ref[...], NN).astype(BF16)
+    left = left_half((own, wide))
+    bars = bars_ref[...].astype(F32)
+    heads, pairs = HEADS // 2, KV_HEADS // 2
+
+    def part(i):
+        return joint_ref[:, i * wide : (i + 1) * wide].astype(F32)
+
+    def turned(i):
+        value = part(i)
+        return value * cos_ref[...] + swap_quarters(value) * sin_ref[...]
+
+    for i in range(HEADS // 2):
+        value = turned(i) * (LOG2E * HEAD_DIM**-0.5)
+        for j, head in ((2 * i, value), (2 * i + 1, roll_half(value))):
+            start = (j % heads) * wide
+            packed_ref[j // heads, :, start : start + wide] = jnp.where(left, head, bars).astype(BF16)
+    for i in range(KV_HEADS // 2):
+        key = turned(HEADS // 2 + i)
+        value = part(HEADS // 2 + KV_HEADS // 2 + i)
+        for j, both in (
+            (2 * i, jnp.where(left, key, roll_half(value))),
+            (2 * i + 1, jnp.where(left, roll_half(key), value)),
+        ):
+            start = heads * wide + (j % pairs) * wide
+            packed_ref[j // pairs, :, start : start + wide] = both.astype(BF16)
+
+
+def project_in(x4, weight, cosines, sines, bars):
+    own = cosines.shape[0]
+    shapes = [
+        jax.ShapeDtypeStruct((own, D), BF16),
+        jax.ShapeDtypeStruct((own, D), BF16),
+        jax.ShapeDtypeStruct((D, ATT + 2 * KEYS), BF16),
+        jax.ShapeDtypeStruct((2, own, ATT + KEYS), BF16),
+        jax.ShapeDtypeStruct((8, D), F32),
+    ]
+    return pl.pallas_call(
+        project_kernel,
+        out_shape=shapes,
+        scratch_shapes=[pltpu.VMEM((own, ATT + 2 * KEYS), BF16)],
+        compiler_params=pltpu.CompilerParams(vmem_limit_bytes=56 * 2**20),
+        cost_estimate=pl.CostEstimate(flops=2 * own * D * (ATT + 2 * KEYS), bytes_accessed=2**24, transcendentals=0),
+        name="project_in",
+    )(x4, weight, cosines, sines, bars)
+
+
+def output_kernel(width, o_ref, w_ref, x_ref, gains_ref, rows_ref, hidden_ref, normed_ref, full_ref):
+    wide = 2 * HEAD_DIM
+    heads = HEADS // 2
+    left = left_half((x_ref.shape[0], wide))
+    for i in range(HEADS // 2):
+        first, second = (
+            o_ref[j // heads, :, (j % heads) * wide : (j % heads + 1) * wide] for j in (2 * i, 2 * i + 1)
+        )
+        first = roll_half(first.astype(F32))
+        rows_ref[:, i * wide : (i + 1) * wide] = jnp.where(left, first, second.astype(F32)).astype(BF16)
+    full_ref[...] = jnp.concatenate([w_ref[c, :, :width] for c in range(w_ref.shape[0])], axis=1)
+    hidden = x_ref[...].astype(F32) + dg(rows_ref[...], full_ref[...], NT)
+    hidden_ref[...] = hidden
+    normed_ref[...] = (hidden * root_mean(hidden) * gains_ref[1:2]).astype(BF16)
+
+
+def project_out(o, late, x, gains, width, padded):
+    own = x.shape[0]
+    place = late.shape[2] // padded - 1
+    return pl.pallas_call(
+        functools.partial(output_kernel, width),
+        grid=(1,),
+        in_specs=[
+            pl.BlockSpec(o.shape, lambda i: (0, 0, 0)),
+            pl.BlockSpec((late.shape[0], D, padded), lambda i: (0, 0, place)),
+            pl.BlockSpec(x.shape, lambda i: (0, 0)),
+            pl.BlockSpec(gains.shape, lambda i: (0, 0)),
+        ],
+        out_specs=[pl.BlockSpec((own, D), lambda i: (0, 0))] * 3 + [pl.BlockSpec((D, ATT), lambda i: (0, 0))],
+        out_shape=[
+            jax.ShapeDtypeStruct((own, ATT), BF16),
+            jax.ShapeDtypeStruct((own, D), F32),
+            jax.ShapeDtypeStruct((own, D), BF16),
+            jax.ShapeDtypeStruct((D, ATT), BF16),
+        ],
+        compiler_params=pltpu.CompilerParams(vmem_limit_bytes=56 * 2**20),
+        cost_estimate=pl.CostEstimate(flops=2 * own * D * ATT, bytes_accessed=2**24, transcendentals=0),
+        name="project_out",
+    )(o, late, x, gains)
+
+
+def norm_back(upstream, value, gain):
+    scale = root_mean(value)
+    weighted = upstream * gain
+    inner = jnp.sum(weighted * value, axis=1, keepdims=True)
+    gain_back = jnp.sum(upstream * value * scale, axis=0, keepdims=True)
+    return scale * weighted - value * (scale * scale * scale * inner / D), gain_back
+
+
+def output_back_kernel(back_ref, hidden_ref, upstream_ref, gains_ref, full_ref, hidden_back_ref, low_ref, do_ref, sums_ref):
+    wide = 2 * HEAD_DIM
+    heads = HEADS // 2
+    part, sums = norm_back(back_ref[...], hidden_ref[...], gains_ref[1:2])
+    hidden_back = upstream_ref[...].astype(F32) + part
+    hidden_back_ref[...] = hidden_back
+    low_ref[...] = hidden_back.astype(BF16)
+    sums_ref[...] = jnp.broadcast_to(sums, sums_ref.shape)
+    attended_back = dg(low_ref[...], full_ref[...], NN)
+    left = left_half((low_ref.shape[0], wide))
+    for i in range(HEADS // 2):
+        value = attended_back[:, i * wide : (i + 1) * wide]
+        for j, head in ((2 * i, roll_half(value)), (2 * i + 1, value)):
+            start = (j % heads) * wide
+            do_ref[j // heads, :, start : start + wide] = jnp.where(left, 0.0, head).astype(BF16)
+
+
+def output_back(back, hidden, upstream, gains, full):
+    own = back.shape[0]
+    return pl.pallas_call(
+        output_back_kernel,
+        out_shape=[
+            jax.ShapeDtypeStruct((own, D), F32),
+            jax.ShapeDtypeStruct((own, D), BF16),
+            jax.ShapeDtypeStruct((2, own, ATT), BF16),
+            jax.ShapeDtypeStruct((8, D), F32),
+        ],
+        compiler_params=pltpu.CompilerParams(vmem_limit_bytes=56 * 2**20),
+        cost_estimate=pl.CostEstimate(flops=2 * own * D * ATT, bytes_accessed=2**24, transcendentals=0),
+        name="output_back",
+    )(back, hidden, upstream, gains, full)
+
+
+def joint_back_kernel(packed_ref, cos_ref, sin_ref, full_ref, x_ref, gains_ref, hidden_back_ref, joint_ref, out_ref, sums_ref):
+    wide = 2 * HEAD_DIM
+    heads, pairs = HEADS // 2, KV_HEADS // 2
+    left = left_half((x_ref.shape[0], wide))
+
+    def queries(j):
+        return packed_ref[j // heads, :, (j % heads) * wide : (j % heads + 1) * wide].astype(F32)
+
+    def both(j):
+        start = (heads + j % pairs) * wide
+        return packed_ref[j // pairs, :, start : start + wide].astype(F32)
+
+    def store(i, value):
+        joint_ref[:, i * wide : (i + 1) * wide] = value.astype(BF16)
+
+    def back(value):
+        return value * cos_ref[...] - swap_quarters(value) * sin_ref[...]
+
+    for i in range(HEADS // 2):
+        store(i, back(jnp.where(left, queries(2 * i), roll_half(queries(2 * i + 1)))))
+    for i in range(KV_HEADS // 2):
+        first, second = both(2 * i), both(2 * i + 1)
+        store(HEADS // 2 + i, back(jnp.where(left, first, roll_half(second))))
+        store(HEADS // 2 + KV_HEADS // 2 + i, jnp.where(left, roll_half(first), second))
+    upstream = dg(joint_ref[...], full_ref[...], NT)
+    part, sums = norm_back(upstream, x_ref[...].astype(F32), gains_ref[0:1])
+    total = (hidden_back_ref[...] + part).astype(BF16)
+    features = out_ref.shape[2]
+    for r in range(out_ref.shape[0]):
+        out_ref[r] = total[:, r * features : (r + 1) * features]
+    sums_ref[...] = jnp.broadcast_to(sums, sums_ref.shape)
+
+
+def joint_back(packed, cosines, sines, full, x, gains, hidden_back, rows):
+    own = x.shape[0]
+    return pl.pallas_call(
+        joint_back_kernel,
+        out_shape=[
+            jax.ShapeDtypeStruct((own, ATT + 2 * KEYS), BF16),
+            jax.ShapeDtypeStruct((rows, own, D // rows), BF16),
+            jax.ShapeDtypeStruct((8, D), F32),
+        ],
+        compiler_params=pltpu.CompilerParams(vmem_limit_bytes=56 * 2**20),
+        cost_estimate=pl.CostEstimate(flops=2 * own * D * (ATT + 2 * KEYS), bytes_accessed=2**24, transcendentals=0),
+        name="joint_back",
+    )(packed, cosines, sines, full, x, gains, hidden_back)
+
+
+def feed_part(width):
+    return width // 2 if width % 256 == 0 else width
 
 
 def feed_kernel(normed_ref, back_ref, gate_ref, up_ref, down_ref, mixed_ref, gate_back_ref, up_back_ref, out_ref, normed_back_ref):
@@ -351,18 +672,18 @@
     normed_back_ref[...] += dg(gate_back, gate_ref[0], NT) + dg(up_back, up_ref[0], NT)
 
 
-def feed_forward(normed, back, pair, down):
+def feed_forward(normed, back, late, width):
     tokens = normed.shape[0]
-    columns, _, width = down.shape
-    parts = 2 if width % 256 == 0 else 1
-    part = width // parts
+    columns = late.shape[0]
+    part = feed_part(width)
+    parts = width // part
     whole = pl.BlockSpec((tokens, D), lambda c, j: (0, 0))
-    block = pl.BlockSpec((1, D, part), lambda c, j: (c, 0, j))
+    blocks = [pl.BlockSpec((1, D, part), lambda c, j, k=k: (c, 0, k * parts + j)) for k in range(3)]
     out = pl.BlockSpec((tokens, part), lambda c, j: (0, c * parts + j))
     return pl.pallas_call(
         feed_kernel,
         grid=(columns, parts),
-        in_specs=[whole, whole, block, pl.BlockSpec((1, D, part), lambda c, j: (c, 0, j + parts)), block],
+        in_specs=[whole, whole, *blocks],
         out_specs=[out, out, out, whole, whole],
         out_shape=[jax.ShapeDtypeStruct((tokens, columns * width), BF16)] * 3 + [jax.ShapeDtypeStruct((tokens, D), F32)] * 2,
         compiler_params=pltpu.CompilerParams(vmem_limit_bytes=56 * 2**20),
@@ -370,14 +691,18 @@
             flops=12 * tokens * D * columns * width, bytes_accessed=6 * D * columns * width, transcendentals=0
         ),
         name="feed_forward",
-    )(normed, back, pair, pair, down)
-
-
-def gradient_kernel(rights, summed, order, left_ref, *refs):
+    )(normed, back, late, late, late)
+
+
+def gradient_kernel(rights, summed, joined, order, left_ref, *refs):
     right_refs, refs = refs[:rights], refs[rights:]
     sums_ref = refs[0] if summed else None
     refs = refs[1:] if summed else refs
-    (mine_ref, other_ref), (lefts, *held) = refs[:2], refs[2:]
+    if joined:
+        both_ref, lefts, *held = refs
+        mine_ref, other_ref = both_ref.at[:, 0], both_ref.at[:, 1]
+    else:
+        mine_ref, other_ref, lefts, *held = refs
     step = pl.program_id(0)
     features = lefts.shape[2]
 
@@ -405,7 +730,7 @@
             target[0, features:, :] = sums_ref[r].astype(BF16)
 
 
-def gradient_parts(order, left, *rights, sums=None):
+def gradient_parts(order, left, *rights, sums=None, joined=False):
     tokens = left.shape[0]
     steps = (order.shape[0] - 1) // 2
     columns = steps // 2
@@ -418,8 +743,12 @@
         right_spec = pl.BlockSpec(rights[0].shape, lambda s, order: (0, 0))
     wide = width * len(rights)
     tall = features if sums is None else features + 16
-    out = pl.BlockSpec((1, tall, wide), lambda s, order: (s, 0, 0))
-    shape = jax.ShapeDtypeStruct((steps, tall, wide), BF16)
+    if joined:
+        outs = [pl.BlockSpec((1, 2, tall, wide), lambda s, order: (s, 0, 0, 0))]
+        shapes = [jax.ShapeDtypeStruct((steps, 2, tall, wide), BF16)]
+    else:
+        outs = [pl.BlockSpec((1, tall, wide), lambda s, order: (s, 0, 0))] * 2
+        shapes = [jax.ShapeDtypeStruct((steps, tall, wide), BF16)] * 2
     held = [] if aligned else [pltpu.VMEM((columns, tokens, width), BF16)]
     more, more_specs = [], []
     if sums is not None:
@@ -427,7 +756,7 @@
         more = [jnp.pad(sums.reshape(4, lines, -1), ((0, 0), (0, 16 - lines), (0, wide - features // lines)))]
         more_specs = [pl.BlockSpec((4, 16, wide), lambda s, order: (0, 0, 0))]
     return pl.pallas_call(
-        functools.partial(gradient_kernel, len(rights), sums is not None),
+        functools.partial(gradient_kernel, len(rights), sums is not None, joined),
         grid_spec=pltpu.PrefetchScalarGridSpec(
             num_scalar_prefetch=1,
             grid=(steps,),
@@ -436,10 +765,10 @@
                 *(right_spec for _ in rights),
                 *more_specs,
             ],
-            out_specs=[out, out],
+            out_specs=outs,
             scratch_shapes=[pltpu.VMEM((4, tokens, features), BF16), *held],
         ),
-        out_shape=[shape, shape],
+        out_shape=shapes,
         compiler_params=pltpu.CompilerParams(vmem_limit_bytes=56 * 2**20),
         cost_estimate=pl.CostEstimate(
             flops=2 * tokens * left.shape[1] * wide * columns, bytes_accessed=2 * left.shape[1] * wide * columns, transcendentals=0
@@ -448,23 +777,6 @@
     )(order, left, *rights, *more)
 
 
-def norm_apply(value, gain):
-    scale_rows = lax.rsqrt(jnp.sum(value * value, axis=1) / D + EPSILON)
-    normed = (value * scale_rows[:, None] * gain[None, :]).astype(BF16)
-    return (normed, scale_rows)
-
-
-def norm_back(upstream, value, scale_rows, gain):
-    weighted = upstream * gain[None, :]
-    inner = jnp.sum(weighted * value, axis=1)
-    value_back = (
-        scale_rows[:, None] * weighted
-        - value * (scale_rows * scale_rows * scale_rows * inner / D)[:, None]
-    )
-    gain_back = jnp.sum(upstream * value * scale_rows[:, None], axis=0)
-    return (value_back, gain_back)
-
-
 ROW = ("high", "core")
 ALL_ROW = ("high", "core", "col")
 ALL_COL = ("col", "high", "core")
@@ -477,53 +789,47 @@
     return ahead, [(b, a) for a, b in ahead]
 
 
-def ring_gather(value, columns):
-    ahead, behind = ring_steps(columns)
-    count = 2 * columns
-    to_next, to_last = value, value
-    fronts, backs = [], []
-    for _ in range(count // 2 - 1):
-        to_next = lax.ppermute(to_next, RING, ahead)
-        to_last = lax.ppermute(to_last, RING, behind)
-        fronts.append(to_next)
-        backs.append(to_last)
-    half = value.shape[0] // 2
-    upper = lax.ppermute(to_next[:half], RING, ahead)
-    lower = lax.ppermute(to_last[half:], RING, behind)
-    return [value, *backs, upper, lower, *reversed(fronts)]
-
-
 class RingScatter:
     def __init__(self, part, columns):
         self.part, (self.ahead, self.behind), self.count = part, ring_steps(columns), 2 * columns
         self.left = self.count // 2
-        self.send(part(self.left, 0), part(self.left, 1))
-
-    def send(self, out, back):
-        out, back = lax.optimization_barrier((out.astype(BF16), back.astype(BF16)))
+        self.arrived = None
+        self.ready = (part(self.left, 0).astype(BF16), part(self.left, 1).astype(BF16))
+
+    def launch(self):
+        out, back = self.ready
         self.arrived = (lax.ppermute(out, RING, self.ahead), lax.ppermute(back, RING, self.behind))
+        self.ready = None
         self.left -= 1
 
-    def step(self):
+    def prepare(self):
         out, back = self.part(self.left, None), self.part(self.count - self.left, None)
         front, rear = (v.astype(F32) for v in self.arrived)
-        if front.shape[0] == out.shape[0]:
-            self.send(out + front, back + rear)
+        half = front.shape[0]
+        if half == out.shape[0]:
+            out, back = out + front, back + rear
         else:
-            half = front.shape[0]
             out = jnp.concatenate([out[:half] + front, out[half:]], axis=0)
-            self.send(out, jnp.concatenate([back[:half], back[half:] + rear], axis=0))
+            back = jnp.concatenate([back[:half], back[half:] + rear], axis=0)
+        self.ready = (out.astype(BF16), back.astype(BF16))
 
     def finish(self):
-        while self.left:
-            self.step()
+        while self.left or self.ready:
+            if self.ready is None:
+                self.prepare()
+            self.ready = lax.optimization_barrier(self.ready)
+            self.launch()
         return self.part(0, None) + self.arrived[0].astype(F32) + self.arrived[1].astype(F32)
 
 
-def after(value, rings):
-    value, arrived = lax.optimization_barrier((value, [r.arrived for r in rings]))
-    for ring, a in zip(rings, arrived, strict=True):
-        ring.arrived = a
+def depart(value, rings):
+    for ring in rings:
+        if ring.ready is None:
+            ring.prepare()
+    value, ready = lax.optimization_barrier((value, [ring.ready for ring in rings]))
+    for ring, r in zip(rings, ready, strict=True):
+        ring.ready = r
+        ring.launch()
     return value
 
 
@@ -532,6 +838,10 @@
         return value
     middle = value.shape[0] // 2
     return value[middle:] if half else value[:middle]
+
+
+def scatter(value, axes):
+    return lax.psum_scatter(value, axes, scatter_dimension=0, tiled=True)
 
 
 def gather(value, axes):
@@ -579,57 +889,81 @@
     lists, counts = block_lists(first, key_index, block, held, tables)
     key_hot = segment_hot(key_index, tables).astype(F32)
     marks = jnp.pad(key_hot, ((0, 0), (HEAD_DIM, HEAD_DIM - key_hot.shape[1]))).astype(BF16)
-    held_hot = segment_hot(first + jnp.arange(held, dtype=jnp.int32), tables).astype(F32)
-    reach = jnp.sum(held_hot[:, :, None] * tables[2][None], axis=1)
-    bars = jnp.pad((reach - 1.0) * BIG, ((0, 0), (0, HEAD_DIM - reach.shape[1]))).astype(BF16)
-
-    def to_tokens(value):
-        return lax.all_to_all(value, ROW, split_axis=0, concat_axis=1, tiled=True)
+    own_hot = segment_hot(index, tables).astype(F32)
+    reach = jnp.sum(own_hot[:, :, None] * tables[2][None], axis=1)
+    bars = jnp.pad((reach - 1.0) * BIG, ((0, 0), (HEAD_DIM, HEAD_DIM - reach.shape[1]))).astype(BF16)
+
+    def exchange(value, axes):
+        return lax.all_to_all(value, axes, split_axis=0, concat_axis=0, tiled=True)
 
     def to_features(value):
-        return lax.all_to_all(value, ROW, split_axis=1, concat_axis=0, tiled=True)
-
-    def swap_cores(value):
-        return lax.all_to_all(value, "core", split_axis=0, concat_axis=0, tiled=True)
-
-    joint_full = gather(joint_weight, ALL_COL).reshape(columns, D, -1)
-    joint_full = joint_full.transpose(1, 0, 2).reshape(D, -1)
+        value = lax.all_to_all(value.reshape(own, rows, -1).transpose(1, 0, 2), ROW, split_axis=0, concat_axis=0)
+        return value.reshape(rows * own, -1)
+
+    joint_blocks = gather(joint_weight, ALL_COL).reshape(columns, D, -1)
     gains = jnp.broadcast_to(jnp.stack([attention_gain, feed_gain])[None], (rows, 2, attention_gain.shape[0]))
     extended = jnp.concatenate([tokens.reshape(rows, own, -1), jnp.pad(gains, ((0, 0), (0, 14), (0, 0)))], axis=1)
-    extended = to_tokens(extended.reshape(rows * (own + 16), -1))
-    stream = extended[:own].astype(F32)
-    gain_one = extended[own].astype(F32)
-    gain_two = extended[own + 1].astype(F32)
-
-    normed_one, scale_one = norm_apply(stream, gain_one)
-    joint = jnp.dot(normed_one, joint_full, preferred_element_type=F32).astype(BF16)
-    raw = joint.astype(F32)
-    queries = turn(raw[:, :ATT].reshape(own, HEADS, HEAD_DIM), cosines, sines)
-    queries = (queries * (LOG2E * HEAD_DIM**-0.5)).astype(BF16).reshape(own, cores, -1)
-    keys = turn(raw[:, ATT : ATT + KEYS].reshape(own, KV_HEADS, HEAD_DIM), cosines, sines).astype(BF16)
-    values = joint[:, ATT + KEYS :].reshape(own, KV_HEADS, HEAD_DIM)
-    pairs = jnp.concatenate([keys, values], axis=2).reshape(own, cores, -1)
-    packed = jnp.concatenate([queries, pairs], axis=2).transpose(1, 0, 2)
-    packed = swap_cores(packed).reshape(held, -1)
-    wide = groups * REPEAT * HEAD_DIM
-    pieces = ring_gather(packed[:, wide:], columns)
-    queries = packed[:, :wide].reshape(held, groups, REPEAT, HEAD_DIM).transpose(1, 2, 0, 3)
-    queries = jnp.concatenate([queries, jnp.broadcast_to(bars, queries.shape)], axis=3)
-    attended, lse = attention_forward(lists, counts, queries, pieces, marks)
-    by_core = attended.reshape(groups * REPEAT, cores, own, HEAD_DIM).transpose(1, 2, 0, 3)
-    attended_rows = swap_cores(by_core.reshape(cores, own, -1)).transpose(1, 0, 2).reshape(own, ATT)
-
-    output_full = gather(output_weight, ALL_ROW).reshape(rows, ATT, -1)
-    output_full = output_full.transpose(1, 0, 2).reshape(ATT, D)
-    pair_full = gather(jnp.concatenate([gate_weight, up_weight], axis=1), ALL_COL).reshape(columns, D, -1)
-    down_full = gather(down_weight.T, ALL_COL).reshape(columns, D, -1)
-    upstream = to_tokens(cotangent)
-    hidden = stream + jnp.dot(attended_rows, output_full, preferred_element_type=F32)
-    normed_two, scale_two = norm_apply(hidden, gain_two)
-    mixed, gate_back, up_back, feed_out, normed_two_back = feed_forward(normed_two, upstream, pair_full, down_full)
+    extended = exchange(extended, ROW)
+
+    x, normed_one, joint_full, packed, gains = project_in(extended, joint_blocks, cosines, sines, bars)
+    packed = exchange(packed, "core").reshape(held, -1)
+    wide = groups * REPEAT * 2 * HEAD_DIM
+    pieces = []
+    state = None
+    ahead, behind = ring_steps(columns)
+    value = packed[:, wide:]
+    to_next, to_last = lax.ppermute(value, RING, ahead), lax.ppermute(value, RING, behind)
+    fronts, backs = [], []
+
+    def attend(state, places, some, ends):
+        keys_here = jnp.concatenate([key_index[i * held // 2 : j * held // 2] for i, j in places])
+        marks_here = jnp.concatenate([marks[i * held // 2 : j * held // 2] for i, j in places])
+        lists_here, counts_here = block_lists(first, keys_here, block, held, tables)
+        return tuple(attention_stage(lists_here, counts_here, packed, some, marks_here, state, ends))
+
+    middle = held // 2
+    for step in range(1, columns):
+        fronts.append(to_next)
+        backs.append(to_last)
+        if step < columns - 1:
+            further = (lax.ppermute(to_next, RING, ahead), lax.ppermute(to_last, RING, behind))
+        else:
+            further = (lax.ppermute(to_next[:middle], RING, ahead), lax.ppermute(to_last[middle:], RING, behind))
+        far = 2 * (2 * columns - step)
+        places, some = [(2 * step, 2 * step + 2), (far, far + 2)], [to_last, to_next]
+        if step == 1:
+            places, some = [(0, 2), *places], [value, *some]
+        state = attend(state, places, some, False)
+        state, further = lax.optimization_barrier((state, further))
+        to_next, to_last = further
+    pieces = [value, *backs, to_next, to_last, *reversed(fronts)]
+    cotangent, to_next = lax.optimization_barrier((cotangent, to_next))
+    state = attend(state, [(2 * columns, 2 * columns + 2)], [to_next, to_last], True)
+    attended, lse = lax.cond(
+        jnp.any(state[1] != state[1]),
+        lambda: tuple(attention_forward(lists, counts, packed, pieces, marks)),
+        lambda: tuple(state),
+    )
+    attended_rows = exchange(attended.reshape(cores, own, -1), "core")
+
+    width = gate_weight.shape[1]
+    part = feed_part(width)
+    padding = jnp.zeros((output_weight.shape[1], -output_weight.shape[0] % part), BF16)
+    late = jnp.concatenate([gate_weight, up_weight, down_weight.T, output_weight.T, padding], axis=1)
+    late = gather(late, ALL_COL).reshape(columns, D, -1)
+    upstream = exchange(cotangent.reshape(rows, own, -1), ROW).transpose(1, 0, 2).reshape(own, D)
+    attended_rows, hidden, normed_two, output_full = project_out(attended_rows, late, x, gains, ATT // columns, late.shape[2] - 3 * width)
+    mixed, gate_back, up_back, feed_out, normed_two_back = feed_forward(normed_two, upstream, late, width)
     layer_output = to_features((hidden + feed_out).astype(BF16))
 
+    steps = jnp.arange(2 * columns, dtype=jnp.int32)
+    plain = jnp.concatenate([steps // 2, steps % 2, jnp.zeros((1,), jnp.int32)])
+
     def scatter_gradient(left, *rights, sums=None):
+        [parts] = gradient_parts(plain, left, *rights, sums=sums, joined=True)
+        return scatter(parts.reshape(-1, parts.shape[3]), ALL_COL).astype(F32)
+
+    def ring_gradient(left, *rights, sums=None):
         mine, other = gradient_parts(order, left, *rights, sums=sums)
         other = lax.ppermute(other, "core", [(0, 1), (1, 0)])
 
@@ -638,59 +972,25 @@
 
         return RingScatter(part, columns)
 
-    down_ring = scatter_gradient(upstream, mixed)
-    pair_ring = scatter_gradient(normed_two, gate_back, up_back)
-    hidden_part, gain_two_part = norm_back(normed_two_back, hidden, scale_two, gain_two)
-    hidden_back = upstream.astype(F32) + hidden_part
-    hidden_low = hidden_back.astype(BF16)
-    attended_back = dg(hidden_low, output_full, NT).astype(BF16)
-    output_ring = scatter_gradient(hidden_low, attended_rows, sums=gain_two_part)
-
-    heads_back = swap_cores(attended_back.reshape(own, cores, -1).transpose(1, 0, 2)).reshape(held, -1)
-    heads_back = heads_back.reshape(held, groups, REPEAT, HEAD_DIM).transpose(1, 2, 0, 3)
-    delta = jnp.sum(heads_back.astype(F32) * attended.astype(F32), axis=3)
-    delta = delta.reshape(groups, REPEAT, -1, block).transpose(0, 2, 1, 3)
-    delta = delta.reshape(groups, -1, 1, REPEAT * block)
-    heads_back = jnp.pad(heads_back, ((0, 0), (0, 0), (0, 0), (HEAD_DIM, 0)))
+    down_gradient = scatter_gradient(upstream, mixed).T
+    pair_gradient = scatter_gradient(normed_two, gate_back, up_back)
+    hidden_back, hidden_low, heads_back, gain_two_part = output_back(normed_two_back, hidden, upstream, gains, output_full)
+    output_summed = scatter_gradient(hidden_low, attended_rows, sums=gain_two_part[0])
+
+    heads_back = exchange(heads_back, "core").reshape(held, -1)
     query_backs, pair_rings = [], []
-    down_ring.step()
-    down_ring.step()
     for g in range(groups):
-        if g == 0:
-            heads_back = after(heads_back, [down_ring, pair_ring])
-            down_ring.step()
-            pair_ring.step()
-        else:
-            rings = [pair_ring, output_ring, *pair_rings] + ([down_ring] if g == 1 else [])
-            heads_back = after(heads_back, rings)
-            for ring in (pair_ring, output_ring, *pair_rings):
-                if ring.left and (ring is not pair_ring or g < 2):
-                    ring.step()
-        query_back, pair_back = attention_backward(g, lists, counts, queries, heads_back, pieces, marks, lse, delta)
+        heads_back = depart(heads_back, pair_rings)
+        query_back, pair_back = attention_backward(g, lists, counts, packed, heads_back, attended, pieces, marks, lse)
         pair_back = pair_back.reshape(2 * columns, held, -1)
         query_backs.append(query_back)
         pair_rings.append(RingScatter(lambda s, half, v=pair_back: halves(v[s], half).astype(F32), columns))
-    pair_backs = [ring.finish() for ring in pair_rings]
-    pair_backs[0] = after(pair_backs[0], [pair_ring, output_ring])
-    held_pairs = jnp.concatenate([p.astype(BF16) for p in pair_backs], axis=1)
-    held_pairs = after(held_pairs, [pair_ring, output_ring])
-    query_back = jnp.concatenate(query_backs, axis=0)
-    query_back = query_back.reshape(groups * REPEAT, held, HEAD_DIM).transpose(1, 0, 2).reshape(held, -1)
-    packed = jnp.concatenate([query_back, held_pairs], axis=1).reshape(cores, own, -1)
-    packed = swap_cores(packed)
-    query_back = packed[:, :, :wide].transpose(1, 0, 2).reshape(own, HEADS, HEAD_DIM)
-    pair_back = packed[:, :, wide:].transpose(1, 0, 2).reshape(own, KV_HEADS, 2 * HEAD_DIM)
-    query_back = turn(query_back.astype(F32), cosines, -sines).astype(BF16).reshape(own, ATT)
-    key_back = turn(pair_back[:, :, :HEAD_DIM].astype(F32), cosines, -sines).astype(BF16).reshape(own, KEYS)
-    value_back = pair_back[:, :, HEAD_DIM:].reshape(own, KEYS)
-    joint_back = jnp.concatenate([query_back, key_back, value_back], axis=1)
-    normed_one_back = dg(joint_back, joint_full, NT)
-    stream_part, gain_one_part = norm_back(normed_one_back, stream, scale_one, gain_one)
-    joint_ring = scatter_gradient(normed_one, joint_back, sums=gain_one_part)
-    input_gradient = to_features((hidden_back + stream_part).astype(BF16)).astype(F32)
-    down_gradient = down_ring.finish().T
-    pair_gradient = pair_ring.finish()
-    output_summed = output_ring.finish()
+    held_pairs = jnp.concatenate([ring.finish().astype(BF16) for ring in pair_rings], axis=1)
+    back = jnp.concatenate([*query_backs, held_pairs], axis=1).reshape(cores, own, -1)
+    back = exchange(back, "core")
+    joint_low, input_part, gain_one_part = joint_back(back, cosines, sines, joint_full, x, gains, hidden_back, rows)
+    joint_ring = ring_gradient(normed_one, joint_low, sums=gain_one_part[0])
+    input_gradient = exchange(input_part, ROW).reshape(rows * own, -1).astype(F32)
     joint_summed = joint_ring.finish()
     features = D // rows
 
@@ -698,7 +998,6 @@
         lines = -(-features // summed.shape[1])
         return summed[features : features + lines, : features // lines].reshape(-1)
 
-    width = gate_weight.shape[1]
     return (
         layer_output,
         input_gradient,

time: 1050 us -> 888 us (0.85)
  local copies, waits for them, and re-layouts: 151 us -> 66.5 us
  other arithmetic: 117 us -> 39.2 us
  Pallas kernels: 190 us -> 254 us
  starting transfers between devices: 253 us -> 229 us
  matrix products: 22.5 us -> 0 us
  waiting for transfers between devices: 264 us -> 247 us
    pallas_call x1 -> x8, Pallas kernels: 36.7 us -> 101 us  [the longest x4 60.7 us: attention_stage(): pl.pallas_call(functools.partial(stage_kernel, state is None, ends), grid...]
    convert_element_type x30 -> x12, other arithmetic: 47.3 us -> 9.21 us  [the longest x8 5.13 us: prepare(): self.ready = (out.astype(BF16), back.astype(BF16))]
    all_gather x4 -> x2, waiting for transfers between devices: 51.2 us -> 17.9 us  [gather(): return lax.all_gather(value, axes, axis=0, tiled=True)]
    ppermute x68 -> x41, starting transfers between devices: 237 us -> 209 us  [the longest x16 174 us: launch(): lax.ppermute(out, RING, self.ahead)]
    reshape x10 -> x3, local copies, waits for them, and re-layouts: 32.5 us -> 6.18 us  [the longest x1 3.65 us: per_device(): exchange(cotangent.reshape(rows, own, -1), ROW).transpose(1, 0, 2)]
    dot_general x4 -> x0, matrix products: 22.5 us -> none  [the longest x2 13.9 us: dg(): return lax.dot_general(a, b, dims, preferred_element_type=F32)]
    concatenate x23 -> x15, other arithmetic: 27.3 us -> 6.56 us  [the longest x1 2.76 us: rotary_tables(): jnp.concatenate([cosines] * 4, axis=1)]
    convert_element_type x8 -> x1, local copies, waits for them, and re-layouts: 20.1 us -> 1.97 us  [per_device(): exchange(input_part, ROW).reshape(rows * own, -1).astype(F32)]
  transfers between devices with their start and end apart: 76 -> 51, of which waited for: 33 -> 30; matrix products, arithmetic and copies ran while one was open for 24% -> 10% of each run, Pallas kernels for 9% -> 20%
where the time goes in v3:
time: 888 us; the launch traced here: 875 us
  Pallas kernels  254 us (29%)
  waiting for transfers between devices  247 us (28%)
  starting transfers between devices  229 us (26%)
  local copies, waits for them, and re-layouts  66.5 us (7%)
  other arithmetic  39.2 us (4%)
  blocking collectives  23.5 us (3%)
  between operations  15.8 us (2%)
    ppermute x16, starting transfers between devices, launch(): lax.ppermute(out, RING, self.ahead)  174 us
    pallas_call x4, Pallas kernels, attention_stage(): pl.pallas_call(functools.partial(stage_kernel, state is None, ends), grid...  60.7 us
    ppermute x16, waiting for transfers between devices, launch(): lax.ppermute(out, RING, self.ahead)  59.4 us
    pallas_call x3, Pallas kernels, attention_backward(): pl.pallas_call(functools.partial(backward_kernel, group), grid_spec=pltpu...  53.7 us
    pallas_call x4, Pallas kernels, gradient_parts(): pl.pallas_call(functools.partial(gradient_kernel, len(rights), sums is no...  52.3 us
    pallas_call x1, Pallas kernels, feed_forward(): pl.pallas_call(feed_kernel, grid=(columns, parts), in_specs=[whole, whole...  47.7 us
    ppermute x16, waiting for transfers between devices, launch(): lax.ppermute(back, RING, self.behind)  43.4 us
    ppermute x1, waiting for transfers between devices, per_device(): lax.ppermute(value, RING, ahead)  40.7 us
  transfers between devices with their start and end apart: 51, of which 30 were waited for; matrix products, arithmetic and copies ran while one was open for 10% of the time, Pallas kernels for 20%

profile of v3, /device:TPU:0, one launch (start us, length us, event | category | flops | bytes accessed | tf_op | source)
XLA Modules:
  0.0 875.3 jit_solution(4292107940578010708)
XLA Ops:
  9.2 3.7 concatenate.80
  16.0 4.5 all-to-all-start
  26.7 4.7 compare_and_fusion
  34.5 2.8 pad_maximum_fusion.3
  38.5 9.6 %all-to-all-done = bf16[4,656,288]{1,2,0:T(8,128)(2,1)} async-done(((bf16[4,656,288]{1,2,0:T(8,128)(2,1)}), bf16[4,656,288]{1,2,0:T(8,128)(2,1)}, u32[]{:S(2)}, u32[]{:S(2)}) %all-to-all-start) | async-done | bytes 1511456 | tf_op jit(solution)/shard_map/all_to_all | solution.py:897
  48.1 3.9 copy.87.x4_ref
  52.0 17.8 %all-gather.3.cloned.1.call-done = bf16[4608,480]{1,0:T(8,128)(2,1)} async-done(((bf16[288,480]{1,0:T(8,128)(2,1)}), bf16[4608,480]{1,0:T(8,128)(2,1)}) %all-gather.3.cloned.1.call-update) | async-done | bytes 4423696 | tf_op jit(solution)/shard_map/all_gather | solution.py:848
  69.9 9.9 %project_in.1 = (bf16[640,1152]{1,0:T(8,128)(2,1)}, bf16[640,1152]{1,0:T(8,128)(2,1)}, bf16[1152,1920]{1,0:T(8,128)(2,1)}, bf16[2,640,1536]{2,1,0:T(8,128)(2,1)}, f32[8,1152]{1,0:T(8,128)}) custom-call(bf16[4,656,288]{2,1,0:T(8,128)(2,1)} %copy.87.x4_ref, bf16[4,1152,480]{2,1,0:T(8,128)(2,1)} %bitcast.103, f32[640,128]{1,0:T(8,128)} %get-tuple-element.343.cos_ref, ...), custom_call_target="tpu_custom_call" | custom-call | flops 2831155200 | bytes 16777216 | tf_op jit(solution)/shard_map/project_in/pallas_call | solution.py:510
  79.7 8.2 all_to_all.40
  94.2 40.7 %collective-permute-done.1.refs_2_.refs_8_ = bf16[1280,384]{1,0:T(8,128)(2,1)} collective-permute-done((bf16[1280,384]{1,0:T(8,128)(2,1)}, bf16[1280,384]{1,0:T(8,128)(2,1)}, u32[]{:S(2)}, u32[]{:S(2)}) %collective-permute-start.1) | collective-permute-done | bytes 983072 | tf_op jit(solution)/shard_map/ppermute | solution.py:915
  137.1 24.4 %attention_stage.4 = (f32[3,5,80,768]{3,2,1,0:T(8,128)S(1)}, f32[3,5,1,768]{3,2,1,0:T(1,128)S(1)}) custom-call(s32[75]{0:T(128)S(1)} %select_n.134.lists, s32[5]{0:T(128)S(1)} %get-tuple-element.269.counts, bf16[1280,1536]{1,0:T(8,128)(2,1)S(1)} %bitcast.88, bf16[3840,128]{1,0:T(8,128)(2,1)S(1)} %pad_maximum_fusion.mark_ref, ...), custom_call_target="tpu_custom_call" | custom-call | flops 11324620800 | bytes 5898240 | tf_op jit(solution)/shard_map/attention_stage/pallas_call | solution.py:323
  163.4 16.9 %collective-permute-done.2.refs_3_.refs_7_ = bf16[1280,384]{1,0:T(8,128)(2,1)} collective-permute-done((bf16[1280,384]{1,0:T(8,128)(2,1)}, bf16[1280,384]{1,0:T(8,128)(2,1)}, u32[]{:S(2)}, u32[]{:S(2)}) %collective-permute-start.2) | collective-permute-done | bytes 983072 | tf_op jit(solution)/shard_map/ppermute | solution.py:929
  187.1 13.8 %attention_stage.5 = (f32[3,5,80,768]{3,2,1,0:T(8,128)S(1)}, f32[3,5,1,768]{3,2,1,0:T(1,128)S(1)}) custom-call(s32[50]{0:T(128)S(1)} %select_n.130.lists, s32[5]{0:T(128)S(1)} %get-tuple-element.332.counts, bf16[1280,1536]{1,0:T(8,128)(2,1)} %bitcast.82, bf16[2560,128]{1,0:T(8,128)(2,1)S(1)} %get-tuple-element.346.mark_ref, f32[3,5,80,768]{3,2,1,0:T(8,128)S(1)} %copy-done.3, ...), custom_call_target="tpu_custom_call" | custom-call | flops 7549747200 | bytes 3932160 | tf_op jit(solution)/shard_map/attention_stage/pallas_call | solution.py:323
  200.9 26.0 %collective-permute-done.5.refs_2_.refs_3_ = bf16[1280,384]{1,0:T(8,128)(2,1)S(1)} collective-permute-done((bf16[1280,384]{1,0:T(8,128)(2,1)}, bf16[1280,384]{1,0:T(8,128)(2,1)S(1)}, u32[]{:S(2)}, u32[]{:S(2)}) %collective-permute-start.5) | collective-permute-done | bytes 983072 | tf_op jit(solution)/shard_map/ppermute | solution.py:929
  230.6 7.5 attention_stage.6
  240.1 11.9 %collective-permute-done.6.refs_2_.refs_4_ = bf16[640,384]{1,0:T(8,128)(2,1)S(1)} collective-permute-done((bf16[640,384]{1,0:T(8,128)(2,1)S(1)}, bf16[640,384]{1,0:T(8,128)(2,1)S(1)}, u32[]{:S(2)}, u32[]{:S(2)}) %collective-permute-start.6) | collective-permute-done | bytes 491552 | tf_op jit(solution)/shard_map/ppermute | solution.py:931
  254.7 4.0 all-to-all-start.3
  261.9 15.0 %attention_stage.7 = (bf16[1280,1152]{1,0:T(8,128)(2,1)}, f32[3,5,1,768]{3,2,1,0:T(1,128)S(1)}) custom-call(s32[25]{0:T(128)S(1)} %select_n.120.lists, s32[5]{0:T(128)S(1)} %get-tuple-element.277.counts, bf16[1280,1536]{1,0:T(8,128)(2,1)} %bitcast.83, bf16[1280,128]{1,0:T(8,128)(2,1)S(1)} %get-tuple-element.322.mark_ref, f32[3,5,80,768]{3,2,1,0:T(8,128)S(1)} %copy-done.1, ...), custom_call_target="tpu_custom_call" | custom-call | flops 3774873600 | bytes 1966080 | tf_op jit(solution)/shard_map/attention_stage/pallas_call | solution.py:323
  278.3 6.0 all-to-all-done.3
  285.5 3.9 all-to-all-start.2
  289.6 3.6 copy.92.back_ref.upstream_ref.left_ref
  294.8 8.5 project_out.1
  303.3 47.7 %feed_forward.1 = (bf16[640,3072]{1,0:T(8,128)(2,1)}, bf16[640,3072]{1,0:T(8,128)(2,1)}, bf16[640,3072]{1,0:T(8,128)(2,1)}, f32[640,1152]{1,0:T(8,128)}, f32[640,1152]{1,0:T(8,128)}) custom-call(bf16[640,1152]{1,0:T(8,128)(2,1)} %get-tuple-element.163.normed_ref.left_ref, bf16[640,1152]{1,0:T(8,128)(2,1)} %copy.92.back_ref.upstream_ref.left_ref, ...), custom_call_target="tpu_custom_call" | custom-call | flops 27179089920 | bytes 21233664 | tf_op jit(solution)/shard_map/feed_forward/pallas_call | solution.py:683
  351.0 9.3 %output_back.1 = (f32[640,1152]{1,0:T(8,128)}, bf16[640,1152]{1,0:T(8,128)(2,1)}, bf16[2,640,1152]{2,1,0:T(8,128)(2,1)}, f32[8,1152]{1,0:T(8,128)}) custom-call(f32[640,1152]{1,0:T(8,128)} %get-tuple-element.166.back_ref, f32[640,1152]{1,0:T(8,128)} %get-tuple-element.162.hidden_ref, bf16[640,1152]{1,0:T(8,128)(2,1)} %copy.92.back_ref.upstream_ref.left_ref, ...), custom_call_target="tpu_custom_call" | custom-call | flops 1698693120 | bytes 16777216 | tf_op jit(solution)/shard_map/output_back/pallas_call | solution.py:588
  361.8 9.9 %gradient_parts.5 = bf16[8,2,304,288]{3,2,1,0:T(8,128)(2,1)} custom-call(s32[17]{0:T(128)} %pad_add_fusion.4.order, bf16[640,1152]{1,0:T(8,128)(2,1)} %get-tuple-element.218.left_ref, bf16[640,1152]{1,0:T(8,128)(2,1)} %get-tuple-element.219.refs_0_, f32[4,16,288]{2,1,0:T(8,128)} %pad.29.refs_1_), custom_call_target="tpu_custom_call" | custom-call | flops 1698693120 | bytes 2654208 | tf_op jit(solution)/shard_map/gradient_parts/pallas_call | solution.py:758
  371.8 13.0 %gradient_parts.7 = bf16[8,2,288,768]{3,2,1,0:T(8,128)(2,1)} custom-call(s32[17]{0:T(128)} %pad_add_fusion.4.order, bf16[640,1152]{1,0:T(8,128)(2,1)} %copy.92.back_ref.upstream_ref.left_ref, bf16[640,3072]{1,0:T(8,128)(2,1)} %get-tuple-element.223.refs_0_), custom_call_target="tpu_custom_call" | custom-call | flops 4529848320 | bytes 7077888 | tf_op jit(solution)/shard_map/gradient_parts/pallas_call | solution.py:758
  386.6 7.3 all_to_all.41
  393.9 19.1 %gradient_parts.6 = bf16[8,2,288,1536]{3,2,1,0:T(8,128)(2,1)} custom-call(s32[17]{0:T(128)} %pad_add_fusion.4.order, bf16[640,1152]{1,0:T(8,128)(2,1)} %get-tuple-element.163.normed_ref.left_ref, bf16[640,3072]{1,0:T(8,128)(2,1)} %get-tuple-element.221.refs_0_, bf16[640,3072]{1,0:T(8,128)(2,1)} %get-tuple-element.222.refs_1_), custom_call_target="tpu_custom_call" | custom-call | flops 9059696640 | bytes 14155776 | tf_op jit(solution)/shard_map/gradient_parts/pallas_call | solution.py:758
  414.9 17.7 %attention_backward.3 = (bf16[1280,384]{1,0:T(8,128)(2,1)}, bf16[10240,128]{1,0:T(8,128)(2,1)}) custom-call(s32[200]{0:T(256)S(1)} %copy-done.26, s32[5]{0:T(128)S(1)} %get-tuple-element.267.counts, bf16[1280,1536]{1,0:T(8,128)(2,1)} %bitcast.85, bf16[1280,1152]{1,0:T(8,128)(2,1)} %bitcast.94, bf16[1280,1152]{1,0:T(8,128)(2,1)} %get-tuple-element.159.o_ref, ...), custom_call_target="tpu_custom_call" | custom-call | flops 25165824000 | bytes 10485760 | tf_op jit(solution)/shard_map/attention_backward/pallas_call | solution.py:412
  433.9 25.3 %collective-permute-start.8 = (bf16[640,128]{1,0:T(8,128)(2,1)S(1)}, bf16[640,128]{1,0:T(8,128)(2,1)S(1)}, u32[]{:S(2)}, u32[]{:S(2)}) collective-permute-start(bf16[640,128]{1,0:T(8,128)(2,1)S(1)} %get-tuple-element.174), channel_id=1, source_target_pairs={{0,1},{1,2},{2,3},{3,11},{11,10},{10,9},{9,8},{8,0},{4,5},{5,6},{6... | collective-permute-start | bytes 491528 | tf_op jit(solution)/shard_map/ppermute | solution.py:801
  461.4 18.2 %attention_backward.4 = (bf16[1280,384]{1,0:T(8,128)(2,1)}, bf16[10240,128]{1,0:T(8,128)(2,1)}) custom-call(s32[200]{0:T(256)S(1)} %copy-done.26, s32[5]{0:T(128)S(1)} %get-tuple-element.267.counts, bf16[1280,1536]{1,0:T(8,128)(2,1)} %bitcast.86, bf16[1280,1152]{1,0:T(8,128)(2,1)} %bitcast.95, bf16[1280,1152]{1,0:T(8,128)(2,1)} %get-tuple-element.159.o_ref, ...), custom_call_target="tpu_custom_call" | custom-call | flops 25165824000 | bytes 10485760 | tf_op jit(solution)/shard_map/attention_backward/pallas_call | solution.py:412
  485.2 46.2 %collective-permute-start.16 = (bf16[640,128]{1,0:T(8,128)(2,1)}, bf16[640,128]{1,0:T(8,128)(2,1)S(1)}, u32[]{:S(2)}, u32[]{:S(2)}) collective-permute-start(bf16[640,128]{1,0:T(8,128)(2,1)} %get-tuple-element.185), channel_id=1, source_target_pairs={{0,1},{1,2},{2,3},{3,11},{11,10},{10,9},{9,8},{8,0},{4,5},{5,6},{6... | collective-permute-start | bytes 491528 | tf_op jit(solution)/shard_map/ppermute | solution.py:801
  531.5 38.9 %collective-permute-start.10 = (bf16[1280,128]{1,0:T(8,128)(2,1)S(1)}, bf16[1280,128]{1,0:T(8,128)(2,1)}, u32[]{:S(2)}, u32[]{:S(2)}) collective-permute-start(bf16[1280,128]{1,0:T(8,128)(2,1)S(1)} %pad_maximum_fusion.5), channel_id=1, source_target_pairs={{0,1},{1,2},{2,3},{3,11},{11,10},{10,9},{9,8},{8,0},{4,5},{5,6},{6... | collective-permute-start | bytes 983048 | tf_op jit(solution)/shard_map/ppermute | solution.py:801
  570.3 17.8 %attention_backward.5 = (bf16[1280,384]{1,0:T(8,128)(2,1)}, bf16[10240,128]{1,0:T(8,128)(2,1)}) custom-call(s32[200]{0:T(256)S(1)} %copy-done.26, s32[5]{0:T(128)S(1)} %get-tuple-element.267.counts, bf16[1280,1536]{1,0:T(8,128)(2,1)} %bitcast.87, bf16[1280,1152]{1,0:T(8,128)(2,1)} %bitcast.96, bf16[1280,1152]{1,0:T(8,128)(2,1)} %get-tuple-element.159.o_ref, ...), custom_call_target="tpu_custom_call" | custom-call | flops 25165824000 | bytes 10485760 | tf_op jit(solution)/shard_map/attention_backward/pallas_call | solution.py:412
  589.8 35.5 %collective-permute-start.24 = (bf16[640,128]{1,0:T(8,128)(2,1)S(1)}, bf16[640,128]{1,0:T(8,128)(2,1)S(1)}, u32[]{:S(2)}, u32[]{:S(2)}) collective-permute-start(bf16[640,128]{1,0:T(8,128)(2,1)S(1)} %get-tuple-element.194), channel_id=1, source_target_pairs={{0,1},{1,2},{2,3},{3,11},{11,10},{10,9},{9,8},{8,0},{4,5},{5,6},{6... | collective-permute-start | bytes 491528 | tf_op jit(solution)/shard_map/ppermute | solution.py:801
  625.2 2.6 constant_dynamic-update-slice_fusion
  628.0 16.4 %collective-permute-start.18 = (bf16[1280,128]{1,0:T(8,128)(2,1)S(1)}, bf16[1280,128]{1,0:T(8,128)(2,1)S(1)}, u32[]{:S(2)}, u32[]{:S(2)}) collective-permute-start(bf16[1280,128]{1,0:T(8,128)(2,1)S(1)} %pad_maximum_fusion.7), channel_id=1, source_target_pairs={{0,1},{1,2},{2,3},{3,11},{11,10},{10,9},{9,8},{8,0},{4,5},{5,6},{6... | collective-permute-start | bytes 983048 | tf_op jit(solution)/shard_map/ppermute | solution.py:801
  644.4 10.0 %collective-permute-start.19 = (bf16[1280,128]{1,0:T(8,128)(2,1)S(1)}, bf16[1280,128]{1,0:T(8,128)(2,1)S(1)}, u32[]{:S(2)}, u32[]{:S(2)}) collective-permute-start(bf16[1280,128]{1,0:T(8,128)(2,1)S(1)} %pad_maximum_fusion.8), channel_id=1, source_target_pairs={{1,0},{2,1},{3,2},{11,3},{10,11},{9,10},{8,9},{0,8},{5,4},{6,5},{7... | collective-permute-start | bytes 983048 | tf_op jit(solution)/shard_map/ppermute | solution.py:801
  654.4 3.2 collective-permute-done.25
  657.8 5.9 collective-permute-start.26
  667.1 8.2 collective-permute-start.13
  675.6 3.2 collective-permute-done.26
  678.8 3.6 collective-permute-start.21
  682.7 8.2 collective-permute-done.12
  690.9 2.9 collective-permute-done.13
  694.0 4.6 collective-permute-done.20
  698.6 2.8 collective-permute-done.21
  701.7 4.0 collective-permute-done.28
  705.9 6.3 collective-permute-done.29
  712.4 6.1 collective-permute-done.14
  718.4 6.5 collective-permute-done.15
  725.1 4.1 collective-permute-done.22
  729.2 6.5 collective-permute-done.23
  737.0 13.5 %collective-permute-done.31 = bf16[1280,128]{1,0:T(8,128)(2,1)S(1)} collective-permute-done((bf16[1280,128]{1,0:T(8,128)(2,1)S(1)}, bf16[1280,128]{1,0:T(8,128)(2,1)S(1)}, u32[]{:S(2)}, u32[]{:S(2)}) %collective-permute-start.31) | collective-permute-done | bytes 327712 | tf_op jit(solution)/shard_map/ppermute | solution.py:801
  750.7 8.0 all_to_all.42.packed_ref
  758.7 12.3 %joint_back.1 = (bf16[640,1920]{1,0:T(8,128)(2,1)}, bf16[4,640,288]{2,1,0:T(8,128)(2,1)}, f32[8,1152]{1,0:T(8,128)}) custom-call(bf16[2,640,1536]{2,1,0:T(8,128)(2,1)} %all_to_all.42.packed_ref, f32[640,128]{1,0:T(8,128)} %get-tuple-element.343.cos_ref, f32[640,128]{1,0:T(8,128)} %get-tuple-element.344.sin_ref, ...), custom_call_target="tpu_custom_call" | custom-call | flops 2831155200 | bytes 16777216 | tf_op jit(solution)/shard_map/joint_back/pallas_call | solution.py:637
  772.5 10.4 %gradient_parts.4 = (bf16[8,304,480]{2,1,0:T(8,128)(2,1)}, bf16[8,304,480]{2,1,0:T(8,128)(2,1)}) custom-call(s32[17]{0:T(128)} %pad_add_fusion.3.order, bf16[640,1152]{1,0:T(8,128)(2,1)} %get-tuple-element.205.left_ref, bf16[640,1920]{1,0:T(8,128)(2,1)} %get-tuple-element.206.refs_0_, f32[4,16,480]{2,1,0:T(8,128)} %pad.28.refs_1_), custom_call_target="tpu_custom_call" | custom-call | flops 2831155200 | bytes 4423680 | tf_op jit(solution)/shard_map/gradient_parts/pallas_call | solution.py:758
  787.3 3.6 all-to-all-start.4
  790.8 2.5 copy.96
  799.7 10.5 %all-to-all-done.4 = bf16[4,640,288]{1,2,0:T(8,128)(2,1)S(1)} async-done(((bf16[4,640,288]{1,2,0:T(8,128)(2,1)}), bf16[4,640,288]{1,2,0:T(8,128)(2,1)S(1)}, u32[]{:S(2)}, u32[]{:S(2)}) %all-to-all-start.4) | async-done | bytes 1474592 | tf_op jit(solution)/shard_map/all_to_all | solution.py:900
  810.3 3.6 all-to-all-start.7
  819.4 20.1 %collective-permute-done.35 = bf16[304,480]{1,0:T(8,128)(2,1)S(1)} collective-permute-done((bf16[304,480]{1,0:T(8,128)(2,1)S(1)}, bf16[304,480]{1,0:T(8,128)(2,1)S(1)}, u32[]{:S(2)}, u32[]{:S(2)}) %collective-permute-start.35) | collective-permute-done | bytes 291872 | tf_op jit(solution)/shard_map/ppermute | solution.py:801
  846.4 3.5 collective-permute-done.37
  855.2 4.4 collective-permute-done.39
  (282 shorter events, 108.9 us)
Async XLA Ops:
  7.2 62.7 %all-gather.3.cloned.1.call-start = ((), (), s32[]{:S(2)}) async-start(), calls=%async_computation.11 | async-start | bytes 5013504 | tf_op jit(solution)/shard_map/all_gather | solution.py:848
  7.9 285.3 %all-gather.5.cloned.1.call-start = ((), (), s32[]{:S(2)}) async-start(), calls=%async_computation.12 | async-start | bytes 26320896 | tf_op jit(solution)/shard_map/all_gather | solution.py:848
  16.0 32.1 %all-to-all-start = ((bf16[4,656,288]{1,2,0:T(8,128)(2,1)}), bf16[4,656,288]{1,2,0:T(8,128)(2,1)}, u32[]{:S(2)}, u32[]{:S(2)}) async-start(bf16[4,656,288]{1,2,0:T(8,128)(2,1)} %copy.84), calls=%async_computation | async-start | bytes 3538944 | tf_op jit(solution)/shard_map/all_to_all | solution.py:897
  32.9 58.3 %copy-start.6 = (bf16[10240,128]{1,0:T(8,128)(2,1)}, bf16[10240,128]{1,0:T(8,128)(2,1)S(1)}, u32[]{:S(2)}) copy-start(bf16[10240,128]{1,0:T(8,128)(2,1)S(1)} %convert_convert_fusion.mark_ref) | copy-start | bytes 7864324
  89.1 45.7 %collective-permute-start.1 = (bf16[1280,384]{1,0:T(8,128)(2,1)}, bf16[1280,384]{1,0:T(8,128)(2,1)}, u32[]{:S(2)}, u32[]{:S(2)}) collective-permute-start(bf16[1280,384]{1,0:T(8,128)(2,1)} %slice.510.refs_0_), channel_id=1, source_target_pairs={{0,1},{1,2},{2,3},{3,11},{11,10},{10,9},{9,8},{8,0},{4,5},{5,6},{6... | collective-permute-start | bytes 2949128 | tf_op jit(solution)/shard_map/ppermute | solution.py:915
  90.7 45.7 %collective-permute-start = (bf16[1280,384]{1,0:T(8,128)(2,1)}, bf16[1280,384]{1,0:T(8,128)(2,1)}, u32[]{:S(2)}, u32[]{:S(2)}) collective-permute-start(bf16[1280,384]{1,0:T(8,128)(2,1)} %slice.510.refs_0_), channel_id=1, source_target_pairs={{1,0},{2,1},{3,2},{11,3},{10,11},{9,10},{8,9},{0,8},{5,4},{6,5},{7... | collective-permute-start | bytes 2949128 | tf_op jit(solution)/shard_map/ppermute | solution.py:915
  91.3 45.8 %copy-start.9 = (bf16[2,640,1536]{2,1,0:T(8,128)(2,1)S(1)}, bf16[2,640,1536]{2,1,0:T(8,128)(2,1)}, u32[]{:S(2)}) copy-start(bf16[2,640,1536]{2,1,0:T(8,128)(2,1)} %copy-done.8) | copy-start | bytes 11796484
  134.9 45.5 %collective-permute-start.2 = (bf16[1280,384]{1,0:T(8,128)(2,1)}, bf16[1280,384]{1,0:T(8,128)(2,1)}, u32[]{:S(2)}, u32[]{:S(2)}) collective-permute-start(bf16[1280,384]{1,0:T(8,128)(2,1)} %collective-permute-done.1.refs_2_.refs_8_), channel_id=1, source_target_pairs={{0,1},{1,2},{2,3},{3,11},{11,10},{10,9},{9,8},{8,0},{4,5},{5,6},{6... | collective-permute-start | bytes 2949128 | tf_op jit(solution)/shard_map/ppermute | solution.py:929
  136.4 45.5 %collective-permute-start.3 = (bf16[1280,384]{1,0:T(8,128)(2,1)}, bf16[1280,384]{1,0:T(8,128)(2,1)}, u32[]{:S(2)}, u32[]{:S(2)}) collective-permute-start(bf16[1280,384]{1,0:T(8,128)(2,1)} %collective-permute-done.refs_1_), channel_id=1, source_target_pairs={{1,0},{2,1},{3,2},{11,3},{10,11},{9,10},{8,9},{0,8},{5,4},{6,5},{7... | collective-permute-start | bytes 2949128 | tf_op jit(solution)/shard_map/ppermute | solution.py:929
  182.0 44.9 %collective-permute-start.5 = (bf16[1280,384]{1,0:T(8,128)(2,1)}, bf16[1280,384]{1,0:T(8,128)(2,1)S(1)}, u32[]{:S(2)}, u32[]{:S(2)}) collective-permute-start(bf16[1280,384]{1,0:T(8,128)(2,1)} %collective-permute-done.3.refs_2_), channel_id=1, source_target_pairs={{1,0},{2,1},{3,2},{11,3},{10,11},{9,10},{8,9},{0,8},{5,4},{6,5},{7... | collective-permute-start | bytes 2949128 | tf_op jit(solution)/shard_map/ppermute | solution.py:929
  182.4 45.0 %collective-permute-start.4 = (bf16[1280,384]{1,0:T(8,128)(2,1)}, bf16[1280,384]{1,0:T(8,128)(2,1)}, u32[]{:S(2)}, u32[]{:S(2)}) collective-permute-start(bf16[1280,384]{1,0:T(8,128)(2,1)} %collective-permute-done.2.refs_3_.refs_7_), channel_id=1, source_target_pairs={{0,1},{1,2},{2,3},{3,11},{11,10},{10,9},{9,8},{8,0},{4,5},{5,6},{6... | collective-permute-start | bytes 2949128 | tf_op jit(solution)/shard_map/ppermute | solution.py:929
  187.1 43.6 %copy-start.10 = (bf16[2,640,1536]{2,1,0:T(8,128)(2,1)S(1)}, bf16[2,640,1536]{2,1,0:T(8,128)(2,1)}, u32[]{:S(2)}) copy-start(bf16[2,640,1536]{2,1,0:T(8,128)(2,1)} %copy-done.8) | copy-start | bytes 11796484
  226.9 51.4 %copy-start.22 = (bf16[1280,384]{1,0:T(8,128)(2,1)}, bf16[1280,384]{1,0:T(8,128)(2,1)S(1)}, u32[]{:S(2)}) copy-start(bf16[1280,384]{1,0:T(8,128)(2,1)S(1)} %collective-permute-done.5.refs_2_.refs_3_) | copy-start | bytes 2949124
  228.6 23.4 %collective-permute-start.6 = (bf16[640,384]{1,0:T(8,128)(2,1)S(1)}, bf16[640,384]{1,0:T(8,128)(2,1)S(1)}, u32[]{:S(2)}, u32[]{:S(2)}) collective-permute-start(bf16[640,384]{1,0:T(8,128)(2,1)S(1)} %slice.419), channel_id=1, source_target_pairs={{0,1},{1,2},{2,3},{3,11},{11,10},{10,9},{9,8},{8,0},{4,5},{5,6},{6... | collective-permute-start | bytes 1474568 | tf_op jit(solution)/shard_map/ppermute | solution.py:931
  230.1 23.3 %collective-permute-start.7 = (bf16[640,384]{1,0:T(8,128)(2,1)S(1)}, bf16[640,384]{1,0:T(8,128)(2,1)S(1)}, u32[]{:S(2)}, u32[]{:S(2)}) collective-permute-start(bf16[640,384]{1,0:T(8,128)(2,1)S(1)} %slice.420), channel_id=1, source_target_pairs={{1,0},{2,1},{3,2},{11,3},{10,11},{9,10},{8,9},{0,8},{5,4},{6,5},{7... | collective-permute-start | bytes 1474568 | tf_op jit(solution)/shard_map/ppermute | solution.py:931
  230.6 22.8 %copy-start.21 = (bf16[2560,288]{0,1:T(8,128)(2,1)S(1)}, bf16[2560,288]{0,1:T(8,128)(2,1)}, u32[]{:S(2)}) copy-start(bf16[2560,288]{0,1:T(8,128)(2,1)} %param.21) | copy-start | bytes 4423684
  254.7 29.7 %all-to-all-start.3 = ((bf16[4,640,288]{1,2,0:T(8,128)(2,1)}), bf16[4,640,288]{1,2,0:T(8,128)(2,1)S(1)}, u32[]{:S(2)}, u32[]{:S(2)}) async-start(bf16[4,640,288]{1,2,0:T(8,128)(2,1)} %bitcast.93), calls=%async_computation.3 | async-start | bytes 2949120 | tf_op jit(solution)/shard_map/all_to_all | solution.py:897
  261.9 16.3 %copy-start.25 = (s32[200]{0:T(256)S(1)}, s32[200]{0:T(256)}, u32[]{:S(2)}) copy-start(s32[200]{0:T(256)} %select_n.138.lists) | copy-start | bytes 2404
  261.9 16.4 %copy-start.30 = (bf16[640,384]{1,0:T(8,128)(2,1)S(1)}, bf16[640,384]{1,0:T(8,128)(2,1)}, u32[]{:S(2)}) copy-start(bf16[640,384]{1,0:T(8,128)(2,1)} %copy-done.29) | copy-start | bytes 1474564
  285.5 7.8 all-to-all-start.2
  289.4 555.9 %reduce-scatter.10.cloned.1.call-start = ((), (), s32[]{:S(2)}) async-start(), calls=%async_computation.15 | async-start | bytes 3969024
  371.7 492.1 %reduce-scatter.8.cloned.1.call-start = ((), (), s32[]{:S(2)}) async-start(), calls=%async_computation.14 | async-start | bytes 7520256 | tf_op jit(solution)/shard_map/reduce_scatter | solution.py:844
  384.8 481.1 %reduce-scatter.6.cloned.1.call-start = ((), (), s32[]{:S(2)}) async-start(), calls=%async_computation.13 | async-start | bytes 15040512 | tf_op jit(solution)/shard_map/reduce_scatter | solution.py:844
  433.9 50.2 %collective-permute-start.8 = (bf16[640,128]{1,0:T(8,128)(2,1)S(1)}, bf16[640,128]{1,0:T(8,128)(2,1)S(1)}, u32[]{:S(2)}, u32[]{:S(2)}) collective-permute-start(bf16[640,128]{1,0:T(8,128)(2,1)S(1)} %get-tuple-element.174), channel_id=1, source_target_pairs={{0,1},{1,2},{2,3},{3,11},{11,10},{10,9},{9,8},{8,0},{4,5},{5,6},{6... | collective-permute-start | bytes 491528 | tf_op jit(solution)/shard_map/ppermute | solution.py:801
  459.2 24.9 %collective-permute-start.9 = (bf16[640,128]{1,0:T(8,128)(2,1)S(1)}, bf16[640,128]{1,0:T(8,128)(2,1)S(1)}, u32[]{:S(2)}, u32[]{:S(2)}) collective-permute-start(bf16[640,128]{1,0:T(8,128)(2,1)S(1)} %get-tuple-element.175), channel_id=1, source_target_pairs={{1,0},{2,1},{3,2},{11,3},{10,11},{9,10},{8,9},{0,8},{5,4},{6,5},{7... | collective-permute-start | bytes 491528 | tf_op jit(solution)/shard_map/ppermute | solution.py:801
  485.2 142.6 %collective-permute-start.16 = (bf16[640,128]{1,0:T(8,128)(2,1)}, bf16[640,128]{1,0:T(8,128)(2,1)S(1)}, u32[]{:S(2)}, u32[]{:S(2)}) collective-permute-start(bf16[640,128]{1,0:T(8,128)(2,1)} %get-tuple-element.185), channel_id=1, source_target_pairs={{0,1},{1,2},{2,3},{3,11},{11,10},{10,9},{9,8},{8,0},{4,5},{5,6},{6... | collective-permute-start | bytes 491528 | tf_op jit(solution)/shard_map/ppermute | solution.py:801
  531.5 96.4 %collective-permute-start.17 = (bf16[640,128]{1,0:T(8,128)(2,1)}, bf16[640,128]{1,0:T(8,128)(2,1)S(1)}, u32[]{:S(2)}, u32[]{:S(2)}) collective-permute-start(bf16[640,128]{1,0:T(8,128)(2,1)} %get-tuple-element.186), channel_id=1, source_target_pairs={{1,0},{2,1},{3,2},{11,3},{10,11},{9,10},{8,9},{0,8},{5,4},{6,5},{7... | collective-permute-start | bytes 491528 | tf_op jit(solution)/shard_map/ppermute | solution.py:801
  531.5 132.3 %collective-permute-start.10 = (bf16[1280,128]{1,0:T(8,128)(2,1)S(1)}, bf16[1280,128]{1,0:T(8,128)(2,1)}, u32[]{:S(2)}, u32[]{:S(2)}) collective-permute-start(bf16[1280,128]{1,0:T(8,128)(2,1)S(1)} %pad_maximum_fusion.5), channel_id=1, source_target_pairs={{0,1},{1,2},{2,3},{3,11},{11,10},{10,9},{9,8},{8,0},{4,5},{5,6},{6... | collective-permute-start | bytes 983048 | tf_op jit(solution)/shard_map/ppermute | solution.py:801
  570.3 93.4 %collective-permute-start.11 = (bf16[1280,128]{1,0:T(8,128)(2,1)S(1)}, bf16[1280,128]{1,0:T(8,128)(2,1)}, u32[]{:S(2)}, u32[]{:S(2)}) collective-permute-start(bf16[1280,128]{1,0:T(8,128)(2,1)S(1)} %pad_maximum_fusion.6), channel_id=1, source_target_pairs={{1,0},{2,1},{3,2},{11,3},{10,11},{9,10},{8,9},{0,8},{5,4},{6,5},{7... | collective-permute-start | bytes 983048 | tf_op jit(solution)/shard_map/ppermute | solution.py:801
  588.2 39.7 %copy-start.15 = (bf16[10240,128]{1,0:T(8,128)(2,1)S(1)}, bf16[10240,128]{1,0:T(8,128)(2,1)}, u32[]{:S(2)}) copy-start(bf16[10240,128]{1,0:T(8,128)(2,1)} %get-tuple-element.176) | copy-start | bytes 7864324
  588.2 69.5 %copy-start.16 = (bf16[10240,128]{1,0:T(8,128)(2,1)S(1)}, bf16[10240,128]{1,0:T(8,128)(2,1)}, u32[]{:S(2)}) copy-start(bf16[10240,128]{1,0:T(8,128)(2,1)} %get-tuple-element.193) | copy-start | bytes 7864324
  589.8 54.6 %collective-permute-start.24 = (bf16[640,128]{1,0:T(8,128)(2,1)S(1)}, bf16[640,128]{1,0:T(8,128)(2,1)S(1)}, u32[]{:S(2)}, u32[]{:S(2)}) collective-permute-start(bf16[640,128]{1,0:T(8,128)(2,1)S(1)} %get-tuple-element.194), channel_id=1, source_target_pairs={{0,1},{1,2},{2,3},{3,11},{11,10},{10,9},{9,8},{8,0},{4,5},{5,6},{6... | collective-permute-start | bytes 491528 | tf_op jit(solution)/shard_map/ppermute | solution.py:801
  627.8 35.9 %copy-start.14 = (bf16[10240,128]{1,0:T(8,128)(2,1)S(1)}, bf16[10240,128]{1,0:T(8,128)(2,1)}, u32[]{:S(2)}) copy-start(bf16[10240,128]{1,0:T(8,128)(2,1)} %get-tuple-element.171) | copy-start | bytes 7864324
  627.8 29.8 %collective-permute-start.25 = (bf16[640,128]{1,0:T(8,128)(2,1)S(1)}, bf16[640,128]{1,0:T(8,128)(2,1)S(1)}, u32[]{:S(2)}, u32[]{:S(2)}) collective-permute-start(bf16[640,128]{1,0:T(8,128)(2,1)S(1)} %get-tuple-element.195), channel_id=1, source_target_pairs={{1,0},{2,1},{3,2},{11,3},{10,11},{9,10},{8,9},{0,8},{5,4},{6,5},{7... | collective-permute-start | bytes 491528 | tf_op jit(solution)/shard_map/ppermute | solution.py:801
  628.0 39.1 %collective-permute-start.18 = (bf16[1280,128]{1,0:T(8,128)(2,1)S(1)}, bf16[1280,128]{1,0:T(8,128)(2,1)S(1)}, u32[]{:S(2)}, u32[]{:S(2)}) collective-permute-start(bf16[1280,128]{1,0:T(8,128)(2,1)S(1)} %pad_maximum_fusion.7), channel_id=1, source_target_pairs={{0,1},{1,2},{2,3},{3,11},{11,10},{10,9},{9,8},{8,0},{4,5},{5,6},{6... | collective-permute-start | bytes 983048 | tf_op jit(solution)/shard_map/ppermute | solution.py:801
  644.4 31.0 %collective-permute-start.19 = (bf16[1280,128]{1,0:T(8,128)(2,1)S(1)}, bf16[1280,128]{1,0:T(8,128)(2,1)S(1)}, u32[]{:S(2)}, u32[]{:S(2)}) collective-permute-start(bf16[1280,128]{1,0:T(8,128)(2,1)S(1)} %pad_maximum_fusion.8), channel_id=1, source_target_pairs={{1,0},{2,1},{3,2},{11,3},{10,11},{9,10},{8,9},{0,8},{5,4},{6,5},{7... | collective-permute-start | bytes 983048 | tf_op jit(solution)/shard_map/ppermute | solution.py:801
  657.8 21.0 %collective-permute-start.26 = (bf16[1280,128]{1,0:T(8,128)(2,1)S(1)}, bf16[1280,128]{1,0:T(8,128)(2,1)S(1)}, u32[]{:S(2)}, u32[]{:S(2)}) collective-permute-start(bf16[1280,128]{1,0:T(8,128)(2,1)S(1)} %pad_maximum_fusion.9), channel_id=1, source_target_pairs={{0,1},{1,2},{2,3},{3,11},{11,10},{10,9},{9,8},{8,0},{4,5},{5,6},{6... | collective-permute-start | bytes 983048 | tf_op jit(solution)/shard_map/ppermute | solution.py:801
  663.7 18.7 %collective-permute-start.27 = (bf16[1280,128]{1,0:T(8,128)(2,1)S(1)}, bf16[1280,128]{1,0:T(8,128)(2,1)S(1)}, u32[]{:S(2)}, u32[]{:S(2)}) collective-permute-start(bf16[1280,128]{1,0:T(8,128)(2,1)S(1)} %pad_maximum_fusion.10), channel_id=1, source_target_pairs={{1,0},{2,1},{3,2},{11,3},{10,11},{9,10},{8,9},{0,8},{5,4},{6,5},{7... | collective-permute-start | bytes 983048 | tf_op jit(solution)/shard_map/ppermute | solution.py:801
  665.0 25.8 %collective-permute-start.12 = (bf16[1280,128]{1,0:T(8,128)(2,1)S(1)}, bf16[1280,128]{1,0:T(8,128)(2,1)S(1)}, u32[]{:S(2)}, u32[]{:S(2)}) collective-permute-start(bf16[1280,128]{1,0:T(8,128)(2,1)S(1)} %get-tuple-element.181), channel_id=1, source_target_pairs={{0,1},{1,2},{2,3},{3,11},{11,10},{10,9},{9,8},{8,0},{4,5},{5,6},{6... | collective-permute-start | bytes 983048 | tf_op jit(solution)/shard_map/ppermute | solution.py:801
  667.1 26.6 %collective-permute-start.13 = (bf16[1280,128]{1,0:T(8,128)(2,1)S(1)}, bf16[1280,128]{1,0:T(8,128)(2,1)S(1)}, u32[]{:S(2)}, u32[]{:S(2)}) collective-permute-start(bf16[1280,128]{1,0:T(8,128)(2,1)S(1)} %get-tuple-element.182), channel_id=1, source_target_pairs={{1,0},{2,1},{3,2},{11,3},{10,11},{9,10},{8,9},{0,8},{5,4},{6,5},{7... | collective-permute-start | bytes 983048 | tf_op jit(solution)/shard_map/ppermute | solution.py:801
  675.6 23.0 %collective-permute-start.20 = (bf16[1280,128]{1,0:T(8,128)(2,1)S(1)}, bf16[1280,128]{1,0:T(8,128)(2,1)S(1)}, u32[]{:S(2)}, u32[]{:S(2)}) collective-permute-start(bf16[1280,128]{1,0:T(8,128)(2,1)S(1)} %get-tuple-element.189), channel_id=1, source_target_pairs={{0,1},{1,2},{2,3},{3,11},{11,10},{10,9},{9,8},{8,0},{4,5},{5,6},{6... | collective-permute-start | bytes 983048 | tf_op jit(solution)/shard_map/ppermute | solution.py:801
  678.8 22.6 %collective-permute-start.21 = (bf16[1280,128]{1,0:T(8,128)(2,1)S(1)}, bf16[1280,128]{1,0:T(8,128)(2,1)S(1)}, u32[]{:S(2)}, u32[]{:S(2)}) collective-permute-start(bf16[1280,128]{1,0:T(8,128)(2,1)S(1)} %get-tuple-element.190), channel_id=1, source_target_pairs={{1,0},{2,1},{3,2},{11,3},{10,11},{9,10},{8,9},{0,8},{5,4},{6,5},{7... | collective-permute-start | bytes 983048 | tf_op jit(solution)/shard_map/ppermute | solution.py:801
  682.6 42.3 %copy-start.11 = (bf16[1280,1536]{1,0:T(8,128)(2,1)S(1)}, bf16[1280,1536]{1,0:T(8,128)(2,1)}, u32[]{:S(2)}) copy-start(bf16[1280,1536]{1,0:T(8,128)(2,1)} %constant_dynamic-update-slice_fusion) | copy-start | bytes 11796484
  682.6 23.0 %collective-permute-start.28 = (bf16[1280,128]{1,0:T(8,128)(2,1)S(1)}, bf16[1280,128]{1,0:T(8,128)(2,1)S(1)}, u32[]{:S(2)}, u32[]{:S(2)}) collective-permute-start(bf16[1280,128]{1,0:T(8,128)(2,1)S(1)} %get-tuple-element.198), channel_id=1, source_target_pairs={{0,1},{1,2},{2,3},{3,11},{11,10},{10,9},{9,8},{8,0},{4,5},{5,6},{6... | collective-permute-start | bytes 983048 | tf_op jit(solution)/shard_map/ppermute | solution.py:801
  690.9 21.3 %collective-permute-start.29 = (bf16[1280,128]{1,0:T(8,128)(2,1)S(1)}, bf16[1280,128]{1,0:T(8,128)(2,1)S(1)}, u32[]{:S(2)}, u32[]{:S(2)}) collective-permute-start(bf16[1280,128]{1,0:T(8,128)(2,1)S(1)} %get-tuple-element.199), channel_id=1, source_target_pairs={{1,0},{2,1},{3,2},{11,3},{10,11},{9,10},{8,9},{0,8},{5,4},{6,5},{7... | collective-permute-start | bytes 983048 | tf_op jit(solution)/shard_map/ppermute | solution.py:801
  693.9 24.5 %collective-permute-start.14 = (bf16[1280,128]{1,0:T(8,128)(2,1)S(1)}, bf16[1280,128]{1,0:T(8,128)(2,1)S(1)}, u32[]{:S(2)}, u32[]{:S(2)}) collective-permute-start(bf16[1280,128]{1,0:T(8,128)(2,1)S(1)} %get-tuple-element.183), channel_id=1, source_target_pairs={{0,1},{1,2},{2,3},{3,11},{11,10},{10,9},{9,8},{8,0},{4,5},{5,6},{6... | collective-permute-start | bytes 983048 | tf_op jit(solution)/shard_map/ppermute | solution.py:801
  698.6 26.3 %collective-permute-start.15 = (bf16[1280,128]{1,0:T(8,128)(2,1)S(1)}, bf16[1280,128]{1,0:T(8,128)(2,1)S(1)}, u32[]{:S(2)}, u32[]{:S(2)}) collective-permute-start(bf16[1280,128]{1,0:T(8,128)(2,1)S(1)} %get-tuple-element.184), channel_id=1, source_target_pairs={{1,0},{2,1},{3,2},{11,3},{10,11},{9,10},{8,9},{0,8},{5,4},{6,5},{7... | collective-permute-start | bytes 983048 | tf_op jit(solution)/shard_map/ppermute | solution.py:801
  701.6 27.6 %collective-permute-start.22 = (bf16[1280,128]{1,0:T(8,128)(2,1)S(1)}, bf16[1280,128]{1,0:T(8,128)(2,1)S(1)}, u32[]{:S(2)}, u32[]{:S(2)}) collective-permute-start(bf16[1280,128]{1,0:T(8,128)(2,1)S(1)} %get-tuple-element.191), channel_id=1, source_target_pairs={{0,1},{1,2},{2,3},{3,11},{11,10},{10,9},{9,8},{8,0},{4,5},{5,6},{6... | collective-permute-start | bytes 983048 | tf_op jit(solution)/shard_map/ppermute | solution.py:801
  705.6 30.0 %collective-permute-start.23 = (bf16[1280,128]{1,0:T(8,128)(2,1)S(1)}, bf16[1280,128]{1,0:T(8,128)(2,1)S(1)}, u32[]{:S(2)}, u32[]{:S(2)}) collective-permute-start(bf16[1280,128]{1,0:T(8,128)(2,1)S(1)} %get-tuple-element.192), channel_id=1, source_target_pairs={{1,0},{2,1},{3,2},{11,3},{10,11},{9,10},{8,9},{0,8},{5,4},{6,5},{7... | collective-permute-start | bytes 983048 | tf_op jit(solution)/shard_map/ppermute | solution.py:801
  712.3 24.7 %collective-permute-start.30 = (bf16[1280,128]{1,0:T(8,128)(2,1)S(1)}, bf16[1280,128]{1,0:T(8,128)(2,1)S(1)}, u32[]{:S(2)}, u32[]{:S(2)}) collective-permute-start(bf16[1280,128]{1,0:T(8,128)(2,1)S(1)} %get-tuple-element.200), channel_id=1, source_target_pairs={{0,1},{1,2},{2,3},{3,11},{11,10},{10,9},{9,8},{8,0},{4,5},{5,6},{6... | collective-permute-start | bytes 983048 | tf_op jit(solution)/shard_map/ppermute | solution.py:801
  718.4 32.1 %collective-permute-start.31 = (bf16[1280,128]{1,0:T(8,128)(2,1)S(1)}, bf16[1280,128]{1,0:T(8,128)(2,1)S(1)}, u32[]{:S(2)}, u32[]{:S(2)}) collective-permute-start(bf16[1280,128]{1,0:T(8,128)(2,1)S(1)} %get-tuple-element.201), channel_id=1, source_target_pairs={{1,0},{2,1},{3,2},{11,3},{10,11},{9,10},{8,9},{0,8},{5,4},{6,5},{7... | collective-permute-start | bytes 983048 | tf_op jit(solution)/shard_map/ppermute | solution.py:801
  772.5 10.6 %copy-start.4 = (f32[640,1152]{1,0:T(8,128)S(1)}, f32[640,1152]{1,0:T(8,128)}, u32[]{:S(2)}) copy-start(f32[640,1152]{1,0:T(8,128)} %get-tuple-element.162.hidden_ref) | copy-start | bytes 8847364
  782.9 10.4 %collective-permute-start.32 = (bf16[8,304,480]{2,1,0:T(8,128)(2,1)}, bf16[8,304,480]{2,1,0:T(8,128)(2,1)}, u32[]{:S(2)}, u32[]{:S(2)}) collective-permute-start(bf16[8,304,480]{2,1,0:T(8,128)(2,1)} %get-tuple-element.209), channel_id=1, source_target_pairs={{0,4},{4,0},{1,5},{5,1},{2,6},{6,2},{3,7},{7,3},{8,12},{12,8},{9,1... | collective-permute-start | bytes 7004168 | tf_op jit(solution)/shard_map/ppermute | solution.py:968
  785.2 5.7 copy-start.17
  787.3 23.0 %all-to-all-start.4 = ((bf16[4,640,288]{1,2,0:T(8,128)(2,1)}), bf16[4,640,288]{1,2,0:T(8,128)(2,1)S(1)}, u32[]{:S(2)}, u32[]{:S(2)}) async-start(bf16[4,640,288]{1,2,0:T(8,128)(2,1)} %bitcast.10), calls=%async_computation.4 | async-start | bytes 2949120 | tf_op jit(solution)/shard_map/all_to_all | solution.py:900
  795.2 19.7 %collective-permute-start.33 = (bf16[152,480]{1,0:T(8,128)(2,1)S(1)}, bf16[152,480]{1,0:T(8,128)(2,1)}, u32[]{:S(2)}, u32[]{:S(2)}) collective-permute-start(bf16[152,480]{1,0:T(8,128)(2,1)S(1)} %get-tuple-element.210), channel_id=1, source_target_pairs={{0,1},{1,2},{2,3},{3,11},{11,10},{10,9},{9,8},{8,0},{4,5},{5,6},{6... | collective-permute-start | bytes 437768 | tf_op jit(solution)/shard_map/ppermute | solution.py:801
  796.1 17.7 %collective-permute-start.34 = (bf16[152,480]{1,0:T(8,128)(2,1)}, bf16[152,480]{1,0:T(8,128)(2,1)}, u32[]{:S(2)}, u32[]{:S(2)}) collective-permute-start(bf16[152,480]{1,0:T(8,128)(2,1)} %get-tuple-element.211), channel_id=1, source_target_pairs={{1,0},{2,1},{3,2},{11,3},{10,11},{9,10},{8,9},{0,8},{5,4},{6,5},{7... | collective-permute-start | bytes 437768 | tf_op jit(solution)/shard_map/ppermute | solution.py:801
  810.3 32.8 %all-to-all-start.7 = ((bf16[4,640,288]{1,2,0:T(8,128)(2,1)}), bf16[4,640,288]{1,2,0:T(8,128)(2,1)S(1)}, u32[]{:S(2)}, u32[]{:S(2)}) async-start(bf16[4,640,288]{1,2,0:T(8,128)(2,1)} %copy.96), calls=%async_computation.7 | async-start | bytes 2949120 | tf_op jit(solution)/shard_map/all_to_all | solution.py:897
  816.0 23.5 %collective-permute-start.35 = (bf16[304,480]{1,0:T(8,128)(2,1)S(1)}, bf16[304,480]{1,0:T(8,128)(2,1)S(1)}, u32[]{:S(2)}, u32[]{:S(2)}) collective-permute-start(bf16[304,480]{1,0:T(8,128)(2,1)S(1)} %pad_maximum_fusion.11), channel_id=1, source_target_pairs={{0,1},{1,2},{2,3},{3,11},{11,10},{10,9},{9,8},{8,0},{4,5},{5,6},{6... | collective-permute-start | bytes 875528 | tf_op jit(solution)/shard_map/ppermute | solution.py:801
  816.5 23.0 %collective-permute-start.36 = (bf16[304,480]{1,0:T(8,128)(2,1)S(1)}, bf16[304,480]{1,0:T(8,128)(2,1)S(1)}, u32[]{:S(2)}, u32[]{:S(2)}) collective-permute-start(bf16[304,480]{1,0:T(8,128)(2,1)S(1)} %pad_maximum_fusion.12), channel_id=1, source_target_pairs={{1,0},{2,1},{3,2},{11,3},{10,11},{9,10},{8,9},{0,8},{5,4},{6,5},{7... | collective-permute-start | bytes 875528 | tf_op jit(solution)/shard_map/ppermute | solution.py:801
  841.0 9.0 %collective-permute-start.37 = (bf16[304,480]{1,0:T(8,128)(2,1)S(1)}, bf16[304,480]{1,0:T(8,128)(2,1)S(1)}, u32[]{:S(2)}, u32[]{:S(2)}) collective-permute-start(bf16[304,480]{1,0:T(8,128)(2,1)S(1)} %get-tuple-element.214), channel_id=1, source_target_pairs={{0,1},{1,2},{2,3},{3,11},{11,10},{10,9},{9,8},{8,0},{4,5},{5,6},{6... | collective-permute-start | bytes 875528 | tf_op jit(solution)/shard_map/ppermute | solution.py:801
  841.1 9.0 %collective-permute-start.38 = (bf16[304,480]{1,0:T(8,128)(2,1)S(1)}, bf16[304,480]{1,0:T(8,128)(2,1)S(1)}, u32[]{:S(2)}, u32[]{:S(2)}) collective-permute-start(bf16[304,480]{1,0:T(8,128)(2,1)S(1)} %get-tuple-element.215), channel_id=1, source_target_pairs={{1,0},{2,1},{3,2},{11,3},{10,11},{9,10},{8,9},{0,8},{5,4},{6,5},{7... | collective-permute-start | bytes 875528 | tf_op jit(solution)/shard_map/ppermute | solution.py:801
  851.5 8.1 collective-permute-start.39
  853.5 7.7 collective-permute-start.40
  (21 other events, 55.3 us)
Sparse Core Ops, SparseCore 0:
  10.3 59.5 all-gather.2
  71.4 205.6 all-gather.4
  371.9 94.0 reduce-scatter.9
  470.4 94.5 reduce-scatter.7
  569.0 184.5 reduce-scatter.5

commit v4 on v3

--- a/solution.py
+++ b/solution.py
@@ -202,7 +202,7 @@
 
 def attention_forward(lists, counts, q, pieces, marks):
     tokens, wide, heads = q.shape[0], 2 * HEAD_DIM, REPEAT
-    groups = q.shape[1] // (wide * (heads + 1))
+    groups = q.shape[1] // (wide * heads)
     total = marks.shape[0]
     blocks = counts.shape[0]
     rows = tokens // blocks
@@ -303,7 +303,7 @@
 
 def attention_stage(lists, counts, q, pieces, marks, state, ends):
     tokens, wide, heads = q.shape[0], 2 * HEAD_DIM, REPEAT
-    groups = q.shape[1] // (wide * (heads + 1))
+    groups = q.shape[1] // (wide * heads)
     total = marks.shape[0]
     blocks = counts.shape[0]
     rows = tokens // blocks
@@ -460,7 +460,7 @@
     return lax.rsqrt(jnp.sum(value * value, axis=1, keepdims=True) / D + EPSILON)
 
 
-def project_kernel(x4_ref, w_ref, cos_ref, sin_ref, bars_ref, x_ref, xa_ref, full_ref, packed_ref, gains_ref, joint_ref):
+def project_kernel(x4_ref, w_ref, cos_ref, sin_ref, bars_ref, x_ref, xa_ref, full_ref, query_ref, pair_ref, gains_ref, joint_ref):
     own = x_ref.shape[0]
     wide = 2 * HEAD_DIM
     x = jnp.concatenate([x4_ref[r, :own, :] for r in range(x4_ref.shape[0])], axis=1)
@@ -486,7 +486,7 @@
         value = turned(i) * (LOG2E * HEAD_DIM**-0.5)
         for j, head in ((2 * i, value), (2 * i + 1, roll_half(value))):
             start = (j % heads) * wide
-            packed_ref[j // heads, :, start : start + wide] = jnp.where(left, head, bars).astype(BF16)
+            query_ref[j // heads, :, start : start + wide] = jnp.where(left, head, bars).astype(BF16)
     for i in range(KV_HEADS // 2):
         key = turned(HEADS // 2 + i)
         value = part(HEADS // 2 + KV_HEADS // 2 + i)
@@ -494,8 +494,8 @@
             (2 * i, jnp.where(left, key, roll_half(value))),
             (2 * i + 1, jnp.where(left, roll_half(key), value)),
         ):
-            start = heads * wide + (j % pairs) * wide
-            packed_ref[j // pairs, :, start : start + wide] = both.astype(BF16)
+            start = (j % pairs) * wide
+            pair_ref[j // pairs, :, start : start + wide] = both.astype(BF16)
 
 
 def project_in(x4, weight, cosines, sines, bars):
@@ -504,7 +504,8 @@
         jax.ShapeDtypeStruct((own, D), BF16),
         jax.ShapeDtypeStruct((own, D), BF16),
         jax.ShapeDtypeStruct((D, ATT + 2 * KEYS), BF16),
-        jax.ShapeDtypeStruct((2, own, ATT + KEYS), BF16),
+        jax.ShapeDtypeStruct((2, own, ATT), BF16),
+        jax.ShapeDtypeStruct((2, own, KEYS), BF16),
         jax.ShapeDtypeStruct((8, D), F32),
     ]
     return pl.pallas_call(
@@ -599,17 +600,17 @@
     )(back, hidden, upstream, gains, full)
 
 
-def joint_back_kernel(packed_ref, cos_ref, sin_ref, full_ref, x_ref, gains_ref, hidden_back_ref, joint_ref, out_ref, sums_ref):
+def joint_back_kernel(query_ref, pair_ref, cos_ref, sin_ref, full_ref, x_ref, gains_ref, hidden_back_ref, joint_ref, out_ref, sums_ref):
     wide = 2 * HEAD_DIM
     heads, pairs = HEADS // 2, KV_HEADS // 2
     left = left_half((x_ref.shape[0], wide))
 
     def queries(j):
-        return packed_ref[j // heads, :, (j % heads) * wide : (j % heads + 1) * wide].astype(F32)
+        return query_ref[j // heads, :, (j % heads) * wide : (j % heads + 1) * wide].astype(F32)
 
     def both(j):
-        start = (heads + j % pairs) * wide
-        return packed_ref[j // pairs, :, start : start + wide].astype(F32)
+        start = (j % pairs) * wide
+        return pair_ref[j // pairs, :, start : start + wide].astype(F32)
 
     def store(i, value):
         joint_ref[:, i * wide : (i + 1) * wide] = value.astype(BF16)
@@ -632,7 +633,7 @@
     sums_ref[...] = jnp.broadcast_to(sums, sums_ref.shape)
 
 
-def joint_back(packed, cosines, sines, full, x, gains, hidden_back, rows):
+def joint_back(queries, pairs, cosines, sines, full, x, gains, hidden_back, rows):
     own = x.shape[0]
     return pl.pallas_call(
         joint_back_kernel,
@@ -644,15 +645,11 @@
         compiler_params=pltpu.CompilerParams(vmem_limit_bytes=56 * 2**20),
         cost_estimate=pl.CostEstimate(flops=2 * own * D * (ATT + 2 * KEYS), bytes_accessed=2**24, transcendentals=0),
         name="joint_back",
-    )(packed, cosines, sines, full, x, gains, hidden_back)
-
-
-def feed_part(width):
-    return width // 2 if width % 256 == 0 else width
+    )(queries, pairs, cosines, sines, full, x, gains, hidden_back)
 
 
 def feed_kernel(normed_ref, back_ref, gate_ref, up_ref, down_ref, mixed_ref, gate_back_ref, up_back_ref, out_ref, normed_back_ref):
-    @pl.when((pl.program_id(0) == 0) & (pl.program_id(1) == 0))
+    @pl.when(pl.program_id(0) == 0)
     def _():
         out_ref[...] = jnp.zeros(out_ref.shape, F32)
         normed_back_ref[...] = jnp.zeros(normed_back_ref.shape, F32)
@@ -675,18 +672,16 @@
 def feed_forward(normed, back, late, width):
     tokens = normed.shape[0]
     columns = late.shape[0]
-    part = feed_part(width)
-    parts = width // part
-    whole = pl.BlockSpec((tokens, D), lambda c, j: (0, 0))
-    blocks = [pl.BlockSpec((1, D, part), lambda c, j, k=k: (c, 0, k * parts + j)) for k in range(3)]
-    out = pl.BlockSpec((tokens, part), lambda c, j: (0, c * parts + j))
+    whole = pl.BlockSpec((tokens, D), lambda c: (0, 0))
+    blocks = [pl.BlockSpec((1, D, width), lambda c, k=k: (c, 0, k)) for k in range(3)]
+    out = pl.BlockSpec((tokens, width), lambda c: (0, c))
     return pl.pallas_call(
         feed_kernel,
-        grid=(columns, parts),
+        grid=(columns,),
         in_specs=[whole, whole, *blocks],
         out_specs=[out, out, out, whole, whole],
         out_shape=[jax.ShapeDtypeStruct((tokens, columns * width), BF16)] * 3 + [jax.ShapeDtypeStruct((tokens, D), F32)] * 2,
-        compiler_params=pltpu.CompilerParams(vmem_limit_bytes=56 * 2**20),
+        compiler_params=pltpu.CompilerParams(vmem_limit_bytes=62 * 2**20),
         cost_estimate=pl.CostEstimate(
             flops=12 * tokens * D * columns * width, bytes_accessed=6 * D * columns * width, transcendentals=0
         ),
@@ -694,87 +689,77 @@
     )(normed, back, late, late, late)
 
 
-def gradient_kernel(rights, summed, joined, order, left_ref, *refs):
-    right_refs, refs = refs[:rights], refs[rights:]
-    sums_ref = refs[0] if summed else None
-    refs = refs[1:] if summed else refs
-    if joined:
-        both_ref, lefts, *held = refs
-        mine_ref, other_ref = both_ref.at[:, 0], both_ref.at[:, 1]
-    else:
-        mine_ref, other_ref, lefts, *held = refs
+def gradient_kernel(counts, blocked, summed, *refs):
+    refs = list(refs)
+    sets = [(refs.pop(0), [refs.pop(0) for _ in range(n)]) for n in counts]
+    sums_ref = refs.pop(0) if summed else None
+    out_ref, turned, held = refs[0], refs[1 : 1 + len(sets)], refs[1 + len(sets) :]
     step = pl.program_id(0)
-    features = lefts.shape[2]
+    rows = out_ref.shape[1]
+    features = sets[0][0].shape[1] // rows
+    rights = [right for _, some in sets for right in some]
+    whole = [right for right, flag in zip(rights, blocked, strict=True) if not flag]
 
     @pl.when(step == 0)
     def _():
-        for r in range(lefts.shape[0]):
-            lefts[r] = left_ref[:, r * features : (r + 1) * features]
-        if held:
-            width = held[0].shape[2]
-            for c in range(held[0].shape[0]):
-                held[0][c] = right_refs[0][:, c * width : (c + 1) * width]
-
-    steps = pl.num_programs(0)
-    column, row, core = order[step], order[steps + step] * 2, order[2 * steps]
-    start = 0
-    for right in right_refs:
-        value = held[0][column] if held else right[...]
-        width = value.shape[1]
-        for target, r in ((mine_ref, row + core), (other_ref, row + 1 - core)):
-            part = lax.dot_general(lefts[r], value, (((0,), (0,)), ((), ())), preferred_element_type=F32)
-            target[0, :features, start : start + width] = part.astype(BF16)
-        start += width
-    if sums_ref is not None:
-        for target, r in ((mine_ref, row + core), (other_ref, row + 1 - core)):
-            target[0, features:, :] = sums_ref[r].astype(BF16)
-
-
-def gradient_parts(order, left, *rights, sums=None, joined=False):
-    tokens = left.shape[0]
-    steps = (order.shape[0] - 1) // 2
-    columns = steps // 2
-    width = rights[0].shape[1] // columns
-    features = left.shape[1] // 4
-    aligned = width % 128 == 0
-    if aligned:
-        right_spec = pl.BlockSpec((tokens, width), lambda s, order: (0, order[s]))
-    else:
-        right_spec = pl.BlockSpec(rights[0].shape, lambda s, order: (0, 0))
-    wide = width * len(rights)
-    tall = features if sums is None else features + 16
-    if joined:
-        outs = [pl.BlockSpec((1, 2, tall, wide), lambda s, order: (s, 0, 0, 0))]
-        shapes = [jax.ShapeDtypeStruct((steps, 2, tall, wide), BF16)]
-    else:
-        outs = [pl.BlockSpec((1, tall, wide), lambda s, order: (s, 0, 0))] * 2
-        shapes = [jax.ShapeDtypeStruct((steps, tall, wide), BF16)] * 2
-    held = [] if aligned else [pltpu.VMEM((columns, tokens, width), BF16)]
-    more, more_specs = [], []
+        for (left, _), target in zip(sets, turned, strict=True):
+            target[...] = left[...].T
+        for right, block in zip(whole, held, strict=True):
+            width = block.shape[2]
+            for c in range(block.shape[0]):
+                block[c] = right[:, c * width : (c + 1) * width]
+
+    spare, flags, start = list(held), list(blocked), 0
+    for (_, some), target in zip(sets, turned, strict=True):
+        for right in some:
+            value = right[...] if flags.pop(0) else spare.pop(0)[step]
+            width = value.shape[1]
+            part = dg(target[...], value, NN).astype(BF16)
+            for r in range(rows):
+                out_ref[0, r, :, start : start + width] = part[r * features : (r + 1) * features]
+            start += width
+    if summed:
+        tail = (rows, features, out_ref.shape[3] - start)
+        out_ref[0, :, :, start:] = jnp.broadcast_to(sums_ref[...], tail).astype(BF16)
+
+
+def gradient_parts(columns, rows, sums, *sets):
+    tokens = sets[0][0].shape[0]
+    features = D // rows
+    operands, specs, turned, held, blocked, wide = [], [], [], [], [], 0
+    for left, rights in sets:
+        operands.append(left)
+        specs.append(pl.BlockSpec(left.shape, lambda c: (0, 0)))
+        turned.append(pltpu.VMEM((left.shape[1], tokens), BF16))
+        for right in rights:
+            width = right.shape[1] // columns
+            operands.append(right)
+            wide += width
+            if width % 128 == 0:
+                specs.append(pl.BlockSpec((tokens, width), lambda c: (0, c)))
+                blocked.append(True)
+            else:
+                specs.append(pl.BlockSpec(right.shape, lambda c: (0, 0)))
+                held.append(pltpu.VMEM((columns, tokens, width), BF16))
+                blocked.append(False)
     if sums is not None:
-        lines = -(-features // wide)
-        more = [jnp.pad(sums.reshape(4, lines, -1), ((0, 0), (0, 16 - lines), (0, wide - features // lines)))]
-        more_specs = [pl.BlockSpec((4, 16, wide), lambda s, order: (0, 0, 0))]
+        wide = (wide // 128 + 1) * 128
+        operands.append(sums.reshape(rows, features, 1))
+        specs.append(pl.BlockSpec((rows, features, 1), lambda c: (0, 0, 0)))
+    shape = (columns, rows, features, wide)
     return pl.pallas_call(
-        functools.partial(gradient_kernel, len(rights), sums is not None, joined),
-        grid_spec=pltpu.PrefetchScalarGridSpec(
-            num_scalar_prefetch=1,
-            grid=(steps,),
-            in_specs=[
-                pl.BlockSpec(left.shape, lambda s, order: (0, 0)),
-                *(right_spec for _ in rights),
-                *more_specs,
-            ],
-            out_specs=outs,
-            scratch_shapes=[pltpu.VMEM((4, tokens, features), BF16), *held],
-        ),
-        out_shape=shapes,
-        compiler_params=pltpu.CompilerParams(vmem_limit_bytes=56 * 2**20),
+        functools.partial(gradient_kernel, [len(rights) for _, rights in sets], blocked, sums is not None),
+        grid=(columns,),
+        in_specs=specs,
+        out_specs=pl.BlockSpec((1, *shape[1:]), lambda c: (c, 0, 0, 0)),
+        out_shape=jax.ShapeDtypeStruct(shape, BF16),
+        scratch_shapes=[*turned, *held],
+        compiler_params=pltpu.CompilerParams(vmem_limit_bytes=60 * 2**20),
         cost_estimate=pl.CostEstimate(
-            flops=2 * tokens * left.shape[1] * wide * columns, bytes_accessed=2 * left.shape[1] * wide * columns, transcendentals=0
+            flops=2 * tokens * D * wide * columns, bytes_accessed=2 * D * wide * columns, transcendentals=0
         ),
         name="gradient_parts",
-    )(order, left, *rights, *more)
+    )(*operands)
 
 
 ROW = ("high", "core")
@@ -822,7 +807,15 @@
         return self.part(0, None) + self.arrived[0].astype(F32) + self.arrived[1].astype(F32)
 
 
+def after(value, rings):
+    value, arrived = lax.optimization_barrier((value, [ring.arrived for ring in rings]))
+    for ring, a in zip(rings, arrived, strict=True):
+        ring.arrived = a
+    return value
+
+
 def depart(value, rings):
+    rings = [ring for ring in rings if ring.left]
     for ring in rings:
         if ring.ready is None:
             ring.prepare()
@@ -881,7 +874,6 @@
     far = spots >= columns
     ring_column = jnp.where(far, 2 * columns - 1 - spots, spots)
     ring_high = far.astype(jnp.int32)
-    order = jnp.concatenate([ring_column, ring_high, jnp.reshape(core, (1,))]).astype(jnp.int32)
     key_first = ring_column * tokens.shape[0] + ring_high * held
     key_index = (key_first[:, None] + jnp.arange(held, dtype=jnp.int32)[None, :]).reshape(-1)
 
@@ -896,30 +888,37 @@
     def exchange(value, axes):
         return lax.all_to_all(value, axes, split_axis=0, concat_axis=0, tiled=True)
 
-    def to_features(value):
-        value = lax.all_to_all(value.reshape(own, rows, -1).transpose(1, 0, 2), ROW, split_axis=0, concat_axis=0)
-        return value.reshape(rows * own, -1)
-
     joint_blocks = gather(joint_weight, ALL_COL).reshape(columns, D, -1)
     gains = jnp.broadcast_to(jnp.stack([attention_gain, feed_gain])[None], (rows, 2, attention_gain.shape[0]))
     extended = jnp.concatenate([tokens.reshape(rows, own, -1), jnp.pad(gains, ((0, 0), (0, 14), (0, 0)))], axis=1)
     extended = exchange(extended, ROW)
 
-    x, normed_one, joint_full, packed, gains = project_in(extended, joint_blocks, cosines, sines, bars)
+    def plan(*places):
+        keys = jnp.concatenate([key_index[i * held : j * held] for i, j in places])
+        return (jnp.concatenate([marks[i * held : j * held] for i, j in places]), *block_lists(first, keys, block, held, tables))
+
+    chips = 2 * columns
+    plans = [plan((0, 2), (chips - 1, chips))]
+    plans += [plan((s, s + 1), (chips - s, chips - s + 1)) for s in range(2, columns)]
+    plans += [plan((columns, columns + 1))]
+    (marks, lists, counts, plans), extended = lax.optimization_barrier(((marks, lists, counts, plans), extended))
+    x, normed_one, joint_full, packed, value, gains = project_in(extended, joint_blocks, cosines, sines, bars)
+    value, packed = lax.optimization_barrier((exchange(value, "core").reshape(held, -1), packed))
     packed = exchange(packed, "core").reshape(held, -1)
-    wide = groups * REPEAT * 2 * HEAD_DIM
+    width = gate_weight.shape[1]
+    unit = width // 2 if width % 256 == 0 else width
+    padding = jnp.zeros((output_weight.shape[1], -output_weight.shape[0] % unit), BF16)
+    late = jnp.concatenate([gate_weight, up_weight, down_weight.T, output_weight.T, padding], axis=1)
+    late = gather(late, ALL_COL).reshape(columns, D, -1)
     pieces = []
     state = None
     ahead, behind = ring_steps(columns)
-    value = packed[:, wide:]
     to_next, to_last = lax.ppermute(value, RING, ahead), lax.ppermute(value, RING, behind)
     fronts, backs = [], []
 
-    def attend(state, places, some, ends):
-        keys_here = jnp.concatenate([key_index[i * held // 2 : j * held // 2] for i, j in places])
-        marks_here = jnp.concatenate([marks[i * held // 2 : j * held // 2] for i, j in places])
-        lists_here, counts_here = block_lists(first, keys_here, block, held, tables)
-        return tuple(attention_stage(lists_here, counts_here, packed, some, marks_here, state, ends))
+    def attend(state, plan, some, ends):
+        keys, lists_here, counts_here = plan
+        return tuple(attention_stage(lists_here, counts_here, packed, some, keys, state, ends))
 
     middle = held // 2
     for step in range(1, columns):
@@ -929,16 +928,16 @@
             further = (lax.ppermute(to_next, RING, ahead), lax.ppermute(to_last, RING, behind))
         else:
             further = (lax.ppermute(to_next[:middle], RING, ahead), lax.ppermute(to_last[middle:], RING, behind))
-        far = 2 * (2 * columns - step)
-        places, some = [(2 * step, 2 * step + 2), (far, far + 2)], [to_last, to_next]
+        some = [value, to_last, to_next] if step == 1 else [to_last, to_next]
         if step == 1:
-            places, some = [(0, 2), *places], [value, *some]
-        state = attend(state, places, some, False)
+            cotangent, further = lax.optimization_barrier((cotangent, further))
+            upstream = exchange(cotangent.reshape(rows, own, -1), ROW).transpose(1, 0, 2).reshape(own, D)
+        state = attend(state, plans[step - 1], some, False)
         state, further = lax.optimization_barrier((state, further))
         to_next, to_last = further
     pieces = [value, *backs, to_next, to_last, *reversed(fronts)]
-    cotangent, to_next = lax.optimization_barrier((cotangent, to_next))
-    state = attend(state, [(2 * columns, 2 * columns + 2)], [to_next, to_last], True)
+    upstream, state = lax.optimization_barrier((upstream, state))
+    state = attend(state, plans[columns - 1], [to_next, to_last], True)
     attended, lse = lax.cond(
         jnp.any(state[1] != state[1]),
         lambda: tuple(attention_forward(lists, counts, packed, pieces, marks)),
@@ -946,36 +945,14 @@
     )
     attended_rows = exchange(attended.reshape(cores, own, -1), "core")
 
-    width = gate_weight.shape[1]
-    part = feed_part(width)
-    padding = jnp.zeros((output_weight.shape[1], -output_weight.shape[0] % part), BF16)
-    late = jnp.concatenate([gate_weight, up_weight, down_weight.T, output_weight.T, padding], axis=1)
-    late = gather(late, ALL_COL).reshape(columns, D, -1)
-    upstream = exchange(cotangent.reshape(rows, own, -1), ROW).transpose(1, 0, 2).reshape(own, D)
     attended_rows, hidden, normed_two, output_full = project_out(attended_rows, late, x, gains, ATT // columns, late.shape[2] - 3 * width)
     mixed, gate_back, up_back, feed_out, normed_two_back = feed_forward(normed_two, upstream, late, width)
-    layer_output = to_features((hidden + feed_out).astype(BF16))
-
-    steps = jnp.arange(2 * columns, dtype=jnp.int32)
-    plain = jnp.concatenate([steps // 2, steps % 2, jnp.zeros((1,), jnp.int32)])
-
-    def scatter_gradient(left, *rights, sums=None):
-        [parts] = gradient_parts(plain, left, *rights, sums=sums, joined=True)
-        return scatter(parts.reshape(-1, parts.shape[3]), ALL_COL).astype(F32)
-
-    def ring_gradient(left, *rights, sums=None):
-        mine, other = gradient_parts(order, left, *rights, sums=sums)
-        other = lax.ppermute(other, "core", [(0, 1), (1, 0)])
-
-        def part(s, half):
-            return halves(mine[s], half).astype(F32) + halves(other[s], half).astype(F32)
-
-        return RingScatter(part, columns)
-
-    down_gradient = scatter_gradient(upstream, mixed).T
-    pair_gradient = scatter_gradient(normed_two, gate_back, up_back)
+
+    feed_parts = gradient_parts(columns, rows, None, (normed_two, [gate_back, up_back]), (upstream, [mixed]))
+    feed_parts, normed_two_back = lax.optimization_barrier((feed_parts, normed_two_back))
+    feed_summed = scatter(feed_parts.reshape(-1, feed_parts.shape[3]), ALL_COL)
     hidden_back, hidden_low, heads_back, gain_two_part = output_back(normed_two_back, hidden, upstream, gains, output_full)
-    output_summed = scatter_gradient(hidden_low, attended_rows, sums=gain_two_part[0])
+    output_parts = gradient_parts(columns, rows, gain_two_part[0], (hidden_low, [attended_rows]))
 
     heads_back = exchange(heads_back, "core").reshape(held, -1)
     query_backs, pair_rings = [], []
@@ -984,30 +961,52 @@
         query_back, pair_back = attention_backward(g, lists, counts, packed, heads_back, attended, pieces, marks, lse)
         pair_back = pair_back.reshape(2 * columns, held, -1)
         query_backs.append(query_back)
+        pair_back = after(pair_back, pair_rings)
         pair_rings.append(RingScatter(lambda s, half, v=pair_back: halves(v[s], half).astype(F32), columns))
+    pair_rings[-1].launch()
+    query_backs, feed_out = after((query_backs, feed_out), pair_rings[-1:])
+    query_back = exchange(jnp.concatenate(query_backs, axis=1).reshape(cores, own, -1), "core")
+    layer_low = (hidden + feed_out).astype(BF16).reshape(own, rows, -1).transpose(1, 0, 2)
     held_pairs = jnp.concatenate([ring.finish().astype(BF16) for ring in pair_rings], axis=1)
-    back = jnp.concatenate([*query_backs, held_pairs], axis=1).reshape(cores, own, -1)
-    back = exchange(back, "core")
-    joint_low, input_part, gain_one_part = joint_back(back, cosines, sines, joint_full, x, gains, hidden_back, rows)
-    joint_ring = ring_gradient(normed_one, joint_low, sums=gain_one_part[0])
+    held_pairs, query_back, layer_low, feed_summed, output_parts = lax.optimization_barrier(
+        (held_pairs, query_back, layer_low, feed_summed, output_parts)
+    )
+    feed_summed = feed_summed.astype(F32)
+    output_summed = scatter(output_parts.reshape(-1, output_parts.shape[3]), ALL_COL).astype(F32)
+    pair_back = exchange(held_pairs.reshape(cores, own, -1), "core")
+    layer_output = exchange(layer_low, ROW).reshape(rows * own, -1)
+    joint_low, input_part, gain_one_part = joint_back(
+        query_back, pair_back, cosines, sines, joint_full, x, gains, hidden_back, rows
+    )
+    joint_low, layer_output = lax.optimization_barrier((joint_low, layer_output))
+    joint_parts = gradient_parts(columns, rows, gain_one_part[0], (normed_one, [joint_low]))
+    joint_parts = joint_parts.reshape(2 * columns, cores, *joint_parts.shape[2:])
+    places = ring_column * 2 + ring_high
+    swap = [(0, 1), (1, 0)]
+    joint_first = lax.dynamic_slice(joint_parts, (places[columns], 1 - core, 0, 0), (1, 1, *joint_parts.shape[2:]))[0, 0]
+    joint_first = lax.ppermute(joint_first, "core", swap)
+    joint_other = lax.dynamic_index_in_dim(joint_parts, 1 - core, 1, keepdims=False)
+    joint_other = lax.ppermute(joint_other, "core", swap)
+
+    def joint_part(s, half):
+        mine = lax.dynamic_slice(joint_parts, (places[s], core, 0, 0), (1, 1, *joint_parts.shape[2:]))[0, 0]
+        other = joint_first if s == columns else lax.dynamic_index_in_dim(joint_other, places[s], 0, keepdims=False)
+        return halves(mine, half).astype(F32) + halves(other, half).astype(F32)
+
+    joint_ring = RingScatter(joint_part, columns)
     input_gradient = exchange(input_part, ROW).reshape(rows * own, -1).astype(F32)
     joint_summed = joint_ring.finish()
-    features = D // rows
-
-    def carried(summed):
-        lines = -(-features // summed.shape[1])
-        return summed[features : features + lines, : features // lines].reshape(-1)
-
+    narrow, joined = ATT // columns, joint_weight.shape[1]
     return (
         layer_output,
         input_gradient,
-        carried(joint_summed),
-        joint_summed[:features],
-        output_summed[:features].T,
-        carried(output_summed),
-        pair_gradient[:, :width],
-        pair_gradient[:, width:],
-        down_gradient,
+        joint_summed[:, joined],
+        joint_summed[:, :joined],
+        output_summed[:, :narrow].T,
+        output_summed[:, narrow],
+        feed_summed[:, :width],
+        feed_summed[:, width : 2 * width],
+        feed_summed[:, 2 * width :].T,
     )
 
 

time: 888 us -> 840 us (0.946)
  waiting for transfers between devices: 247 us -> 203 us
  Pallas kernels: 254 us -> 238 us
  between operations: 15.8 us -> 31 us
    ppermute x2, waiting for transfers between devices: 27.7 us -> 1.79 us  [per_device(): lax.ppermute(to_last, RING, behind)]
    ppermute x16, waiting for transfers between devices: 43.4 us -> 20.9 us  [launch(): lax.ppermute(back, RING, self.behind)]
    ppermute x16, waiting for transfers between devices: 59.4 us -> 37.5 us  [launch(): lax.ppermute(out, RING, self.ahead)]
    ppermute x2, waiting for transfers between devices: 17.4 us -> 39 us  [per_device(): lax.ppermute(to_next, RING, ahead)]
    pallas_call x5 -> x4, Pallas kernels: 100 us -> 79.2 us  [the longest x3 40.8 us: gradient_parts(): pl.pallas_call(functools.partial(gradient_kernel, [len(rights) for _, rig...]
    ppermute x1, waiting for transfers between devices: 11.9 us -> 31.4 us  [per_device(): lax.ppermute(to_next[:middle], RING, ahead)]
    all_to_all x4 -> x7, starting transfers between devices: 16 us -> 30.1 us  [exchange(): return lax.all_to_all(value, axes, split_axis=0, concat_axis=0, tiled=True)]
    unnamed x71 -> x68, local copies, waits for them, and re-layouts: 24.3 us -> 13.2 us
  transfers between devices with their start and end apart: 51 -> 53, of which waited for: 30 -> 24; matrix products, arithmetic and copies ran while one was open for 10% -> 11% of each run, Pallas kernels for 20% -> 20%
where the time goes in v4:
time: 840 us; the launch traced here: 831 us
  Pallas kernels  238 us (28%)
  starting transfers between devices  229 us (27%)
  waiting for transfers between devices  203 us (24%)
  local copies, waits for them, and re-layouts  60 us (7%)
  other arithmetic  43.4 us (5%)
  between operations  31 us (4%)
  blocking collectives  25.5 us (3%)
    ppermute x16, starting transfers between devices, launch(): lax.ppermute(out, RING, self.ahead)  172 us
    pallas_call x4, Pallas kernels, attention_stage(): pl.pallas_call(functools.partial(stage_kernel, state is None, ends), grid...  64.1 us
    pallas_call x3, Pallas kernels, attention_backward(): pl.pallas_call(functools.partial(backward_kernel, group), grid_spec=pltpu...  54 us
    pallas_call x3, Pallas kernels, gradient_parts(): pl.pallas_call(functools.partial(gradient_kernel, [len(rights) for _, rig...  40.8 us
    ppermute x2, waiting for transfers between devices, per_device(): lax.ppermute(to_next, RING, ahead)  39 us
    ppermute x1, waiting for transfers between devices, per_device(): lax.ppermute(value, RING, ahead)  38.5 us
    pallas_call x1, Pallas kernels, feed_forward(): pl.pallas_call(feed_kernel, grid=(columns,), in_specs=[whole, whole, *blo...  38.4 us
    ppermute x16, waiting for transfers between devices, launch(): lax.ppermute(out, RING, self.ahead)  37.5 us
  transfers between devices with their start and end apart: 53, of which 24 were waited for; matrix products, arithmetic and copies ran while one was open for 11% of the time, Pallas kernels for 20%

profile of v4, /device:TPU:0, one launch (start us, length us, event | category | flops | bytes accessed | tf_op | source)
XLA Modules:
  0.0 830.7 jit_solution(6595219154713035319)
XLA Ops:
  9.2 3.7 concatenate.77
  16.2 4.6 all-to-all-start
  26.7 4.7 compare_and_fusion
  38.5 10.0 %all-to-all-done = bf16[4,656,288]{1,2,0:T(8,128)(2,1)} async-done(((bf16[4,656,288]{1,2,0:T(8,128)(2,1)}), bf16[4,656,288]{1,2,0:T(8,128)(2,1)}, u32[]{:S(2)}, u32[]{:S(2)}) %all-to-all-start) | async-done | bytes 1511456 | tf_op jit(solution)/shard_map/all_to_all | solution.py:889
  48.5 3.9 copy.99.x4_ref
  52.4 17.4 %all-gather.3.cloned.1.call-done = bf16[4608,480]{1,0:T(8,128)(2,1)} async-done(((bf16[288,480]{1,0:T(8,128)(2,1)}), bf16[4608,480]{1,0:T(8,128)(2,1)}) %all-gather.3.cloned.1.call-update) | async-done | bytes 4423696 | tf_op jit(solution)/shard_map/all_gather | solution.py:841
  69.8 11.0 %project_in.1 = (bf16[640,1152]{1,0:T(8,128)(2,1)}, bf16[640,1152]{1,0:T(8,128)(2,1)}, bf16[1152,1920]{1,0:T(8,128)(2,1)}, bf16[2,640,1152]{2,1,0:T(8,128)(2,1)}...) custom-call(bf16[4,656,288]{2,1,0:T(8,128)(2,1)} %copy.99.x4_ref, bf16[4,1152,480]{2,1,0:T(8,128)(2,1)} %bitcast.246, ...), custom_call_target="tpu_custom_call" | custom-call | flops 2831155200 | bytes 16777216 | tf_op jit(solution)/shard_map/project_in/pallas_call | solution.py:511
  80.8 6.5 all_to_all.50
  89.4 5.1 all-to-all-start.2
  94.5 38.5 %collective-permute-done.refs_2_.refs_8_ = bf16[1280,384]{1,0:T(8,128)(2,1)} collective-permute-done((bf16[1280,384]{1,0:T(8,128)(2,1)}, bf16[1280,384]{1,0:T(8,128)(2,1)}, u32[]{:S(2)}, u32[]{:S(2)}) %collective-permute-start) | collective-permute-done | bytes 983072 | tf_op jit(solution)/shard_map/ppermute | solution.py:916
  135.4 25.0 %attention_stage.4 = (f32[3,5,80,768]{3,2,1,0:T(8,128)S(1)}, f32[3,5,1,768]{3,2,1,0:T(1,128)S(1)}) custom-call(s32[75]{0:T(128)S(1)} %select_n.164.lists, s32[5]{0:T(128)S(1)} %get-tuple-element.198.counts, bf16[1280,1152]{1,0:T(8,128)(2,1)} %bitcast.3.q_ref, bf16[3840,128]{1,0:T(8,128)(2,1)S(1)} %pad_maximum_fusion.1.mark_ref, ...), custom_call_target="tpu_custom_call" | custom-call | flops 11324620800 | bytes 5898240 | tf_op jit(solution)/shard_map/attention_stage/pallas_call | solution.py:323
  162.3 16.2 %collective-permute-done.1.refs_3_.refs_7_ = bf16[1280,384]{1,0:T(8,128)(2,1)} collective-permute-done((bf16[1280,384]{1,0:T(8,128)(2,1)}, bf16[1280,384]{1,0:T(8,128)(2,1)}, u32[]{:S(2)}, u32[]{:S(2)}) %collective-permute-start.1) | collective-permute-done | bytes 983072 | tf_op jit(solution)/shard_map/ppermute | solution.py:928
  183.6 4.4 all-to-all-start.3
  190.0 13.5 %attention_stage.5 = (f32[3,5,80,768]{3,2,1,0:T(8,128)S(1)}, f32[3,5,1,768]{3,2,1,0:T(1,128)S(1)}) custom-call(s32[50]{0:T(128)S(1)} %select_n.168.lists, s32[5]{0:T(128)S(1)} %get-tuple-element.195.counts, bf16[1280,1152]{1,0:T(8,128)(2,1)} %bitcast.3.q_ref, bf16[2560,128]{1,0:T(8,128)(2,1)S(1)} %pad_maximum_fusion.3.mark_ref, ...), custom_call_target="tpu_custom_call" | custom-call | flops 7549747200 | bytes 3932160 | tf_op jit(solution)/shard_map/attention_stage/pallas_call | solution.py:323
  203.4 22.8 %collective-permute-done.4.refs_3_.refs_6_ = bf16[1280,384]{1,0:T(8,128)(2,1)} collective-permute-done((bf16[1280,384]{1,0:T(8,128)(2,1)}, bf16[1280,384]{1,0:T(8,128)(2,1)}, u32[]{:S(2)}, u32[]{:S(2)}) %collective-permute-start.4) | collective-permute-done | bytes 983072 | tf_op jit(solution)/shard_map/ppermute | solution.py:928
  231.1 13.5 %attention_stage.6 = (f32[3,5,80,768]{3,2,1,0:T(8,128)S(1)}, f32[3,5,1,768]{3,2,1,0:T(1,128)S(1)}) custom-call(s32[50]{0:T(128)S(1)} %select_n.172.lists, s32[5]{0:T(128)S(1)} %get-tuple-element.192.counts, bf16[1280,1152]{1,0:T(8,128)(2,1)} %bitcast.3.q_ref, bf16[2560,128]{1,0:T(8,128)(2,1)S(1)} %pad_maximum_fusion.4.mark_ref, ...), custom_call_target="tpu_custom_call" | custom-call | flops 7549747200 | bytes 3932160 | tf_op jit(solution)/shard_map/attention_stage/pallas_call | solution.py:323
  246.5 31.4 %collective-permute-done.6.refs_2_.refs_4_ = bf16[640,384]{1,0:T(8,128)(2,1)S(1)} collective-permute-done((bf16[640,384]{1,0:T(8,128)(2,1)S(1)}, bf16[640,384]{1,0:T(8,128)(2,1)S(1)}, u32[]{:S(2)}, u32[]{:S(2)}) %collective-permute-start.6) | collective-permute-done | bytes 491552 | tf_op jit(solution)/shard_map/ppermute | solution.py:930
  277.9 2.4 copy-done.1
  280.3 12.1 %attention_stage.7 = (bf16[1280,1152]{1,0:T(8,128)(2,1)}, f32[3,5,1,768]{3,2,1,0:T(1,128)S(1)}) custom-call(s32[25]{0:T(128)S(1)} %select_n.176.lists, s32[5]{0:T(128)S(1)} %get-tuple-element.187.counts, bf16[1280,1152]{1,0:T(8,128)(2,1)} %bitcast.3.q_ref, bf16[1280,128]{1,0:T(8,128)(2,1)S(1)} %get-tuple-element.188.mark_ref, ...), custom_call_target="tpu_custom_call" | custom-call | flops 3774873600 | bytes 1966080 | tf_op jit(solution)/shard_map/attention_stage/pallas_call | solution.py:323
  293.9 3.9 all-to-all-start.4
  298.0 3.7 copy.102.back_ref.refs_3_.upstream_ref
  303.4 8.4 %project_out.1 = (bf16[640,1152]{1,0:T(8,128)(2,1)}, f32[640,1152]{1,0:T(8,128)}, bf16[640,1152]{1,0:T(8,128)(2,1)}, bf16[1152,1152]{1,0:T(8,128)(2,1)}) custom-call(bf16[2,640,1152]{2,1,0:T(8,128)(2,1)} %copy-done.6, bf16[4,1152,2688]{2,1,0:T(8,128)(2,1)} %bitcast.204, bf16[640,1152]{1,0:T(8,128)(2,1)} %get-tuple-element.225.x_ref, ...), custom_call_target="tpu_custom_call" | custom-call | flops 1698693120 | bytes 16777216 | tf_op jit(solution)/shard_map/project_out/pallas_call | solution.py:540
  311.8 38.4 %feed_forward.1 = (bf16[640,3072]{1,0:T(8,128)(2,1)}, bf16[640,3072]{1,0:T(8,128)(2,1)}, bf16[640,3072]{1,0:T(8,128)(2,1)}, f32[640,1152]{1,0:T(8,128)}, f32[640,1152]{1,0:T(8,128)}) custom-call(bf16[640,1152]{1,0:T(8,128)(2,1)} %get-tuple-element.227.normed_ref.refs_0_, bf16[640,1152]{1,0:T(8,128)(2,1)} %copy.102.back_ref.refs_3_.upstream_ref, ...), custom_call_target="tpu_custom_call" | custom-call | flops 27179089920 | bytes 21233664 | tf_op jit(solution)/shard_map/feed_forward/pallas_call | solution.py:678
  350.3 23.8 %gradient_parts.3 = bf16[4,4,288,2304]{3,2,1,0:T(8,128)(2,1)} custom-call(bf16[640,1152]{1,0:T(8,128)(2,1)} %get-tuple-element.227.normed_ref.refs_0_, bf16[640,3072]{1,0:T(8,128)(2,1)} %get-tuple-element.229.refs_1_, bf16[640,3072]{1,0:T(8,128)(2,1)} %get-tuple-element.230.refs_2_, bf16[640,1152]{1,0:T(8,128)(2,1)} %copy.102.back_ref.refs_3_.upstream_ref, ...), custom_call_target="tpu_custom_call" | custom-call | flops 13589544960 | bytes 21233664 | tf_op jit(solution)/shard_map/gradient_parts/pallas_call | solution.py:750
  374.1 9.3 %output_back.1 = (f32[640,1152]{1,0:T(8,128)}, bf16[640,1152]{1,0:T(8,128)(2,1)}, bf16[2,640,1152]{2,1,0:T(8,128)(2,1)}, f32[8,1152]{1,0:T(8,128)}) custom-call(f32[640,1152]{1,0:T(8,128)} %get-tuple-element.233.back_ref, f32[640,1152]{1,0:T(8,128)} %get-tuple-element.234.hidden_ref, bf16[640,1152]{1,0:T(8,128)(2,1)} %copy.102.back_ref.refs_3_.upstream_ref, ...), custom_call_target="tpu_custom_call" | custom-call | flops 1698693120 | bytes 16777216 | tf_op jit(solution)/shard_map/output_back/pallas_call | solution.py:589
  385.5 12.4 %all_to_all.51 = bf16[2,640,1152]{2,1,0:T(8,128)(2,1)} all-to-all(bf16[2,640,1152]{2,1,0:T(8,128)(2,1)} %get-tuple-element.236), channel_id=1, replica_groups=mesh['leaf'=2,'high'=2,'core'=2,'col'=4] {'core'}, dimensions={0} | all-to-all | bytes 5898240 | tf_op jit(solution)/shard_map/all_to_all | solution.py:889
  397.9 18.3 %attention_backward.3 = (bf16[1280,384]{1,0:T(8,128)(2,1)}, bf16[10240,128]{1,0:T(8,128)(2,1)}) custom-call(s32[200]{0:T(256)S(1)} %select_n.160.lists, s32[5]{0:T(128)S(1)} %get-tuple-element.181.counts, bf16[1280,1152]{1,0:T(8,128)(2,1)} %bitcast.3.q_ref, bf16[1280,1152]{1,0:T(8,128)(2,1)} %bitcast.221, bf16[1280,1152]{1,0:T(8,128)(2,1)} %get-tuple-element.224.o_ref, ...), custom_call_target="tpu_custom_call" | custom-call | flops 25165824000 | bytes 10485760 | tf_op jit(solution)/shard_map/attention_backward/pallas_call | solution.py:412
  417.5 14.5 %collective-permute-start.9 = (bf16[640,128]{1,0:T(8,128)(2,1)S(1)}, bf16[640,128]{1,0:T(8,128)(2,1)S(1)}, u32[]{:S(2)}, u32[]{:S(2)}) collective-permute-start(bf16[640,128]{1,0:T(8,128)(2,1)S(1)} %get-tuple-element.242), channel_id=1, source_target_pairs={{1,0},{2,1},{3,2},{11,3},{10,11},{9,10},{8,9},{0,8},{5,4},{6,5},{7... | collective-permute-start | bytes 491528 | tf_op jit(solution)/shard_map/ppermute | solution.py:786
  432.0 17.9 %attention_backward.4 = (bf16[1280,384]{1,0:T(8,128)(2,1)}, bf16[10240,128]{1,0:T(8,128)(2,1)}) custom-call(s32[200]{0:T(256)S(1)} %select_n.160.lists, s32[5]{0:T(128)S(1)} %get-tuple-element.181.counts, bf16[1280,1152]{1,0:T(8,128)(2,1)} %bitcast.3.q_ref, bf16[1280,1152]{1,0:T(8,128)(2,1)} %bitcast.222, bf16[1280,1152]{1,0:T(8,128)(2,1)} %get-tuple-element.224.o_ref, ...), custom_call_target="tpu_custom_call" | custom-call | flops 25165824000 | bytes 10485760 | tf_op jit(solution)/shard_map/attention_backward/pallas_call | solution.py:412
  449.8 8.0 gradient_parts.4
  460.9 38.0 %collective-permute-start.10 = (bf16[1280,128]{1,0:T(8,128)(2,1)S(1)}, bf16[1280,128]{1,0:T(8,128)(2,1)S(1)}, u32[]{:S(2)}, u32[]{:S(2)}) collective-permute-start(bf16[1280,128]{1,0:T(8,128)(2,1)S(1)} %pad_maximum_fusion.7), channel_id=1, source_target_pairs={{0,1},{1,2},{2,3},{3,11},{11,10},{10,9},{9,8},{8,0},{4,5},{5,6},{6... | collective-permute-start | bytes 983048 | tf_op jit(solution)/shard_map/ppermute | solution.py:786
  498.9 53.1 %collective-permute-start.12 = (bf16[640,128]{1,0:T(8,128)(2,1)}, bf16[640,128]{1,0:T(8,128)(2,1)}, u32[]{:S(2)}, u32[]{:S(2)}) collective-permute-start(bf16[640,128]{1,0:T(8,128)(2,1)} %get-tuple-element.250), channel_id=1, source_target_pairs={{0,1},{1,2},{2,3},{3,11},{11,10},{10,9},{9,8},{8,0},{4,5},{5,6},{6... | collective-permute-start | bytes 491528 | tf_op jit(solution)/shard_map/ppermute | solution.py:786
  551.9 17.9 %attention_backward.5 = (bf16[1280,384]{1,0:T(8,128)(2,1)}, bf16[10240,128]{1,0:T(8,128)(2,1)}) custom-call(s32[200]{0:T(256)S(1)} %select_n.160.lists, s32[5]{0:T(128)S(1)} %get-tuple-element.181.counts, bf16[1280,1152]{1,0:T(8,128)(2,1)} %bitcast.3.q_ref, bf16[1280,1152]{1,0:T(8,128)(2,1)} %bitcast.223, bf16[1280,1152]{1,0:T(8,128)(2,1)} %get-tuple-element.224.o_ref, ...), custom_call_target="tpu_custom_call" | custom-call | flops 25165824000 | bytes 10485760 | tf_op jit(solution)/shard_map/attention_backward/pallas_call | solution.py:412
  569.8 6.0 collective-permute-done.13
  577.9 31.5 %collective-permute-start.24 = (bf16[640,128]{1,0:T(8,128)(2,1)S(1)}, bf16[640,128]{1,0:T(8,128)(2,1)S(1)}, u32[]{:S(2)}, u32[]{:S(2)}) collective-permute-start(bf16[640,128]{1,0:T(8,128)(2,1)S(1)} %get-tuple-element.390), channel_id=1, source_target_pairs={{0,1},{1,2},{2,3},{3,11},{11,10},{10,9},{9,8},{8,0},{4,5},{5,6},{6... | collective-permute-start | bytes 491528 | tf_op jit(solution)/shard_map/ppermute | solution.py:786
  609.4 2.2 fusion.15
  611.6 15.5 %collective-permute-start.14 = (bf16[1280,128]{1,0:T(8,128)(2,1)}, bf16[1280,128]{1,0:T(8,128)(2,1)}, u32[]{:S(2)}, u32[]{:S(2)}) collective-permute-start(bf16[1280,128]{1,0:T(8,128)(2,1)} %get-tuple-element.254), channel_id=1, source_target_pairs={{0,1},{1,2},{2,3},{3,11},{11,10},{10,9},{9,8},{8,0},{4,5},{5,6},{6... | collective-permute-start | bytes 983048 | tf_op jit(solution)/shard_map/ppermute | solution.py:786
  629.8 11.7 %collective-permute-start.18 = (bf16[1280,128]{1,0:T(8,128)(2,1)}, bf16[1280,128]{1,0:T(8,128)(2,1)}, u32[]{:S(2)}, u32[]{:S(2)}) collective-permute-start(bf16[1280,128]{1,0:T(8,128)(2,1)} %pad_maximum_fusion.9), channel_id=1, source_target_pairs={{0,1},{1,2},{2,3},{3,11},{11,10},{10,9},{9,8},{8,0},{4,5},{5,6},{6... | collective-permute-start | bytes 983048 | tf_op jit(solution)/shard_map/ppermute | solution.py:786
  642.2 2.1 add_convert_fusion
  644.3 2.1 copy.105
  646.4 3.1 pad_maximum_fusion
  649.5 4.0 all-to-all-start.6
  655.0 2.1 collective-permute-start.26
  658.5 2.1 collective-permute-start.16
  667.7 2.1 collective-permute-start.28
  669.8 9.8 %collective-permute-done.20 = bf16[1280,128]{1,0:T(8,128)(2,1)S(1)} collective-permute-done((bf16[1280,128]{1,0:T(8,128)(2,1)S(1)}, bf16[1280,128]{1,0:T(8,128)(2,1)S(1)}, u32[]{:S(2)}, u32[]{:S(2)}) %collective-permute-start.20) | collective-permute-done | bytes 327712 | tf_op jit(solution)/shard_map/ppermute | solution.py:786
  686.6 3.6 collective-permute-done.29
  690.4 2.1 collective-permute-start.30
  693.6 3.6 collective-permute-done.23
  697.4 2.9 collective-permute-done.30
  700.2 2.6 collective-permute-done.31
  704.0 6.5 all_to_all.52.pair_ref
  710.5 4.3 all-to-all-start.8
  714.9 12.3 %joint_back.1 = (bf16[640,1920]{1,0:T(8,128)(2,1)}, bf16[4,640,288]{2,1,0:T(8,128)(2,1)}, f32[8,1152]{1,0:T(8,128)}) custom-call(bf16[2,640,1152]{2,1,0:T(8,128)(2,1)} %copy-done.5, bf16[2,640,384]{2,1,0:T(8,128)(2,1)} %all_to_all.52.pair_ref, f32[640,128]{1,0:T(8,128)} %get-tuple-element.433.cos_ref, f32[640,128]{1,0:T(8,128)} %get-tuple-element.434.sin_ref, ...), custom_call_target="tpu_custom_call" | custom-call | flops 2831155200 | bytes 16777216 | tf_op jit(solution)/shard_map/joint_back/pallas_call | solution.py:638
  729.3 4.6 all-to-all-done.8
  734.0 2.6 copy.116
  736.6 9.0 %gradient_parts.5 = bf16[4,4,288,512]{3,2,1,0:T(8,128)(2,1)} custom-call(bf16[640,1152]{1,0:T(8,128)(2,1)} %get-tuple-element.295.refs_0_, bf16[640,1920]{1,0:T(8,128)(2,1)} %get-tuple-element.296.refs_1_, f32[4,288,1]{2,1,0:T(8,128)} %reshape_squeeze.9.refs_2_), custom_call_target="tpu_custom_call" | custom-call | flops 3019898880 | bytes 4718592 | tf_op jit(solution)/shard_map/gradient_parts/pallas_call | solution.py:750
  763.3 4.3 collective-permute-done.34
  768.3 5.3 collective-permute-start.36
  773.6 2.4 copy.108
  776.0 3.7 all-to-all-start.9
  791.2 2.4 collective-permute-start.38
  795.9 11.4 %collective-permute-done.38 = bf16[288,512]{1,0:T(8,128)(2,1)S(1)} collective-permute-done((bf16[288,512]{1,0:T(8,128)(2,1)S(1)}, bf16[288,512]{1,0:T(8,128)(2,1)S(1)}, u32[]{:S(2)}, u32[]{:S(2)}) %collective-permute-start.38) | collective-permute-done | bytes 294944 | tf_op jit(solution)/shard_map/ppermute | solution.py:786
  813.1 4.4 collective-permute-done.40
  (282 shorter events, 103.2 us)
Async XLA Ops:
  7.2 62.7 %all-gather.3.cloned.1.call-start = ((), (), s32[]{:S(2)}) async-start(), calls=%async_computation.12 | async-start | bytes 5013504 | tf_op jit(solution)/shard_map/all_gather | solution.py:841
  7.9 293.8 %all-gather.5.cloned.1.call-start = ((), (), s32[]{:S(2)}) async-start(), calls=%async_computation.13 | async-start | bytes 26320896 | tf_op jit(solution)/shard_map/all_gather | solution.py:841
  16.2 32.3 %all-to-all-start = ((bf16[4,656,288]{1,2,0:T(8,128)(2,1)}), bf16[4,656,288]{1,2,0:T(8,128)(2,1)}, u32[]{:S(2)}, u32[]{:S(2)}) async-start(bf16[4,656,288]{1,2,0:T(8,128)(2,1)} %copy.96), calls=%async_computation | async-start | bytes 3538944 | tf_op jit(solution)/shard_map/all_to_all | solution.py:889
  87.4 45.7 %collective-permute-start = (bf16[1280,384]{1,0:T(8,128)(2,1)}, bf16[1280,384]{1,0:T(8,128)(2,1)}, u32[]{:S(2)}, u32[]{:S(2)}) collective-permute-start(bf16[1280,384]{1,0:T(8,128)(2,1)} %bitcast.2.refs_0_), channel_id=1, source_target_pairs={{0,1},{1,2},{2,3},{3,11},{11,10},{10,9},{9,8},{8,0},{4,5},{5,6},{6... | collective-permute-start | bytes 2949128 | tf_op jit(solution)/shard_map/ppermute | solution.py:916
  89.0 45.7 %collective-permute-start.2 = (bf16[1280,384]{1,0:T(8,128)(2,1)}, bf16[1280,384]{1,0:T(8,128)(2,1)}, u32[]{:S(2)}, u32[]{:S(2)}) collective-permute-start(bf16[1280,384]{1,0:T(8,128)(2,1)} %bitcast.2.refs_0_), channel_id=1, source_target_pairs={{1,0},{2,1},{3,2},{11,3},{10,11},{9,10},{8,9},{0,8},{5,4},{6,5},{7... | collective-permute-start | bytes 2949128 | tf_op jit(solution)/shard_map/ppermute | solution.py:916
  89.4 46.0 %all-to-all-start.2 = ((bf16[2,640,1152]{2,1,0:T(8,128)(2,1)}), bf16[2,640,1152]{2,1,0:T(8,128)(2,1)}, u32[]{:S(2)}, u32[]{:S(2)}) async-start(bf16[2,640,1152]{2,1,0:T(8,128)(2,1)} %get-tuple-element.185), calls=%async_computation.2 | async-start | bytes 5898240 | tf_op jit(solution)/shard_map/all_to_all | solution.py:889
  133.1 45.4 %collective-permute-start.1 = (bf16[1280,384]{1,0:T(8,128)(2,1)}, bf16[1280,384]{1,0:T(8,128)(2,1)}, u32[]{:S(2)}, u32[]{:S(2)}) collective-permute-start(bf16[1280,384]{1,0:T(8,128)(2,1)} %collective-permute-done.refs_2_.refs_8_), channel_id=1, source_target_pairs={{0,1},{1,2},{2,3},{3,11},{11,10},{10,9},{9,8},{8,0},{4,5},{5,6},{6... | collective-permute-start | bytes 2949128 | tf_op jit(solution)/shard_map/ppermute | solution.py:928
  134.7 45.6 %collective-permute-start.3 = (bf16[1280,384]{1,0:T(8,128)(2,1)}, bf16[1280,384]{1,0:T(8,128)(2,1)}, u32[]{:S(2)}, u32[]{:S(2)}) collective-permute-start(bf16[1280,384]{1,0:T(8,128)(2,1)} %collective-permute-done.2.refs_1_), channel_id=1, source_target_pairs={{1,0},{2,1},{3,2},{11,3},{10,11},{9,10},{8,9},{0,8},{5,4},{6,5},{7... | collective-permute-start | bytes 2949128 | tf_op jit(solution)/shard_map/ppermute | solution.py:928
  135.4 46.9 %copy-start.14 = (bf16[2560,288]{0,1:T(8,128)(2,1)S(1)}, bf16[2560,288]{0,1:T(8,128)(2,1)}, u32[]{:S(2)}) copy-start(bf16[2560,288]{0,1:T(8,128)(2,1)} %param.21) | copy-start | bytes 4423684
  180.3 46.0 %collective-permute-start.4 = (bf16[1280,384]{1,0:T(8,128)(2,1)}, bf16[1280,384]{1,0:T(8,128)(2,1)}, u32[]{:S(2)}, u32[]{:S(2)}) collective-permute-start(bf16[1280,384]{1,0:T(8,128)(2,1)} %collective-permute-done.1.refs_3_.refs_7_), channel_id=1, source_target_pairs={{0,1},{1,2},{2,3},{3,11},{11,10},{10,9},{9,8},{8,0},{4,5},{5,6},{6... | collective-permute-start | bytes 2949128 | tf_op jit(solution)/shard_map/ppermute | solution.py:928
  181.2 45.0 %collective-permute-start.5 = (bf16[1280,384]{1,0:T(8,128)(2,1)}, bf16[1280,384]{1,0:T(8,128)(2,1)}, u32[]{:S(2)}, u32[]{:S(2)}) collective-permute-start(bf16[1280,384]{1,0:T(8,128)(2,1)} %collective-permute-done.3.refs_2_), channel_id=1, source_target_pairs={{1,0},{2,1},{3,2},{11,3},{10,11},{9,10},{8,9},{0,8},{5,4},{6,5},{7... | collective-permute-start | bytes 2949128 | tf_op jit(solution)/shard_map/ppermute | solution.py:928
  183.6 94.3 %all-to-all-start.3 = ((bf16[4,640,288]{1,2,0:T(8,128)(2,1)}), bf16[4,640,288]{1,2,0:T(8,128)(2,1)}, u32[]{:S(2)}, u32[]{:S(2)}) async-start(bf16[4,640,288]{1,2,0:T(8,128)(2,1)} %bitcast.211), calls=%async_computation.3 | async-start | bytes 2949120 | tf_op jit(solution)/shard_map/all_to_all | solution.py:889
  227.4 50.5 %collective-permute-start.6 = (bf16[640,384]{1,0:T(8,128)(2,1)S(1)}, bf16[640,384]{1,0:T(8,128)(2,1)S(1)}, u32[]{:S(2)}, u32[]{:S(2)}) collective-permute-start(bf16[640,384]{1,0:T(8,128)(2,1)S(1)} %slice.405), channel_id=1, source_target_pairs={{0,1},{1,2},{2,3},{3,11},{11,10},{10,9},{9,8},{8,0},{4,5},{5,6},{6... | collective-permute-start | bytes 1474568 | tf_op jit(solution)/shard_map/ppermute | solution.py:930
  229.4 48.5 %collective-permute-start.7 = (bf16[640,384]{1,0:T(8,128)(2,1)S(1)}, bf16[640,384]{1,0:T(8,128)(2,1)S(1)}, u32[]{:S(2)}, u32[]{:S(2)}) collective-permute-start(bf16[640,384]{1,0:T(8,128)(2,1)S(1)} %slice.406), channel_id=1, source_target_pairs={{1,0},{2,1},{3,2},{11,3},{10,11},{9,10},{8,9},{0,8},{5,4},{6,5},{7... | collective-permute-start | bytes 1474568 | tf_op jit(solution)/shard_map/ppermute | solution.py:930
  277.9 15.9 %copy-start.29 = (bf16[640,384]{1,0:T(8,128)(2,1)}, bf16[640,384]{1,0:T(8,128)(2,1)S(1)}, u32[]{:S(2)}) copy-start(bf16[640,384]{1,0:T(8,128)(2,1)S(1)} %collective-permute-done.6.refs_2_.refs_4_) | copy-start | bytes 1474564
  277.9 15.9 %copy-start.31 = (bf16[640,384]{1,0:T(8,128)(2,1)}, bf16[640,384]{1,0:T(8,128)(2,1)S(1)}, u32[]{:S(2)}) copy-start(bf16[640,384]{1,0:T(8,128)(2,1)S(1)} %collective-permute-done.7.refs_3_.refs_5_) | copy-start | bytes 1474564
  293.9 138.1 %copy-start.23 = (f32[3,5,1,768]{3,2,1,0:T(1,128)}, f32[3,5,1,768]{3,2,1,0:T(1,128)S(1)}, u32[]{:S(2)}) copy-start(f32[3,5,1,768]{3,2,1,0:T(1,128)S(1)} %get-tuple-element.237.lse_ref) | copy-start | bytes 138244
  293.9 7.8 all-to-all-start.4
  297.8 406.2 %reduce-scatter.5.cloned.1.call-start = ((), (), s32[]{:S(2)}) async-start(), calls=%async_computation.14 | async-start | bytes 22560768 | tf_op jit(solution)/shard_map/reduce_scatter | solution.py:837
  385.5 12.4 %copy-start.8 = (bf16[10240,128]{1,0:T(8,128)(2,1)S(1)}, bf16[10240,128]{1,0:T(8,128)(2,1)}, u32[]{:S(2)}) copy-start(bf16[10240,128]{1,0:T(8,128)(2,1)} %copy-done.7) | copy-start | bytes 7864324
  385.5 12.4 %copy-start.30 = (bf16[640,384]{1,0:T(8,128)(2,1)S(1)}, bf16[640,384]{1,0:T(8,128)(2,1)}, u32[]{:S(2)}) copy-start(bf16[640,384]{1,0:T(8,128)(2,1)} %copy-done.29) | copy-start | bytes 1474564
  385.5 12.4 %copy-start.32 = (bf16[640,384]{1,0:T(8,128)(2,1)S(1)}, bf16[640,384]{1,0:T(8,128)(2,1)}, u32[]{:S(2)}) copy-start(bf16[640,384]{1,0:T(8,128)(2,1)} %copy-done.31) | copy-start | bytes 1474564
  417.4 40.4 %collective-permute-start.8 = (bf16[640,128]{1,0:T(8,128)(2,1)S(1)}, bf16[640,128]{1,0:T(8,128)(2,1)S(1)}, u32[]{:S(2)}, u32[]{:S(2)}) collective-permute-start(bf16[640,128]{1,0:T(8,128)(2,1)S(1)} %get-tuple-element.241), channel_id=1, source_target_pairs={{0,1},{1,2},{2,3},{3,11},{11,10},{10,9},{9,8},{8,0},{4,5},{5,6},{6... | collective-permute-start | bytes 491528 | tf_op jit(solution)/shard_map/ppermute | solution.py:786
  417.5 40.3 %collective-permute-start.9 = (bf16[640,128]{1,0:T(8,128)(2,1)S(1)}, bf16[640,128]{1,0:T(8,128)(2,1)S(1)}, u32[]{:S(2)}, u32[]{:S(2)}) collective-permute-start(bf16[640,128]{1,0:T(8,128)(2,1)S(1)} %get-tuple-element.242), channel_id=1, source_target_pairs={{1,0},{2,1},{3,2},{11,3},{10,11},{9,10},{8,9},{0,8},{5,4},{6,5},{7... | collective-permute-start | bytes 491528 | tf_op jit(solution)/shard_map/ppermute | solution.py:786
  460.9 115.0 %collective-permute-start.10 = (bf16[1280,128]{1,0:T(8,128)(2,1)S(1)}, bf16[1280,128]{1,0:T(8,128)(2,1)S(1)}, u32[]{:S(2)}, u32[]{:S(2)}) collective-permute-start(bf16[1280,128]{1,0:T(8,128)(2,1)S(1)} %pad_maximum_fusion.7), channel_id=1, source_target_pairs={{0,1},{1,2},{2,3},{3,11},{11,10},{10,9},{9,8},{8,0},{4,5},{5,6},{6... | collective-permute-start | bytes 983048 | tf_op jit(solution)/shard_map/ppermute | solution.py:786
  498.9 77.0 %collective-permute-start.11 = (bf16[1280,128]{1,0:T(8,128)(2,1)S(1)}, bf16[1280,128]{1,0:T(8,128)(2,1)}, u32[]{:S(2)}, u32[]{:S(2)}) collective-permute-start(bf16[1280,128]{1,0:T(8,128)(2,1)S(1)} %pad_maximum_fusion.8), channel_id=1, source_target_pairs={{1,0},{2,1},{3,2},{11,3},{10,11},{9,10},{8,9},{0,8},{5,4},{6,5},{7... | collective-permute-start | bytes 983048 | tf_op jit(solution)/shard_map/ppermute | solution.py:786
  498.9 70.9 %collective-permute-start.12 = (bf16[640,128]{1,0:T(8,128)(2,1)}, bf16[640,128]{1,0:T(8,128)(2,1)}, u32[]{:S(2)}, u32[]{:S(2)}) collective-permute-start(bf16[640,128]{1,0:T(8,128)(2,1)} %get-tuple-element.250), channel_id=1, source_target_pairs={{0,1},{1,2},{2,3},{3,11},{11,10},{10,9},{9,8},{8,0},{4,5},{5,6},{6... | collective-permute-start | bytes 491528 | tf_op jit(solution)/shard_map/ppermute | solution.py:786
  551.9 23.9 %collective-permute-start.13 = (bf16[640,128]{1,0:T(8,128)(2,1)S(1)}, bf16[640,128]{1,0:T(8,128)(2,1)}, u32[]{:S(2)}, u32[]{:S(2)}) collective-permute-start(bf16[640,128]{1,0:T(8,128)(2,1)S(1)} %get-tuple-element.251), channel_id=1, source_target_pairs={{1,0},{2,1},{3,2},{11,3},{10,11},{9,10},{8,9},{0,8},{5,4},{6,5},{7... | collective-permute-start | bytes 491528 | tf_op jit(solution)/shard_map/ppermute | solution.py:786
  575.8 66.4 %copy-start.4 = (f32[640,1152]{1,0:T(8,128)S(1)}, f32[640,1152]{1,0:T(8,128)}, u32[]{:S(2)}) copy-start(f32[640,1152]{1,0:T(8,128)} %get-tuple-element.234.hidden_ref) | copy-start | bytes 8847364
  577.9 63.6 %collective-permute-start.24 = (bf16[640,128]{1,0:T(8,128)(2,1)S(1)}, bf16[640,128]{1,0:T(8,128)(2,1)S(1)}, u32[]{:S(2)}, u32[]{:S(2)}) collective-permute-start(bf16[640,128]{1,0:T(8,128)(2,1)S(1)} %get-tuple-element.390), channel_id=1, source_target_pairs={{0,1},{1,2},{2,3},{3,11},{11,10},{10,9},{9,8},{8,0},{4,5},{5,6},{6... | collective-permute-start | bytes 491528 | tf_op jit(solution)/shard_map/ppermute | solution.py:786
  609.4 32.1 %collective-permute-start.25 = (bf16[640,128]{1,0:T(8,128)(2,1)S(1)}, bf16[640,128]{1,0:T(8,128)(2,1)S(1)}, u32[]{:S(2)}, u32[]{:S(2)}) collective-permute-start(bf16[640,128]{1,0:T(8,128)(2,1)S(1)} %get-tuple-element.389), channel_id=1, source_target_pairs={{1,0},{2,1},{3,2},{11,3},{10,11},{9,10},{8,9},{0,8},{5,4},{6,5},{7... | collective-permute-start | bytes 491528 | tf_op jit(solution)/shard_map/ppermute | solution.py:786
  611.6 45.5 %collective-permute-start.14 = (bf16[1280,128]{1,0:T(8,128)(2,1)}, bf16[1280,128]{1,0:T(8,128)(2,1)}, u32[]{:S(2)}, u32[]{:S(2)}) collective-permute-start(bf16[1280,128]{1,0:T(8,128)(2,1)} %get-tuple-element.254), channel_id=1, source_target_pairs={{0,1},{1,2},{2,3},{3,11},{11,10},{10,9},{9,8},{8,0},{4,5},{5,6},{6... | collective-permute-start | bytes 983048 | tf_op jit(solution)/shard_map/ppermute | solution.py:786
  627.0 30.0 %collective-permute-start.15 = (bf16[1280,128]{1,0:T(8,128)(2,1)}, bf16[1280,128]{1,0:T(8,128)(2,1)}, u32[]{:S(2)}, u32[]{:S(2)}) collective-permute-start(bf16[1280,128]{1,0:T(8,128)(2,1)} %get-tuple-element.255), channel_id=1, source_target_pairs={{1,0},{2,1},{3,2},{11,3},{10,11},{9,10},{8,9},{0,8},{5,4},{6,5},{7... | collective-permute-start | bytes 983048 | tf_op jit(solution)/shard_map/ppermute | solution.py:786
  629.8 30.8 %collective-permute-start.18 = (bf16[1280,128]{1,0:T(8,128)(2,1)}, bf16[1280,128]{1,0:T(8,128)(2,1)}, u32[]{:S(2)}, u32[]{:S(2)}) collective-permute-start(bf16[1280,128]{1,0:T(8,128)(2,1)} %pad_maximum_fusion.9), channel_id=1, source_target_pairs={{0,1},{1,2},{2,3},{3,11},{11,10},{10,9},{9,8},{8,0},{4,5},{5,6},{6... | collective-permute-start | bytes 983048 | tf_op jit(solution)/shard_map/ppermute | solution.py:786
  641.5 19.1 %collective-permute-start.19 = (bf16[1280,128]{1,0:T(8,128)(2,1)}, bf16[1280,128]{1,0:T(8,128)(2,1)}, u32[]{:S(2)}, u32[]{:S(2)}) collective-permute-start(bf16[1280,128]{1,0:T(8,128)(2,1)} %pad_maximum_fusion.10), channel_id=1, source_target_pairs={{1,0},{2,1},{3,2},{11,3},{10,11},{9,10},{8,9},{0,8},{5,4},{6,5},{7... | collective-permute-start | bytes 983048 | tf_op jit(solution)/shard_map/ppermute | solution.py:786
  649.5 54.5 %all-to-all-start.6 = ((bf16[2,640,1152]{2,1,0:T(8,128)(2,1)}), bf16[2,640,1152]{2,1,0:T(8,128)(2,1)S(1)}, u32[]{:S(2)}, u32[]{:S(2)}) async-start(bf16[2,640,1152]{2,1,0:T(8,128)(2,1)} %bitcast.209), calls=%async_computation.6 | async-start | bytes 5898240 | tf_op jit(solution)/shard_map/all_to_all | solution.py:889
  654.9 12.7 %copy-start.11 = (bf16[10240,128]{1,0:T(8,128)(2,1)S(1)}, bf16[10240,128]{1,0:T(8,128)(2,1)}, u32[]{:S(2)}) copy-start(bf16[10240,128]{1,0:T(8,128)(2,1)} %get-tuple-element.247) | copy-start | bytes 7864324
  655.0 10.6 %collective-permute-start.26 = (bf16[1280,128]{1,0:T(8,128)(2,1)S(1)}, bf16[1280,128]{1,0:T(8,128)(2,1)S(1)}, u32[]{:S(2)}, u32[]{:S(2)}) collective-permute-start(bf16[1280,128]{1,0:T(8,128)(2,1)S(1)} %pad_maximum_fusion.11), channel_id=1, source_target_pairs={{0,1},{1,2},{2,3},{3,11},{11,10},{10,9},{9,8},{8,0},{4,5},{5,6},{6... | collective-permute-start | bytes 983048 | tf_op jit(solution)/shard_map/ppermute | solution.py:786
  657.0 10.5 %collective-permute-start.27 = (bf16[1280,128]{1,0:T(8,128)(2,1)S(1)}, bf16[1280,128]{1,0:T(8,128)(2,1)S(1)}, u32[]{:S(2)}, u32[]{:S(2)}) collective-permute-start(bf16[1280,128]{1,0:T(8,128)(2,1)S(1)} %pad_maximum_fusion.12), channel_id=1, source_target_pairs={{1,0},{2,1},{3,2},{11,3},{10,11},{9,10},{8,9},{0,8},{5,4},{6,5},{7... | collective-permute-start | bytes 983048 | tf_op jit(solution)/shard_map/ppermute | solution.py:786
  658.5 24.9 %collective-permute-start.16 = (bf16[1280,128]{1,0:T(8,128)(2,1)S(1)}, bf16[1280,128]{1,0:T(8,128)(2,1)S(1)}, u32[]{:S(2)}, u32[]{:S(2)}) collective-permute-start(bf16[1280,128]{1,0:T(8,128)(2,1)S(1)} %get-tuple-element.256), channel_id=1, source_target_pairs={{0,1},{1,2},{2,3},{3,11},{11,10},{10,9},{9,8},{8,0},{4,5},{5,6},{6... | collective-permute-start | bytes 983048 | tf_op jit(solution)/shard_map/ppermute | solution.py:786
  660.6 22.9 %collective-permute-start.17 = (bf16[1280,128]{1,0:T(8,128)(2,1)S(1)}, bf16[1280,128]{1,0:T(8,128)(2,1)S(1)}, u32[]{:S(2)}, u32[]{:S(2)}) collective-permute-start(bf16[1280,128]{1,0:T(8,128)(2,1)S(1)} %get-tuple-element.257), channel_id=1, source_target_pairs={{1,0},{2,1},{3,2},{11,3},{10,11},{9,10},{8,9},{0,8},{5,4},{6,5},{7... | collective-permute-start | bytes 983048 | tf_op jit(solution)/shard_map/ppermute | solution.py:786
  661.9 17.7 %collective-permute-start.20 = (bf16[1280,128]{1,0:T(8,128)(2,1)S(1)}, bf16[1280,128]{1,0:T(8,128)(2,1)S(1)}, u32[]{:S(2)}, u32[]{:S(2)}) collective-permute-start(bf16[1280,128]{1,0:T(8,128)(2,1)S(1)} %get-tuple-element.262), channel_id=1, source_target_pairs={{0,1},{1,2},{2,3},{3,11},{11,10},{10,9},{9,8},{8,0},{4,5},{5,6},{6... | collective-permute-start | bytes 983048 | tf_op jit(solution)/shard_map/ppermute | solution.py:786
  665.5 15.6 %collective-permute-start.21 = (bf16[1280,128]{1,0:T(8,128)(2,1)S(1)}, bf16[1280,128]{1,0:T(8,128)(2,1)S(1)}, u32[]{:S(2)}, u32[]{:S(2)}) collective-permute-start(bf16[1280,128]{1,0:T(8,128)(2,1)S(1)} %get-tuple-element.263), channel_id=1, source_target_pairs={{1,0},{2,1},{3,2},{11,3},{10,11},{9,10},{8,9},{0,8},{5,4},{6,5},{7... | collective-permute-start | bytes 983048 | tf_op jit(solution)/shard_map/ppermute | solution.py:786
  667.7 18.9 %collective-permute-start.28 = (bf16[1280,128]{1,0:T(8,128)(2,1)S(1)}, bf16[1280,128]{1,0:T(8,128)(2,1)S(1)}, u32[]{:S(2)}, u32[]{:S(2)}) collective-permute-start(bf16[1280,128]{1,0:T(8,128)(2,1)S(1)} %get-tuple-element.275), channel_id=1, source_target_pairs={{0,1},{1,2},{2,3},{3,11},{11,10},{10,9},{9,8},{8,0},{4,5},{5,6},{6... | collective-permute-start | bytes 983048 | tf_op jit(solution)/shard_map/ppermute | solution.py:786
  679.6 10.6 %collective-permute-start.29 = (bf16[1280,128]{1,0:T(8,128)(2,1)S(1)}, bf16[1280,128]{1,0:T(8,128)(2,1)S(1)}, u32[]{:S(2)}, u32[]{:S(2)}) collective-permute-start(bf16[1280,128]{1,0:T(8,128)(2,1)S(1)} %get-tuple-element.276), channel_id=1, source_target_pairs={{1,0},{2,1},{3,2},{11,3},{10,11},{9,10},{8,9},{0,8},{5,4},{6,5},{7... | collective-permute-start | bytes 983048 | tf_op jit(solution)/shard_map/ppermute | solution.py:786
  681.4 12.3 %collective-permute-start.22 = (bf16[1280,128]{1,0:T(8,128)(2,1)S(1)}, bf16[1280,128]{1,0:T(8,128)(2,1)S(1)}, u32[]{:S(2)}, u32[]{:S(2)}) collective-permute-start(bf16[1280,128]{1,0:T(8,128)(2,1)S(1)} %get-tuple-element.264), channel_id=1, source_target_pairs={{0,1},{1,2},{2,3},{3,11},{11,10},{10,9},{9,8},{8,0},{4,5},{5,6},{6... | collective-permute-start | bytes 983048 | tf_op jit(solution)/shard_map/ppermute | solution.py:786
  683.4 13.9 %collective-permute-start.23 = (bf16[1280,128]{1,0:T(8,128)(2,1)S(1)}, bf16[1280,128]{1,0:T(8,128)(2,1)S(1)}, u32[]{:S(2)}, u32[]{:S(2)}) collective-permute-start(bf16[1280,128]{1,0:T(8,128)(2,1)S(1)} %get-tuple-element.265), channel_id=1, source_target_pairs={{1,0},{2,1},{3,2},{11,3},{10,11},{9,10},{8,9},{0,8},{5,4},{6,5},{7... | collective-permute-start | bytes 983048 | tf_op jit(solution)/shard_map/ppermute | solution.py:786
  690.4 9.8 %collective-permute-start.30 = (bf16[1280,128]{1,0:T(8,128)(2,1)S(1)}, bf16[1280,128]{1,0:T(8,128)(2,1)S(1)}, u32[]{:S(2)}, u32[]{:S(2)}) collective-permute-start(bf16[1280,128]{1,0:T(8,128)(2,1)S(1)} %get-tuple-element.277), channel_id=1, source_target_pairs={{0,1},{1,2},{2,3},{3,11},{11,10},{10,9},{9,8},{8,0},{4,5},{5,6},{6... | collective-permute-start | bytes 983048 | tf_op jit(solution)/shard_map/ppermute | solution.py:786
  692.5 10.3 %collective-permute-start.31 = (bf16[1280,128]{1,0:T(8,128)(2,1)S(1)}, bf16[1280,128]{1,0:T(8,128)(2,1)S(1)}, u32[]{:S(2)}, u32[]{:S(2)}) collective-permute-start(bf16[1280,128]{1,0:T(8,128)(2,1)S(1)} %get-tuple-element.278), channel_id=1, source_target_pairs={{1,0},{2,1},{3,2},{11,3},{10,11},{9,10},{8,9},{0,8},{5,4},{6,5},{7... | collective-permute-start | bytes 983048 | tf_op jit(solution)/shard_map/ppermute | solution.py:786
  710.5 23.4 %all-to-all-start.8 = ((bf16[4,640,288]{1,2,0:T(8,128)(2,1)}), bf16[4,640,288]{1,2,0:T(8,128)(2,1)}, u32[]{:S(2)}, u32[]{:S(2)}) async-start(bf16[4,640,288]{1,2,0:T(8,128)(2,1)} %bitcast.210), calls=%async_computation.9 | async-start | bytes 2949120 | tf_op jit(solution)/shard_map/all_to_all | solution.py:889
  714.9 106.5 %reduce-scatter.7.cloned.1.call-start = ((), (), s32[]{:S(2)}) async-start(), calls=%async_computation.15 | async-start | bytes 3760128
  747.6 13.3 %collective-permute-start.32 = (bf16[8,288,512]{2,1,0:T(8,128)(2,1)S(1)}, bf16[8,288,512]{2,1,0:T(8,128)(2,1)}, u32[]{:S(2)}, u32[]{:S(2)}) collective-permute-start(bf16[8,288,512]{2,1,0:T(8,128)(2,1)S(1)} %dynamic-slice_bitcast_fusion), channel_id=1, source_target_pairs={{0,4},{4,0},{1,5},{5,1},{2,6},{6,2},{3,7},{7,3},{8,12},{12,8},{9,1... | collective-permute-start | bytes 7077896 | tf_op jit(solution)/shard_map/ppermute | solution.py:989
  751.3 1.8 collective-permute-start.33
  754.8 7.6 collective-permute-start.35
  759.1 8.4 %collective-permute-start.34 = (bf16[144,512]{1,0:T(8,128)(2,1)}, bf16[144,512]{1,0:T(8,128)(2,1)S(1)}, u32[]{:S(2)}, u32[]{:S(2)}) collective-permute-start(bf16[144,512]{1,0:T(8,128)(2,1)} %get-tuple-element.298), channel_id=1, source_target_pairs={{0,1},{1,2},{2,3},{3,11},{11,10},{10,9},{9,8},{8,0},{4,5},{5,6},{6... | collective-permute-start | bytes 442376 | tf_op jit(solution)/shard_map/ppermute | solution.py:786
  760.9 12.7 %copy-start.12 = (bf16[4,640,288]{2,1,0:T(8,128)(2,1)S(1)}, bf16[4,640,288]{2,1,0:T(8,128)(2,1)}, u32[]{:S(2)}) copy-start(bf16[4,640,288]{2,1,0:T(8,128)(2,1)} %get-tuple-element.294) | copy-start | bytes 4423684
  768.3 21.2 %collective-permute-start.36 = (bf16[288,512]{1,0:T(8,128)(2,1)}, bf16[288,512]{1,0:T(8,128)(2,1)}, u32[]{:S(2)}, u32[]{:S(2)}) collective-permute-start(bf16[288,512]{1,0:T(8,128)(2,1)} %pad_maximum_fusion.13), channel_id=1, source_target_pairs={{0,1},{1,2},{2,3},{3,11},{11,10},{10,9},{9,8},{8,0},{4,5},{5,6},{6... | collective-permute-start | bytes 884744 | tf_op jit(solution)/shard_map/ppermute | solution.py:786
  773.6 16.0 %collective-permute-start.37 = (bf16[288,512]{1,0:T(8,128)(2,1)}, bf16[288,512]{1,0:T(8,128)(2,1)}, u32[]{:S(2)}, u32[]{:S(2)}) collective-permute-start(bf16[288,512]{1,0:T(8,128)(2,1)} %pad_maximum_fusion.14), channel_id=1, source_target_pairs={{1,0},{2,1},{3,2},{11,3},{10,11},{9,10},{8,9},{0,8},{5,4},{6,5},{7... | collective-permute-start | bytes 884744 | tf_op jit(solution)/shard_map/ppermute | solution.py:786
  773.6 15.8 %copy-start.9 = (bf16[288,2304]{1,0:T(8,128)(2,1)S(1)}, bf16[288,2304]{1,0:T(8,128)(2,1)}, u32[]{:S(2)}) copy-start(bf16[288,2304]{1,0:T(8,128)(2,1)} %reduce-scatter.5.cloned.1.call-done) | copy-start | bytes 3981316
  776.0 35.0 %all-to-all-start.9 = ((bf16[4,640,288]{1,2,0:T(8,128)(2,1)}), bf16[4,640,288]{1,2,0:T(8,128)(2,1)S(1)}, u32[]{:S(2)}, u32[]{:S(2)}) async-start(bf16[4,640,288]{1,2,0:T(8,128)(2,1)} %copy.108), calls=%async_computation.10 | async-start | bytes 2949120 | tf_op jit(solution)/shard_map/all_to_all | solution.py:889
  791.2 16.2 %collective-permute-start.38 = (bf16[288,512]{1,0:T(8,128)(2,1)S(1)}, bf16[288,512]{1,0:T(8,128)(2,1)S(1)}, u32[]{:S(2)}, u32[]{:S(2)}) collective-permute-start(bf16[288,512]{1,0:T(8,128)(2,1)S(1)} %get-tuple-element.302), channel_id=1, source_target_pairs={{0,1},{1,2},{2,3},{3,11},{11,10},{10,9},{9,8},{8,0},{4,5},{5,6},{6... | collective-permute-start | bytes 884744 | tf_op jit(solution)/shard_map/ppermute | solution.py:786
  793.6 13.7 %collective-permute-start.39 = (bf16[288,512]{1,0:T(8,128)(2,1)S(1)}, bf16[288,512]{1,0:T(8,128)(2,1)S(1)}, u32[]{:S(2)}, u32[]{:S(2)}) collective-permute-start(bf16[288,512]{1,0:T(8,128)(2,1)S(1)} %get-tuple-element.303), channel_id=1, source_target_pairs={{1,0},{2,1},{3,2},{11,3},{10,11},{9,10},{8,9},{0,8},{5,4},{6,5},{7... | collective-permute-start | bytes 884744 | tf_op jit(solution)/shard_map/ppermute | solution.py:786
  808.8 8.6 %collective-permute-start.40 = (bf16[288,512]{1,0:T(8,128)(2,1)S(1)}, bf16[288,512]{1,0:T(8,128)(2,1)S(1)}, u32[]{:S(2)}, u32[]{:S(2)}) collective-permute-start(bf16[288,512]{1,0:T(8,128)(2,1)S(1)} %get-tuple-element.304), channel_id=1, source_target_pairs={{0,1},{1,2},{2,3},{3,11},{11,10},{10,9},{9,8},{8,0},{4,5},{5,6},{6... | collective-permute-start | bytes 884744 | tf_op jit(solution)/shard_map/ppermute | solution.py:786
  809.2 10.2 %collective-permute-start.41 = (bf16[288,512]{1,0:T(8,128)(2,1)S(1)}, bf16[288,512]{1,0:T(8,128)(2,1)S(1)}, u32[]{:S(2)}, u32[]{:S(2)}) collective-permute-start(bf16[288,512]{1,0:T(8,128)(2,1)S(1)} %get-tuple-element.305), channel_id=1, source_target_pairs={{1,0},{2,1},{3,2},{11,3},{10,11},{9,10},{8,9},{0,8},{5,4},{6,5},{7... | collective-permute-start | bytes 884744 | tf_op jit(solution)/shard_map/ppermute | solution.py:786
  (23 other events, 77.3 us)
Sparse Core Ops, SparseCore 0:
  10.3 59.5 all-gather.2
  71.4 214.6 all-gather.4
  374.2 241.0 reduce-scatter.4
  729.5 86.3 reduce-scatter.6

commit v5 on v4

--- a/solution.py
+++ b/solution.py
@@ -21,6 +21,7 @@
 BIG = 2.0**30
 LOG2E = 1.4426950408889634
 UNROLL = 8
+DOWN_STEPS = 2
 BF16 = jnp.bfloat16
 F32 = jnp.float32
 NT = (((1,), (1,)), ((), ()))
@@ -648,7 +649,17 @@
     )(queries, pairs, cosines, sines, full, x, gains, hidden_back)
 
 
-def feed_kernel(normed_ref, back_ref, gate_ref, up_ref, down_ref, mixed_ref, gate_back_ref, up_back_ref, out_ref, normed_back_ref):
+def feed_kernel(
+    places, normed_ref, back_ref, gate_ref, up_ref, *refs
+):
+    mine, others = refs[:2], refs[2:4]
+    mixed_ref, gate_back_ref, up_back_ref, out_ref, normed_back_ref, down_ref = refs[4:]
+    core = places[places.shape[0] - 1]
+    features = mine[0].shape[1]
+    for high in range(2):
+        for block, row in ((mine[high], 2 * high + core), (others[high], 2 * high + 1 - core)):
+            down_ref[pl.ds(pl.multiple_of(row * features, 32), features), :] = block[0]
+
     @pl.when(pl.program_id(0) == 0)
     def _():
         out_ref[...] = jnp.zeros(out_ref.shape, F32)
@@ -656,7 +667,7 @@
 
     gate = dg(normed_ref[...], gate_ref[0], NN)
     up_value = dg(normed_ref[...], up_ref[0], NN)
-    mixed_back = dg(back_ref[...], down_ref[0], NN)
+    mixed_back = dg(back_ref[...], down_ref[...], NN)
     sigmoid = jax.nn.sigmoid(gate)
     silu = gate * sigmoid
     mixed = (silu * up_value).astype(BF16)
@@ -665,28 +676,33 @@
     mixed_ref[...] = mixed
     gate_back_ref[...] = gate_back
     up_back_ref[...] = up_back
-    out_ref[...] += dg(mixed, down_ref[0], NT)
+    out_ref[...] += dg(mixed, down_ref[...], NT)
     normed_back_ref[...] += dg(gate_back, gate_ref[0], NT) + dg(up_back, up_ref[0], NT)
 
 
-def feed_forward(normed, back, late, width):
+def feed_forward(places, normed, back, late, mine, others):
     tokens = normed.shape[0]
-    columns = late.shape[0]
-    whole = pl.BlockSpec((tokens, D), lambda c: (0, 0))
-    blocks = [pl.BlockSpec((1, D, width), lambda c, k=k: (c, 0, k)) for k in range(3)]
-    out = pl.BlockSpec((tokens, width), lambda c: (0, c))
+    columns, (_, features, width) = late.shape[0], mine.shape
+    whole = pl.BlockSpec((tokens, D), lambda c, places: (0, 0))
+    blocks = [pl.BlockSpec((1, D, width), lambda c, places, k=k: (c, 0, k)) for k in range(2)]
+    downs = [pl.BlockSpec((1, features, width), lambda c, places, h=h: (places[2 * c + h], 0, 0)) for h in range(2)]
+    out = pl.BlockSpec((tokens, width), lambda c, places: (0, c))
     return pl.pallas_call(
         feed_kernel,
-        grid=(columns,),
-        in_specs=[whole, whole, *blocks],
-        out_specs=[out, out, out, whole, whole],
+        grid_spec=pltpu.PrefetchScalarGridSpec(
+            num_scalar_prefetch=1,
+            grid=(columns,),
+            in_specs=[whole, whole, *blocks, *downs, *downs],
+            out_specs=[out, out, out, whole, whole],
+            scratch_shapes=[pltpu.VMEM((D, width), BF16)],
+        ),
         out_shape=[jax.ShapeDtypeStruct((tokens, columns * width), BF16)] * 3 + [jax.ShapeDtypeStruct((tokens, D), F32)] * 2,
         compiler_params=pltpu.CompilerParams(vmem_limit_bytes=62 * 2**20),
         cost_estimate=pl.CostEstimate(
             flops=12 * tokens * D * columns * width, bytes_accessed=6 * D * columns * width, transcendentals=0
         ),
         name="feed_forward",
-    )(normed, back, late, late, late)
+    )(places, normed, back, late, late, mine, mine, others, others)
 
 
 def gradient_kernel(counts, blocked, summed, *refs):
@@ -902,17 +918,36 @@
     plans += [plan((s, s + 1), (chips - s, chips - s + 1)) for s in range(2, columns)]
     plans += [plan((columns, columns + 1))]
     (marks, lists, counts, plans), extended = lax.optimization_barrier(((marks, lists, counts, plans), extended))
+    ahead, behind = ring_steps(columns)
+    down_own = down_weight.T
+    down_next, down_last = lax.ppermute(down_own, RING, ahead), lax.ppermute(down_own, RING, behind)
+    down_fronts, down_backs = [], []
+
+    def down_step(beside):
+        nonlocal down_next, down_last
+        beside, down_next, down_last = lax.optimization_barrier((beside, down_next, down_last))
+        down_fronts.append(down_next)
+        down_backs.append(down_last)
+        if len(down_fronts) < columns - 1:
+            down_next, down_last = lax.ppermute(down_next, RING, ahead), lax.ppermute(down_last, RING, behind)
+        else:
+            half = down_own.shape[0] // 2
+            down_next = lax.ppermute(down_next[:half], RING, ahead)
+            down_last = lax.ppermute(down_last[half:], RING, behind)
+        return beside
+
+    while len(down_fronts) < DOWN_STEPS:
+        extended = down_step(extended)
     x, normed_one, joint_full, packed, value, gains = project_in(extended, joint_blocks, cosines, sines, bars)
     value, packed = lax.optimization_barrier((exchange(value, "core").reshape(held, -1), packed))
     packed = exchange(packed, "core").reshape(held, -1)
     width = gate_weight.shape[1]
     unit = width // 2 if width % 256 == 0 else width
     padding = jnp.zeros((output_weight.shape[1], -output_weight.shape[0] % unit), BF16)
-    late = jnp.concatenate([gate_weight, up_weight, down_weight.T, output_weight.T, padding], axis=1)
+    late = jnp.concatenate([gate_weight, up_weight, output_weight.T, padding], axis=1)
     late = gather(late, ALL_COL).reshape(columns, D, -1)
     pieces = []
     state = None
-    ahead, behind = ring_steps(columns)
     to_next, to_last = lax.ppermute(value, RING, ahead), lax.ppermute(value, RING, behind)
     fronts, backs = [], []
 
@@ -930,10 +965,16 @@
             further = (lax.ppermute(to_next[:middle], RING, ahead), lax.ppermute(to_last[middle:], RING, behind))
         some = [value, to_last, to_next] if step == 1 else [to_last, to_next]
         if step == 1:
+            while len(down_fronts) < columns - 1:
+                to_next = down_step(to_next)
             cotangent, further = lax.optimization_barrier((cotangent, further))
             upstream = exchange(cotangent.reshape(rows, own, -1), ROW).transpose(1, 0, 2).reshape(own, D)
         state = attend(state, plans[step - 1], some, False)
         state, further = lax.optimization_barrier((state, further))
+        if step == 1:
+            down_mine = jnp.concatenate([down_own, *down_backs, down_next, down_last, *reversed(down_fronts)])
+            down_mine, further = lax.optimization_barrier((down_mine.reshape(chips, *down_own.shape), further))
+            down_others = lax.ppermute(down_mine, "core", [(0, 1), (1, 0)])
         to_next, to_last = further
     pieces = [value, *backs, to_next, to_last, *reversed(fronts)]
     upstream, state = lax.optimization_barrier((upstream, state))
@@ -945,16 +986,20 @@
     )
     attended_rows = exchange(attended.reshape(cores, own, -1), "core")
 
-    attended_rows, hidden, normed_two, output_full = project_out(attended_rows, late, x, gains, ATT // columns, late.shape[2] - 3 * width)
-    mixed, gate_back, up_back, feed_out, normed_two_back = feed_forward(normed_two, upstream, late, width)
-
+    steps = jnp.arange(chips, dtype=jnp.int32)
+    away = jnp.where(steps % 2 == 0, steps // 2, chips - 1 - steps // 2) - spot
+    down_places = jnp.concatenate([lax.rem(away + chips, chips), jnp.reshape(core, (1,))]).astype(jnp.int32)
+    attended_rows, hidden, normed_two, output_full = project_out(attended_rows, late, x, gains, ATT // columns, late.shape[2] - 2 * width)
+    mixed, gate_back, up_back, feed_out, normed_two_back = feed_forward(down_places, normed_two, upstream, late, down_mine, down_others)
+
+    hidden_back, hidden_low, heads_back, gain_two_part = output_back(normed_two_back, hidden, upstream, gains, output_full)
+    heads_back, mixed = lax.optimization_barrier((heads_back, mixed))
+    heads_back = exchange(heads_back, "core").reshape(held, -1)
     feed_parts = gradient_parts(columns, rows, None, (normed_two, [gate_back, up_back]), (upstream, [mixed]))
-    feed_parts, normed_two_back = lax.optimization_barrier((feed_parts, normed_two_back))
+    feed_parts, heads_back = lax.optimization_barrier((feed_parts, heads_back))
     feed_summed = scatter(feed_parts.reshape(-1, feed_parts.shape[3]), ALL_COL)
-    hidden_back, hidden_low, heads_back, gain_two_part = output_back(normed_two_back, hidden, upstream, gains, output_full)
     output_parts = gradient_parts(columns, rows, gain_two_part[0], (hidden_low, [attended_rows]))
 
-    heads_back = exchange(heads_back, "core").reshape(held, -1)
     query_backs, pair_rings = [], []
     for g in range(groups):
         heads_back = depart(heads_back, pair_rings)

time: 840 us -> 856 us (1.019)
  starting transfers between devices: 229 us -> 257 us
  waiting for transfers between devices: 203 us -> 187 us
  local copies, waits for them, and re-layouts: 60 us -> 74.8 us
  blocking collectives: 25.5 us -> 13 us
    ppermute x0 -> x9, waiting for transfers between devices: none -> 67.6 us  [the longest x2 61.6 us: down_step(): lax.ppermute(down_next, RING, ahead)]
    ppermute x1, waiting for transfers between devices: 38.5 us -> 0.01 us  [per_device(): lax.ppermute(value, RING, ahead)]
    ppermute x1, waiting for transfers between devices: 31.4 us -> 0.01 us  [per_device(): lax.ppermute(to_next[:middle], RING, ahead)]
    ppermute x2, waiting for transfers between devices: 39 us -> 18.5 us  [per_device(): lax.ppermute(to_next, RING, ahead)]
    ppermute x16, waiting for transfers between devices: 20.9 us -> 38.6 us  [launch(): lax.ppermute(back, RING, self.behind)]
    all_gather x2, waiting for transfers between devices: 17.4 us -> 0.01 us  [gather(): return lax.all_gather(value, axes, axis=0, tiled=True)]
    ppermute x16, starting transfers between devices: 172 us -> 185 us  [launch(): lax.ppermute(out, RING, self.ahead)]
    all_to_all x3 -> x2, blocking collectives: 25.5 us -> 13 us  [exchange(): return lax.all_to_all(value, axes, split_axis=0, concat_axis=0, tiled=True)]
  transfers between devices with their start and end apart: 53 -> 63, of which waited for: 24 -> 27; matrix products, arithmetic and copies ran while one was open for 11% -> 12% of each run, Pallas kernels for 20% -> 23%
where the time goes in v5:
time: 856 us; the launch traced here: 850 us
  starting transfers between devices  257 us (30%)
  Pallas kernels  243 us (28%)
  waiting for transfers between devices  187 us (22%)
  local copies, waits for them, and re-layouts  74.8 us (9%)
  other arithmetic  44.2 us (5%)
  between operations  31.1 us (4%)
  blocking collectives  13 us (2%)
    ppermute x16, starting transfers between devices, launch(): lax.ppermute(out, RING, self.ahead)  185 us
    pallas_call x4, Pallas kernels, attention_stage(): pl.pallas_call(functools.partial(stage_kernel, state is None, ends), grid...  63.9 us
    ppermute x2, waiting for transfers between devices, down_step(): lax.ppermute(down_next, RING, ahead)  61.6 us
    pallas_call x3, Pallas kernels, attention_backward(): pl.pallas_call(functools.partial(backward_kernel, group), grid_spec=pltpu...  55 us
    pallas_call x1, Pallas kernels, feed_forward(): pl.pallas_call(feed_kernel, grid_spec=pltpu.PrefetchScalarGridSpec(num_sc...  42.4 us
    pallas_call x3, Pallas kernels, gradient_parts(): pl.pallas_call(functools.partial(gradient_kernel, [len(rights) for _, rig...  40.9 us
    ppermute x16, waiting for transfers between devices, launch(): lax.ppermute(back, RING, self.behind)  38.6 us
    ppermute x16, waiting for transfers between devices, launch(): lax.ppermute(out, RING, self.ahead)  38.2 us
  transfers between devices with their start and end apart: 63, of which 27 were waited for; matrix products, arithmetic and copies ran while one was open for 12% of the time, Pallas kernels for 23%

profile of v5, /device:TPU:0, one launch (start us, length us, event | category | flops | bytes accessed | tf_op | source)
XLA Modules:
  0.0 850.3 jit_solution(7639910557157171664)
XLA Ops:
  9.1 3.2 concatenate.84
  12.3 3.1 collective-permute-start
  18.4 4.4 all-to-all-start
  28.7 4.7 compare_and_fusion
  37.9 14.7 %all-to-all-done = bf16[4,656,288]{1,2,0:T(8,128)(2,1)} async-done(((bf16[4,656,288]{1,2,0:T(8,128)(2,1)}), bf16[4,656,288]{1,2,0:T(8,128)(2,1)}, u32[]{:S(2)}, u32[]{:S(2)}) %all-to-all-start) | async-done | bytes 1511456 | tf_op jit(solution)/shard_map/all_to_all | solution.py:905
  52.6 2.8 collective-permute-start.3
  58.0 12.0 %collective-permute-done.2 = bf16[288,768]{1,0:T(8,128)(2,1)} collective-permute-done((bf16[288,768]{1,0:T(8,128)(2,1)}, bf16[288,768]{1,0:T(8,128)(2,1)}, u32[]{:S(2)}, u32[]{:S(2)}) %collective-permute-start.2) | collective-permute-done | bytes 442400 | tf_op jit(solution)/shard_map/ppermute | solution.py:932
  70.1 3.6 collective-permute-done.3
  73.7 3.9 copy.99.x4_ref
  77.6 11.1 %project_in.1 = (bf16[640,1152]{1,0:T(8,128)(2,1)}, bf16[640,1152]{1,0:T(8,128)(2,1)}, bf16[1152,1920]{1,0:T(8,128)(2,1)}, bf16[2,640,1152]{2,1,0:T(8,128)(2,1)}...) custom-call(bf16[4,656,288]{2,1,0:T(8,128)(2,1)} %copy.99.x4_ref, bf16[4,1152,480]{2,1,0:T(8,128)(2,1)} %bitcast.247, ...), custom_call_target="tpu_custom_call" | custom-call | flops 2831155200 | bytes 16777216 | tf_op jit(solution)/shard_map/project_in/pallas_call | solution.py:512
  88.7 6.5 all_to_all.50
  95.2 3.3 collective-permute-start.4
  106.0 5.2 all-to-all-start.2
  111.2 49.6 %collective-permute-done.8 = bf16[288,768]{1,0:T(8,128)(2,1)S(1)} collective-permute-done((bf16[288,768]{1,0:T(8,128)(2,1)}, bf16[288,768]{1,0:T(8,128)(2,1)S(1)}, u32[]{:S(2)}, u32[]{:S(2)}) %collective-permute-start.8) | collective-permute-done | bytes 442400 | tf_op jit(solution)/shard_map/ppermute | solution.py:932
  160.8 2.4 collective-permute-done.9
  169.5 25.1 %attention_stage.4 = (f32[3,5,80,768]{3,2,1,0:T(8,128)S(1)}, f32[3,5,1,768]{3,2,1,0:T(1,128)S(1)}) custom-call(s32[75]{0:T(128)S(1)} %select_n.178.lists, s32[5]{0:T(128)S(1)} %get-tuple-element.215.counts, bf16[1280,1152]{1,0:T(8,128)(2,1)} %bitcast.4.q_ref, bf16[3840,128]{1,0:T(8,128)(2,1)S(1)} %pad_maximum_fusion.1.mark_ref, ...), custom_call_target="tpu_custom_call" | custom-call | flops 11324620800 | bytes 5898240 | tf_op jit(solution)/shard_map/attention_stage/pallas_call | solution.py:324
  203.7 15.0 %collective-permute-done.5.refs_3_.refs_7_ = bf16[1280,384]{1,0:T(8,128)(2,1)} collective-permute-done((bf16[1280,384]{1,0:T(8,128)(2,1)}, bf16[1280,384]{1,0:T(8,128)(2,1)}, u32[]{:S(2)}, u32[]{:S(2)}) %collective-permute-start.5) | collective-permute-done | bytes 983072 | tf_op jit(solution)/shard_map/ppermute | solution.py:963
  218.7 2.5 collective-permute-done.7.refs_2_
  225.2 4.8 all-to-all-start.3
  232.1 13.4 %attention_stage.5 = (f32[3,5,80,768]{3,2,1,0:T(8,128)S(1)}, f32[3,5,1,768]{3,2,1,0:T(1,128)S(1)}) custom-call(s32[50]{0:T(128)S(1)} %select_n.182.lists, s32[5]{0:T(128)S(1)} %get-tuple-element.212.counts, bf16[1280,1152]{1,0:T(8,128)(2,1)} %bitcast.4.q_ref, bf16[2560,128]{1,0:T(8,128)(2,1)S(1)} %pad_maximum_fusion.3.mark_ref, ...), custom_call_target="tpu_custom_call" | custom-call | flops 7549747200 | bytes 3932160 | tf_op jit(solution)/shard_map/attention_stage/pallas_call | solution.py:324
  245.5 3.4 collective-permute-done.12.refs_3_.refs_6_
  250.0 10.7 %collective-permute-start.14 = (bf16[640,384]{1,0:T(8,128)(2,1)S(1)}, bf16[640,384]{1,0:T(8,128)(2,1)S(1)}, u32[]{:S(2)}, u32[]{:S(2)}) collective-permute-start(bf16[640,384]{1,0:T(8,128)(2,1)S(1)} %slice.413), channel_id=1, source_target_pairs={{0,1},{1,2},{2,3},{3,11},{11,10},{10,9},{9,8},{8,0},{4,5},{5,6},{6... | collective-permute-start | bytes 1474568 | tf_op jit(solution)/shard_map/ppermute | solution.py:965
  261.9 13.4 %attention_stage.6 = (f32[3,5,80,768]{3,2,1,0:T(8,128)S(1)}, f32[3,5,1,768]{3,2,1,0:T(1,128)S(1)}) custom-call(s32[50]{0:T(128)S(1)} %select_n.186.lists, s32[5]{0:T(128)S(1)} %get-tuple-element.209.counts, bf16[1280,1152]{1,0:T(8,128)(2,1)} %bitcast.4.q_ref, bf16[2560,128]{1,0:T(8,128)(2,1)S(1)} %pad_maximum_fusion.4.mark_ref, ...), custom_call_target="tpu_custom_call" | custom-call | flops 7549747200 | bytes 3932160 | tf_op jit(solution)/shard_map/attention_stage/pallas_call | solution.py:324
  277.2 2.4 copy-done.1
  279.5 12.1 %attention_stage.7 = (bf16[1280,1152]{1,0:T(8,128)(2,1)}, f32[3,5,1,768]{3,2,1,0:T(1,128)S(1)}) custom-call(s32[25]{0:T(128)S(1)} %select_n.190.lists, s32[5]{0:T(128)S(1)} %get-tuple-element.204.counts, bf16[1280,1152]{1,0:T(8,128)(2,1)} %bitcast.4.q_ref, bf16[1280,128]{1,0:T(8,128)(2,1)S(1)} %get-tuple-element.205.mark_ref, ...), custom_call_target="tpu_custom_call" | custom-call | flops 3774873600 | bytes 1966080 | tf_op jit(solution)/shard_map/attention_stage/pallas_call | solution.py:324
  293.0 4.1 all-to-all-start.4
  297.1 3.6 copy.102.back_ref.upstream_ref.refs_3_
  302.3 8.4 project_out.1
  310.7 42.4 %feed_forward.1 = (bf16[640,3072]{1,0:T(8,128)(2,1)}, bf16[640,3072]{1,0:T(8,128)(2,1)}, bf16[640,3072]{1,0:T(8,128)(2,1)}, f32[640,1152]{1,0:T(8,128)}, f32[640,1152]{1,0:T(8,128)}) custom-call(s32[9]{0:T(128)} %pad_add_fusion.3.places, bf16[640,1152]{1,0:T(8,128)(2,1)} %get-tuple-element.250.normed_ref.refs_0_, ...), custom_call_target="tpu_custom_call" | custom-call | flops 27179089920 | bytes 21233664 | tf_op jit(solution)/shard_map/feed_forward/pallas_call | solution.py:690
  353.1 9.3 %output_back.1 = (f32[640,1152]{1,0:T(8,128)}, bf16[640,1152]{1,0:T(8,128)(2,1)}, bf16[2,640,1152]{2,1,0:T(8,128)(2,1)}, f32[8,1152]{1,0:T(8,128)}) custom-call(f32[640,1152]{1,0:T(8,128)} %get-tuple-element.255.back_ref, f32[640,1152]{1,0:T(8,128)} %get-tuple-element.256.hidden_ref, bf16[640,1152]{1,0:T(8,128)(2,1)} %copy.102.back_ref.upstream_ref.refs_3_, ...), custom_call_target="tpu_custom_call" | custom-call | flops 1698693120 | bytes 16777216 | tf_op jit(solution)/shard_map/output_back/pallas_call | solution.py:590
  362.4 3.9 all-to-all-start.5
  366.4 23.5 %gradient_parts.3 = bf16[4,4,288,2304]{3,2,1,0:T(8,128)(2,1)} custom-call(bf16[640,1152]{1,0:T(8,128)(2,1)} %get-tuple-element.250.normed_ref.refs_0_, bf16[640,3072]{1,0:T(8,128)(2,1)} %get-tuple-element.253.refs_1_, bf16[640,3072]{1,0:T(8,128)(2,1)} %get-tuple-element.254.refs_2_, bf16[640,1152]{1,0:T(8,128)(2,1)} %copy.102.back_ref.upstream_ref.refs_3_, ...), custom_call_target="tpu_custom_call" | custom-call | flops 13589544960 | bytes 21233664 | tf_op jit(solution)/shard_map/gradient_parts/pallas_call | solution.py:766
  393.7 18.1 %attention_backward.3 = (bf16[1280,384]{1,0:T(8,128)(2,1)}, bf16[10240,128]{1,0:T(8,128)(2,1)}) custom-call(s32[200]{0:T(256)S(1)} %select_n.174.lists, s32[5]{0:T(128)S(1)} %get-tuple-element.194.counts, bf16[1280,1152]{1,0:T(8,128)(2,1)} %bitcast.4.q_ref, bf16[1280,1152]{1,0:T(8,128)(2,1)} %bitcast.223, bf16[1280,1152]{1,0:T(8,128)(2,1)} %get-tuple-element.247.o_ref, ...), custom_call_target="tpu_custom_call" | custom-call | flops 25165824000 | bytes 10485760 | tf_op jit(solution)/shard_map/attention_backward/pallas_call | solution.py:413
  413.0 27.7 %collective-permute-start.17 = (bf16[640,128]{1,0:T(8,128)(2,1)S(1)}, bf16[640,128]{1,0:T(8,128)(2,1)S(1)}, u32[]{:S(2)}, u32[]{:S(2)}) collective-permute-start(bf16[640,128]{1,0:T(8,128)(2,1)S(1)} %get-tuple-element.267), channel_id=1, source_target_pairs={{0,1},{1,2},{2,3},{3,11},{11,10},{10,9},{9,8},{8,0},{4,5},{5,6},{6... | collective-permute-start | bytes 491528 | tf_op jit(solution)/shard_map/ppermute | solution.py:802
  440.7 18.9 %attention_backward.4 = (bf16[1280,384]{1,0:T(8,128)(2,1)}, bf16[10240,128]{1,0:T(8,128)(2,1)}) custom-call(s32[200]{0:T(256)S(1)} %select_n.174.lists, s32[5]{0:T(128)S(1)} %get-tuple-element.194.counts, bf16[1280,1152]{1,0:T(8,128)(2,1)} %bitcast.4.q_ref, bf16[1280,1152]{1,0:T(8,128)(2,1)} %bitcast.224, bf16[1280,1152]{1,0:T(8,128)(2,1)} %get-tuple-element.247.o_ref, ...), custom_call_target="tpu_custom_call" | custom-call | flops 25165824000 | bytes 10485760 | tf_op jit(solution)/shard_map/attention_backward/pallas_call | solution.py:413
  459.6 8.4 gradient_parts.4
  467.9 20.4 %collective-permute-done.18 = bf16[640,128]{1,0:T(8,128)(2,1)S(1)} collective-permute-done((bf16[640,128]{1,0:T(8,128)(2,1)S(1)}, bf16[640,128]{1,0:T(8,128)(2,1)S(1)}, u32[]{:S(2)}, u32[]{:S(2)}) %collective-permute-start.18) | collective-permute-done | bytes 163872 | tf_op jit(solution)/shard_map/ppermute | solution.py:802
  490.7 37.5 %collective-permute-start.19 = (bf16[1280,128]{1,0:T(8,128)(2,1)S(1)}, bf16[1280,128]{1,0:T(8,128)(2,1)}, u32[]{:S(2)}, u32[]{:S(2)}) collective-permute-start(bf16[1280,128]{1,0:T(8,128)(2,1)S(1)} %pad_maximum_fusion.7), channel_id=1, source_target_pairs={{0,1},{1,2},{2,3},{3,11},{11,10},{10,9},{9,8},{8,0},{4,5},{5,6},{6... | collective-permute-start | bytes 983048 | tf_op jit(solution)/shard_map/ppermute | solution.py:802
  528.2 33.0 %collective-permute-start.21 = (bf16[640,128]{1,0:T(8,128)(2,1)S(1)}, bf16[640,128]{1,0:T(8,128)(2,1)}, u32[]{:S(2)}, u32[]{:S(2)}) collective-permute-start(bf16[640,128]{1,0:T(8,128)(2,1)S(1)} %get-tuple-element.276), channel_id=1, source_target_pairs={{0,1},{1,2},{2,3},{3,11},{11,10},{10,9},{9,8},{8,0},{4,5},{5,6},{6... | collective-permute-start | bytes 491528 | tf_op jit(solution)/shard_map/ppermute | solution.py:802
  561.2 18.0 %attention_backward.5 = (bf16[1280,384]{1,0:T(8,128)(2,1)}, bf16[10240,128]{1,0:T(8,128)(2,1)}) custom-call(s32[200]{0:T(256)S(1)} %select_n.174.lists, s32[5]{0:T(128)S(1)} %get-tuple-element.194.counts, bf16[1280,1152]{1,0:T(8,128)(2,1)} %bitcast.4.q_ref, bf16[1280,1152]{1,0:T(8,128)(2,1)} %bitcast.225, bf16[1280,1152]{1,0:T(8,128)(2,1)} %get-tuple-element.247.o_ref, ...), custom_call_target="tpu_custom_call" | custom-call | flops 25165824000 | bytes 10485760 | tf_op jit(solution)/shard_map/attention_backward/pallas_call | solution.py:413
  579.3 4.1 collective-permute-done.22
  585.3 39.6 %collective-permute-start.33 = (bf16[640,128]{1,0:T(8,128)(2,1)S(1)}, bf16[640,128]{1,0:T(8,128)(2,1)S(1)}, u32[]{:S(2)}, u32[]{:S(2)}) collective-permute-start(bf16[640,128]{1,0:T(8,128)(2,1)S(1)} %get-tuple-element.416), channel_id=1, source_target_pairs={{0,1},{1,2},{2,3},{3,11},{11,10},{10,9},{9,8},{8,0},{4,5},{5,6},{6... | collective-permute-start | bytes 491528 | tf_op jit(solution)/shard_map/ppermute | solution.py:802
  627.2 17.5 %collective-permute-start.23 = (bf16[1280,128]{1,0:T(8,128)(2,1)}, bf16[1280,128]{1,0:T(8,128)(2,1)}, u32[]{:S(2)}, u32[]{:S(2)}) collective-permute-start(bf16[1280,128]{1,0:T(8,128)(2,1)} %get-tuple-element.280), channel_id=1, source_target_pairs={{0,1},{1,2},{2,3},{3,11},{11,10},{10,9},{9,8},{8,0},{4,5},{5,6},{6... | collective-permute-start | bytes 983048 | tf_op jit(solution)/shard_map/ppermute | solution.py:802
  647.5 8.4 collective-permute-start.27
  661.6 3.1 pad_maximum_fusion
  664.7 4.1 all-to-all-start.6
  670.2 6.2 collective-permute-start.35
  687.9 10.5 %collective-permute-done.29 = bf16[1280,128]{1,0:T(8,128)(2,1)S(1)} collective-permute-done((bf16[1280,128]{1,0:T(8,128)(2,1)S(1)}, bf16[1280,128]{1,0:T(8,128)(2,1)S(1)}, u32[]{:S(2)}, u32[]{:S(2)}) %collective-permute-start.29) | collective-permute-done | bytes 327712 | tf_op jit(solution)/shard_map/ppermute | solution.py:802
  705.5 4.1 collective-permute-done.38
  712.5 4.1 collective-permute-done.32
  716.7 2.4 collective-permute-done.39
  719.1 3.0 collective-permute-done.40
  723.4 6.5 all_to_all.51.pair_ref
  729.9 4.3 all-to-all-start.8
  734.3 12.3 %joint_back.1 = (bf16[640,1920]{1,0:T(8,128)(2,1)}, bf16[4,640,288]{2,1,0:T(8,128)(2,1)}, f32[8,1152]{1,0:T(8,128)}) custom-call(bf16[2,640,1152]{2,1,0:T(8,128)(2,1)} %copy-done.6, bf16[2,640,384]{2,1,0:T(8,128)(2,1)} %all_to_all.51.pair_ref, f32[640,128]{1,0:T(8,128)} %get-tuple-element.459.cos_ref, f32[640,128]{1,0:T(8,128)} %get-tuple-element.460.sin_ref, ...), custom_call_target="tpu_custom_call" | custom-call | flops 2831155200 | bytes 16777216 | tf_op jit(solution)/shard_map/joint_back/pallas_call | solution.py:639
  748.6 4.7 all-to-all-done.8
  753.3 2.7 copy.116
  756.0 9.0 %gradient_parts.5 = bf16[4,4,288,512]{3,2,1,0:T(8,128)(2,1)} custom-call(bf16[640,1152]{1,0:T(8,128)(2,1)} %get-tuple-element.321.refs_0_, bf16[640,1920]{1,0:T(8,128)(2,1)} %get-tuple-element.322.refs_1_, f32[4,288,1]{2,1,0:T(8,128)} %reshape_squeeze.9.refs_2_), custom_call_target="tpu_custom_call" | custom-call | flops 3019898880 | bytes 4718592 | tf_op jit(solution)/shard_map/gradient_parts/pallas_call | solution.py:766
  782.7 5.1 collective-permute-done.43
  788.6 3.4 collective-permute-start.45
  793.9 2.4 copy.108
  796.3 3.7 all-to-all-start.9
  816.0 11.8 %collective-permute-done.47 = bf16[288,512]{1,0:T(8,128)(2,1)S(1)} collective-permute-done((bf16[288,512]{1,0:T(8,128)(2,1)S(1)}, bf16[288,512]{1,0:T(8,128)(2,1)S(1)}, u32[]{:S(2)}, u32[]{:S(2)}) %collective-permute-start.47) | collective-permute-done | bytes 294944 | tf_op jit(solution)/shard_map/ppermute | solution.py:802
  833.4 4.7 collective-permute-done.49
  (310 shorter events, 131.2 us)
Async XLA Ops:
  7.2 70.4 %all-gather.3.cloned.1.call-start = ((), (), s32[]{:S(2)}) async-start(), calls=%async_computation.12 | async-start | bytes 5013504 | tf_op jit(solution)/shard_map/all_gather | solution.py:857
  7.9 292.8 %all-gather.5.cloned.1.call-start = ((), (), s32[]{:S(2)}) async-start(), calls=%async_computation.13 | async-start | bytes 18800640 | tf_op jit(solution)/shard_map/all_gather | solution.py:857
  12.3 40.2 %collective-permute-start = (bf16[288,768]{1,0:T(8,128)(2,1)}, bf16[288,768]{1,0:T(8,128)(2,1)}, u32[]{:S(2)}, u32[]{:S(2)}) collective-permute-start(bf16[288,768]{1,0:T(8,128)(2,1)} %bitcast.1), channel_id=1, source_target_pairs={{0,1},{1,2},{2,3},{3,11},{11,10},{10,9},{9,8},{8,0},{4,5},{5,6},{6... | collective-permute-start | bytes 1327112 | tf_op jit(solution)/shard_map/ppermute | solution.py:923
  15.4 37.2 %collective-permute-start.1 = (bf16[288,768]{1,0:T(8,128)(2,1)}, bf16[288,768]{1,0:T(8,128)(2,1)}, u32[]{:S(2)}, u32[]{:S(2)}) collective-permute-start(bf16[288,768]{1,0:T(8,128)(2,1)} %bitcast.1), channel_id=1, source_target_pairs={{1,0},{2,1},{3,2},{11,3},{10,11},{9,10},{8,9},{0,8},{5,4},{6,5},{7... | collective-permute-start | bytes 1327112 | tf_op jit(solution)/shard_map/ppermute | solution.py:923
  18.4 34.1 %all-to-all-start = ((bf16[4,656,288]{1,2,0:T(8,128)(2,1)}), bf16[4,656,288]{1,2,0:T(8,128)(2,1)}, u32[]{:S(2)}, u32[]{:S(2)}) async-start(bf16[4,656,288]{1,2,0:T(8,128)(2,1)} %copy.96), calls=%async_computation | async-start | bytes 3538944 | tf_op jit(solution)/shard_map/all_to_all | solution.py:905
  52.6 17.5 %collective-permute-start.2 = (bf16[288,768]{1,0:T(8,128)(2,1)}, bf16[288,768]{1,0:T(8,128)(2,1)}, u32[]{:S(2)}, u32[]{:S(2)}) collective-permute-start(bf16[288,768]{1,0:T(8,128)(2,1)} %collective-permute-done), channel_id=1, source_target_pairs={{0,1},{1,2},{2,3},{3,11},{11,10},{10,9},{9,8},{8,0},{4,5},{5,6},{6... | collective-permute-start | bytes 1327112 | tf_op jit(solution)/shard_map/ppermute | solution.py:932
  52.6 21.1 %collective-permute-start.3 = (bf16[288,768]{1,0:T(8,128)(2,1)}, bf16[288,768]{1,0:T(8,128)(2,1)}, u32[]{:S(2)}, u32[]{:S(2)}) collective-permute-start(bf16[288,768]{1,0:T(8,128)(2,1)} %collective-permute-done.1), channel_id=1, source_target_pairs={{1,0},{2,1},{3,2},{11,3},{10,11},{9,10},{8,9},{0,8},{5,4},{6,5},{7... | collective-permute-start | bytes 1327112 | tf_op jit(solution)/shard_map/ppermute | solution.py:932
  95.2 67.9 %collective-permute-start.4 = (bf16[1280,384]{1,0:T(8,128)(2,1)}, bf16[1280,384]{1,0:T(8,128)(2,1)}, u32[]{:S(2)}, u32[]{:S(2)}) collective-permute-start(bf16[1280,384]{1,0:T(8,128)(2,1)} %bitcast.3.refs_0_), channel_id=1, source_target_pairs={{0,1},{1,2},{2,3},{3,11},{11,10},{10,9},{9,8},{8,0},{4,5},{5,6},{6... | collective-permute-start | bytes 2949128 | tf_op jit(solution)/shard_map/ppermute | solution.py:951
  98.5 70.0 %collective-permute-start.6 = (bf16[1280,384]{1,0:T(8,128)(2,1)}, bf16[1280,384]{1,0:T(8,128)(2,1)}, u32[]{:S(2)}, u32[]{:S(2)}) collective-permute-start(bf16[1280,384]{1,0:T(8,128)(2,1)} %bitcast.3.refs_0_), channel_id=1, source_target_pairs={{1,0},{2,1},{3,2},{11,3},{10,11},{9,10},{8,9},{0,8},{5,4},{6,5},{7... | collective-permute-start | bytes 2949128 | tf_op jit(solution)/shard_map/ppermute | solution.py:951
  98.5 62.2 %collective-permute-start.8 = (bf16[288,768]{1,0:T(8,128)(2,1)}, bf16[288,768]{1,0:T(8,128)(2,1)S(1)}, u32[]{:S(2)}, u32[]{:S(2)}) collective-permute-start(bf16[288,768]{1,0:T(8,128)(2,1)} %collective-permute-done.2), channel_id=1, source_target_pairs={{0,1},{1,2},{2,3},{3,11},{11,10},{10,9},{9,8},{8,0},{4,5},{5,6},{6... | collective-permute-start | bytes 1327112 | tf_op jit(solution)/shard_map/ppermute | solution.py:932
  100.5 62.6 %collective-permute-start.9 = (bf16[288,768]{1,0:T(8,128)(2,1)}, bf16[288,768]{1,0:T(8,128)(2,1)}, u32[]{:S(2)}, u32[]{:S(2)}) collective-permute-start(bf16[288,768]{1,0:T(8,128)(2,1)} %collective-permute-done.3), channel_id=1, source_target_pairs={{1,0},{2,1},{3,2},{11,3},{10,11},{9,10},{8,9},{0,8},{5,4},{6,5},{7... | collective-permute-start | bytes 1327112 | tf_op jit(solution)/shard_map/ppermute | solution.py:932
  106.0 63.5 %all-to-all-start.2 = ((bf16[2,640,1152]{2,1,0:T(8,128)(2,1)}), bf16[2,640,1152]{2,1,0:T(8,128)(2,1)}, u32[]{:S(2)}, u32[]{:S(2)}) async-start(bf16[2,640,1152]{2,1,0:T(8,128)(2,1)} %get-tuple-element.202), calls=%async_computation.2 | async-start | bytes 5898240 | tf_op jit(solution)/shard_map/all_to_all | solution.py:905
  163.8 33.1 %collective-permute-start.10 = (bf16[144,768]{1,0:T(8,128)(2,1)}, bf16[144,768]{1,0:T(8,128)(2,1)}, u32[]{:S(2)}, u32[]{:S(2)}) collective-permute-start(bf16[144,768]{1,0:T(8,128)(2,1)} %slice.411), channel_id=1, source_target_pairs={{0,1},{1,2},{2,3},{3,11},{11,10},{10,9},{9,8},{8,0},{4,5},{5,6},{6... | collective-permute-start | bytes 663560 | tf_op jit(solution)/shard_map/ppermute | solution.py:935
  166.5 32.1 %collective-permute-start.11 = (bf16[144,768]{1,0:T(8,128)(2,1)}, bf16[144,768]{1,0:T(8,128)(2,1)S(1)}, u32[]{:S(2)}, u32[]{:S(2)}) collective-permute-start(bf16[144,768]{1,0:T(8,128)(2,1)} %slice.412), channel_id=1, source_target_pairs={{1,0},{2,1},{3,2},{11,3},{10,11},{9,10},{8,9},{0,8},{5,4},{6,5},{7... | collective-permute-start | bytes 663560 | tf_op jit(solution)/shard_map/ppermute | solution.py:936
  167.5 51.2 %collective-permute-start.5 = (bf16[1280,384]{1,0:T(8,128)(2,1)}, bf16[1280,384]{1,0:T(8,128)(2,1)}, u32[]{:S(2)}, u32[]{:S(2)}) collective-permute-start(bf16[1280,384]{1,0:T(8,128)(2,1)} %collective-permute-done.4.refs_2_.refs_8_), channel_id=1, source_target_pairs={{0,1},{1,2},{2,3},{3,11},{11,10},{10,9},{9,8},{8,0},{4,5},{5,6},{6... | collective-permute-start | bytes 2949128 | tf_op jit(solution)/shard_map/ppermute | solution.py:963
  168.5 52.7 %collective-permute-start.7 = (bf16[1280,384]{1,0:T(8,128)(2,1)}, bf16[1280,384]{1,0:T(8,128)(2,1)}, u32[]{:S(2)}, u32[]{:S(2)}) collective-permute-start(bf16[1280,384]{1,0:T(8,128)(2,1)} %collective-permute-done.6.refs_1_), channel_id=1, source_target_pairs={{1,0},{2,1},{3,2},{11,3},{10,11},{9,10},{8,9},{0,8},{5,4},{6,5},{7... | collective-permute-start | bytes 2949128 | tf_op jit(solution)/shard_map/ppermute | solution.py:963
  221.2 89.5 %collective-permute-start.16 = (bf16[8,288,768]{2,1,0:T(8,128)(2,1)}, bf16[8,288,768]{2,1,0:T(8,128)(2,1)}, u32[]{:S(2)}, u32[]{:S(2)}) collective-permute-start(bf16[8,288,768]{2,1,0:T(8,128)(2,1)} %bitcast.7.refs_0_.refs_1_), channel_id=1, source_target_pairs={{0,4},{4,0},{1,5},{5,1},{2,6},{6,2},{3,7},{7,3},{8,12},{12,8},{9,1... | collective-permute-start | bytes 10616840 | tf_op jit(solution)/shard_map/ppermute | solution.py:977
  221.2 27.7 %collective-permute-start.12 = (bf16[1280,384]{1,0:T(8,128)(2,1)}, bf16[1280,384]{1,0:T(8,128)(2,1)}, u32[]{:S(2)}, u32[]{:S(2)}) collective-permute-start(bf16[1280,384]{1,0:T(8,128)(2,1)} %collective-permute-done.5.refs_3_.refs_7_), channel_id=1, source_target_pairs={{0,1},{1,2},{2,3},{3,11},{11,10},{10,9},{9,8},{8,0},{4,5},{5,6},{6... | collective-permute-start | bytes 2949128 | tf_op jit(solution)/shard_map/ppermute | solution.py:963
  221.4 27.5 %collective-permute-start.13 = (bf16[1280,384]{1,0:T(8,128)(2,1)}, bf16[1280,384]{1,0:T(8,128)(2,1)}, u32[]{:S(2)}, u32[]{:S(2)}) collective-permute-start(bf16[1280,384]{1,0:T(8,128)(2,1)} %collective-permute-done.7.refs_2_), channel_id=1, source_target_pairs={{1,0},{2,1},{3,2},{11,3},{10,11},{9,10},{8,9},{0,8},{5,4},{6,5},{7... | collective-permute-start | bytes 2949128 | tf_op jit(solution)/shard_map/ppermute | solution.py:963
  225.2 52.0 %all-to-all-start.3 = ((bf16[4,640,288]{1,2,0:T(8,128)(2,1)}), bf16[4,640,288]{1,2,0:T(8,128)(2,1)}, u32[]{:S(2)}, u32[]{:S(2)}) async-start(bf16[4,640,288]{1,2,0:T(8,128)(2,1)} %bitcast.213), calls=%async_computation.3 | async-start | bytes 2949120 | tf_op jit(solution)/shard_map/all_to_all | solution.py:905
  250.0 27.1 %collective-permute-start.14 = (bf16[640,384]{1,0:T(8,128)(2,1)S(1)}, bf16[640,384]{1,0:T(8,128)(2,1)S(1)}, u32[]{:S(2)}, u32[]{:S(2)}) collective-permute-start(bf16[640,384]{1,0:T(8,128)(2,1)S(1)} %slice.413), channel_id=1, source_target_pairs={{0,1},{1,2},{2,3},{3,11},{11,10},{10,9},{9,8},{8,0},{4,5},{5,6},{6... | collective-permute-start | bytes 1474568 | tf_op jit(solution)/shard_map/ppermute | solution.py:965
  261.8 15.3 %collective-permute-start.15 = (bf16[640,384]{1,0:T(8,128)(2,1)S(1)}, bf16[640,384]{1,0:T(8,128)(2,1)S(1)}, u32[]{:S(2)}, u32[]{:S(2)}) collective-permute-start(bf16[640,384]{1,0:T(8,128)(2,1)S(1)} %slice.414), channel_id=1, source_target_pairs={{1,0},{2,1},{3,2},{11,3},{10,11},{9,10},{8,9},{0,8},{5,4},{6,5},{7... | collective-permute-start | bytes 1474568 | tf_op jit(solution)/shard_map/ppermute | solution.py:965
  277.1 116.6 %copy-start.29 = (bf16[640,384]{1,0:T(8,128)(2,1)}, bf16[640,384]{1,0:T(8,128)(2,1)S(1)}, u32[]{:S(2)}) copy-start(bf16[640,384]{1,0:T(8,128)(2,1)S(1)} %collective-permute-done.14.refs_2_.refs_4_) | copy-start | bytes 1474564
  293.0 7.7 all-to-all-start.4
  362.4 27.5 %all-to-all-start.5 = ((bf16[2,640,1152]{2,1,0:T(8,128)(2,1)}), bf16[2,640,1152]{2,1,0:T(8,128)(2,1)S(1)}, u32[]{:S(2)}, u32[]{:S(2)}) async-start(bf16[2,640,1152]{2,1,0:T(8,128)(2,1)} %get-tuple-element.261), calls=%async_computation.5 | async-start | bytes 5898240 | tf_op jit(solution)/shard_map/all_to_all | solution.py:905
  366.3 357.1 %reduce-scatter.5.cloned.1.call-start = ((), (), s32[]{:S(2)}) async-start(), calls=%async_computation.14 | async-start | bytes 22560768 | tf_op jit(solution)/shard_map/reduce_scatter | solution.py:853
  413.0 54.9 %collective-permute-start.17 = (bf16[640,128]{1,0:T(8,128)(2,1)S(1)}, bf16[640,128]{1,0:T(8,128)(2,1)S(1)}, u32[]{:S(2)}, u32[]{:S(2)}) collective-permute-start(bf16[640,128]{1,0:T(8,128)(2,1)S(1)} %get-tuple-element.267), channel_id=1, source_target_pairs={{0,1},{1,2},{2,3},{3,11},{11,10},{10,9},{9,8},{8,0},{4,5},{5,6},{6... | collective-permute-start | bytes 491528 | tf_op jit(solution)/shard_map/ppermute | solution.py:802
  440.7 47.7 %collective-permute-start.18 = (bf16[640,128]{1,0:T(8,128)(2,1)S(1)}, bf16[640,128]{1,0:T(8,128)(2,1)S(1)}, u32[]{:S(2)}, u32[]{:S(2)}) collective-permute-start(bf16[640,128]{1,0:T(8,128)(2,1)S(1)} %get-tuple-element.268), channel_id=1, source_target_pairs={{1,0},{2,1},{3,2},{11,3},{10,11},{9,10},{8,9},{0,8},{5,4},{6,5},{7... | collective-permute-start | bytes 491528 | tf_op jit(solution)/shard_map/ppermute | solution.py:802
  490.7 92.7 %collective-permute-start.19 = (bf16[1280,128]{1,0:T(8,128)(2,1)S(1)}, bf16[1280,128]{1,0:T(8,128)(2,1)}, u32[]{:S(2)}, u32[]{:S(2)}) collective-permute-start(bf16[1280,128]{1,0:T(8,128)(2,1)S(1)} %pad_maximum_fusion.7), channel_id=1, source_target_pairs={{0,1},{1,2},{2,3},{3,11},{11,10},{10,9},{9,8},{8,0},{4,5},{5,6},{6... | collective-permute-start | bytes 983048 | tf_op jit(solution)/shard_map/ppermute | solution.py:802
  528.2 55.2 %collective-permute-start.20 = (bf16[1280,128]{1,0:T(8,128)(2,1)S(1)}, bf16[1280,128]{1,0:T(8,128)(2,1)}, u32[]{:S(2)}, u32[]{:S(2)}) collective-permute-start(bf16[1280,128]{1,0:T(8,128)(2,1)S(1)} %pad_maximum_fusion.8), channel_id=1, source_target_pairs={{1,0},{2,1},{3,2},{11,3},{10,11},{9,10},{8,9},{0,8},{5,4},{6,5},{7... | collective-permute-start | bytes 983048 | tf_op jit(solution)/shard_map/ppermute | solution.py:802
  528.2 51.0 %collective-permute-start.21 = (bf16[640,128]{1,0:T(8,128)(2,1)S(1)}, bf16[640,128]{1,0:T(8,128)(2,1)}, u32[]{:S(2)}, u32[]{:S(2)}) collective-permute-start(bf16[640,128]{1,0:T(8,128)(2,1)S(1)} %get-tuple-element.276), channel_id=1, source_target_pairs={{0,1},{1,2},{2,3},{3,11},{11,10},{10,9},{9,8},{8,0},{4,5},{5,6},{6... | collective-permute-start | bytes 491528 | tf_op jit(solution)/shard_map/ppermute | solution.py:802
  561.2 22.2 %collective-permute-start.22 = (bf16[640,128]{1,0:T(8,128)(2,1)S(1)}, bf16[640,128]{1,0:T(8,128)(2,1)}, u32[]{:S(2)}, u32[]{:S(2)}) collective-permute-start(bf16[640,128]{1,0:T(8,128)(2,1)S(1)} %get-tuple-element.277), channel_id=1, source_target_pairs={{1,0},{2,1},{3,2},{11,3},{10,11},{9,10},{8,9},{0,8},{5,4},{6,5},{7... | collective-permute-start | bytes 491528 | tf_op jit(solution)/shard_map/ppermute | solution.py:802
  585.3 70.5 %collective-permute-start.33 = (bf16[640,128]{1,0:T(8,128)(2,1)S(1)}, bf16[640,128]{1,0:T(8,128)(2,1)S(1)}, u32[]{:S(2)}, u32[]{:S(2)}) collective-permute-start(bf16[640,128]{1,0:T(8,128)(2,1)S(1)} %get-tuple-element.416), channel_id=1, source_target_pairs={{0,1},{1,2},{2,3},{3,11},{11,10},{10,9},{9,8},{8,0},{4,5},{5,6},{6... | collective-permute-start | bytes 491528 | tf_op jit(solution)/shard_map/ppermute | solution.py:802
  624.9 31.8 %collective-permute-start.34 = (bf16[640,128]{1,0:T(8,128)(2,1)S(1)}, bf16[640,128]{1,0:T(8,128)(2,1)S(1)}, u32[]{:S(2)}, u32[]{:S(2)}) collective-permute-start(bf16[640,128]{1,0:T(8,128)(2,1)S(1)} %get-tuple-element.415), channel_id=1, source_target_pairs={{1,0},{2,1},{3,2},{11,3},{10,11},{9,10},{8,9},{0,8},{5,4},{6,5},{7... | collective-permute-start | bytes 491528 | tf_op jit(solution)/shard_map/ppermute | solution.py:802
  627.2 49.2 %collective-permute-start.23 = (bf16[1280,128]{1,0:T(8,128)(2,1)}, bf16[1280,128]{1,0:T(8,128)(2,1)}, u32[]{:S(2)}, u32[]{:S(2)}) collective-permute-start(bf16[1280,128]{1,0:T(8,128)(2,1)} %get-tuple-element.280), channel_id=1, source_target_pairs={{0,1},{1,2},{2,3},{3,11},{11,10},{10,9},{9,8},{8,0},{4,5},{5,6},{6... | collective-permute-start | bytes 983048 | tf_op jit(solution)/shard_map/ppermute | solution.py:802
  644.7 31.6 %collective-permute-start.24 = (bf16[1280,128]{1,0:T(8,128)(2,1)}, bf16[1280,128]{1,0:T(8,128)(2,1)}, u32[]{:S(2)}, u32[]{:S(2)}) collective-permute-start(bf16[1280,128]{1,0:T(8,128)(2,1)} %get-tuple-element.281), channel_id=1, source_target_pairs={{1,0},{2,1},{3,2},{11,3},{10,11},{9,10},{8,9},{0,8},{5,4},{6,5},{7... | collective-permute-start | bytes 983048 | tf_op jit(solution)/shard_map/ppermute | solution.py:802
  647.5 32.4 %collective-permute-start.27 = (bf16[1280,128]{1,0:T(8,128)(2,1)}, bf16[1280,128]{1,0:T(8,128)(2,1)}, u32[]{:S(2)}, u32[]{:S(2)}) collective-permute-start(bf16[1280,128]{1,0:T(8,128)(2,1)} %pad_maximum_fusion.9), channel_id=1, source_target_pairs={{0,1},{1,2},{2,3},{3,11},{11,10},{10,9},{9,8},{8,0},{4,5},{5,6},{6... | collective-permute-start | bytes 983048 | tf_op jit(solution)/shard_map/ppermute | solution.py:802
  655.9 24.0 %collective-permute-start.28 = (bf16[1280,128]{1,0:T(8,128)(2,1)}, bf16[1280,128]{1,0:T(8,128)(2,1)}, u32[]{:S(2)}, u32[]{:S(2)}) collective-permute-start(bf16[1280,128]{1,0:T(8,128)(2,1)} %pad_maximum_fusion.10), channel_id=1, source_target_pairs={{1,0},{2,1},{3,2},{11,3},{10,11},{9,10},{8,9},{0,8},{5,4},{6,5},{7... | collective-permute-start | bytes 983048 | tf_op jit(solution)/shard_map/ppermute | solution.py:802
  664.7 58.7 %all-to-all-start.6 = ((bf16[2,640,1152]{2,1,0:T(8,128)(2,1)}), bf16[2,640,1152]{2,1,0:T(8,128)(2,1)S(1)}, u32[]{:S(2)}, u32[]{:S(2)}) async-start(bf16[2,640,1152]{2,1,0:T(8,128)(2,1)} %bitcast.211), calls=%async_computation.6 | async-start | bytes 5898240 | tf_op jit(solution)/shard_map/all_to_all | solution.py:905
  670.2 14.2 %collective-permute-start.35 = (bf16[1280,128]{1,0:T(8,128)(2,1)S(1)}, bf16[1280,128]{1,0:T(8,128)(2,1)S(1)}, u32[]{:S(2)}, u32[]{:S(2)}) collective-permute-start(bf16[1280,128]{1,0:T(8,128)(2,1)S(1)} %pad_maximum_fusion.11), channel_id=1, source_target_pairs={{0,1},{1,2},{2,3},{3,11},{11,10},{10,9},{9,8},{8,0},{4,5},{5,6},{6... | collective-permute-start | bytes 983048 | tf_op jit(solution)/shard_map/ppermute | solution.py:802
  676.4 10.6 %collective-permute-start.36 = (bf16[1280,128]{1,0:T(8,128)(2,1)S(1)}, bf16[1280,128]{1,0:T(8,128)(2,1)S(1)}, u32[]{:S(2)}, u32[]{:S(2)}) collective-permute-start(bf16[1280,128]{1,0:T(8,128)(2,1)S(1)} %pad_maximum_fusion.12), channel_id=1, source_target_pairs={{1,0},{2,1},{3,2},{11,3},{10,11},{9,10},{8,9},{0,8},{5,4},{6,5},{7... | collective-permute-start | bytes 983048 | tf_op jit(solution)/shard_map/ppermute | solution.py:802
  677.8 23.4 %collective-permute-start.25 = (bf16[1280,128]{1,0:T(8,128)(2,1)S(1)}, bf16[1280,128]{1,0:T(8,128)(2,1)S(1)}, u32[]{:S(2)}, u32[]{:S(2)}) collective-permute-start(bf16[1280,128]{1,0:T(8,128)(2,1)S(1)} %get-tuple-element.282), channel_id=1, source_target_pairs={{0,1},{1,2},{2,3},{3,11},{11,10},{10,9},{9,8},{8,0},{4,5},{5,6},{6... | collective-permute-start | bytes 983048 | tf_op jit(solution)/shard_map/ppermute | solution.py:802
  679.9 22.6 %collective-permute-start.26 = (bf16[1280,128]{1,0:T(8,128)(2,1)S(1)}, bf16[1280,128]{1,0:T(8,128)(2,1)S(1)}, u32[]{:S(2)}, u32[]{:S(2)}) collective-permute-start(bf16[1280,128]{1,0:T(8,128)(2,1)S(1)} %get-tuple-element.283), channel_id=1, source_target_pairs={{1,0},{2,1},{3,2},{11,3},{10,11},{9,10},{8,9},{0,8},{5,4},{6,5},{7... | collective-permute-start | bytes 983048 | tf_op jit(solution)/shard_map/ppermute | solution.py:802
  681.2 17.3 %collective-permute-start.29 = (bf16[1280,128]{1,0:T(8,128)(2,1)S(1)}, bf16[1280,128]{1,0:T(8,128)(2,1)S(1)}, u32[]{:S(2)}, u32[]{:S(2)}) collective-permute-start(bf16[1280,128]{1,0:T(8,128)(2,1)S(1)} %get-tuple-element.288), channel_id=1, source_target_pairs={{0,1},{1,2},{2,3},{3,11},{11,10},{10,9},{9,8},{8,0},{4,5},{5,6},{6... | collective-permute-start | bytes 983048 | tf_op jit(solution)/shard_map/ppermute | solution.py:802
  684.4 15.8 %collective-permute-start.30 = (bf16[1280,128]{1,0:T(8,128)(2,1)S(1)}, bf16[1280,128]{1,0:T(8,128)(2,1)S(1)}, u32[]{:S(2)}, u32[]{:S(2)}) collective-permute-start(bf16[1280,128]{1,0:T(8,128)(2,1)S(1)} %get-tuple-element.289), channel_id=1, source_target_pairs={{1,0},{2,1},{3,2},{11,3},{10,11},{9,10},{8,9},{0,8},{5,4},{6,5},{7... | collective-permute-start | bytes 983048 | tf_op jit(solution)/shard_map/ppermute | solution.py:802
  687.1 18.4 %collective-permute-start.37 = (bf16[1280,128]{1,0:T(8,128)(2,1)S(1)}, bf16[1280,128]{1,0:T(8,128)(2,1)S(1)}, u32[]{:S(2)}, u32[]{:S(2)}) collective-permute-start(bf16[1280,128]{1,0:T(8,128)(2,1)S(1)} %get-tuple-element.301), channel_id=1, source_target_pairs={{0,1},{1,2},{2,3},{3,11},{11,10},{10,9},{9,8},{8,0},{4,5},{5,6},{6... | collective-permute-start | bytes 983048 | tf_op jit(solution)/shard_map/ppermute | solution.py:802
  698.4 11.1 %collective-permute-start.38 = (bf16[1280,128]{1,0:T(8,128)(2,1)S(1)}, bf16[1280,128]{1,0:T(8,128)(2,1)S(1)}, u32[]{:S(2)}, u32[]{:S(2)}) collective-permute-start(bf16[1280,128]{1,0:T(8,128)(2,1)S(1)} %get-tuple-element.302), channel_id=1, source_target_pairs={{1,0},{2,1},{3,2},{11,3},{10,11},{9,10},{8,9},{0,8},{5,4},{6,5},{7... | collective-permute-start | bytes 983048 | tf_op jit(solution)/shard_map/ppermute | solution.py:802
  700.4 12.1 %collective-permute-start.31 = (bf16[1280,128]{1,0:T(8,128)(2,1)S(1)}, bf16[1280,128]{1,0:T(8,128)(2,1)S(1)}, u32[]{:S(2)}, u32[]{:S(2)}) collective-permute-start(bf16[1280,128]{1,0:T(8,128)(2,1)S(1)} %get-tuple-element.290), channel_id=1, source_target_pairs={{0,1},{1,2},{2,3},{3,11},{11,10},{10,9},{9,8},{8,0},{4,5},{5,6},{6... | collective-permute-start | bytes 983048 | tf_op jit(solution)/shard_map/ppermute | solution.py:802
  701.2 15.3 %collective-permute-start.32 = (bf16[1280,128]{1,0:T(8,128)(2,1)S(1)}, bf16[1280,128]{1,0:T(8,128)(2,1)S(1)}, u32[]{:S(2)}, u32[]{:S(2)}) collective-permute-start(bf16[1280,128]{1,0:T(8,128)(2,1)S(1)} %get-tuple-element.291), channel_id=1, source_target_pairs={{1,0},{2,1},{3,2},{11,3},{10,11},{9,10},{8,9},{0,8},{5,4},{6,5},{7... | collective-permute-start | bytes 983048 | tf_op jit(solution)/shard_map/ppermute | solution.py:802
  709.7 9.4 %collective-permute-start.39 = (bf16[1280,128]{1,0:T(8,128)(2,1)S(1)}, bf16[1280,128]{1,0:T(8,128)(2,1)S(1)}, u32[]{:S(2)}, u32[]{:S(2)}) collective-permute-start(bf16[1280,128]{1,0:T(8,128)(2,1)S(1)} %get-tuple-element.303), channel_id=1, source_target_pairs={{0,1},{1,2},{2,3},{3,11},{11,10},{10,9},{9,8},{8,0},{4,5},{5,6},{6... | collective-permute-start | bytes 983048 | tf_op jit(solution)/shard_map/ppermute | solution.py:802
  711.8 10.3 %collective-permute-start.40 = (bf16[1280,128]{1,0:T(8,128)(2,1)S(1)}, bf16[1280,128]{1,0:T(8,128)(2,1)S(1)}, u32[]{:S(2)}, u32[]{:S(2)}) collective-permute-start(bf16[1280,128]{1,0:T(8,128)(2,1)S(1)} %get-tuple-element.304), channel_id=1, source_target_pairs={{1,0},{2,1},{3,2},{11,3},{10,11},{9,10},{8,9},{0,8},{5,4},{6,5},{7... | collective-permute-start | bytes 983048 | tf_op jit(solution)/shard_map/ppermute | solution.py:802
  729.9 23.4 %all-to-all-start.8 = ((bf16[4,640,288]{1,2,0:T(8,128)(2,1)}), bf16[4,640,288]{1,2,0:T(8,128)(2,1)}, u32[]{:S(2)}, u32[]{:S(2)}) async-start(bf16[4,640,288]{1,2,0:T(8,128)(2,1)} %bitcast.212), calls=%async_computation.9 | async-start | bytes 2949120 | tf_op jit(solution)/shard_map/all_to_all | solution.py:905
  734.2 106.8 %reduce-scatter.7.cloned.1.call-start = ((), (), s32[]{:S(2)}) async-start(), calls=%async_computation.15 | async-start | bytes 3760128
  767.1 13.2 %collective-permute-start.41 = (bf16[8,288,512]{2,1,0:T(8,128)(2,1)S(1)}, bf16[8,288,512]{2,1,0:T(8,128)(2,1)}, u32[]{:S(2)}, u32[]{:S(2)}) collective-permute-start(bf16[8,288,512]{2,1,0:T(8,128)(2,1)S(1)} %dynamic-slice_bitcast_fusion), channel_id=1, source_target_pairs={{0,4},{4,0},{1,5},{5,1},{2,6},{6,2},{3,7},{7,3},{8,12},{12,8},{9,1... | collective-permute-start | bytes 7077896 | tf_op jit(solution)/shard_map/ppermute | solution.py:1034
  770.8 1.8 collective-permute-start.42
  774.3 7.5 collective-permute-start.44
  778.6 9.3 %collective-permute-start.43 = (bf16[144,512]{1,0:T(8,128)(2,1)}, bf16[144,512]{1,0:T(8,128)(2,1)S(1)}, u32[]{:S(2)}, u32[]{:S(2)}) collective-permute-start(bf16[144,512]{1,0:T(8,128)(2,1)} %get-tuple-element.324), channel_id=1, source_target_pairs={{0,1},{1,2},{2,3},{3,11},{11,10},{10,9},{9,8},{8,0},{4,5},{5,6},{6... | collective-permute-start | bytes 442376 | tf_op jit(solution)/shard_map/ppermute | solution.py:802
  788.6 21.3 %collective-permute-start.45 = (bf16[288,512]{1,0:T(8,128)(2,1)}, bf16[288,512]{1,0:T(8,128)(2,1)}, u32[]{:S(2)}, u32[]{:S(2)}) collective-permute-start(bf16[288,512]{1,0:T(8,128)(2,1)} %pad_maximum_fusion.13), channel_id=1, source_target_pairs={{0,1},{1,2},{2,3},{3,11},{11,10},{10,9},{9,8},{8,0},{4,5},{5,6},{6... | collective-permute-start | bytes 884744 | tf_op jit(solution)/shard_map/ppermute | solution.py:802
  792.0 17.9 %collective-permute-start.46 = (bf16[288,512]{1,0:T(8,128)(2,1)}, bf16[288,512]{1,0:T(8,128)(2,1)}, u32[]{:S(2)}, u32[]{:S(2)}) collective-permute-start(bf16[288,512]{1,0:T(8,128)(2,1)} %pad_maximum_fusion.14), channel_id=1, source_target_pairs={{1,0},{2,1},{3,2},{11,3},{10,11},{9,10},{8,9},{0,8},{5,4},{6,5},{7... | collective-permute-start | bytes 884744 | tf_op jit(solution)/shard_map/ppermute | solution.py:802
  796.3 35.0 %all-to-all-start.9 = ((bf16[4,640,288]{1,2,0:T(8,128)(2,1)}), bf16[4,640,288]{1,2,0:T(8,128)(2,1)S(1)}, u32[]{:S(2)}, u32[]{:S(2)}) async-start(bf16[4,640,288]{1,2,0:T(8,128)(2,1)} %copy.108), calls=%async_computation.10 | async-start | bytes 2949120 | tf_op jit(solution)/shard_map/all_to_all | solution.py:905
  811.5 16.2 %collective-permute-start.47 = (bf16[288,512]{1,0:T(8,128)(2,1)S(1)}, bf16[288,512]{1,0:T(8,128)(2,1)S(1)}, u32[]{:S(2)}, u32[]{:S(2)}) collective-permute-start(bf16[288,512]{1,0:T(8,128)(2,1)S(1)} %get-tuple-element.328), channel_id=1, source_target_pairs={{0,1},{1,2},{2,3},{3,11},{11,10},{10,9},{9,8},{8,0},{4,5},{5,6},{6... | collective-permute-start | bytes 884744 | tf_op jit(solution)/shard_map/ppermute | solution.py:802
  812.0 15.7 %collective-permute-start.48 = (bf16[288,512]{1,0:T(8,128)(2,1)S(1)}, bf16[288,512]{1,0:T(8,128)(2,1)S(1)}, u32[]{:S(2)}, u32[]{:S(2)}) collective-permute-start(bf16[288,512]{1,0:T(8,128)(2,1)S(1)} %get-tuple-element.329), channel_id=1, source_target_pairs={{1,0},{2,1},{3,2},{11,3},{10,11},{9,10},{8,9},{0,8},{5,4},{6,5},{7... | collective-permute-start | bytes 884744 | tf_op jit(solution)/shard_map/ppermute | solution.py:802
  829.2 9.0 %collective-permute-start.49 = (bf16[288,512]{1,0:T(8,128)(2,1)S(1)}, bf16[288,512]{1,0:T(8,128)(2,1)S(1)}, u32[]{:S(2)}, u32[]{:S(2)}) collective-permute-start(bf16[288,512]{1,0:T(8,128)(2,1)S(1)} %get-tuple-element.330), channel_id=1, source_target_pairs={{0,1},{1,2},{2,3},{3,11},{11,10},{10,9},{9,8},{8,0},{4,5},{5,6},{6... | collective-permute-start | bytes 884744 | tf_op jit(solution)/shard_map/ppermute | solution.py:802
  830.5 8.5 collective-permute-start.50
  (31 other events, 299.8 us)
Sparse Core Ops, SparseCore 0:
  10.3 63.9 all-gather.2
  75.9 156.6 all-gather.4
  391.6 282.4 reduce-scatter.4
  748.7 80.3 reduce-scatter.6

commit v6 on v4

--- a/solution.py
+++ b/solution.py
@@ -948,13 +948,14 @@
     attended_rows, hidden, normed_two, output_full = project_out(attended_rows, late, x, gains, ATT // columns, late.shape[2] - 3 * width)
     mixed, gate_back, up_back, feed_out, normed_two_back = feed_forward(normed_two, upstream, late, width)
 
+    hidden_back, hidden_low, heads_back, gain_two_part = output_back(normed_two_back, hidden, upstream, gains, output_full)
+    heads_back, mixed = lax.optimization_barrier((heads_back, mixed))
+    heads_back = exchange(heads_back, "core").reshape(held, -1)
     feed_parts = gradient_parts(columns, rows, None, (normed_two, [gate_back, up_back]), (upstream, [mixed]))
-    feed_parts, normed_two_back = lax.optimization_barrier((feed_parts, normed_two_back))
+    feed_parts, heads_back = lax.optimization_barrier((feed_parts, heads_back))
     feed_summed = scatter(feed_parts.reshape(-1, feed_parts.shape[3]), ALL_COL)
-    hidden_back, hidden_low, heads_back, gain_two_part = output_back(normed_two_back, hidden, upstream, gains, output_full)
     output_parts = gradient_parts(columns, rows, gain_two_part[0], (hidden_low, [attended_rows]))
 
-    heads_back = exchange(heads_back, "core").reshape(held, -1)
     query_backs, pair_rings = [], []
     for g in range(groups):
         heads_back = depart(heads_back, pair_rings)

time: 840 us -> 832 us (level)
  blocking collectives: 25.5 us -> 13.1 us
    all_to_all x3 -> x2, blocking collectives: 25.5 us -> 13.1 us  [exchange(): return lax.all_to_all(value, axes, split_axis=0, concat_axis=0, tiled=True)]
    all_to_all x7 -> x8, starting transfers between devices: 30.1 us -> 34.2 us  [exchange(): return lax.all_to_all(value, axes, split_axis=0, concat_axis=0, tiled=True)]
  transfers between devices with their start and end apart: 53 -> 54, of which waited for: 24 -> 23; matrix products, arithmetic and copies ran while one was open for 11% -> 11% of each run, Pallas kernels for 20% -> 22%
where the time goes in v6:
time: 832 us; the launch traced here: 820 us
  Pallas kernels  239 us (29%)
  starting transfers between devices  234 us (28%)
  waiting for transfers between devices  199 us (24%)
  local copies, waits for them, and re-layouts  61.2 us (7%)
  other arithmetic  43.6 us (5%)
  between operations  30.9 us (4%)
  blocking collectives  13.1 us (2%)
    ppermute x16, starting transfers between devices, launch(): lax.ppermute(out, RING, self.ahead)  167 us
    pallas_call x4, Pallas kernels, attention_stage(): pl.pallas_call(functools.partial(stage_kernel, state is None, ends), grid...  64.1 us
    pallas_call x3, Pallas kernels, attention_backward(): pl.pallas_call(functools.partial(backward_kernel, group), grid_spec=pltpu...  54.6 us
    pallas_call x3, Pallas kernels, gradient_parts(): pl.pallas_call(functools.partial(gradient_kernel, [len(rights) for _, rig...  40.4 us
    ppermute x2, waiting for transfers between devices, per_device(): lax.ppermute(to_next, RING, ahead)  39 us
    pallas_call x1, Pallas kernels, feed_forward(): pl.pallas_call(feed_kernel, grid=(columns,), in_specs=[whole, whole, *blo...  38.6 us
    ppermute x16, waiting for transfers between devices, launch(): lax.ppermute(out, RING, self.ahead)  38.6 us
    ppermute x1, waiting for transfers between devices, per_device(): lax.ppermute(value, RING, ahead)  38.5 us
  transfers between devices with their start and end apart: 54, of which 23 were waited for; matrix products, arithmetic and copies ran while one was open for 11% of the time, Pallas kernels for 22%

profile of v6, /device:TPU:0, one launch (start us, length us, event | category | flops | bytes accessed | tf_op | source)
XLA Modules:
  0.0 820.1 jit_solution(15637343805965004058)
XLA Ops:
  9.2 3.7 concatenate.77
  16.2 4.6 all-to-all-start
  26.7 4.7 compare_and_fusion
  38.5 10.0 %all-to-all-done = bf16[4,656,288]{1,2,0:T(8,128)(2,1)} async-done(((bf16[4,656,288]{1,2,0:T(8,128)(2,1)}), bf16[4,656,288]{1,2,0:T(8,128)(2,1)}, u32[]{:S(2)}, u32[]{:S(2)}) %all-to-all-start) | async-done | bytes 1511456 | tf_op jit(solution)/shard_map/all_to_all | solution.py:889
  48.5 3.9 copy.99.x4_ref
  52.4 17.4 %all-gather.3.cloned.1.call-done = bf16[4608,480]{1,0:T(8,128)(2,1)} async-done(((bf16[288,480]{1,0:T(8,128)(2,1)}), bf16[4608,480]{1,0:T(8,128)(2,1)}) %all-gather.3.cloned.1.call-update) | async-done | bytes 4423696 | tf_op jit(solution)/shard_map/all_gather | solution.py:841
  69.8 11.0 %project_in.1 = (bf16[640,1152]{1,0:T(8,128)(2,1)}, bf16[640,1152]{1,0:T(8,128)(2,1)}, bf16[1152,1920]{1,0:T(8,128)(2,1)}, bf16[2,640,1152]{2,1,0:T(8,128)(2,1)}...) custom-call(bf16[4,656,288]{2,1,0:T(8,128)(2,1)} %copy.99.x4_ref, bf16[4,1152,480]{2,1,0:T(8,128)(2,1)} %bitcast.246, ...), custom_call_target="tpu_custom_call" | custom-call | flops 2831155200 | bytes 16777216 | tf_op jit(solution)/shard_map/project_in/pallas_call | solution.py:511
  80.9 6.5 all_to_all.50
  89.4 5.1 all-to-all-start.2
  94.6 38.5 %collective-permute-done.refs_2_.refs_8_ = bf16[1280,384]{1,0:T(8,128)(2,1)} collective-permute-done((bf16[1280,384]{1,0:T(8,128)(2,1)}, bf16[1280,384]{1,0:T(8,128)(2,1)}, u32[]{:S(2)}, u32[]{:S(2)}) %collective-permute-start) | collective-permute-done | bytes 983072 | tf_op jit(solution)/shard_map/ppermute | solution.py:916
  135.4 25.0 %attention_stage.4 = (f32[3,5,80,768]{3,2,1,0:T(8,128)S(1)}, f32[3,5,1,768]{3,2,1,0:T(1,128)S(1)}) custom-call(s32[75]{0:T(128)S(1)} %select_n.164.lists, s32[5]{0:T(128)S(1)} %get-tuple-element.200.counts, bf16[1280,1152]{1,0:T(8,128)(2,1)} %bitcast.3.q_ref, bf16[3840,128]{1,0:T(8,128)(2,1)S(1)} %pad_maximum_fusion.1.mark_ref, ...), custom_call_target="tpu_custom_call" | custom-call | flops 11324620800 | bytes 5898240 | tf_op jit(solution)/shard_map/attention_stage/pallas_call | solution.py:323
  162.4 16.2 %collective-permute-done.1.refs_3_.refs_7_ = bf16[1280,384]{1,0:T(8,128)(2,1)} collective-permute-done((bf16[1280,384]{1,0:T(8,128)(2,1)}, bf16[1280,384]{1,0:T(8,128)(2,1)}, u32[]{:S(2)}, u32[]{:S(2)}) %collective-permute-start.1) | collective-permute-done | bytes 983072 | tf_op jit(solution)/shard_map/ppermute | solution.py:928
  183.6 4.3 all-to-all-start.3
  190.0 13.5 %attention_stage.5 = (f32[3,5,80,768]{3,2,1,0:T(8,128)S(1)}, f32[3,5,1,768]{3,2,1,0:T(1,128)S(1)}) custom-call(s32[50]{0:T(128)S(1)} %select_n.168.lists, s32[5]{0:T(128)S(1)} %get-tuple-element.197.counts, bf16[1280,1152]{1,0:T(8,128)(2,1)} %bitcast.3.q_ref, bf16[2560,128]{1,0:T(8,128)(2,1)S(1)} %pad_maximum_fusion.3.mark_ref, ...), custom_call_target="tpu_custom_call" | custom-call | flops 7549747200 | bytes 3932160 | tf_op jit(solution)/shard_map/attention_stage/pallas_call | solution.py:323
  203.5 22.8 %collective-permute-done.4.refs_3_.refs_6_ = bf16[1280,384]{1,0:T(8,128)(2,1)} collective-permute-done((bf16[1280,384]{1,0:T(8,128)(2,1)}, bf16[1280,384]{1,0:T(8,128)(2,1)}, u32[]{:S(2)}, u32[]{:S(2)}) %collective-permute-start.4) | collective-permute-done | bytes 983072 | tf_op jit(solution)/shard_map/ppermute | solution.py:928
  231.2 13.5 %attention_stage.6 = (f32[3,5,80,768]{3,2,1,0:T(8,128)S(1)}, f32[3,5,1,768]{3,2,1,0:T(1,128)S(1)}) custom-call(s32[50]{0:T(128)S(1)} %select_n.172.lists, s32[5]{0:T(128)S(1)} %get-tuple-element.194.counts, bf16[1280,1152]{1,0:T(8,128)(2,1)} %bitcast.3.q_ref, bf16[2560,128]{1,0:T(8,128)(2,1)S(1)} %pad_maximum_fusion.4.mark_ref, ...), custom_call_target="tpu_custom_call" | custom-call | flops 7549747200 | bytes 3932160 | tf_op jit(solution)/shard_map/attention_stage/pallas_call | solution.py:323
  246.5 31.4 %collective-permute-done.6.refs_2_.refs_4_ = bf16[640,384]{1,0:T(8,128)(2,1)S(1)} collective-permute-done((bf16[640,384]{1,0:T(8,128)(2,1)S(1)}, bf16[640,384]{1,0:T(8,128)(2,1)S(1)}, u32[]{:S(2)}, u32[]{:S(2)}) %collective-permute-start.6) | collective-permute-done | bytes 491552 | tf_op jit(solution)/shard_map/ppermute | solution.py:930
  277.9 2.4 copy-done.1
  280.3 12.1 %attention_stage.7 = (bf16[1280,1152]{1,0:T(8,128)(2,1)}, f32[3,5,1,768]{3,2,1,0:T(1,128)S(1)}) custom-call(s32[25]{0:T(128)S(1)} %select_n.176.lists, s32[5]{0:T(128)S(1)} %get-tuple-element.189.counts, bf16[1280,1152]{1,0:T(8,128)(2,1)} %bitcast.3.q_ref, bf16[1280,128]{1,0:T(8,128)(2,1)S(1)} %get-tuple-element.190.mark_ref, ...), custom_call_target="tpu_custom_call" | custom-call | flops 3774873600 | bytes 1966080 | tf_op jit(solution)/shard_map/attention_stage/pallas_call | solution.py:323
  293.9 4.1 all-to-all-start.4
  298.0 3.6 copy.102.back_ref.upstream_ref.refs_3_
  303.3 8.6 %project_out.1 = (bf16[640,1152]{1,0:T(8,128)(2,1)}, f32[640,1152]{1,0:T(8,128)}, bf16[640,1152]{1,0:T(8,128)(2,1)}, bf16[1152,1152]{1,0:T(8,128)(2,1)}) custom-call(bf16[2,640,1152]{2,1,0:T(8,128)(2,1)} %copy-done.6, bf16[4,1152,2688]{2,1,0:T(8,128)(2,1)} %bitcast.204, bf16[640,1152]{1,0:T(8,128)(2,1)} %get-tuple-element.227.x_ref, ...), custom_call_target="tpu_custom_call" | custom-call | flops 1698693120 | bytes 16777216 | tf_op jit(solution)/shard_map/project_out/pallas_call | solution.py:540
  311.9 38.6 %feed_forward.1 = (bf16[640,3072]{1,0:T(8,128)(2,1)}, bf16[640,3072]{1,0:T(8,128)(2,1)}, bf16[640,3072]{1,0:T(8,128)(2,1)}, f32[640,1152]{1,0:T(8,128)}, f32[640,1152]{1,0:T(8,128)}) custom-call(bf16[640,1152]{1,0:T(8,128)(2,1)} %get-tuple-element.229.normed_ref.refs_0_, bf16[640,1152]{1,0:T(8,128)(2,1)} %copy.102.back_ref.upstream_ref.refs_3_, ...), custom_call_target="tpu_custom_call" | custom-call | flops 27179089920 | bytes 21233664 | tf_op jit(solution)/shard_map/feed_forward/pallas_call | solution.py:678
  350.5 9.3 %output_back.1 = (f32[640,1152]{1,0:T(8,128)}, bf16[640,1152]{1,0:T(8,128)(2,1)}, bf16[2,640,1152]{2,1,0:T(8,128)(2,1)}, f32[8,1152]{1,0:T(8,128)}) custom-call(f32[640,1152]{1,0:T(8,128)} %get-tuple-element.233.back_ref, f32[640,1152]{1,0:T(8,128)} %get-tuple-element.234.hidden_ref, bf16[640,1152]{1,0:T(8,128)(2,1)} %copy.102.back_ref.upstream_ref.refs_3_, ...), custom_call_target="tpu_custom_call" | custom-call | flops 1698693120 | bytes 16777216 | tf_op jit(solution)/shard_map/output_back/pallas_call | solution.py:589
  359.8 3.9 all-to-all-start.5
  363.8 23.5 %gradient_parts.3 = bf16[4,4,288,2304]{3,2,1,0:T(8,128)(2,1)} custom-call(bf16[640,1152]{1,0:T(8,128)(2,1)} %get-tuple-element.229.normed_ref.refs_0_, bf16[640,3072]{1,0:T(8,128)(2,1)} %get-tuple-element.231.refs_1_, bf16[640,3072]{1,0:T(8,128)(2,1)} %get-tuple-element.232.refs_2_, bf16[640,1152]{1,0:T(8,128)(2,1)} %copy.102.back_ref.upstream_ref.refs_3_, ...), custom_call_target="tpu_custom_call" | custom-call | flops 13589544960 | bytes 21233664 | tf_op jit(solution)/shard_map/gradient_parts/pallas_call | solution.py:750
  391.2 18.1 %attention_backward.3 = (bf16[1280,384]{1,0:T(8,128)(2,1)}, bf16[10240,128]{1,0:T(8,128)(2,1)}) custom-call(s32[200]{0:T(256)S(1)} %select_n.160.lists, s32[5]{0:T(128)S(1)} %get-tuple-element.183.counts, bf16[1280,1152]{1,0:T(8,128)(2,1)} %bitcast.3.q_ref, bf16[1280,1152]{1,0:T(8,128)(2,1)} %bitcast.221, bf16[1280,1152]{1,0:T(8,128)(2,1)} %get-tuple-element.226.o_ref, ...), custom_call_target="tpu_custom_call" | custom-call | flops 25165824000 | bytes 10485760 | tf_op jit(solution)/shard_map/attention_backward/pallas_call | solution.py:412
  412.3 13.3 %collective-permute-start.9 = (bf16[640,128]{1,0:T(8,128)(2,1)S(1)}, bf16[640,128]{1,0:T(8,128)(2,1)S(1)}, u32[]{:S(2)}, u32[]{:S(2)}) collective-permute-start(bf16[640,128]{1,0:T(8,128)(2,1)S(1)} %get-tuple-element.246), channel_id=1, source_target_pairs={{1,0},{2,1},{3,2},{11,3},{10,11},{9,10},{8,9},{0,8},{5,4},{6,5},{7... | collective-permute-start | bytes 491528 | tf_op jit(solution)/shard_map/ppermute | solution.py:786
  425.6 18.6 %attention_backward.4 = (bf16[1280,384]{1,0:T(8,128)(2,1)}, bf16[10240,128]{1,0:T(8,128)(2,1)}) custom-call(s32[200]{0:T(256)S(1)} %select_n.160.lists, s32[5]{0:T(128)S(1)} %get-tuple-element.183.counts, bf16[1280,1152]{1,0:T(8,128)(2,1)} %bitcast.3.q_ref, bf16[1280,1152]{1,0:T(8,128)(2,1)} %bitcast.222, bf16[1280,1152]{1,0:T(8,128)(2,1)} %get-tuple-element.226.o_ref, ...), custom_call_target="tpu_custom_call" | custom-call | flops 25165824000 | bytes 10485760 | tf_op jit(solution)/shard_map/attention_backward/pallas_call | solution.py:412
  444.2 7.9 gradient_parts.4
  454.5 37.1 %collective-permute-start.10 = (bf16[1280,128]{1,0:T(8,128)(2,1)S(1)}, bf16[1280,128]{1,0:T(8,128)(2,1)}, u32[]{:S(2)}, u32[]{:S(2)}) collective-permute-start(bf16[1280,128]{1,0:T(8,128)(2,1)S(1)} %pad_maximum_fusion.7), channel_id=1, source_target_pairs={{0,1},{1,2},{2,3},{3,11},{11,10},{10,9},{9,8},{8,0},{4,5},{5,6},{6... | collective-permute-start | bytes 983048 | tf_op jit(solution)/shard_map/ppermute | solution.py:786
  491.6 49.7 %collective-permute-start.12 = (bf16[640,128]{1,0:T(8,128)(2,1)S(1)}, bf16[640,128]{1,0:T(8,128)(2,1)}, u32[]{:S(2)}, u32[]{:S(2)}) collective-permute-start(bf16[640,128]{1,0:T(8,128)(2,1)S(1)} %get-tuple-element.254), channel_id=1, source_target_pairs={{0,1},{1,2},{2,3},{3,11},{11,10},{10,9},{9,8},{8,0},{4,5},{5,6},{6... | collective-permute-start | bytes 491528 | tf_op jit(solution)/shard_map/ppermute | solution.py:786
  541.2 17.9 %attention_backward.5 = (bf16[1280,384]{1,0:T(8,128)(2,1)}, bf16[10240,128]{1,0:T(8,128)(2,1)}) custom-call(s32[200]{0:T(256)S(1)} %select_n.160.lists, s32[5]{0:T(128)S(1)} %get-tuple-element.183.counts, bf16[1280,1152]{1,0:T(8,128)(2,1)} %bitcast.3.q_ref, bf16[1280,1152]{1,0:T(8,128)(2,1)} %bitcast.223, bf16[1280,1152]{1,0:T(8,128)(2,1)} %get-tuple-element.226.o_ref, ...), custom_call_target="tpu_custom_call" | custom-call | flops 25165824000 | bytes 10485760 | tf_op jit(solution)/shard_map/attention_backward/pallas_call | solution.py:412
  559.2 2.1 slice_bitcast_fusion.13
  561.3 36.2 %collective-permute-start.24 = (bf16[640,128]{1,0:T(8,128)(2,1)S(1)}, bf16[640,128]{1,0:T(8,128)(2,1)S(1)}, u32[]{:S(2)}, u32[]{:S(2)}) collective-permute-start(bf16[640,128]{1,0:T(8,128)(2,1)S(1)} %get-tuple-element.394), channel_id=1, source_target_pairs={{0,1},{1,2},{2,3},{3,11},{11,10},{10,9},{9,8},{8,0},{4,5},{5,6},{6... | collective-permute-start | bytes 491528 | tf_op jit(solution)/shard_map/ppermute | solution.py:786
  597.4 2.3 fusion.15
  599.7 15.0 %collective-permute-start.14 = (bf16[1280,128]{1,0:T(8,128)(2,1)}, bf16[1280,128]{1,0:T(8,128)(2,1)}, u32[]{:S(2)}, u32[]{:S(2)}) collective-permute-start(bf16[1280,128]{1,0:T(8,128)(2,1)} %get-tuple-element.258), channel_id=1, source_target_pairs={{0,1},{1,2},{2,3},{3,11},{11,10},{10,9},{9,8},{8,0},{4,5},{5,6},{6... | collective-permute-start | bytes 983048 | tf_op jit(solution)/shard_map/ppermute | solution.py:786
  617.4 10.7 %collective-permute-start.18 = (bf16[1280,128]{1,0:T(8,128)(2,1)}, bf16[1280,128]{1,0:T(8,128)(2,1)}, u32[]{:S(2)}, u32[]{:S(2)}) collective-permute-start(bf16[1280,128]{1,0:T(8,128)(2,1)} %pad_maximum_fusion.9), channel_id=1, source_target_pairs={{0,1},{1,2},{2,3},{3,11},{11,10},{10,9},{9,8},{8,0},{4,5},{5,6},{6... | collective-permute-start | bytes 983048 | tf_op jit(solution)/shard_map/ppermute | solution.py:786
  628.9 2.1 add_convert_fusion
  631.0 2.1 copy.105
  633.1 3.1 pad_maximum_fusion
  636.1 4.0 all-to-all-start.6
  641.6 5.3 collective-permute-start.26
  648.4 2.1 collective-permute-start.16
  655.4 2.1 collective-permute-done.27
  658.1 10.9 %collective-permute-done.20 = bf16[1280,128]{1,0:T(8,128)(2,1)S(1)} collective-permute-done((bf16[1280,128]{1,0:T(8,128)(2,1)S(1)}, bf16[1280,128]{1,0:T(8,128)(2,1)S(1)}, u32[]{:S(2)}, u32[]{:S(2)}) %collective-permute-start.20) | collective-permute-done | bytes 327712 | tf_op jit(solution)/shard_map/ppermute | solution.py:786
  676.0 4.1 collective-permute-done.29
  680.3 2.1 collective-permute-start.30
  683.0 4.1 collective-permute-done.23
  687.3 2.4 collective-permute-done.30
  689.7 3.0 collective-permute-done.31
  694.0 6.5 all_to_all.51.pair_ref
  700.5 4.3 all-to-all-start.8
  704.9 12.3 %joint_back.1 = (bf16[640,1920]{1,0:T(8,128)(2,1)}, bf16[4,640,288]{2,1,0:T(8,128)(2,1)}, f32[8,1152]{1,0:T(8,128)}) custom-call(bf16[2,640,1152]{2,1,0:T(8,128)(2,1)} %copy-done.5, bf16[2,640,384]{2,1,0:T(8,128)(2,1)} %all_to_all.51.pair_ref, f32[640,128]{1,0:T(8,128)} %get-tuple-element.437.cos_ref, f32[640,128]{1,0:T(8,128)} %get-tuple-element.438.sin_ref, ...), custom_call_target="tpu_custom_call" | custom-call | flops 2831155200 | bytes 16777216 | tf_op jit(solution)/shard_map/joint_back/pallas_call | solution.py:638
  719.3 4.7 all-to-all-done.8
  724.0 2.6 copy.116
  726.6 9.0 %gradient_parts.5 = bf16[4,4,288,512]{3,2,1,0:T(8,128)(2,1)} custom-call(bf16[640,1152]{1,0:T(8,128)(2,1)} %get-tuple-element.299.refs_0_, bf16[640,1920]{1,0:T(8,128)(2,1)} %get-tuple-element.300.refs_1_, f32[4,288,1]{2,1,0:T(8,128)} %reshape_squeeze.9.refs_2_), custom_call_target="tpu_custom_call" | custom-call | flops 3019898880 | bytes 4718592 | tf_op jit(solution)/shard_map/gradient_parts/pallas_call | solution.py:750
  753.2 5.4 collective-permute-done.34
  759.4 2.2 collective-permute-start.36
  761.6 3.2 collective-permute-start.37
  764.9 2.4 copy.108
  767.3 3.7 all-to-all-start.9
  786.8 11.9 %collective-permute-done.38 = bf16[288,512]{1,0:T(8,128)(2,1)S(1)} collective-permute-done((bf16[288,512]{1,0:T(8,128)(2,1)S(1)}, bf16[288,512]{1,0:T(8,128)(2,1)S(1)}, u32[]{:S(2)}, u32[]{:S(2)}) %collective-permute-start.38) | collective-permute-done | bytes 294944 | tf_op jit(solution)/shard_map/ppermute | solution.py:786
  804.4 4.3 collective-permute-done.40
  (279 shorter events, 102.0 us)
Async XLA Ops:
  7.2 62.7 %all-gather.3.cloned.1.call-start = ((), (), s32[]{:S(2)}) async-start(), calls=%async_computation.12 | async-start | bytes 5013504 | tf_op jit(solution)/shard_map/all_gather | solution.py:841
  7.9 293.7 %all-gather.5.cloned.1.call-start = ((), (), s32[]{:S(2)}) async-start(), calls=%async_computation.13 | async-start | bytes 26320896 | tf_op jit(solution)/shard_map/all_gather | solution.py:841
  16.2 5.8 copy-start.25
  16.2 32.3 %all-to-all-start = ((bf16[4,656,288]{1,2,0:T(8,128)(2,1)}), bf16[4,656,288]{1,2,0:T(8,128)(2,1)}, u32[]{:S(2)}, u32[]{:S(2)}) async-start(bf16[4,656,288]{1,2,0:T(8,128)(2,1)} %copy.96), calls=%async_computation | async-start | bytes 3538944 | tf_op jit(solution)/shard_map/all_to_all | solution.py:889
  87.4 45.7 %collective-permute-start = (bf16[1280,384]{1,0:T(8,128)(2,1)}, bf16[1280,384]{1,0:T(8,128)(2,1)}, u32[]{:S(2)}, u32[]{:S(2)}) collective-permute-start(bf16[1280,384]{1,0:T(8,128)(2,1)} %bitcast.2.refs_0_), channel_id=1, source_target_pairs={{0,1},{1,2},{2,3},{3,11},{11,10},{10,9},{9,8},{8,0},{4,5},{5,6},{6... | collective-permute-start | bytes 2949128 | tf_op jit(solution)/shard_map/ppermute | solution.py:916
  89.0 45.7 %collective-permute-start.2 = (bf16[1280,384]{1,0:T(8,128)(2,1)}, bf16[1280,384]{1,0:T(8,128)(2,1)}, u32[]{:S(2)}, u32[]{:S(2)}) collective-permute-start(bf16[1280,384]{1,0:T(8,128)(2,1)} %bitcast.2.refs_0_), channel_id=1, source_target_pairs={{1,0},{2,1},{3,2},{11,3},{10,11},{9,10},{8,9},{0,8},{5,4},{6,5},{7... | collective-permute-start | bytes 2949128 | tf_op jit(solution)/shard_map/ppermute | solution.py:916
  89.4 46.0 %all-to-all-start.2 = ((bf16[2,640,1152]{2,1,0:T(8,128)(2,1)}), bf16[2,640,1152]{2,1,0:T(8,128)(2,1)}, u32[]{:S(2)}, u32[]{:S(2)}) async-start(bf16[2,640,1152]{2,1,0:T(8,128)(2,1)} %get-tuple-element.187), calls=%async_computation.2 | async-start | bytes 5898240 | tf_op jit(solution)/shard_map/all_to_all | solution.py:889
  133.1 45.4 %collective-permute-start.1 = (bf16[1280,384]{1,0:T(8,128)(2,1)}, bf16[1280,384]{1,0:T(8,128)(2,1)}, u32[]{:S(2)}, u32[]{:S(2)}) collective-permute-start(bf16[1280,384]{1,0:T(8,128)(2,1)} %collective-permute-done.refs_2_.refs_8_), channel_id=1, source_target_pairs={{0,1},{1,2},{2,3},{3,11},{11,10},{10,9},{9,8},{8,0},{4,5},{5,6},{6... | collective-permute-start | bytes 2949128 | tf_op jit(solution)/shard_map/ppermute | solution.py:928
  134.7 45.6 %collective-permute-start.3 = (bf16[1280,384]{1,0:T(8,128)(2,1)}, bf16[1280,384]{1,0:T(8,128)(2,1)}, u32[]{:S(2)}, u32[]{:S(2)}) collective-permute-start(bf16[1280,384]{1,0:T(8,128)(2,1)} %collective-permute-done.2.refs_1_), channel_id=1, source_target_pairs={{1,0},{2,1},{3,2},{11,3},{10,11},{9,10},{8,9},{0,8},{5,4},{6,5},{7... | collective-permute-start | bytes 2949128 | tf_op jit(solution)/shard_map/ppermute | solution.py:928
  135.4 46.9 %copy-start.15 = (bf16[2560,288]{0,1:T(8,128)(2,1)S(1)}, bf16[2560,288]{0,1:T(8,128)(2,1)}, u32[]{:S(2)}) copy-start(bf16[2560,288]{0,1:T(8,128)(2,1)} %param.21) | copy-start | bytes 4423684
  180.3 46.0 %collective-permute-start.4 = (bf16[1280,384]{1,0:T(8,128)(2,1)}, bf16[1280,384]{1,0:T(8,128)(2,1)}, u32[]{:S(2)}, u32[]{:S(2)}) collective-permute-start(bf16[1280,384]{1,0:T(8,128)(2,1)} %collective-permute-done.1.refs_3_.refs_7_), channel_id=1, source_target_pairs={{0,1},{1,2},{2,3},{3,11},{11,10},{10,9},{9,8},{8,0},{4,5},{5,6},{6... | collective-permute-start | bytes 2949128 | tf_op jit(solution)/shard_map/ppermute | solution.py:928
  181.3 45.0 %collective-permute-start.5 = (bf16[1280,384]{1,0:T(8,128)(2,1)}, bf16[1280,384]{1,0:T(8,128)(2,1)}, u32[]{:S(2)}, u32[]{:S(2)}) collective-permute-start(bf16[1280,384]{1,0:T(8,128)(2,1)} %collective-permute-done.3.refs_2_), channel_id=1, source_target_pairs={{1,0},{2,1},{3,2},{11,3},{10,11},{9,10},{8,9},{0,8},{5,4},{6,5},{7... | collective-permute-start | bytes 2949128 | tf_op jit(solution)/shard_map/ppermute | solution.py:928
  183.6 94.3 %all-to-all-start.3 = ((bf16[4,640,288]{1,2,0:T(8,128)(2,1)}), bf16[4,640,288]{1,2,0:T(8,128)(2,1)}, u32[]{:S(2)}, u32[]{:S(2)}) async-start(bf16[4,640,288]{1,2,0:T(8,128)(2,1)} %bitcast.211), calls=%async_computation.3 | async-start | bytes 2949120 | tf_op jit(solution)/shard_map/all_to_all | solution.py:889
  227.4 50.5 %collective-permute-start.6 = (bf16[640,384]{1,0:T(8,128)(2,1)S(1)}, bf16[640,384]{1,0:T(8,128)(2,1)S(1)}, u32[]{:S(2)}, u32[]{:S(2)}) collective-permute-start(bf16[640,384]{1,0:T(8,128)(2,1)S(1)} %slice.405), channel_id=1, source_target_pairs={{0,1},{1,2},{2,3},{3,11},{11,10},{10,9},{9,8},{8,0},{4,5},{5,6},{6... | collective-permute-start | bytes 1474568 | tf_op jit(solution)/shard_map/ppermute | solution.py:930
  229.3 48.6 %collective-permute-start.7 = (bf16[640,384]{1,0:T(8,128)(2,1)S(1)}, bf16[640,384]{1,0:T(8,128)(2,1)S(1)}, u32[]{:S(2)}, u32[]{:S(2)}) collective-permute-start(bf16[640,384]{1,0:T(8,128)(2,1)S(1)} %slice.406), channel_id=1, source_target_pairs={{1,0},{2,1},{3,2},{11,3},{10,11},{9,10},{8,9},{0,8},{5,4},{6,5},{7... | collective-permute-start | bytes 1474568 | tf_op jit(solution)/shard_map/ppermute | solution.py:930
  277.9 113.3 %copy-start.29 = (bf16[640,384]{1,0:T(8,128)(2,1)}, bf16[640,384]{1,0:T(8,128)(2,1)S(1)}, u32[]{:S(2)}) copy-start(bf16[640,384]{1,0:T(8,128)(2,1)S(1)} %collective-permute-done.6.refs_2_.refs_4_) | copy-start | bytes 1474564
  277.9 15.9 %copy-start.30 = (bf16[640,384]{1,0:T(8,128)(2,1)}, bf16[640,384]{1,0:T(8,128)(2,1)S(1)}, u32[]{:S(2)}) copy-start(bf16[640,384]{1,0:T(8,128)(2,1)S(1)} %collective-permute-done.7.refs_3_.refs_5_) | copy-start | bytes 1474564
  293.9 7.7 all-to-all-start.4
  359.8 27.5 %all-to-all-start.5 = ((bf16[2,640,1152]{2,1,0:T(8,128)(2,1)}), bf16[2,640,1152]{2,1,0:T(8,128)(2,1)S(1)}, u32[]{:S(2)}, u32[]{:S(2)}) async-start(bf16[2,640,1152]{2,1,0:T(8,128)(2,1)} %get-tuple-element.239), calls=%async_computation.5 | async-start | bytes 5898240 | tf_op jit(solution)/shard_map/all_to_all | solution.py:889
  363.8 330.2 %reduce-scatter.5.cloned.1.call-start = ((), (), s32[]{:S(2)}) async-start(), calls=%async_computation.14 | async-start | bytes 22560768 | tf_op jit(solution)/shard_map/reduce_scatter | solution.py:837
  410.6 41.5 %collective-permute-start.8 = (bf16[640,128]{1,0:T(8,128)(2,1)S(1)}, bf16[640,128]{1,0:T(8,128)(2,1)S(1)}, u32[]{:S(2)}, u32[]{:S(2)}) collective-permute-start(bf16[640,128]{1,0:T(8,128)(2,1)S(1)} %get-tuple-element.245), channel_id=1, source_target_pairs={{0,1},{1,2},{2,3},{3,11},{11,10},{10,9},{9,8},{8,0},{4,5},{5,6},{6... | collective-permute-start | bytes 491528 | tf_op jit(solution)/shard_map/ppermute | solution.py:786
  412.3 39.8 %collective-permute-start.9 = (bf16[640,128]{1,0:T(8,128)(2,1)S(1)}, bf16[640,128]{1,0:T(8,128)(2,1)S(1)}, u32[]{:S(2)}, u32[]{:S(2)}) collective-permute-start(bf16[640,128]{1,0:T(8,128)(2,1)S(1)} %get-tuple-element.246), channel_id=1, source_target_pairs={{1,0},{2,1},{3,2},{11,3},{10,11},{9,10},{8,9},{0,8},{5,4},{6,5},{7... | collective-permute-start | bytes 491528 | tf_op jit(solution)/shard_map/ppermute | solution.py:786
  454.5 104.6 %collective-permute-start.10 = (bf16[1280,128]{1,0:T(8,128)(2,1)S(1)}, bf16[1280,128]{1,0:T(8,128)(2,1)}, u32[]{:S(2)}, u32[]{:S(2)}) collective-permute-start(bf16[1280,128]{1,0:T(8,128)(2,1)S(1)} %pad_maximum_fusion.7), channel_id=1, source_target_pairs={{0,1},{1,2},{2,3},{3,11},{11,10},{10,9},{9,8},{8,0},{4,5},{5,6},{6... | collective-permute-start | bytes 983048 | tf_op jit(solution)/shard_map/ppermute | solution.py:786
  491.6 67.6 %collective-permute-start.11 = (bf16[1280,128]{1,0:T(8,128)(2,1)S(1)}, bf16[1280,128]{1,0:T(8,128)(2,1)}, u32[]{:S(2)}, u32[]{:S(2)}) collective-permute-start(bf16[1280,128]{1,0:T(8,128)(2,1)S(1)} %pad_maximum_fusion.8), channel_id=1, source_target_pairs={{1,0},{2,1},{3,2},{11,3},{10,11},{9,10},{8,9},{0,8},{5,4},{6,5},{7... | collective-permute-start | bytes 983048 | tf_op jit(solution)/shard_map/ppermute | solution.py:786
  491.6 67.6 %collective-permute-start.12 = (bf16[640,128]{1,0:T(8,128)(2,1)S(1)}, bf16[640,128]{1,0:T(8,128)(2,1)}, u32[]{:S(2)}, u32[]{:S(2)}) collective-permute-start(bf16[640,128]{1,0:T(8,128)(2,1)S(1)} %get-tuple-element.254), channel_id=1, source_target_pairs={{0,1},{1,2},{2,3},{3,11},{11,10},{10,9},{9,8},{8,0},{4,5},{5,6},{6... | collective-permute-start | bytes 491528 | tf_op jit(solution)/shard_map/ppermute | solution.py:786
  541.2 17.9 %collective-permute-start.13 = (bf16[640,128]{1,0:T(8,128)(2,1)S(1)}, bf16[640,128]{1,0:T(8,128)(2,1)}, u32[]{:S(2)}, u32[]{:S(2)}) collective-permute-start(bf16[640,128]{1,0:T(8,128)(2,1)S(1)} %get-tuple-element.255), channel_id=1, source_target_pairs={{1,0},{2,1},{3,2},{11,3},{10,11},{9,10},{8,9},{0,8},{5,4},{6,5},{7... | collective-permute-start | bytes 491528 | tf_op jit(solution)/shard_map/ppermute | solution.py:786
  559.2 69.7 %copy-start.4 = (f32[640,1152]{1,0:T(8,128)S(1)}, f32[640,1152]{1,0:T(8,128)}, u32[]{:S(2)}) copy-start(f32[640,1152]{1,0:T(8,128)} %get-tuple-element.234.hidden_ref) | copy-start | bytes 8847364
  561.3 66.9 %collective-permute-start.24 = (bf16[640,128]{1,0:T(8,128)(2,1)S(1)}, bf16[640,128]{1,0:T(8,128)(2,1)S(1)}, u32[]{:S(2)}, u32[]{:S(2)}) collective-permute-start(bf16[640,128]{1,0:T(8,128)(2,1)S(1)} %get-tuple-element.394), channel_id=1, source_target_pairs={{0,1},{1,2},{2,3},{3,11},{11,10},{10,9},{9,8},{8,0},{4,5},{5,6},{6... | collective-permute-start | bytes 491528 | tf_op jit(solution)/shard_map/ppermute | solution.py:786
  597.4 30.7 %collective-permute-start.25 = (bf16[640,128]{1,0:T(8,128)(2,1)S(1)}, bf16[640,128]{1,0:T(8,128)(2,1)S(1)}, u32[]{:S(2)}, u32[]{:S(2)}) collective-permute-start(bf16[640,128]{1,0:T(8,128)(2,1)S(1)} %get-tuple-element.393), channel_id=1, source_target_pairs={{1,0},{2,1},{3,2},{11,3},{10,11},{9,10},{8,9},{0,8},{5,4},{6,5},{7... | collective-permute-start | bytes 491528 | tf_op jit(solution)/shard_map/ppermute | solution.py:786
  599.7 47.2 %collective-permute-start.14 = (bf16[1280,128]{1,0:T(8,128)(2,1)}, bf16[1280,128]{1,0:T(8,128)(2,1)}, u32[]{:S(2)}, u32[]{:S(2)}) collective-permute-start(bf16[1280,128]{1,0:T(8,128)(2,1)} %get-tuple-element.258), channel_id=1, source_target_pairs={{0,1},{1,2},{2,3},{3,11},{11,10},{10,9},{9,8},{8,0},{4,5},{5,6},{6... | collective-permute-start | bytes 983048 | tf_op jit(solution)/shard_map/ppermute | solution.py:786
  614.7 32.3 %collective-permute-start.15 = (bf16[1280,128]{1,0:T(8,128)(2,1)}, bf16[1280,128]{1,0:T(8,128)(2,1)}, u32[]{:S(2)}, u32[]{:S(2)}) collective-permute-start(bf16[1280,128]{1,0:T(8,128)(2,1)} %get-tuple-element.259), channel_id=1, source_target_pairs={{1,0},{2,1},{3,2},{11,3},{10,11},{9,10},{8,9},{0,8},{5,4},{6,5},{7... | collective-permute-start | bytes 983048 | tf_op jit(solution)/shard_map/ppermute | solution.py:786
  617.4 33.1 %collective-permute-start.18 = (bf16[1280,128]{1,0:T(8,128)(2,1)}, bf16[1280,128]{1,0:T(8,128)(2,1)}, u32[]{:S(2)}, u32[]{:S(2)}) collective-permute-start(bf16[1280,128]{1,0:T(8,128)(2,1)} %pad_maximum_fusion.9), channel_id=1, source_target_pairs={{0,1},{1,2},{2,3},{3,11},{11,10},{10,9},{9,8},{8,0},{4,5},{5,6},{6... | collective-permute-start | bytes 983048 | tf_op jit(solution)/shard_map/ppermute | solution.py:786
  628.1 22.3 %collective-permute-start.19 = (bf16[1280,128]{1,0:T(8,128)(2,1)}, bf16[1280,128]{1,0:T(8,128)(2,1)}, u32[]{:S(2)}, u32[]{:S(2)}) collective-permute-start(bf16[1280,128]{1,0:T(8,128)(2,1)} %pad_maximum_fusion.10), channel_id=1, source_target_pairs={{1,0},{2,1},{3,2},{11,3},{10,11},{9,10},{8,9},{0,8},{5,4},{6,5},{7... | collective-permute-start | bytes 983048 | tf_op jit(solution)/shard_map/ppermute | solution.py:786
  636.1 57.8 %all-to-all-start.6 = ((bf16[2,640,1152]{2,1,0:T(8,128)(2,1)}), bf16[2,640,1152]{2,1,0:T(8,128)(2,1)S(1)}, u32[]{:S(2)}, u32[]{:S(2)}) async-start(bf16[2,640,1152]{2,1,0:T(8,128)(2,1)} %bitcast.209), calls=%async_computation.6 | async-start | bytes 5898240 | tf_op jit(solution)/shard_map/all_to_all | solution.py:889
  640.2 10.3 %copy-start.11 = (bf16[10240,128]{1,0:T(8,128)(2,1)S(1)}, bf16[10240,128]{1,0:T(8,128)(2,1)}, u32[]{:S(2)}) copy-start(bf16[10240,128]{1,0:T(8,128)(2,1)} %get-tuple-element.244) | copy-start | bytes 7864324
  641.5 15.9 %copy-start.12 = (bf16[10240,128]{1,0:T(8,128)(2,1)S(1)}, bf16[10240,128]{1,0:T(8,128)(2,1)}, u32[]{:S(2)}) copy-start(bf16[10240,128]{1,0:T(8,128)(2,1)} %get-tuple-element.251) | copy-start | bytes 7864324
  641.6 13.3 %collective-permute-start.26 = (bf16[1280,128]{1,0:T(8,128)(2,1)S(1)}, bf16[1280,128]{1,0:T(8,128)(2,1)S(1)}, u32[]{:S(2)}, u32[]{:S(2)}) collective-permute-start(bf16[1280,128]{1,0:T(8,128)(2,1)S(1)} %pad_maximum_fusion.11), channel_id=1, source_target_pairs={{0,1},{1,2},{2,3},{3,11},{11,10},{10,9},{9,8},{8,0},{4,5},{5,6},{6... | collective-permute-start | bytes 983048 | tf_op jit(solution)/shard_map/ppermute | solution.py:786
  646.9 10.6 %collective-permute-start.27 = (bf16[1280,128]{1,0:T(8,128)(2,1)S(1)}, bf16[1280,128]{1,0:T(8,128)(2,1)S(1)}, u32[]{:S(2)}, u32[]{:S(2)}) collective-permute-start(bf16[1280,128]{1,0:T(8,128)(2,1)S(1)} %pad_maximum_fusion.12), channel_id=1, source_target_pairs={{1,0},{2,1},{3,2},{11,3},{10,11},{9,10},{8,9},{0,8},{5,4},{6,5},{7... | collective-permute-start | bytes 983048 | tf_op jit(solution)/shard_map/ppermute | solution.py:786
  648.4 23.3 %collective-permute-start.16 = (bf16[1280,128]{1,0:T(8,128)(2,1)S(1)}, bf16[1280,128]{1,0:T(8,128)(2,1)S(1)}, u32[]{:S(2)}, u32[]{:S(2)}) collective-permute-start(bf16[1280,128]{1,0:T(8,128)(2,1)S(1)} %get-tuple-element.260), channel_id=1, source_target_pairs={{0,1},{1,2},{2,3},{3,11},{11,10},{10,9},{9,8},{8,0},{4,5},{5,6},{6... | collective-permute-start | bytes 983048 | tf_op jit(solution)/shard_map/ppermute | solution.py:786
  650.5 22.6 %collective-permute-start.17 = (bf16[1280,128]{1,0:T(8,128)(2,1)S(1)}, bf16[1280,128]{1,0:T(8,128)(2,1)S(1)}, u32[]{:S(2)}, u32[]{:S(2)}) collective-permute-start(bf16[1280,128]{1,0:T(8,128)(2,1)S(1)} %get-tuple-element.261), channel_id=1, source_target_pairs={{1,0},{2,1},{3,2},{11,3},{10,11},{9,10},{8,9},{0,8},{5,4},{6,5},{7... | collective-permute-start | bytes 983048 | tf_op jit(solution)/shard_map/ppermute | solution.py:786
  651.7 17.3 %collective-permute-start.20 = (bf16[1280,128]{1,0:T(8,128)(2,1)S(1)}, bf16[1280,128]{1,0:T(8,128)(2,1)S(1)}, u32[]{:S(2)}, u32[]{:S(2)}) collective-permute-start(bf16[1280,128]{1,0:T(8,128)(2,1)S(1)} %get-tuple-element.266), channel_id=1, source_target_pairs={{0,1},{1,2},{2,3},{3,11},{11,10},{10,9},{9,8},{8,0},{4,5},{5,6},{6... | collective-permute-start | bytes 983048 | tf_op jit(solution)/shard_map/ppermute | solution.py:786
  655.0 15.8 %collective-permute-start.21 = (bf16[1280,128]{1,0:T(8,128)(2,1)S(1)}, bf16[1280,128]{1,0:T(8,128)(2,1)S(1)}, u32[]{:S(2)}, u32[]{:S(2)}) collective-permute-start(bf16[1280,128]{1,0:T(8,128)(2,1)S(1)} %get-tuple-element.267), channel_id=1, source_target_pairs={{1,0},{2,1},{3,2},{11,3},{10,11},{9,10},{8,9},{0,8},{5,4},{6,5},{7... | collective-permute-start | bytes 983048 | tf_op jit(solution)/shard_map/ppermute | solution.py:786
  657.7 18.4 %collective-permute-start.28 = (bf16[1280,128]{1,0:T(8,128)(2,1)S(1)}, bf16[1280,128]{1,0:T(8,128)(2,1)S(1)}, u32[]{:S(2)}, u32[]{:S(2)}) collective-permute-start(bf16[1280,128]{1,0:T(8,128)(2,1)S(1)} %get-tuple-element.279), channel_id=1, source_target_pairs={{0,1},{1,2},{2,3},{3,11},{11,10},{10,9},{9,8},{8,0},{4,5},{5,6},{6... | collective-permute-start | bytes 983048 | tf_op jit(solution)/shard_map/ppermute | solution.py:786
  669.0 11.1 %collective-permute-start.29 = (bf16[1280,128]{1,0:T(8,128)(2,1)S(1)}, bf16[1280,128]{1,0:T(8,128)(2,1)S(1)}, u32[]{:S(2)}, u32[]{:S(2)}) collective-permute-start(bf16[1280,128]{1,0:T(8,128)(2,1)S(1)} %get-tuple-element.280), channel_id=1, source_target_pairs={{1,0},{2,1},{3,2},{11,3},{10,11},{9,10},{8,9},{0,8},{5,4},{6,5},{7... | collective-permute-start | bytes 983048 | tf_op jit(solution)/shard_map/ppermute | solution.py:786
  671.0 12.1 %collective-permute-start.22 = (bf16[1280,128]{1,0:T(8,128)(2,1)S(1)}, bf16[1280,128]{1,0:T(8,128)(2,1)S(1)}, u32[]{:S(2)}, u32[]{:S(2)}) collective-permute-start(bf16[1280,128]{1,0:T(8,128)(2,1)S(1)} %get-tuple-element.268), channel_id=1, source_target_pairs={{0,1},{1,2},{2,3},{3,11},{11,10},{10,9},{9,8},{8,0},{4,5},{5,6},{6... | collective-permute-start | bytes 983048 | tf_op jit(solution)/shard_map/ppermute | solution.py:786
  671.7 15.4 %collective-permute-start.23 = (bf16[1280,128]{1,0:T(8,128)(2,1)S(1)}, bf16[1280,128]{1,0:T(8,128)(2,1)S(1)}, u32[]{:S(2)}, u32[]{:S(2)}) collective-permute-start(bf16[1280,128]{1,0:T(8,128)(2,1)S(1)} %get-tuple-element.269), channel_id=1, source_target_pairs={{1,0},{2,1},{3,2},{11,3},{10,11},{9,10},{8,9},{0,8},{5,4},{6,5},{7... | collective-permute-start | bytes 983048 | tf_op jit(solution)/shard_map/ppermute | solution.py:786
  680.3 9.4 %collective-permute-start.30 = (bf16[1280,128]{1,0:T(8,128)(2,1)S(1)}, bf16[1280,128]{1,0:T(8,128)(2,1)S(1)}, u32[]{:S(2)}, u32[]{:S(2)}) collective-permute-start(bf16[1280,128]{1,0:T(8,128)(2,1)S(1)} %get-tuple-element.281), channel_id=1, source_target_pairs={{0,1},{1,2},{2,3},{3,11},{11,10},{10,9},{9,8},{8,0},{4,5},{5,6},{6... | collective-permute-start | bytes 983048 | tf_op jit(solution)/shard_map/ppermute | solution.py:786
  682.4 10.3 %collective-permute-start.31 = (bf16[1280,128]{1,0:T(8,128)(2,1)S(1)}, bf16[1280,128]{1,0:T(8,128)(2,1)S(1)}, u32[]{:S(2)}, u32[]{:S(2)}) collective-permute-start(bf16[1280,128]{1,0:T(8,128)(2,1)S(1)} %get-tuple-element.282), channel_id=1, source_target_pairs={{1,0},{2,1},{3,2},{11,3},{10,11},{9,10},{8,9},{0,8},{5,4},{6,5},{7... | collective-permute-start | bytes 983048 | tf_op jit(solution)/shard_map/ppermute | solution.py:786
  694.0 10.9 %copy-start.5 = (bf16[2,640,1152]{2,1,0:T(8,128)(2,1)}, bf16[2,640,1152]{2,1,0:T(8,128)(2,1)S(1)}, u32[]{:S(2)}) copy-start(bf16[2,640,1152]{2,1,0:T(8,128)(2,1)S(1)} %all-to-all-done.6.query_ref) | copy-start | bytes 8847364
  700.5 23.4 %all-to-all-start.8 = ((bf16[4,640,288]{1,2,0:T(8,128)(2,1)}), bf16[4,640,288]{1,2,0:T(8,128)(2,1)}, u32[]{:S(2)}, u32[]{:S(2)}) async-start(bf16[4,640,288]{1,2,0:T(8,128)(2,1)} %bitcast.210), calls=%async_computation.9 | async-start | bytes 2949120 | tf_op jit(solution)/shard_map/all_to_all | solution.py:889
  704.9 105.9 %reduce-scatter.7.cloned.1.call-start = ((), (), s32[]{:S(2)}) async-start(), calls=%async_computation.15 | async-start | bytes 3760128
  737.7 13.2 %collective-permute-start.32 = (bf16[8,288,512]{2,1,0:T(8,128)(2,1)S(1)}, bf16[8,288,512]{2,1,0:T(8,128)(2,1)}, u32[]{:S(2)}, u32[]{:S(2)}) collective-permute-start(bf16[8,288,512]{2,1,0:T(8,128)(2,1)S(1)} %dynamic-slice_bitcast_fusion), channel_id=1, source_target_pairs={{0,4},{4,0},{1,5},{5,1},{2,6},{6,2},{3,7},{7,3},{8,12},{12,8},{9,1... | collective-permute-start | bytes 7077896 | tf_op jit(solution)/shard_map/ppermute | solution.py:990
  741.3 1.8 collective-permute-start.33
  744.9 7.5 collective-permute-start.35
  749.1 9.5 %collective-permute-start.34 = (bf16[144,512]{1,0:T(8,128)(2,1)}, bf16[144,512]{1,0:T(8,128)(2,1)S(1)}, u32[]{:S(2)}, u32[]{:S(2)}) collective-permute-start(bf16[144,512]{1,0:T(8,128)(2,1)} %get-tuple-element.302), channel_id=1, source_target_pairs={{0,1},{1,2},{2,3},{3,11},{11,10},{10,9},{9,8},{8,0},{4,5},{5,6},{6... | collective-permute-start | bytes 442376 | tf_op jit(solution)/shard_map/ppermute | solution.py:786
  750.8 14.0 %copy-start.13 = (bf16[4,640,288]{2,1,0:T(8,128)(2,1)S(1)}, bf16[4,640,288]{2,1,0:T(8,128)(2,1)}, u32[]{:S(2)}) copy-start(bf16[4,640,288]{2,1,0:T(8,128)(2,1)} %get-tuple-element.298) | copy-start | bytes 4423684
  759.4 21.2 %collective-permute-start.36 = (bf16[288,512]{1,0:T(8,128)(2,1)}, bf16[288,512]{1,0:T(8,128)(2,1)}, u32[]{:S(2)}, u32[]{:S(2)}) collective-permute-start(bf16[288,512]{1,0:T(8,128)(2,1)} %pad_maximum_fusion.13), channel_id=1, source_target_pairs={{0,1},{1,2},{2,3},{3,11},{11,10},{10,9},{9,8},{8,0},{4,5},{5,6},{6... | collective-permute-start | bytes 884744 | tf_op jit(solution)/shard_map/ppermute | solution.py:786
  761.6 19.1 %collective-permute-start.37 = (bf16[288,512]{1,0:T(8,128)(2,1)}, bf16[288,512]{1,0:T(8,128)(2,1)}, u32[]{:S(2)}, u32[]{:S(2)}) collective-permute-start(bf16[288,512]{1,0:T(8,128)(2,1)} %pad_maximum_fusion.14), channel_id=1, source_target_pairs={{1,0},{2,1},{3,2},{11,3},{10,11},{9,10},{8,9},{0,8},{5,4},{6,5},{7... | collective-permute-start | bytes 884744 | tf_op jit(solution)/shard_map/ppermute | solution.py:786
  764.9 15.6 %copy-start.9 = (bf16[288,2304]{1,0:T(8,128)(2,1)S(1)}, bf16[288,2304]{1,0:T(8,128)(2,1)}, u32[]{:S(2)}) copy-start(bf16[288,2304]{1,0:T(8,128)(2,1)} %reduce-scatter.5.cloned.1.call-done) | copy-start | bytes 3981316
  767.3 34.9 %all-to-all-start.9 = ((bf16[4,640,288]{1,2,0:T(8,128)(2,1)}), bf16[4,640,288]{1,2,0:T(8,128)(2,1)S(1)}, u32[]{:S(2)}, u32[]{:S(2)}) async-start(bf16[4,640,288]{1,2,0:T(8,128)(2,1)} %copy.108), calls=%async_computation.10 | async-start | bytes 2949120 | tf_op jit(solution)/shard_map/all_to_all | solution.py:889
  782.4 16.3 %collective-permute-start.38 = (bf16[288,512]{1,0:T(8,128)(2,1)S(1)}, bf16[288,512]{1,0:T(8,128)(2,1)S(1)}, u32[]{:S(2)}, u32[]{:S(2)}) collective-permute-start(bf16[288,512]{1,0:T(8,128)(2,1)S(1)} %get-tuple-element.306), channel_id=1, source_target_pairs={{0,1},{1,2},{2,3},{3,11},{11,10},{10,9},{9,8},{8,0},{4,5},{5,6},{6... | collective-permute-start | bytes 884744 | tf_op jit(solution)/shard_map/ppermute | solution.py:786
  782.4 16.2 %collective-permute-start.39 = (bf16[288,512]{1,0:T(8,128)(2,1)S(1)}, bf16[288,512]{1,0:T(8,128)(2,1)S(1)}, u32[]{:S(2)}, u32[]{:S(2)}) collective-permute-start(bf16[288,512]{1,0:T(8,128)(2,1)S(1)} %get-tuple-element.307), channel_id=1, source_target_pairs={{1,0},{2,1},{3,2},{11,3},{10,11},{9,10},{8,9},{0,8},{5,4},{6,5},{7... | collective-permute-start | bytes 884744 | tf_op jit(solution)/shard_map/ppermute | solution.py:786
  800.1 8.6 %collective-permute-start.40 = (bf16[288,512]{1,0:T(8,128)(2,1)S(1)}, bf16[288,512]{1,0:T(8,128)(2,1)S(1)}, u32[]{:S(2)}, u32[]{:S(2)}) collective-permute-start(bf16[288,512]{1,0:T(8,128)(2,1)S(1)} %get-tuple-element.308), channel_id=1, source_target_pairs={{0,1},{1,2},{2,3},{3,11},{11,10},{10,9},{9,8},{8,0},{4,5},{5,6},{6... | collective-permute-start | bytes 884744 | tf_op jit(solution)/shard_map/ppermute | solution.py:786
  800.3 8.5 %collective-permute-start.41 = (bf16[288,512]{1,0:T(8,128)(2,1)S(1)}, bf16[288,512]{1,0:T(8,128)(2,1)S(1)}, u32[]{:S(2)}, u32[]{:S(2)}) collective-permute-start(bf16[288,512]{1,0:T(8,128)(2,1)S(1)} %get-tuple-element.309), channel_id=1, source_target_pairs={{1,0},{2,1},{3,2},{11,3},{10,11},{9,10},{8,9},{0,8},{5,4},{6,5},{7... | collective-permute-start | bytes 884744 | tf_op jit(solution)/shard_map/ppermute | solution.py:786
  (22 other events, 57.3 us)
Sparse Core Ops, SparseCore 0:
  10.3 59.5 all-gather.2
  71.4 214.6 all-gather.4
  389.1 255.6 reduce-scatter.4
  719.4 78.8 reduce-scatter.6

commit v7 on v6

--- a/solution.py
+++ b/solution.py
@@ -965,15 +965,15 @@
         pair_back = after(pair_back, pair_rings)
         pair_rings.append(RingScatter(lambda s, half, v=pair_back: halves(v[s], half).astype(F32), columns))
     pair_rings[-1].launch()
-    query_backs, feed_out = after((query_backs, feed_out), pair_rings[-1:])
+    query_backs, feed_out, feed_summed, output_parts = after(
+        (query_backs, feed_out, feed_summed, output_parts), pair_rings[-1:]
+    )
+    output_summed = scatter(output_parts.reshape(-1, output_parts.shape[3]), ALL_COL).astype(F32)
     query_back = exchange(jnp.concatenate(query_backs, axis=1).reshape(cores, own, -1), "core")
     layer_low = (hidden + feed_out).astype(BF16).reshape(own, rows, -1).transpose(1, 0, 2)
     held_pairs = jnp.concatenate([ring.finish().astype(BF16) for ring in pair_rings], axis=1)
-    held_pairs, query_back, layer_low, feed_summed, output_parts = lax.optimization_barrier(
-        (held_pairs, query_back, layer_low, feed_summed, output_parts)
-    )
+    held_pairs, query_back, layer_low = lax.optimization_barrier((held_pairs, query_back, layer_low))
     feed_summed = feed_summed.astype(F32)
-    output_summed = scatter(output_parts.reshape(-1, output_parts.shape[3]), ALL_COL).astype(F32)
     pair_back = exchange(held_pairs.reshape(cores, own, -1), "core")
     layer_output = exchange(layer_low, ROW).reshape(rows * own, -1)
     joint_low, input_part, gain_one_part = joint_back(

time: 832 us -> 851 us (1.023)
  starting transfers between devices: 234 us -> 248 us
    ppermute x16, starting transfers between devices: 22.7 us -> 48.1 us  [launch(): lax.ppermute(back, RING, self.behind)]
    ppermute x16, starting transfers between devices: 167 us -> 157 us  [launch(): lax.ppermute(out, RING, self.ahead)]
  transfers between devices with their start and end apart: 54 -> 54, of which waited for: 23 -> 26; matrix products, arithmetic and copies ran while one was open for 11% -> 11% of each run, Pallas kernels for 22% -> 22%
where the time goes in v7:
time: 851 us; the launch traced here: 839 us
  starting transfers between devices  248 us (29%)
  Pallas kernels  239 us (28%)
  waiting for transfers between devices  200 us (24%)
  local copies, waits for them, and re-layouts  63.5 us (7%)
  other arithmetic  44.3 us (5%)
  between operations  31.2 us (4%)
  blocking collectives  13.1 us (2%)
    ppermute x16, starting transfers between devices, launch(): lax.ppermute(out, RING, self.ahead)  157 us
    pallas_call x4, Pallas kernels, attention_stage(): pl.pallas_call(functools.partial(stage_kernel, state is None, ends), grid...  64 us
    pallas_call x3, Pallas kernels, attention_backward(): pl.pallas_call(functools.partial(backward_kernel, group), grid_spec=pltpu...  54.5 us
    ppermute x16, starting transfers between devices, launch(): lax.ppermute(back, RING, self.behind)  48.1 us
    ppermute x16, waiting for transfers between devices, launch(): lax.ppermute(out, RING, self.ahead)  43.7 us
    pallas_call x3, Pallas kernels, gradient_parts(): pl.pallas_call(functools.partial(gradient_kernel, [len(rights) for _, rig...  40.4 us
    ppermute x2, waiting for transfers between devices, per_device(): lax.ppermute(to_next, RING, ahead)  38.9 us
    pallas_call x1, Pallas kernels, feed_forward(): pl.pallas_call(feed_kernel, grid=(columns,), in_specs=[whole, whole, *blo...  38.8 us
  transfers between devices with their start and end apart: 54, of which 26 were waited for; matrix products, arithmetic and copies ran while one was open for 11% of the time, Pallas kernels for 22%

profile of v7, /device:TPU:0, one launch (start us, length us, event | category | flops | bytes accessed | tf_op | source)
XLA Modules:
  0.0 838.9 jit_solution(11706956315489085832)
XLA Ops:
  9.2 3.7 concatenate.77
  16.2 4.6 all-to-all-start
  26.6 4.7 compare_and_fusion
  38.4 9.9 %all-to-all-done = bf16[4,656,288]{1,2,0:T(8,128)(2,1)} async-done(((bf16[4,656,288]{1,2,0:T(8,128)(2,1)}), bf16[4,656,288]{1,2,0:T(8,128)(2,1)}, u32[]{:S(2)}, u32[]{:S(2)}) %all-to-all-start) | async-done | bytes 1511456 | tf_op jit(solution)/shard_map/all_to_all | solution.py:889
  48.4 3.9 copy.99.x4_ref
  52.3 17.5 %all-gather.3.cloned.1.call-done = bf16[4608,480]{1,0:T(8,128)(2,1)} async-done(((bf16[288,480]{1,0:T(8,128)(2,1)}), bf16[4608,480]{1,0:T(8,128)(2,1)}) %all-gather.3.cloned.1.call-update) | async-done | bytes 4423696 | tf_op jit(solution)/shard_map/all_gather | solution.py:841
  69.8 11.0 %project_in.1 = (bf16[640,1152]{1,0:T(8,128)(2,1)}, bf16[640,1152]{1,0:T(8,128)(2,1)}, bf16[1152,1920]{1,0:T(8,128)(2,1)}, bf16[2,640,1152]{2,1,0:T(8,128)(2,1)}...) custom-call(bf16[4,656,288]{2,1,0:T(8,128)(2,1)} %copy.99.x4_ref, bf16[4,1152,480]{2,1,0:T(8,128)(2,1)} %bitcast.246, ...), custom_call_target="tpu_custom_call" | custom-call | flops 2831155200 | bytes 16777216 | tf_op jit(solution)/shard_map/project_in/pallas_call | solution.py:511
  80.9 6.5 all_to_all.50
  89.4 5.1 all-to-all-start.2
  94.6 38.5 %collective-permute-done.refs_2_.refs_8_ = bf16[1280,384]{1,0:T(8,128)(2,1)} collective-permute-done((bf16[1280,384]{1,0:T(8,128)(2,1)}, bf16[1280,384]{1,0:T(8,128)(2,1)}, u32[]{:S(2)}, u32[]{:S(2)}) %collective-permute-start) | collective-permute-done | bytes 983072 | tf_op jit(solution)/shard_map/ppermute | solution.py:916
  135.6 25.0 %attention_stage.4 = (f32[3,5,80,768]{3,2,1,0:T(8,128)S(1)}, f32[3,5,1,768]{3,2,1,0:T(1,128)S(1)}) custom-call(s32[75]{0:T(128)S(1)} %select_n.164.lists, s32[5]{0:T(128)S(1)} %get-tuple-element.200.counts, bf16[1280,1152]{1,0:T(8,128)(2,1)} %bitcast.3.q_ref, bf16[3840,128]{1,0:T(8,128)(2,1)S(1)} %pad_maximum_fusion.1.mark_ref, ...), custom_call_target="tpu_custom_call" | custom-call | flops 11324620800 | bytes 5898240 | tf_op jit(solution)/shard_map/attention_stage/pallas_call | solution.py:323
  162.5 16.0 %collective-permute-done.1.refs_3_.refs_7_ = bf16[1280,384]{1,0:T(8,128)(2,1)} collective-permute-done((bf16[1280,384]{1,0:T(8,128)(2,1)}, bf16[1280,384]{1,0:T(8,128)(2,1)}, u32[]{:S(2)}, u32[]{:S(2)}) %collective-permute-start.1) | collective-permute-done | bytes 983072 | tf_op jit(solution)/shard_map/ppermute | solution.py:928
  183.7 4.3 all-to-all-start.3
  190.1 13.4 %attention_stage.5 = (f32[3,5,80,768]{3,2,1,0:T(8,128)S(1)}, f32[3,5,1,768]{3,2,1,0:T(1,128)S(1)}) custom-call(s32[50]{0:T(128)S(1)} %select_n.168.lists, s32[5]{0:T(128)S(1)} %get-tuple-element.197.counts, bf16[1280,1152]{1,0:T(8,128)(2,1)} %bitcast.3.q_ref, bf16[2560,128]{1,0:T(8,128)(2,1)S(1)} %pad_maximum_fusion.3.mark_ref, ...), custom_call_target="tpu_custom_call" | custom-call | flops 7549747200 | bytes 3932160 | tf_op jit(solution)/shard_map/attention_stage/pallas_call | solution.py:323
  203.6 22.9 %collective-permute-done.4.refs_3_.refs_6_ = bf16[1280,384]{1,0:T(8,128)(2,1)} collective-permute-done((bf16[1280,384]{1,0:T(8,128)(2,1)}, bf16[1280,384]{1,0:T(8,128)(2,1)}, u32[]{:S(2)}, u32[]{:S(2)}) %collective-permute-start.4) | collective-permute-done | bytes 983072 | tf_op jit(solution)/shard_map/ppermute | solution.py:928
  230.9 13.5 %attention_stage.6 = (f32[3,5,80,768]{3,2,1,0:T(8,128)S(1)}, f32[3,5,1,768]{3,2,1,0:T(1,128)S(1)}) custom-call(s32[50]{0:T(128)S(1)} %select_n.172.lists, s32[5]{0:T(128)S(1)} %get-tuple-element.194.counts, bf16[1280,1152]{1,0:T(8,128)(2,1)} %bitcast.3.q_ref, bf16[2560,128]{1,0:T(8,128)(2,1)S(1)} %pad_maximum_fusion.4.mark_ref, ...), custom_call_target="tpu_custom_call" | custom-call | flops 7549747200 | bytes 3932160 | tf_op jit(solution)/shard_map/attention_stage/pallas_call | solution.py:323
  246.3 31.7 %collective-permute-done.6.refs_2_.refs_4_ = bf16[640,384]{1,0:T(8,128)(2,1)S(1)} collective-permute-done((bf16[640,384]{1,0:T(8,128)(2,1)S(1)}, bf16[640,384]{1,0:T(8,128)(2,1)S(1)}, u32[]{:S(2)}, u32[]{:S(2)}) %collective-permute-start.6) | collective-permute-done | bytes 491552 | tf_op jit(solution)/shard_map/ppermute | solution.py:930
  278.1 2.4 copy-done.1
  280.5 12.1 %attention_stage.7 = (bf16[1280,1152]{1,0:T(8,128)(2,1)}, f32[3,5,1,768]{3,2,1,0:T(1,128)S(1)}) custom-call(s32[25]{0:T(128)S(1)} %select_n.176.lists, s32[5]{0:T(128)S(1)} %get-tuple-element.189.counts, bf16[1280,1152]{1,0:T(8,128)(2,1)} %bitcast.3.q_ref, bf16[1280,128]{1,0:T(8,128)(2,1)S(1)} %get-tuple-element.190.mark_ref, ...), custom_call_target="tpu_custom_call" | custom-call | flops 3774873600 | bytes 1966080 | tf_op jit(solution)/shard_map/attention_stage/pallas_call | solution.py:323
  294.0 4.1 all-to-all-start.4
  298.1 3.6 copy.102.back_ref.upstream_ref.refs_3_
  303.5 8.6 %project_out.1 = (bf16[640,1152]{1,0:T(8,128)(2,1)}, f32[640,1152]{1,0:T(8,128)}, bf16[640,1152]{1,0:T(8,128)(2,1)}, bf16[1152,1152]{1,0:T(8,128)(2,1)}) custom-call(bf16[2,640,1152]{2,1,0:T(8,128)(2,1)} %copy-done.6, bf16[4,1152,2688]{2,1,0:T(8,128)(2,1)} %bitcast.204, bf16[640,1152]{1,0:T(8,128)(2,1)} %get-tuple-element.227.x_ref, ...), custom_call_target="tpu_custom_call" | custom-call | flops 1698693120 | bytes 16777216 | tf_op jit(solution)/shard_map/project_out/pallas_call | solution.py:540
  312.0 38.8 %feed_forward.1 = (bf16[640,3072]{1,0:T(8,128)(2,1)}, bf16[640,3072]{1,0:T(8,128)(2,1)}, bf16[640,3072]{1,0:T(8,128)(2,1)}, f32[640,1152]{1,0:T(8,128)}, f32[640,1152]{1,0:T(8,128)}) custom-call(bf16[640,1152]{1,0:T(8,128)(2,1)} %get-tuple-element.229.normed_ref.refs_0_, bf16[640,1152]{1,0:T(8,128)(2,1)} %copy.102.back_ref.upstream_ref.refs_3_, ...), custom_call_target="tpu_custom_call" | custom-call | flops 27179089920 | bytes 21233664 | tf_op jit(solution)/shard_map/feed_forward/pallas_call | solution.py:678
  350.8 9.3 %output_back.1 = (f32[640,1152]{1,0:T(8,128)}, bf16[640,1152]{1,0:T(8,128)(2,1)}, bf16[2,640,1152]{2,1,0:T(8,128)(2,1)}, f32[8,1152]{1,0:T(8,128)}) custom-call(f32[640,1152]{1,0:T(8,128)} %get-tuple-element.233.back_ref, f32[640,1152]{1,0:T(8,128)} %get-tuple-element.234.hidden_ref, bf16[640,1152]{1,0:T(8,128)(2,1)} %copy.102.back_ref.upstream_ref.refs_3_, ...), custom_call_target="tpu_custom_call" | custom-call | flops 1698693120 | bytes 16777216 | tf_op jit(solution)/shard_map/output_back/pallas_call | solution.py:589
  360.1 3.9 all-to-all-start.5
  364.1 23.5 %gradient_parts.3 = bf16[4,4,288,2304]{3,2,1,0:T(8,128)(2,1)} custom-call(bf16[640,1152]{1,0:T(8,128)(2,1)} %get-tuple-element.229.normed_ref.refs_0_, bf16[640,3072]{1,0:T(8,128)(2,1)} %get-tuple-element.231.refs_1_, bf16[640,3072]{1,0:T(8,128)(2,1)} %get-tuple-element.232.refs_2_, bf16[640,1152]{1,0:T(8,128)(2,1)} %copy.102.back_ref.upstream_ref.refs_3_, ...), custom_call_target="tpu_custom_call" | custom-call | flops 13589544960 | bytes 21233664 | tf_op jit(solution)/shard_map/gradient_parts/pallas_call | solution.py:750
  391.5 17.8 %attention_backward.3 = (bf16[1280,384]{1,0:T(8,128)(2,1)}, bf16[10240,128]{1,0:T(8,128)(2,1)}) custom-call(s32[200]{0:T(256)S(1)} %select_n.160.lists, s32[5]{0:T(128)S(1)} %get-tuple-element.183.counts, bf16[1280,1152]{1,0:T(8,128)(2,1)} %bitcast.3.q_ref, bf16[1280,1152]{1,0:T(8,128)(2,1)} %bitcast.221, bf16[1280,1152]{1,0:T(8,128)(2,1)} %get-tuple-element.226.o_ref, ...), custom_call_target="tpu_custom_call" | custom-call | flops 25165824000 | bytes 10485760 | tf_op jit(solution)/shard_map/attention_backward/pallas_call | solution.py:412
  412.1 13.6 %collective-permute-start.9 = (bf16[640,128]{1,0:T(8,128)(2,1)S(1)}, bf16[640,128]{1,0:T(8,128)(2,1)S(1)}, u32[]{:S(2)}, u32[]{:S(2)}) collective-permute-start(bf16[640,128]{1,0:T(8,128)(2,1)S(1)} %get-tuple-element.246), channel_id=1, source_target_pairs={{1,0},{2,1},{3,2},{11,3},{10,11},{9,10},{8,9},{0,8},{5,4},{6,5},{7... | collective-permute-start | bytes 491528 | tf_op jit(solution)/shard_map/ppermute | solution.py:786
  425.7 18.6 %attention_backward.4 = (bf16[1280,384]{1,0:T(8,128)(2,1)}, bf16[10240,128]{1,0:T(8,128)(2,1)}) custom-call(s32[200]{0:T(256)S(1)} %select_n.160.lists, s32[5]{0:T(128)S(1)} %get-tuple-element.183.counts, bf16[1280,1152]{1,0:T(8,128)(2,1)} %bitcast.3.q_ref, bf16[1280,1152]{1,0:T(8,128)(2,1)} %bitcast.222, bf16[1280,1152]{1,0:T(8,128)(2,1)} %get-tuple-element.226.o_ref, ...), custom_call_target="tpu_custom_call" | custom-call | flops 25165824000 | bytes 10485760 | tf_op jit(solution)/shard_map/attention_backward/pallas_call | solution.py:412
  444.3 7.9 gradient_parts.4
  454.6 36.9 %collective-permute-start.10 = (bf16[1280,128]{1,0:T(8,128)(2,1)S(1)}, bf16[1280,128]{1,0:T(8,128)(2,1)}, u32[]{:S(2)}, u32[]{:S(2)}) collective-permute-start(bf16[1280,128]{1,0:T(8,128)(2,1)S(1)} %pad_maximum_fusion.7), channel_id=1, source_target_pairs={{0,1},{1,2},{2,3},{3,11},{11,10},{10,9},{9,8},{8,0},{4,5},{5,6},{6... | collective-permute-start | bytes 983048 | tf_op jit(solution)/shard_map/ppermute | solution.py:786
  491.5 49.2 %collective-permute-start.12 = (bf16[640,128]{1,0:T(8,128)(2,1)S(1)}, bf16[640,128]{1,0:T(8,128)(2,1)}, u32[]{:S(2)}, u32[]{:S(2)}) collective-permute-start(bf16[640,128]{1,0:T(8,128)(2,1)S(1)} %get-tuple-element.254), channel_id=1, source_target_pairs={{0,1},{1,2},{2,3},{3,11},{11,10},{10,9},{9,8},{8,0},{4,5},{5,6},{6... | collective-permute-start | bytes 491528 | tf_op jit(solution)/shard_map/ppermute | solution.py:786
  540.7 18.1 %attention_backward.5 = (bf16[1280,384]{1,0:T(8,128)(2,1)}, bf16[10240,128]{1,0:T(8,128)(2,1)}) custom-call(s32[200]{0:T(256)S(1)} %select_n.160.lists, s32[5]{0:T(128)S(1)} %get-tuple-element.183.counts, bf16[1280,1152]{1,0:T(8,128)(2,1)} %bitcast.3.q_ref, bf16[1280,1152]{1,0:T(8,128)(2,1)} %bitcast.223, bf16[1280,1152]{1,0:T(8,128)(2,1)} %get-tuple-element.226.o_ref, ...), custom_call_target="tpu_custom_call" | custom-call | flops 25165824000 | bytes 10485760 | tf_op jit(solution)/shard_map/attention_backward/pallas_call | solution.py:412
  560.3 35.5 %collective-permute-start.24 = (bf16[640,128]{1,0:T(8,128)(2,1)S(1)}, bf16[640,128]{1,0:T(8,128)(2,1)S(1)}, u32[]{:S(2)}, u32[]{:S(2)}) collective-permute-start(bf16[640,128]{1,0:T(8,128)(2,1)S(1)} %get-tuple-element.394), channel_id=1, source_target_pairs={{0,1},{1,2},{2,3},{3,11},{11,10},{10,9},{9,8},{8,0},{4,5},{5,6},{6... | collective-permute-start | bytes 491528 | tf_op jit(solution)/shard_map/ppermute | solution.py:786
  597.1 15.0 %collective-permute-start.18 = (bf16[1280,128]{1,0:T(8,128)(2,1)S(1)}, bf16[1280,128]{1,0:T(8,128)(2,1)S(1)}, u32[]{:S(2)}, u32[]{:S(2)}) collective-permute-start(bf16[1280,128]{1,0:T(8,128)(2,1)S(1)} %pad_maximum_fusion.9), channel_id=1, source_target_pairs={{0,1},{1,2},{2,3},{3,11},{11,10},{10,9},{9,8},{8,0},{4,5},{5,6},{6... | collective-permute-start | bytes 983048 | tf_op jit(solution)/shard_map/ppermute | solution.py:786
  613.3 10.1 %collective-permute-start.14 = (bf16[1280,128]{1,0:T(8,128)(2,1)S(1)}, bf16[1280,128]{1,0:T(8,128)(2,1)S(1)}, u32[]{:S(2)}, u32[]{:S(2)}) collective-permute-start(bf16[1280,128]{1,0:T(8,128)(2,1)S(1)} %get-tuple-element.258), channel_id=1, source_target_pairs={{0,1},{1,2},{2,3},{3,11},{11,10},{10,9},{9,8},{8,0},{4,5},{5,6},{6... | collective-permute-start | bytes 983048 | tf_op jit(solution)/shard_map/ppermute | solution.py:786
  623.4 4.0 collective-permute-done.18
  627.3 13.4 %collective-permute-start.15 = (bf16[1280,128]{1,0:T(8,128)(2,1)S(1)}, bf16[1280,128]{1,0:T(8,128)(2,1)S(1)}, u32[]{:S(2)}, u32[]{:S(2)}) collective-permute-start(bf16[1280,128]{1,0:T(8,128)(2,1)S(1)} %get-tuple-element.259), channel_id=1, source_target_pairs={{1,0},{2,1},{3,2},{11,3},{10,11},{9,10},{8,9},{0,8},{5,4},{6,5},{7... | collective-permute-start | bytes 983048 | tf_op jit(solution)/shard_map/ppermute | solution.py:786
  642.1 6.2 collective-permute-start.21
  648.9 3.5 collective-permute-done.20
  652.4 2.9 collective-permute-start.17
  657.1 2.3 collective-permute-done.16
  659.4 2.9 collective-permute-start.23
  666.7 4.1 collective-permute-done.23
  673.9 2.9 collective-permute-done.27
  680.8 2.2 add_convert_fusion
  683.0 4.9 collective-permute-done.28
  693.9 2.1 copy.106
  696.0 3.9 all-to-all-start.6
  701.3 2.1 pad_maximum_fusion.2
  703.4 6.5 all_to_all.51.pair_ref
  710.0 4.3 all-to-all-start.8
  714.9 12.3 %joint_back.1 = (bf16[640,1920]{1,0:T(8,128)(2,1)}, bf16[4,640,288]{2,1,0:T(8,128)(2,1)}, f32[8,1152]{1,0:T(8,128)}) custom-call(bf16[2,640,1152]{2,1,0:T(8,128)(2,1)} %copy-done.5, bf16[2,640,384]{2,1,0:T(8,128)(2,1)} %all_to_all.51.pair_ref, f32[640,128]{1,0:T(8,128)} %get-tuple-element.437.cos_ref, f32[640,128]{1,0:T(8,128)} %get-tuple-element.438.sin_ref, ...), custom_call_target="tpu_custom_call" | custom-call | flops 2831155200 | bytes 16777216 | tf_op jit(solution)/shard_map/joint_back/pallas_call | solution.py:638
  729.2 4.2 all-to-all-done.8
  733.4 2.7 copy.116
  736.1 9.0 %gradient_parts.5 = bf16[4,4,288,512]{3,2,1,0:T(8,128)(2,1)} custom-call(bf16[640,1152]{1,0:T(8,128)(2,1)} %get-tuple-element.299.refs_0_, bf16[640,1920]{1,0:T(8,128)(2,1)} %get-tuple-element.300.refs_1_, f32[4,288,1]{2,1,0:T(8,128)} %reshape_squeeze.9.refs_2_), custom_call_target="tpu_custom_call" | custom-call | flops 3019898880 | bytes 4718592 | tf_op jit(solution)/shard_map/gradient_parts/pallas_call | solution.py:750
  745.1 3.4 dynamic-slice_bitcast_fusion
  772.6 2.5 copy.108
  775.1 3.7 all-to-all-start.9
  782.1 18.9 %collective-permute-done.34 = bf16[144,512]{1,0:T(8,128)(2,1)S(1)} collective-permute-done((bf16[144,512]{1,0:T(8,128)(2,1)S(1)}, bf16[144,512]{1,0:T(8,128)(2,1)S(1)}, u32[]{:S(2)}, u32[]{:S(2)}) %collective-permute-start.34) | collective-permute-done | bytes 147488 | tf_op jit(solution)/shard_map/ppermute | solution.py:786
  803.1 2.1 slice_bitcast_fusion
  806.6 3.1 collective-permute-done.36
  815.4 3.5 collective-permute-done.38
  826.4 2.4 collective-permute-done.40
  (273 shorter events, 110.3 us)
Async XLA Ops:
  7.2 62.7 %all-gather.3.cloned.1.call-start = ((), (), s32[]{:S(2)}) async-start(), calls=%async_computation.12 | async-start | bytes 5013504 | tf_op jit(solution)/shard_map/all_gather | solution.py:841
  7.9 293.9 %all-gather.5.cloned.1.call-start = ((), (), s32[]{:S(2)}) async-start(), calls=%async_computation.13 | async-start | bytes 26320896 | tf_op jit(solution)/shard_map/all_gather | solution.py:841
  16.2 32.2 %all-to-all-start = ((bf16[4,656,288]{1,2,0:T(8,128)(2,1)}), bf16[4,656,288]{1,2,0:T(8,128)(2,1)}, u32[]{:S(2)}, u32[]{:S(2)}) async-start(bf16[4,656,288]{1,2,0:T(8,128)(2,1)} %copy.96), calls=%async_computation | async-start | bytes 3538944 | tf_op jit(solution)/shard_map/all_to_all | solution.py:889
  87.4 45.7 %collective-permute-start = (bf16[1280,384]{1,0:T(8,128)(2,1)}, bf16[1280,384]{1,0:T(8,128)(2,1)}, u32[]{:S(2)}, u32[]{:S(2)}) collective-permute-start(bf16[1280,384]{1,0:T(8,128)(2,1)} %bitcast.2.refs_0_), channel_id=1, source_target_pairs={{0,1},{1,2},{2,3},{3,11},{11,10},{10,9},{9,8},{8,0},{4,5},{5,6},{6... | collective-permute-start | bytes 2949128 | tf_op jit(solution)/shard_map/ppermute | solution.py:916
  89.0 45.7 %collective-permute-start.2 = (bf16[1280,384]{1,0:T(8,128)(2,1)}, bf16[1280,384]{1,0:T(8,128)(2,1)}, u32[]{:S(2)}, u32[]{:S(2)}) collective-permute-start(bf16[1280,384]{1,0:T(8,128)(2,1)} %bitcast.2.refs_0_), channel_id=1, source_target_pairs={{1,0},{2,1},{3,2},{11,3},{10,11},{9,10},{8,9},{0,8},{5,4},{6,5},{7... | collective-permute-start | bytes 2949128 | tf_op jit(solution)/shard_map/ppermute | solution.py:916
  89.4 46.1 %all-to-all-start.2 = ((bf16[2,640,1152]{2,1,0:T(8,128)(2,1)}), bf16[2,640,1152]{2,1,0:T(8,128)(2,1)}, u32[]{:S(2)}, u32[]{:S(2)}) async-start(bf16[2,640,1152]{2,1,0:T(8,128)(2,1)} %get-tuple-element.187), calls=%async_computation.2 | async-start | bytes 5898240 | tf_op jit(solution)/shard_map/all_to_all | solution.py:889
  133.1 45.4 %collective-permute-start.1 = (bf16[1280,384]{1,0:T(8,128)(2,1)}, bf16[1280,384]{1,0:T(8,128)(2,1)}, u32[]{:S(2)}, u32[]{:S(2)}) collective-permute-start(bf16[1280,384]{1,0:T(8,128)(2,1)} %collective-permute-done.refs_2_.refs_8_), channel_id=1, source_target_pairs={{0,1},{1,2},{2,3},{3,11},{11,10},{10,9},{9,8},{8,0},{4,5},{5,6},{6... | collective-permute-start | bytes 2949128 | tf_op jit(solution)/shard_map/ppermute | solution.py:928
  134.7 45.8 %collective-permute-start.3 = (bf16[1280,384]{1,0:T(8,128)(2,1)}, bf16[1280,384]{1,0:T(8,128)(2,1)}, u32[]{:S(2)}, u32[]{:S(2)}) collective-permute-start(bf16[1280,384]{1,0:T(8,128)(2,1)} %collective-permute-done.2.refs_1_), channel_id=1, source_target_pairs={{1,0},{2,1},{3,2},{11,3},{10,11},{9,10},{8,9},{0,8},{5,4},{6,5},{7... | collective-permute-start | bytes 2949128 | tf_op jit(solution)/shard_map/ppermute | solution.py:928
  135.6 46.9 %copy-start.15 = (bf16[2560,288]{0,1:T(8,128)(2,1)S(1)}, bf16[2560,288]{0,1:T(8,128)(2,1)}, u32[]{:S(2)}) copy-start(bf16[2560,288]{0,1:T(8,128)(2,1)} %param.21) | copy-start | bytes 4423684
  180.5 46.0 %collective-permute-start.4 = (bf16[1280,384]{1,0:T(8,128)(2,1)}, bf16[1280,384]{1,0:T(8,128)(2,1)}, u32[]{:S(2)}, u32[]{:S(2)}) collective-permute-start(bf16[1280,384]{1,0:T(8,128)(2,1)} %collective-permute-done.1.refs_3_.refs_7_), channel_id=1, source_target_pairs={{0,1},{1,2},{2,3},{3,11},{11,10},{10,9},{9,8},{8,0},{4,5},{5,6},{6... | collective-permute-start | bytes 2949128 | tf_op jit(solution)/shard_map/ppermute | solution.py:928
  181.4 45.0 %collective-permute-start.5 = (bf16[1280,384]{1,0:T(8,128)(2,1)}, bf16[1280,384]{1,0:T(8,128)(2,1)}, u32[]{:S(2)}, u32[]{:S(2)}) collective-permute-start(bf16[1280,384]{1,0:T(8,128)(2,1)} %collective-permute-done.3.refs_2_), channel_id=1, source_target_pairs={{1,0},{2,1},{3,2},{11,3},{10,11},{9,10},{8,9},{0,8},{5,4},{6,5},{7... | collective-permute-start | bytes 2949128 | tf_op jit(solution)/shard_map/ppermute | solution.py:928
  183.7 94.3 %all-to-all-start.3 = ((bf16[4,640,288]{1,2,0:T(8,128)(2,1)}), bf16[4,640,288]{1,2,0:T(8,128)(2,1)}, u32[]{:S(2)}, u32[]{:S(2)}) async-start(bf16[4,640,288]{1,2,0:T(8,128)(2,1)} %bitcast.211), calls=%async_computation.3 | async-start | bytes 2949120 | tf_op jit(solution)/shard_map/all_to_all | solution.py:889
  227.5 50.5 %collective-permute-start.6 = (bf16[640,384]{1,0:T(8,128)(2,1)S(1)}, bf16[640,384]{1,0:T(8,128)(2,1)S(1)}, u32[]{:S(2)}, u32[]{:S(2)}) collective-permute-start(bf16[640,384]{1,0:T(8,128)(2,1)S(1)} %slice.405), channel_id=1, source_target_pairs={{0,1},{1,2},{2,3},{3,11},{11,10},{10,9},{9,8},{8,0},{4,5},{5,6},{6... | collective-permute-start | bytes 1474568 | tf_op jit(solution)/shard_map/ppermute | solution.py:930
  229.5 48.6 %collective-permute-start.7 = (bf16[640,384]{1,0:T(8,128)(2,1)S(1)}, bf16[640,384]{1,0:T(8,128)(2,1)S(1)}, u32[]{:S(2)}, u32[]{:S(2)}) collective-permute-start(bf16[640,384]{1,0:T(8,128)(2,1)S(1)} %slice.406), channel_id=1, source_target_pairs={{1,0},{2,1},{3,2},{11,3},{10,11},{9,10},{8,9},{0,8},{5,4},{6,5},{7... | collective-permute-start | bytes 1474568 | tf_op jit(solution)/shard_map/ppermute | solution.py:930
  278.1 113.5 %copy-start.26 = (bf16[640,384]{1,0:T(8,128)(2,1)}, bf16[640,384]{1,0:T(8,128)(2,1)S(1)}, u32[]{:S(2)}) copy-start(bf16[640,384]{1,0:T(8,128)(2,1)S(1)} %collective-permute-done.6.refs_2_.refs_4_) | copy-start | bytes 1474564
  278.1 15.9 %copy-start.27 = (bf16[640,384]{1,0:T(8,128)(2,1)}, bf16[640,384]{1,0:T(8,128)(2,1)S(1)}, u32[]{:S(2)}) copy-start(bf16[640,384]{1,0:T(8,128)(2,1)S(1)} %collective-permute-done.7.refs_3_.refs_5_) | copy-start | bytes 1474564
  294.0 7.8 all-to-all-start.4
  360.1 27.5 %all-to-all-start.5 = ((bf16[2,640,1152]{2,1,0:T(8,128)(2,1)}), bf16[2,640,1152]{2,1,0:T(8,128)(2,1)S(1)}, u32[]{:S(2)}, u32[]{:S(2)}) async-start(bf16[2,640,1152]{2,1,0:T(8,128)(2,1)} %get-tuple-element.239), calls=%async_computation.5 | async-start | bytes 5898240 | tf_op jit(solution)/shard_map/all_to_all | solution.py:889
  364.1 298.7 %reduce-scatter.5.cloned.1.call-start = ((), (), s32[]{:S(2)}) async-start(), calls=%async_computation.14 | async-start | bytes 22560768 | tf_op jit(solution)/shard_map/reduce_scatter | solution.py:837
  410.9 41.4 %collective-permute-start.8 = (bf16[640,128]{1,0:T(8,128)(2,1)S(1)}, bf16[640,128]{1,0:T(8,128)(2,1)S(1)}, u32[]{:S(2)}, u32[]{:S(2)}) collective-permute-start(bf16[640,128]{1,0:T(8,128)(2,1)S(1)} %get-tuple-element.245), channel_id=1, source_target_pairs={{0,1},{1,2},{2,3},{3,11},{11,10},{10,9},{9,8},{8,0},{4,5},{5,6},{6... | collective-permute-start | bytes 491528 | tf_op jit(solution)/shard_map/ppermute | solution.py:786
  412.1 40.1 %collective-permute-start.9 = (bf16[640,128]{1,0:T(8,128)(2,1)S(1)}, bf16[640,128]{1,0:T(8,128)(2,1)S(1)}, u32[]{:S(2)}, u32[]{:S(2)}) collective-permute-start(bf16[640,128]{1,0:T(8,128)(2,1)S(1)} %get-tuple-element.246), channel_id=1, source_target_pairs={{1,0},{2,1},{3,2},{11,3},{10,11},{9,10},{8,9},{0,8},{5,4},{6,5},{7... | collective-permute-start | bytes 491528 | tf_op jit(solution)/shard_map/ppermute | solution.py:786
  454.6 104.3 %collective-permute-start.10 = (bf16[1280,128]{1,0:T(8,128)(2,1)S(1)}, bf16[1280,128]{1,0:T(8,128)(2,1)}, u32[]{:S(2)}, u32[]{:S(2)}) collective-permute-start(bf16[1280,128]{1,0:T(8,128)(2,1)S(1)} %pad_maximum_fusion.7), channel_id=1, source_target_pairs={{0,1},{1,2},{2,3},{3,11},{11,10},{10,9},{9,8},{8,0},{4,5},{5,6},{6... | collective-permute-start | bytes 983048 | tf_op jit(solution)/shard_map/ppermute | solution.py:786
  491.5 67.4 %collective-permute-start.11 = (bf16[1280,128]{1,0:T(8,128)(2,1)S(1)}, bf16[1280,128]{1,0:T(8,128)(2,1)}, u32[]{:S(2)}, u32[]{:S(2)}) collective-permute-start(bf16[1280,128]{1,0:T(8,128)(2,1)S(1)} %pad_maximum_fusion.8), channel_id=1, source_target_pairs={{1,0},{2,1},{3,2},{11,3},{10,11},{9,10},{8,9},{0,8},{5,4},{6,5},{7... | collective-permute-start | bytes 983048 | tf_op jit(solution)/shard_map/ppermute | solution.py:786
  491.5 67.3 %collective-permute-start.12 = (bf16[640,128]{1,0:T(8,128)(2,1)S(1)}, bf16[640,128]{1,0:T(8,128)(2,1)}, u32[]{:S(2)}, u32[]{:S(2)}) collective-permute-start(bf16[640,128]{1,0:T(8,128)(2,1)S(1)} %get-tuple-element.254), channel_id=1, source_target_pairs={{0,1},{1,2},{2,3},{3,11},{11,10},{10,9},{9,8},{8,0},{4,5},{5,6},{6... | collective-permute-start | bytes 491528 | tf_op jit(solution)/shard_map/ppermute | solution.py:786
  540.7 18.2 %collective-permute-start.13 = (bf16[640,128]{1,0:T(8,128)(2,1)S(1)}, bf16[640,128]{1,0:T(8,128)(2,1)}, u32[]{:S(2)}, u32[]{:S(2)}) collective-permute-start(bf16[640,128]{1,0:T(8,128)(2,1)S(1)} %get-tuple-element.255), channel_id=1, source_target_pairs={{1,0},{2,1},{3,2},{11,3},{10,11},{9,10},{8,9},{0,8},{5,4},{6,5},{7... | collective-permute-start | bytes 491528 | tf_op jit(solution)/shard_map/ppermute | solution.py:786
  558.8 53.2 %copy-start.12 = (bf16[10240,128]{1,0:T(8,128)(2,1)S(1)}, bf16[10240,128]{1,0:T(8,128)(2,1)}, u32[]{:S(2)}) copy-start(bf16[10240,128]{1,0:T(8,128)(2,1)} %get-tuple-element.242) | copy-start | bytes 7864324
  558.9 81.9 %copy-start.11 = (bf16[10240,128]{1,0:T(8,128)(2,1)S(1)}, bf16[10240,128]{1,0:T(8,128)(2,1)}, u32[]{:S(2)}) copy-start(bf16[10240,128]{1,0:T(8,128)(2,1)} %get-tuple-element.244) | copy-start | bytes 7864324
  560.3 102.4 %collective-permute-start.24 = (bf16[640,128]{1,0:T(8,128)(2,1)S(1)}, bf16[640,128]{1,0:T(8,128)(2,1)S(1)}, u32[]{:S(2)}, u32[]{:S(2)}) collective-permute-start(bf16[640,128]{1,0:T(8,128)(2,1)S(1)} %get-tuple-element.394), channel_id=1, source_target_pairs={{0,1},{1,2},{2,3},{3,11},{11,10},{10,9},{9,8},{8,0},{4,5},{5,6},{6... | collective-permute-start | bytes 491528 | tf_op jit(solution)/shard_map/ppermute | solution.py:786
  595.7 67.0 %collective-permute-start.25 = (bf16[640,128]{1,0:T(8,128)(2,1)S(1)}, bf16[640,128]{1,0:T(8,128)(2,1)}, u32[]{:S(2)}, u32[]{:S(2)}) collective-permute-start(bf16[640,128]{1,0:T(8,128)(2,1)S(1)} %get-tuple-element.393), channel_id=1, source_target_pairs={{1,0},{2,1},{3,2},{11,3},{10,11},{9,10},{8,9},{0,8},{5,4},{6,5},{7... | collective-permute-start | bytes 491528 | tf_op jit(solution)/shard_map/ppermute | solution.py:786
  597.1 30.3 %collective-permute-start.18 = (bf16[1280,128]{1,0:T(8,128)(2,1)S(1)}, bf16[1280,128]{1,0:T(8,128)(2,1)S(1)}, u32[]{:S(2)}, u32[]{:S(2)}) collective-permute-start(bf16[1280,128]{1,0:T(8,128)(2,1)S(1)} %pad_maximum_fusion.9), channel_id=1, source_target_pairs={{0,1},{1,2},{2,3},{3,11},{11,10},{10,9},{9,8},{8,0},{4,5},{5,6},{6... | collective-permute-start | bytes 983048 | tf_op jit(solution)/shard_map/ppermute | solution.py:786
  612.0 28.7 %collective-permute-start.19 = (bf16[1280,128]{1,0:T(8,128)(2,1)S(1)}, bf16[1280,128]{1,0:T(8,128)(2,1)S(1)}, u32[]{:S(2)}, u32[]{:S(2)}) collective-permute-start(bf16[1280,128]{1,0:T(8,128)(2,1)S(1)} %pad_maximum_fusion.10), channel_id=1, source_target_pairs={{1,0},{2,1},{3,2},{11,3},{10,11},{9,10},{8,9},{0,8},{5,4},{6,5},{7... | collective-permute-start | bytes 983048 | tf_op jit(solution)/shard_map/ppermute | solution.py:786
  613.3 28.8 %collective-permute-start.14 = (bf16[1280,128]{1,0:T(8,128)(2,1)S(1)}, bf16[1280,128]{1,0:T(8,128)(2,1)S(1)}, u32[]{:S(2)}, u32[]{:S(2)}) collective-permute-start(bf16[1280,128]{1,0:T(8,128)(2,1)S(1)} %get-tuple-element.258), channel_id=1, source_target_pairs={{0,1},{1,2},{2,3},{3,11},{11,10},{10,9},{9,8},{8,0},{4,5},{5,6},{6... | collective-permute-start | bytes 983048 | tf_op jit(solution)/shard_map/ppermute | solution.py:786
  627.3 20.9 %collective-permute-start.15 = (bf16[1280,128]{1,0:T(8,128)(2,1)S(1)}, bf16[1280,128]{1,0:T(8,128)(2,1)S(1)}, u32[]{:S(2)}, u32[]{:S(2)}) collective-permute-start(bf16[1280,128]{1,0:T(8,128)(2,1)S(1)} %get-tuple-element.259), channel_id=1, source_target_pairs={{1,0},{2,1},{3,2},{11,3},{10,11},{9,10},{8,9},{0,8},{5,4},{6,5},{7... | collective-permute-start | bytes 983048 | tf_op jit(solution)/shard_map/ppermute | solution.py:786
  641.0 11.4 %collective-permute-start.20 = (bf16[1280,128]{1,0:T(8,128)(2,1)S(1)}, bf16[1280,128]{1,0:T(8,128)(2,1)S(1)}, u32[]{:S(2)}, u32[]{:S(2)}) collective-permute-start(bf16[1280,128]{1,0:T(8,128)(2,1)S(1)} %get-tuple-element.266), channel_id=1, source_target_pairs={{0,1},{1,2},{2,3},{3,11},{11,10},{10,9},{9,8},{8,0},{4,5},{5,6},{6... | collective-permute-start | bytes 983048 | tf_op jit(solution)/shard_map/ppermute | solution.py:786
  642.1 13.4 %collective-permute-start.21 = (bf16[1280,128]{1,0:T(8,128)(2,1)S(1)}, bf16[1280,128]{1,0:T(8,128)(2,1)S(1)}, u32[]{:S(2)}, u32[]{:S(2)}) collective-permute-start(bf16[1280,128]{1,0:T(8,128)(2,1)S(1)} %get-tuple-element.267), channel_id=1, source_target_pairs={{1,0},{2,1},{3,2},{11,3},{10,11},{9,10},{8,9},{0,8},{5,4},{6,5},{7... | collective-permute-start | bytes 983048 | tf_op jit(solution)/shard_map/ppermute | solution.py:786
  648.5 10.9 %collective-permute-start.16 = (bf16[1280,128]{1,0:T(8,128)(2,1)S(1)}, bf16[1280,128]{1,0:T(8,128)(2,1)S(1)}, u32[]{:S(2)}, u32[]{:S(2)}) collective-permute-start(bf16[1280,128]{1,0:T(8,128)(2,1)S(1)} %get-tuple-element.260), channel_id=1, source_target_pairs={{0,1},{1,2},{2,3},{3,11},{11,10},{10,9},{9,8},{8,0},{4,5},{5,6},{6... | collective-permute-start | bytes 983048 | tf_op jit(solution)/shard_map/ppermute | solution.py:786
  652.4 10.2 %collective-permute-start.17 = (bf16[1280,128]{1,0:T(8,128)(2,1)S(1)}, bf16[1280,128]{1,0:T(8,128)(2,1)S(1)}, u32[]{:S(2)}, u32[]{:S(2)}) collective-permute-start(bf16[1280,128]{1,0:T(8,128)(2,1)S(1)} %get-tuple-element.261), channel_id=1, source_target_pairs={{1,0},{2,1},{3,2},{11,3},{10,11},{9,10},{8,9},{0,8},{5,4},{6,5},{7... | collective-permute-start | bytes 983048 | tf_op jit(solution)/shard_map/ppermute | solution.py:786
  656.5 10.2 %collective-permute-start.22 = (bf16[1280,128]{1,0:T(8,128)(2,1)}, bf16[1280,128]{1,0:T(8,128)(2,1)}, u32[]{:S(2)}, u32[]{:S(2)}) collective-permute-start(bf16[1280,128]{1,0:T(8,128)(2,1)} %get-tuple-element.268), channel_id=1, source_target_pairs={{0,1},{1,2},{2,3},{3,11},{11,10},{10,9},{9,8},{8,0},{4,5},{5,6},{6... | collective-permute-start | bytes 983048 | tf_op jit(solution)/shard_map/ppermute | solution.py:786
  659.4 11.4 %collective-permute-start.23 = (bf16[1280,128]{1,0:T(8,128)(2,1)}, bf16[1280,128]{1,0:T(8,128)(2,1)}, u32[]{:S(2)}, u32[]{:S(2)}) collective-permute-start(bf16[1280,128]{1,0:T(8,128)(2,1)} %get-tuple-element.269), channel_id=1, source_target_pairs={{1,0},{2,1},{3,2},{11,3},{10,11},{9,10},{8,9},{0,8},{5,4},{6,5},{7... | collective-permute-start | bytes 983048 | tf_op jit(solution)/shard_map/ppermute | solution.py:786
  662.8 18.1 %copy-start.4 = (f32[640,1152]{1,0:T(8,128)S(1)}, f32[640,1152]{1,0:T(8,128)}, u32[]{:S(2)}) copy-start(f32[640,1152]{1,0:T(8,128)} %get-tuple-element.234.hidden_ref) | copy-start | bytes 8847364
  664.1 9.8 %collective-permute-start.26 = (bf16[1280,128]{1,0:T(8,128)(2,1)S(1)}, bf16[1280,128]{1,0:T(8,128)(2,1)S(1)}, u32[]{:S(2)}, u32[]{:S(2)}) collective-permute-start(bf16[1280,128]{1,0:T(8,128)(2,1)S(1)} %pad_maximum_fusion.11), channel_id=1, source_target_pairs={{0,1},{1,2},{2,3},{3,11},{11,10},{10,9},{9,8},{8,0},{4,5},{5,6},{6... | collective-permute-start | bytes 983048 | tf_op jit(solution)/shard_map/ppermute | solution.py:786
  665.1 11.7 %collective-permute-start.27 = (bf16[1280,128]{1,0:T(8,128)(2,1)S(1)}, bf16[1280,128]{1,0:T(8,128)(2,1)S(1)}, u32[]{:S(2)}, u32[]{:S(2)}) collective-permute-start(bf16[1280,128]{1,0:T(8,128)(2,1)S(1)} %pad_maximum_fusion.12), channel_id=1, source_target_pairs={{1,0},{2,1},{3,2},{11,3},{10,11},{9,10},{8,9},{0,8},{5,4},{6,5},{7... | collective-permute-start | bytes 983048 | tf_op jit(solution)/shard_map/ppermute | solution.py:786
  678.1 9.9 %collective-permute-start.28 = (bf16[1280,128]{1,0:T(8,128)(2,1)S(1)}, bf16[1280,128]{1,0:T(8,128)(2,1)S(1)}, u32[]{:S(2)}, u32[]{:S(2)}) collective-permute-start(bf16[1280,128]{1,0:T(8,128)(2,1)S(1)} %get-tuple-element.283), channel_id=1, source_target_pairs={{0,1},{1,2},{2,3},{3,11},{11,10},{10,9},{9,8},{8,0},{4,5},{5,6},{6... | collective-permute-start | bytes 983048 | tf_op jit(solution)/shard_map/ppermute | solution.py:786
  679.2 8.7 %collective-permute-start.29 = (bf16[1280,128]{1,0:T(8,128)(2,1)S(1)}, bf16[1280,128]{1,0:T(8,128)(2,1)S(1)}, u32[]{:S(2)}, u32[]{:S(2)}) collective-permute-start(bf16[1280,128]{1,0:T(8,128)(2,1)S(1)} %get-tuple-element.284), channel_id=1, source_target_pairs={{1,0},{2,1},{3,2},{11,3},{10,11},{9,10},{8,9},{0,8},{5,4},{6,5},{7... | collective-permute-start | bytes 983048 | tf_op jit(solution)/shard_map/ppermute | solution.py:786
  680.8 11.2 %copy-start.18 = (bf16[1280,384]{1,0:T(8,128)(2,1)S(1)}, bf16[1280,384]{1,0:T(8,128)(2,1)}, u32[]{:S(2)}) copy-start(bf16[1280,384]{1,0:T(8,128)(2,1)} %get-tuple-element.289) | copy-start | bytes 2949124
  690.0 10.0 %collective-permute-start.30 = (bf16[1280,128]{1,0:T(8,128)(2,1)}, bf16[1280,128]{1,0:T(8,128)(2,1)}, u32[]{:S(2)}, u32[]{:S(2)}) collective-permute-start(bf16[1280,128]{1,0:T(8,128)(2,1)} %get-tuple-element.285), channel_id=1, source_target_pairs={{0,1},{1,2},{2,3},{3,11},{11,10},{10,9},{9,8},{8,0},{4,5},{5,6},{6... | collective-permute-start | bytes 983048 | tf_op jit(solution)/shard_map/ppermute | solution.py:786
  690.3 9.6 %collective-permute-start.31 = (bf16[1280,128]{1,0:T(8,128)(2,1)}, bf16[1280,128]{1,0:T(8,128)(2,1)}, u32[]{:S(2)}, u32[]{:S(2)}) collective-permute-start(bf16[1280,128]{1,0:T(8,128)(2,1)} %get-tuple-element.286), channel_id=1, source_target_pairs={{1,0},{2,1},{3,2},{11,3},{10,11},{9,10},{8,9},{0,8},{5,4},{6,5},{7... | collective-permute-start | bytes 983048 | tf_op jit(solution)/shard_map/ppermute | solution.py:786
  696.0 7.4 all-to-all-start.6
  703.4 11.5 %copy-start.5 = (bf16[2,640,1152]{2,1,0:T(8,128)(2,1)}, bf16[2,640,1152]{2,1,0:T(8,128)(2,1)S(1)}, u32[]{:S(2)}) copy-start(bf16[2,640,1152]{2,1,0:T(8,128)(2,1)S(1)} %all-to-all-done.6.query_ref) | copy-start | bytes 8847364
  710.0 23.4 %all-to-all-start.8 = ((bf16[4,640,288]{1,2,0:T(8,128)(2,1)}), bf16[4,640,288]{1,2,0:T(8,128)(2,1)}, u32[]{:S(2)}, u32[]{:S(2)}) async-start(bf16[4,640,288]{1,2,0:T(8,128)(2,1)} %bitcast.210), calls=%async_computation.9 | async-start | bytes 2949120 | tf_op jit(solution)/shard_map/all_to_all | solution.py:889
  714.3 109.4 %reduce-scatter.7.cloned.1.call-start = ((), (), s32[]{:S(2)}) async-start(), calls=%async_computation.15 | async-start | bytes 3760128
  745.1 25.8 %copy-start.9 = (bf16[288,2304]{1,0:T(8,128)(2,1)S(1)}, bf16[288,2304]{1,0:T(8,128)(2,1)}, u32[]{:S(2)}) copy-start(bf16[288,2304]{1,0:T(8,128)(2,1)} %reduce-scatter.5.cloned.1.call-done) | copy-start | bytes 3981316
  748.5 32.0 %collective-permute-start.32 = (bf16[8,288,512]{2,1,0:T(8,128)(2,1)}, bf16[8,288,512]{2,1,0:T(8,128)(2,1)}, u32[]{:S(2)}, u32[]{:S(2)}) collective-permute-start(bf16[8,288,512]{2,1,0:T(8,128)(2,1)} %dynamic-slice_bitcast_fusion), channel_id=1, source_target_pairs={{0,4},{4,0},{1,5},{5,1},{2,6},{6,2},{3,7},{7,3},{8,12},{12,8},{9,1... | collective-permute-start | bytes 7077896 | tf_op jit(solution)/shard_map/ppermute | solution.py:990
  752.9 19.7 %copy-start.13 = (bf16[4,640,288]{2,1,0:T(8,128)(2,1)S(1)}, bf16[4,640,288]{2,1,0:T(8,128)(2,1)}, u32[]{:S(2)}) copy-start(bf16[4,640,288]{2,1,0:T(8,128)(2,1)} %get-tuple-element.298) | copy-start | bytes 4423684
  752.9 2.1 collective-permute-start.33
  756.8 25.2 %collective-permute-start.35 = (bf16[144,512]{1,0:T(8,128)(2,1)}, bf16[144,512]{1,0:T(8,128)(2,1)S(1)}, u32[]{:S(2)}, u32[]{:S(2)}) collective-permute-start(bf16[144,512]{1,0:T(8,128)(2,1)} %get-tuple-element.303), channel_id=1, source_target_pairs={{1,0},{2,1},{3,2},{11,3},{10,11},{9,10},{8,9},{0,8},{5,4},{6,5},{7... | collective-permute-start | bytes 442376 | tf_op jit(solution)/shard_map/ppermute | solution.py:786
  775.1 38.1 %all-to-all-start.9 = ((bf16[4,640,288]{1,2,0:T(8,128)(2,1)}), bf16[4,640,288]{1,2,0:T(8,128)(2,1)S(1)}, u32[]{:S(2)}, u32[]{:S(2)}) async-start(bf16[4,640,288]{1,2,0:T(8,128)(2,1)} %copy.108), calls=%async_computation.10 | async-start | bytes 2949120 | tf_op jit(solution)/shard_map/all_to_all | solution.py:889
  778.8 22.1 %collective-permute-start.34 = (bf16[144,512]{1,0:T(8,128)(2,1)S(1)}, bf16[144,512]{1,0:T(8,128)(2,1)S(1)}, u32[]{:S(2)}, u32[]{:S(2)}) collective-permute-start(bf16[144,512]{1,0:T(8,128)(2,1)S(1)} %copy-done.20), channel_id=1, source_target_pairs={{0,1},{1,2},{2,3},{3,11},{11,10},{10,9},{9,8},{8,0},{4,5},{5,6},{6... | collective-permute-start | bytes 442376 | tf_op jit(solution)/shard_map/ppermute | solution.py:786
  801.0 8.6 %collective-permute-start.36 = (bf16[288,512]{1,0:T(8,128)(2,1)S(1)}, bf16[288,512]{1,0:T(8,128)(2,1)S(1)}, u32[]{:S(2)}, u32[]{:S(2)}) collective-permute-start(bf16[288,512]{1,0:T(8,128)(2,1)S(1)} %pad_maximum_fusion.13), channel_id=1, source_target_pairs={{0,1},{1,2},{2,3},{3,11},{11,10},{10,9},{9,8},{8,0},{4,5},{5,6},{6... | collective-permute-start | bytes 884744 | tf_op jit(solution)/shard_map/ppermute | solution.py:786
  801.1 8.6 %collective-permute-start.37 = (bf16[288,512]{1,0:T(8,128)(2,1)S(1)}, bf16[288,512]{1,0:T(8,128)(2,1)S(1)}, u32[]{:S(2)}, u32[]{:S(2)}) collective-permute-start(bf16[288,512]{1,0:T(8,128)(2,1)S(1)} %pad_maximum_fusion.14), channel_id=1, source_target_pairs={{1,0},{2,1},{3,2},{11,3},{10,11},{9,10},{8,9},{0,8},{5,4},{6,5},{7... | collective-permute-start | bytes 884744 | tf_op jit(solution)/shard_map/ppermute | solution.py:786
  811.2 7.7 collective-permute-start.38
  811.8 8.4 %collective-permute-start.39 = (bf16[288,512]{1,0:T(8,128)(2,1)S(1)}, bf16[288,512]{1,0:T(8,128)(2,1)S(1)}, u32[]{:S(2)}, u32[]{:S(2)}) collective-permute-start(bf16[288,512]{1,0:T(8,128)(2,1)S(1)} %get-tuple-element.307), channel_id=1, source_target_pairs={{1,0},{2,1},{3,2},{11,3},{10,11},{9,10},{8,9},{0,8},{5,4},{6,5},{7... | collective-permute-start | bytes 884744 | tf_op jit(solution)/shard_map/ppermute | solution.py:786
  821.7 7.1 collective-permute-start.40
  823.5 6.7 collective-permute-start.41
  (19 other events, 63.1 us)
Sparse Core Ops, SparseCore 0:
  10.3 59.4 all-gather.2
  71.4 214.6 all-gather.4
  389.4 259.4 reduce-scatter.4
  719.2 72.3 reduce-scatter.6
